TPU v7x, 256 devices: a whole 4x4x8 slice. The times are simulated.
256 devices in a mesh: node: 32 (over z, y), local: 8 (over x, core).
Axes of the slice: x: 4, y: 4, z: 8, core: 2. Of those that a mesh axis runs over, the one named last changes fastest.
Arguments:
- tokens: bfloat16 [32768, 7168], P(('node', 'local')), may hold values from -6 to 6
- w_gate: bfloat16 [32, 7168, 1024], P('node', None, 'local'), may hold values from -0.0625 to 0.0625
- w_up: bfloat16 [32, 7168, 1024], P('node', None, 'local'), may hold values from -0.0625 to 0.0625
- w_down: bfloat16 [32, 1024, 7168], P('node', 'local'), may hold values from -0.1875 to 0.1875
- chosen: int32 [32, 384], replicated, may hold values from 0 to 32767, as said below
- counts: int32 [32], replicated, may hold values from 3 to 384, as said below
- gates: float32 [32, 384], replicated, may hold values from 0.2 to 1
Outputs:
- mixed: bfloat16 [32768, 7168], P(('node', 'local'))
Inputs may be any that keep to these rules, and one draw needn't show every extreme that they name: `chosen`: each expert's list holds distinct tokens; in each list at most 3 entries lie in one device's block of 128 consecutive tokens, and for every expert some block holds exactly 3 live entries. `counts`: some expert has exactly 384 live entries.
All inputs are finite; a program needn't handle non-finite values.
Results may differ from a plain program's by a relative error of at most 0.014.
Values may be sent and summed in bfloat16 or wider, within the bound.
No kernel may reach another device: no remote copies, remote signals or barrier semaphores. Data moves between devices by JAX's collectives and lax.ppermute only.
A program may use at most 128 MiB of HBM per device.

v0:
```python
import jax
import jax.numpy as jnp
from jax import lax
from jax.sharding import Mesh
from jax.sharding import PartitionSpec as P

SLOT = 3
LOCAL = ("local_0", "local_1")
NODE_LOCAL = ("node", "local_0", "local_1")


def laid_out(parts, dim):
    parts = jnp.moveaxis(parts, 0, dim)
    shape = parts.shape
    return parts.reshape(*shape[:dim], shape[dim] * shape[dim + 1], *shape[dim + 2 :])


def all_blocks(value, axes, order):
    parts = value[None]
    for k in order:
        parts = lax.all_gather(parts, axes[k], axis=0, tiled=True)
    held = [lax.axis_size(axes[k]) for k in reversed(order)]
    parts = parts.reshape(*held, *value.shape)
    turned = sorted(range(len(order)), key=lambda place: order[len(order) - 1 - place])
    return parts.transpose(*turned, *range(len(order), parts.ndim)).reshape(-1, *value.shape)


def whole_of(value, axes, order, dim):
    return laid_out(all_blocks(value, axes, order), dim)


def split_up(value, dim, peers):
    shape = value.shape
    parts = value.reshape(*shape[:dim], peers, shape[dim] // peers, *shape[dim + 1 :])
    return jnp.moveaxis(parts, dim, 0)


def joined_exchange(value, axis, axes, splits, concats):
    sizes = [lax.axis_size(a) for a in axes]
    parts = split_up(value, splits[0], sizes[0])
    parts = jnp.moveaxis(split_up(parts, splits[1] + 1, sizes[1]), 0, 1)
    inside = parts.shape[2:]
    parts = parts.reshape(-1, *inside)
    parts = lax.all_to_all(parts, axis, split_axis=0, concat_axis=0, tiled=True)
    parts = laid_out(parts.reshape(*sizes, *inside), concats[0] + 1)
    return laid_out(parts, concats[1])


def shards(tokens, w_gate, w_up, w_down, chosen, counts, gates):
    tok_dev = tokens.shape[0]
    width = tokens.shape[1]
    n_node = lax.axis_size("node")
    n_local = lax.axis_size(LOCAL)
    devices = n_node * n_local
    cap = chosen.shape[1]
    experts = chosen.shape[0]
    myself = lax.axis_index("node") * n_local + lax.axis_index(LOCAL)
    live = jnp.arange(cap, dtype=jnp.int32)[None, :] < counts[:, None]
    owner = chosen // tok_dev
    mine = live & (owner == myself)
    rank = jnp.cumsum(mine.astype(jnp.int32), axis=1) - 1
    select = (
        mine[:, :, None] & (rank[:, :, None] == jnp.arange(SLOT, dtype=jnp.int32)[None, None, :])
    ).astype(jnp.int32)
    position = chosen - owner * tok_dev
    token_slot = jnp.sum(select * position[:, :, None], axis=1)
    present = jnp.sum(select, axis=1)
    outgoing = tokens[token_slot.reshape(-1)].reshape(experts, SLOT, width)
    outgoing = outgoing * present[:, :, None].astype(jnp.bfloat16)
    expert = lax.axis_index("node")
    picked = lax.dynamic_index_in_dim(chosen, expert, 0, keepdims=False)
    count = lax.dynamic_index_in_dim(counts, expert, 0, keepdims=False)
    weight = lax.dynamic_index_in_dim(gates, expert, 0, keepdims=False)
    valid = jnp.arange(cap, dtype=jnp.int32) < count
    holder = picked // tok_dev
    member = (
        (holder[:, None] == jnp.arange(devices, dtype=jnp.int32)[None, :]) & valid[:, None]
    ).astype(jnp.int32)
    order_in = jnp.sum(member * jnp.cumsum(member, axis=0), axis=1) - 1
    column = holder * SLOT + order_in
    table = jnp.sum(
        jnp.where(
            valid[:, None]
            & (column[:, None] == jnp.arange(devices * SLOT, dtype=jnp.int32)[None, :]),
            weight[:, None],
            jnp.float32(0.0),
        ),
        axis=0,
    )
    table = table.reshape(n_node, n_local, SLOT).transpose(1, 0, 2)
    gate_mat = w_gate[0]
    up_mat = w_up[0]
    down_mat = w_down[0]
    ff_dev = gate_mat.shape[1]
    arrived = lax.all_to_all(outgoing, "node", split_axis=0, concat_axis=0, tiled=True)
    piece = lax.all_gather(arrived[None], LOCAL, axis=0, tiled=True)
    flat = piece.reshape(-1, width)
    gate_val = jnp.dot(flat, gate_mat, preferred_element_type=jnp.float32)
    up_val = jnp.dot(flat, up_mat, preferred_element_type=jnp.float32)
    hidden = (jax.nn.silu(gate_val) * up_val).astype(jnp.bfloat16)
    partial_value = hidden.reshape(piece.shape[0], n_node, SLOT, ff_dev)
    groups = whole_of(partial_value[None], LOCAL, (0, 1), 0)
    row_count = n_local * n_node * SLOT
    groups = groups.reshape(n_local, row_count, ff_dev)
    down_block = lax.all_to_all(down_mat, LOCAL, split_axis=1, concat_axis=0, tiled=True)
    scale_rows = table.reshape(row_count)
    block_width = down_block.shape[1]
    answer = jnp.zeros((row_count, block_width), jnp.float32)
    for group in range(n_local):
        low = group * ff_dev
        down_val = jnp.dot(
            groups[group], down_block[low : low + ff_dev], preferred_element_type=jnp.float32
        )
        part = (scale_rows[:, None] * down_val).astype(jnp.bfloat16)
        answer = answer + part.astype(jnp.float32)
    answer = answer.astype(jnp.bfloat16).reshape(n_local, n_node, SLOT, block_width)
    returned = joined_exchange(answer, NODE_LOCAL, ("node", LOCAL), (1, 0), (1, 3))
    answers = returned[0].reshape(experts * SLOT, width)
    placing = (jnp.arange(tok_dev, dtype=jnp.int32)[:, None] == token_slot.reshape(-1)[None, :]) & (
        present.reshape(-1)[None, :] > 0
    )
    mixed = jnp.dot(placing.astype(jnp.bfloat16), answers, preferred_element_type=jnp.float32)
    return mixed.astype(jnp.bfloat16)


def solution(mesh):
    split = Mesh(mesh.devices.reshape(mesh.shape["node"], 4, 2), ("node", "local_0", "local_1"))
    in_specs = (
        P(NODE_LOCAL, None),
        P("node", None, LOCAL),
        P("node", None, LOCAL),
        P("node", LOCAL, None),
        P(),
        P(),
        P(),
    )
    out_specs = P(NODE_LOCAL, None)
    return jax.shard_map(
        shards, mesh=split, in_specs=in_specs, out_specs=out_specs, check_vma=False
    )
```

profile of v0, /device:TPU:1, one launch (start us, length us, event | category | flops | bytes accessed | tf_op | source)
XLA Modules:
  0.0 324.4 jit_solution(6535636557275334973)
XLA Ops:
  13.4 55.1 %all_to_all.26 = bf16[32,3,7168]{2,1,0:T(4,128)(2,1)S(1)} all-to-all(bf16[32,3,7168]{2,1,0:T(4,128)(2,1)S(1)} %broadcast_multiply_fusion), channel_id=1, replica_groups=mesh['node'=32,'local_0'=4,'local_1'=2] {'node'}, dimensions={0} | all-to-all | bytes 2752512 | tf_op jit(solution)/shard_map/all_to_all | solution.py:95
  68.5 1.6 copy.64
  70.1 3.9 %copy.68 = bf16[1,128,7168]{1,2,0:T(8,128)(2,1)} copy(bf16[1,128,7168]{2,1,0:T(8,128)(2,1)} %param.10) | data formatting | bytes 3670016 | tf_op args[3]
  74.0 7.9 %all-to-all-start.1 = ((bf16[128,8,896]{0,2,1:T(8,128)(2,1)}), bf16[128,8,896]{0,2,1:T(8,128)(2,1)}, u32[]{:S(2)}, u32[]{:S(2)}) async-start(bf16[128,8,896]{0,2,1:T(8,128)(2,1)} %bitcast.11), calls=%async_computation.1 | async-start | bytes 3670016 | tf_op jit(solution)/shard_map/all_to_all | solution.py:105
  83.3 68.6 %all-gather.6.cloned.1.call-done = bf16[256,3,7168]{2,0,1:T(8,128)(2,1)} async-done(((bf16[32,3,7168]{2,0,1:T(8,128)(2,1)}), bf16[256,3,7168]{2,0,1:T(8,128)(2,1)}) %all-gather.6.cloned.1.call-update) | async-done | bytes 11010064 | tf_op jit(solution)/shard_map/all_gather | solution.py:96
  151.9 17.8 %copy.65 = bf16[256,3,7168]{2,1,0:T(4,128)(2,1)} copy(bf16[256,3,7168]{2,0,1:T(8,128)(2,1)} %all-gather.6.cloned.1.call-done) | data formatting | bytes 22020096 | tf_op jit(solution)/shard_map/all_gather | solution.py:96
  169.7 24.9 %reshape.182 = bf16[768,7168]{1,0:T(8,128)(2,1)} reshape(bf16[256,3,7168]{2,1,0:T(4,128)(2,1)} %copy.65) | data formatting | bytes 22020096 | tf_op jit(solution)/shard_map/reshape | solution.py:97
  194.6 7.0 %fusion.2 = f32[768,128]{1,0:T(8,128)S(1)} fusion(bf16[768,7168]{1,0:T(8,128)(2,1)} %reshape.182, bf16[1,7168,128]{2,1,0:T(8,128)(2,1)} %param.8), kind=kOutput, calls=%fused_computation.13 | convolution fusion | flops 1409286144 | bytes 13238272 | tf_op jit(solution)/shard_map/dot_general | solution.py:98
  203.0 3.0 fusion.8
  206.1 12.0 %all_gather.10 = bf16[4,1,8,32,3,128]{5,3,4,2,1,0:T(8,128)(2,1)} all-gather(bf16[1,1,8,32,3,128]{5,3,4,2,1,0:T(8,128)(2,1)S(1)} %copy.66), channel_id=1, replica_groups=mesh['node'=32,'local_0'=4,'local_1'=2] {'local_0'}, dimensions={0}, use_global_device_ids=true | all-gather | bytes 983040 | tf_op jit(solution)/shard_map/all_gather | solution.py:21
  222.0 9.7 %all-gather.4.cloned.1.call-done = bf16[8,1,8,32,3,128]{5,3,4,2,1,0:T(8,128)(2,1)} async-done(((bf16[4,1,8,32,3,128]{5,3,4,2,1,0:T(8,128)(2,1)}), bf16[8,1,8,32,3,128]{5,3,4,2,1,0:T(8,128)(2,1)}) %all-gather.4.cloned.1.call-update) | async-done | bytes 1572880 | tf_op jit(solution)/shard_map/all_gather | solution.py:21
  231.7 3.0 copy.67
  234.8 3.3 %fusion.50 = (bf16[1,768,128]{2,0,1:T(2,128)(2,1)}, bf16[1,768,128]{2,0,1:T(2,128)(2,1)S(1)}, bf16[1,768,128]{2,0,1:T(2,128)(2,1)S(1)}, bf16[1,768,128]{2,0,1:T(...) fusion(bf16[8,768,128]{2,0,1:T(8,128)(2,1)S(1)} %bitcast.128), kind=kLoop, calls=%fused_computation.106 | loop fusion | bytes 3145728 | tf_op jit(solution)/shard_map/slice | solution.py:112
  238.1 1.7 multiply_convert_fusion.3
  239.8 1.5 multiply_convert_fusion.4
  241.2 1.5 multiply_convert_fusion.5
  242.7 1.5 multiply_convert_fusion.6
  244.2 1.5 multiply_convert_fusion.2
  245.7 1.5 multiply_convert_fusion.1
  248.7 2.6 add_convert_fusion
  253.1 2.4 copy.78
  255.5 12.4 %all-to-all-start.2 = ((bf16[256,1,1,3,896]{4,3,2,1,0:T(4,128)(2,1)}), bf16[256,1,1,3,896]{4,3,2,1,0:T(4,128)(2,1)S(1)}, u32[]{:S(2)}, u32[]{:S(2)}) async-start(bf16[256,1,1,3,896]{4,3,2,1,0:T(4,128)(2,1)} %copy.78), calls=%async_computation.2 | async-start | bytes 3670016 | tf_op jit(solution)/shard_map/all_to_all | solution.py:44
  268.2 47.0 %all-to-all-done.2 = bf16[256,1,1,3,896]{4,3,2,1,0:T(4,128)(2,1)S(1)} async-done(((bf16[256,1,1,3,896]{4,3,2,1,0:T(4,128)(2,1)}), bf16[256,1,1,3,896]{4,3,2,1,0:T(4,128)(2,1)S(1)}, u32[]{:S(2)}, u32[]{:S(2)}) %all-to-all-start.2) | async-done | bytes 1376288 | tf_op jit(solution)/shard_map/all_to_all | solution.py:44
  315.7 1.8 convolution_convert_fusion
  (68 shorter events, 17.4 us)
Async XLA Ops:
  6.5 3.5 %copy-start = (bf16[128,7168]{1,0:T(8,128)(2,1)S(1)}, bf16[128,7168]{1,0:T(8,128)(2,1)}, u32[]{:S(2)}) copy-start(bf16[128,7168]{1,0:T(8,128)(2,1)} %param.7) | copy-start | bytes 5505028
  6.5 145.4 %all-gather.6.cloned.1.call-start = ((), (), s32[]{:S(2)}) async-start(), calls=%async_computation.4 | async-start | bytes 12386304 | tf_op jit(solution)/shard_map/all_gather | solution.py:96
  74.0 7.9 %copy-start.6 = (s32[32]{0:T(128)S(1)}, s32[32]{0:T(128)}, u32[]{:S(2)}) copy-start(s32[32]{0:T(128)} %param.12) | copy-start | bytes 388
  74.0 164.1 %all-to-all-start.1 = ((bf16[128,8,896]{0,2,1:T(8,128)(2,1)}), bf16[128,8,896]{0,2,1:T(8,128)(2,1)}, u32[]{:S(2)}, u32[]{:S(2)}) async-start(bf16[128,8,896]{0,2,1:T(8,128)(2,1)} %bitcast.11), calls=%async_computation.1 | async-start | bytes 3670016 | tf_op jit(solution)/shard_map/all_to_all | solution.py:105
  81.9 149.8 %all-gather.4.cloned.1.call-start = ((), (), s32[]{:S(2)}) async-start(), calls=%async_computation.3 | async-start | bytes 2359296 | tf_op jit(solution)/shard_map/all_gather | solution.py:21
  194.6 7.8 %copy-start.2 = (bf16[768,7168]{1,0:T(8,128)(2,1)S(1)}, bf16[768,7168]{1,0:T(8,128)(2,1)}, u32[]{:S(2)}) copy-start(bf16[768,7168]{1,0:T(8,128)(2,1)} %reshape.182) | copy-start | bytes 33030148
  194.6 8.3 %copy-start.7 = (bf16[1,7168,128]{2,1,0:T(8,128)(2,1)S(1)}, bf16[1,7168,128]{2,1,0:T(8,128)(2,1)}, u32[]{:S(2)}) copy-start(bf16[1,7168,128]{2,1,0:T(8,128)(2,1)} %param.9) | copy-start | bytes 5505028
  238.1 3.2 copy-start.3
  238.1 1.7 copy-start.4
  245.7 3.0 copy-start.5
  255.5 59.8 %all-to-all-start.2 = ((bf16[256,1,1,3,896]{4,3,2,1,0:T(4,128)(2,1)}), bf16[256,1,1,3,896]{4,3,2,1,0:T(4,128)(2,1)S(1)}, u32[]{:S(2)}, u32[]{:S(2)}) async-start(bf16[256,1,1,3,896]{4,3,2,1,0:T(4,128)(2,1)} %copy.78), calls=%async_computation.2 | async-start | bytes 3670016 | tf_op jit(solution)/shard_map/all_to_all | solution.py:44
  315.4 2.1 copy-start.1
Sparse Core Ops, SparseCore 0:
  70.2 81.6 all-gather.5
  218.3 13.3 all-gather.3
where the time goes:
time: 326 us; the launch traced here: 324 us
  waiting for transfers between devices  125 us (38%)
  blocking collectives  67.1 us (21%)
  local copies, waits for them, and re-layouts  66.5 us (20%)
  matrix products  25 us (8%)
  starting transfers between devices  20.3 us (6%)
  between operations  13.8 us (4%)
  other arithmetic  6.37 us (2%)
    all_gather x1, waiting for transfers between devices, shards(): piece = lax.all_gather(arrived[None], LOCAL, axis=0, tiled=True)  68.6 us
    all_to_all x1, blocking collectives, shards(): lax.all_to_all(outgoing, 'node', split_axis=0, concat_axis=0, tiled=True)  55.1 us
    all_to_all x1, waiting for transfers between devices, joined_exchange(): parts = lax.all_to_all(parts, axis, split_axis=0, concat_axis=0, tiled=True)  47 us
    reshape x1, local copies, waits for them, and re-layouts, shards(): flat = piece.reshape(-1, width)  24.9 us
    all_gather x1, local copies, waits for them, and re-layouts, shards(): piece = lax.all_gather(arrived[None], LOCAL, axis=0, tiled=True)  17.8 us
    dot_general x8, matrix products, shards(): jnp.dot(groups[group], down_block[low:low + ff_dev], preferred_element_ty...  13.2 us
    all_to_all x1, starting transfers between devices, joined_exchange(): parts = lax.all_to_all(parts, axis, split_axis=0, concat_axis=0, tiled=True)  12.4 us
    all_gather x1, blocking collectives, all_blocks(): parts = lax.all_gather(parts, axes[k], axis=0, tiled=True)  12 us
  transfers between devices with their start and end apart: 4, of which 3 were waited for; matrix products, arithmetic and copies ran while one was open for 21% of the time, Pallas kernels for 0%

commit v1 on v0

v1 whole, which is shorter than its diff:
```python
import jax
import jax.numpy as jnp
from jax import lax
from jax.sharding import Mesh
from jax.sharding import PartitionSpec as P

SLOT = 3
LANE = 128
LOCAL = ("x", "core")
AXES = ("node", "x", "core")
BF16 = jnp.bfloat16


def shards(tokens, w_gate, w_up, w_down, chosen, counts, gates):
    tok_dev, width = tokens.shape
    n_node = lax.axis_size("node")
    n_local = lax.axis_size(LOCAL)
    devices = n_node * n_local
    experts, cap = chosen.shape
    cut = width // n_local
    tiles = cut // LANE
    expert = lax.axis_index("node")
    myself = expert * n_local + lax.axis_index(LOCAL)

    down_parts = w_down[0].reshape(-1, n_local, cut).transpose(1, 0, 2)
    down_block = lax.all_to_all(down_parts, LOCAL, split_axis=0, concat_axis=0, tiled=True)

    place = jnp.arange(cap, dtype=jnp.int32)[None, :]
    mine = (place < counts[:, None]) & (chosen // tok_dev == myself)
    position = chosen % tok_dev
    token_slot = []
    present = []
    rest = mine
    for _ in range(SLOT):
        first = jnp.min(jnp.where(rest, place, cap), axis=1)
        hit = place == first[:, None]
        token_slot.append(jnp.sum(jnp.where(hit, position, 0), axis=1))
        present.append(first < cap)
        rest = rest & ~hit
    token_slot = jnp.stack(token_slot, axis=1).reshape(-1)
    present = jnp.stack(present, axis=1).reshape(-1)

    placing = (jnp.arange(tok_dev, dtype=jnp.int32)[:, None] == token_slot[None, :]) & present[None, :]
    placing = placing.astype(BF16)
    rows = lax.dot_general(
        placing, tokens, (((0,), (0,)), ((), ())), preferred_element_type=jnp.float32
    ).astype(BF16)
    rows = rows.reshape(experts, SLOT, n_local, tiles, LANE)
    outgoing = rows.transpose(0, 2, 1, 3, 4).reshape(devices, SLOT, tiles, LANE)
    arrived = lax.all_to_all(outgoing, AXES, split_axis=0, concat_axis=0, tiled=True)

    picked = lax.dynamic_index_in_dim(chosen, expert, 0, keepdims=False)
    count = lax.dynamic_index_in_dim(counts, expert, 0, keepdims=False)
    weight = lax.dynamic_index_in_dim(gates, expert, 0, keepdims=False)
    entry = jnp.arange(cap, dtype=jnp.int32)
    live = entry < count
    holder = picked // tok_dev
    before = (holder[:, None] == holder[None, :]) & (entry[None, :] < entry[:, None])
    column = holder * SLOT + jnp.sum(before.astype(jnp.int32), axis=1)
    slots = jnp.arange(devices * SLOT, dtype=jnp.int32)
    spread = ((slots[:, None] == column[None, :]) & live[None, :]).astype(BF16)

    flat = arrived.reshape(devices * SLOT, cut)
    compact = lax.dot_general(
        spread, flat, (((0,), (0,)), ((), ())), preferred_element_type=jnp.float32
    ).astype(BF16)
    gathered = lax.all_gather(compact, LOCAL, axis=0, tiled=False)

    gate_mat = w_gate[0].reshape(n_local, cut, -1)
    up_mat = w_up[0].reshape(n_local, cut, -1)
    gate_val = jnp.einsum("kjd,kdf->jf", gathered, gate_mat, preferred_element_type=jnp.float32)
    up_val = jnp.einsum("kjd,kdf->jf", gathered, up_mat, preferred_element_type=jnp.float32)
    hidden = (jax.nn.silu(gate_val) * up_val).astype(BF16)
    groups = lax.all_gather(hidden, LOCAL, axis=0, tiled=False)

    down_val = jnp.einsum("kjf,kfd->jd", groups, down_block, preferred_element_type=jnp.float32)
    answer = (weight[:, None] * down_val).astype(BF16)
    back = jnp.dot(spread, answer, preferred_element_type=jnp.float32).astype(BF16)
    back = back.reshape(devices, SLOT, tiles, LANE)
    returned = lax.all_to_all(back, AXES, split_axis=0, concat_axis=0, tiled=True)

    answers = returned.reshape(experts, n_local, SLOT, cut).transpose(0, 2, 1, 3)
    answers = answers.reshape(experts * SLOT, width)
    mixed = jnp.dot(placing, answers, preferred_element_type=jnp.float32)
    return mixed.astype(BF16)


def solution(mesh):
    split = Mesh(mesh.devices.reshape(mesh.shape["node"], 4, 2), AXES)
    in_specs = (
        P(AXES, None),
        P("node", None, LOCAL),
        P("node", None, LOCAL),
        P("node", LOCAL, None),
        P(),
        P(),
        P(),
    )
    return jax.shard_map(
        shards, mesh=split, in_specs=in_specs, out_specs=P(AXES, None), check_vma=False
    )
```

time: 326 us -> 228 us (0.70)
  waiting for transfers between devices: 125 us -> 76.4 us
  local copies, waits for them, and re-layouts: 66.5 us -> 25.3 us
  matrix products: 25 us -> 16.9 us
    all_gather x2 -> x1, waiting for transfers between devices: 78.3 us -> 37.1 us  [shards(): gathered = lax.all_gather(compact, LOCAL, axis=0, tiled=False)]
    all_gather x1 -> x0, local copies, waits for them, and re-layouts: 17.8 us -> none  [shards(): piece = lax.all_gather(arrived[None], LOCAL, axis=0, tiled=True)]
    reshape x6 -> x4, local copies, waits for them, and re-layouts: 29.3 us -> 13.1 us  [the longest x1 4.81 us: shards(): returned.reshape(experts, n_local, SLOT, cut).transpose(0, 2, 1, 3)]
    dot_general x11 -> x6, matrix products: 25 us -> 16.9 us  [the longest x1 4.34 us: shards(): jnp.dot(spread, answer, preferred_element_type=jnp.float32).astype(BF16)]
    all_to_all x2, waiting for transfers between devices: 47 us -> 39.3 us  [the longest x1 39.3 us: shards(): lax.all_to_all(outgoing, AXES, split_axis=0, concat_axis=0, tiled=True)]
    transpose x2 -> x3, local copies, waits for them, and re-layouts: 1.04 us -> 5.83 us  [the longest x1 3.83 us: shards(): down_parts = w_down[0].reshape(-1, n_local, cut).transpose(1, 0, 2)]
    all_gather x1, blocking collectives: 12 us -> 15.7 us  [shards(): groups = lax.all_gather(hidden, LOCAL, axis=0, tiled=False)]
    slice x2 -> x0, local copies, waits for them, and re-layouts: 3.53 us -> none  [the longest x1 3.31 us: shards(): groups[group]]
  transfers between devices with their start and end apart: 4 -> 3, of which waited for: 3 -> 2; matrix products, arithmetic and copies ran while one was open for 21% -> 7% of each run, Pallas kernels for 0% -> 0%
where the time goes in v1:
time: 228 us; the launch traced here: 227 us
  waiting for transfers between devices  76.4 us (34%)
  blocking collectives  70.1 us (31%)
  local copies, waits for them, and re-layouts  25.3 us (11%)
  starting transfers between devices  21.3 us (9%)
  matrix products  16.9 us (7%)
  between operations  13.5 us (6%)
  other arithmetic  3.48 us (2%)
    all_to_all x1, blocking collectives, shards(): lax.all_to_all(back, AXES, split_axis=0, concat_axis=0, tiled=True)  54.4 us
    all_to_all x1, waiting for transfers between devices, shards(): lax.all_to_all(outgoing, AXES, split_axis=0, concat_axis=0, tiled=True)  39.3 us
    all_gather x1, waiting for transfers between devices, shards(): gathered = lax.all_gather(compact, LOCAL, axis=0, tiled=False)  37.1 us
    all_to_all x1, starting transfers between devices, shards(): lax.all_to_all(outgoing, AXES, split_axis=0, concat_axis=0, tiled=True)  15.7 us
    all_gather x1, blocking collectives, shards(): groups = lax.all_gather(hidden, LOCAL, axis=0, tiled=False)  15.7 us
    all_to_all x1, starting transfers between devices, shards(): lax.all_to_all(down_parts, LOCAL, split_axis=0, concat_axis=0, tiled=True)  5.59 us
    reshape x1, local copies, waits for them, and re-layouts, shards(): returned.reshape(experts, n_local, SLOT, cut).transpose(0, 2, 1, 3)  4.81 us
    unnamed x10, local copies, waits for them, and re-layouts  4.57 us
  transfers between devices with their start and end apart: 3, of which 2 were waited for; matrix products, arithmetic and copies ran while one was open for 7% of the time, Pallas kernels for 0%

profile of v1, /device:TPU:1, one launch (start us, length us, event | category | flops | bytes accessed | tf_op | source)
XLA Modules:
  0.0 227.0 jit_solution(17426399589439806114)
XLA Ops:
  6.5 1.1 select_reduce_fusion.5
  8.8 3.2 %convolution_convert_fusion.1 = bf16[96,7168]{1,0:T(8,128)(2,1)} fusion(bf16[128,7168]{1,0:T(8,128)(2,1)} %param.7, s32[96]{0:T(128)S(1)} %eq.116, pred[96]{0:T(512)(128)(4,1)S(1)} %and.67), kind=kOutput, calls=%fused_computation.1 | convolution fusion | flops 176873472 | bytes 3211744 | tf_op jit(solution)/shard_map/dot_general | solution.py:45
  11.9 3.1 %reshape.86 = bf16[32,3,8,7,128]{4,3,2,1,0:T(8,128)(2,1)S(1)} reshape(bf16[96,7168]{1,0:T(8,128)(2,1)} %convolution_convert_fusion.1) | data formatting | bytes 2752512 | tf_op jit(solution)/shard_map/reshape | solution.py:48
  15.4 2.1 copy.33
  17.4 15.7 %all-to-all-start = ((bf16[256,3,7,128]{3,2,1,0:T(8,128)(2,1)}), bf16[256,3,7,128]{3,2,1,0:T(8,128)(2,1)S(1)}, u32[]{:S(2)}, u32[]{:S(2)}) async-start(bf16[256,3,7,128]{3,2,1,0:T(8,128)(2,1)} %copy.33), calls=%async_computation | async-start | bytes 3145728 | tf_op jit(solution)/shard_map/all_to_all | solution.py:50
  33.2 0.7 dynamic_slice.13
  33.8 0.7 iota_compare_fusion.7
  34.5 0.7 fusion.36
  35.5 39.3 %all-to-all-done = bf16[256,3,7,128]{3,2,1,0:T(8,128)(2,1)S(1)} async-done(((bf16[256,3,7,128]{3,2,1,0:T(8,128)(2,1)}), bf16[256,3,7,128]{3,2,1,0:T(8,128)(2,1)S(1)}, u32[]{:S(2)}, u32[]{:S(2)}) %all-to-all-start) | async-done | bytes 1376288 | tf_op jit(solution)/shard_map/all_to_all | solution.py:50
  74.8 1.7 fusion.5
  76.5 3.9 %copy.34 = bf16[1,128,7168]{1,2,0:T(8,128)(2,1)} copy(bf16[1,128,7168]{2,1,0:T(8,128)(2,1)} %param.10) | data formatting | bytes 3670016 | tf_op args[3]
  80.4 3.8 %copy.35 = bf16[8,128,896]{2,1,0:T(8,128)(2,1)} copy(bf16[8,128,896]{1,2,0:T(8,128)(2,1)} %bitcast.58) | data formatting | bytes 3670016 | tf_op jit(solution)/shard_map/transpose | solution.py:25
  84.2 5.6 %all-to-all-start.1 = ((bf16[8,128,896]{2,1,0:T(8,128)(2,1)}), bf16[8,128,896]{2,1,0:T(8,128)(2,1)}, u32[]{:S(2)}, u32[]{:S(2)}) async-start(bf16[8,128,896]{2,1,0:T(8,128)(2,1)} %copy.35), calls=%async_computation.1 | async-start | bytes 3670016 | tf_op jit(solution)/shard_map/all_to_all | solution.py:26
  89.8 0.7 dynamic-slice_reduce_fusion
  90.6 37.1 %all-gather.4.cloned.1.call-done = bf16[3072,896]{1,0:T(8,128)(2,1)} async-done(((bf16[384,896]{1,0:T(8,128)(2,1)}), bf16[3072,896]{1,0:T(8,128)(2,1)}) %all-gather.4.cloned.1.call-update) | async-done | bytes 5505040 | tf_op jit(solution)/shard_map/all_gather | solution.py:67
  127.7 4.3 %convolution_bitcast_fusion.2 = f32[384,128]{1,0:T(8,128)S(1)} fusion(bf16[8,384,896]{2,1,0:T(8,128)(2,1)} %bitcast.60, bf16[8,896,128]{2,1,0:T(8,128)(2,1)S(1)} %bitcast.57), kind=kOutput, calls=%fused_computation.15 | convolution fusion | flops 704643072 | bytes 7536640 | tf_op jit(solution)/shard_map/kjd,kdf->jf/dot_general | solution.py:71
  132.5 1.6 fusion.12
  134.0 15.7 %all-gather.1 = bf16[3072,128]{1,0:T(8,128)(2,1)S(1)} all-gather(bf16[384,128]{1,0:T(8,128)(2,1)S(1)} %fusion.12), channel_id=3, replica_groups=mesh['node'=32,'x'=4,'core'=2] {'x','core'}, dimensions={0}, use_global_device_ids=true | all-gather | bytes 884736 | tf_op jit(solution)/shard_map/all_gather | solution.py:74
  149.7 4.3 %convolution_convert_fusion.2 = bf16[768,896]{1,0:T(8,128)(2,1)} fusion(bf16[8,384,128]{2,1,0:T(8,128)(2,1)S(1)} %bitcast.66, bf16[8,128,896]{2,1,0:T(8,128)(2,1)} %all-to-all-done.1, f32[384]{0:T(512)S(1)} %dynamic-slice_reduce_fusion, s32[384]{0:T(512)S(1)} %add_reduce_fusion, pred[384]{0:T(512)(128)(4,1)S(1)} %iota_compare_fusion.7), kind=kOutput, calls=%fused_computation.2 | convolution fusion | flops 1235091456 | bytes 4001152 | tf_op jit(solution)/shard_map/dot_general | solution.py:78
  154.0 3.1 %reshape.89 = bf16[256,3,7,128]{3,2,1,0:T(8,128)(2,1)S(1)} reshape(bf16[768,896]{1,0:T(8,128)(2,1)} %convolution_convert_fusion.2) | data formatting | bytes 2752512 | tf_op jit(solution)/shard_map/reshape | solution.py:79
  157.1 54.4 %all_to_all.15 = bf16[256,3,7,128]{3,2,1,0:T(8,128)(2,1)} all-to-all(bf16[256,3,7,128]{3,2,1,0:T(8,128)(2,1)S(1)} %reshape.89), channel_id=1, replica_groups=mesh['node'=32,'x'=4,'core'=2] {'node','x','core'}, dimensions={0} | all-to-all | bytes 2752512 | tf_op jit(solution)/shard_map/all_to_all | solution.py:80
  211.5 4.8 %reshape.97 = bf16[32,8,3,896]{3,2,1,0:T(4,128)(2,1)} reshape(bf16[256,3,7,128]{3,2,1,0:T(8,128)(2,1)} %all_to_all.15) | data formatting | bytes 2752512 | tf_op jit(solution)/shard_map/reshape | solution.py:82
  216.3 1.7 copy.39
  218.3 1.9 convolution_convert_fusion
  (27 shorter events, 2.4 us)
Async XLA Ops:
  6.5 121.2 %copy-start = (bf16[1,7168,128]{2,1,0:T(8,128)(2,1)S(1)}, bf16[1,7168,128]{2,1,0:T(8,128)(2,1)}, u32[]{:S(2)}) copy-start(bf16[1,7168,128]{2,1,0:T(8,128)(2,1)} %param.8) | copy-start | bytes 5505028
  17.4 15.7 %copy-start.2 = (s32[32]{0:T(128)S(1)}, s32[32]{0:T(128)}, u32[]{:S(2)}) copy-start(s32[32]{0:T(128)} %param.12) | copy-start | bytes 388
  17.4 57.4 %all-to-all-start = ((bf16[256,3,7,128]{3,2,1,0:T(8,128)(2,1)}), bf16[256,3,7,128]{3,2,1,0:T(8,128)(2,1)S(1)}, u32[]{:S(2)}, u32[]{:S(2)}) async-start(bf16[256,3,7,128]{3,2,1,0:T(8,128)(2,1)} %copy.33), calls=%async_computation | async-start | bytes 3145728 | tf_op jit(solution)/shard_map/all_to_all | solution.py:50
  33.1 94.6 %all-gather.4.cloned.1.call-start = ((), (), s32[]{:S(2)}) async-start(), calls=%async_computation.3 | async-start | bytes 6193152 | tf_op jit(solution)/shard_map/all_gather | solution.py:67
  84.2 65.4 %all-to-all-start.1 = ((bf16[8,128,896]{2,1,0:T(8,128)(2,1)}), bf16[8,128,896]{2,1,0:T(8,128)(2,1)}, u32[]{:S(2)}, u32[]{:S(2)}) async-start(bf16[8,128,896]{2,1,0:T(8,128)(2,1)} %copy.35), calls=%async_computation.1 | async-start | bytes 3670016 | tf_op jit(solution)/shard_map/all_to_all | solution.py:26
  127.7 4.3 %copy-start.1 = (bf16[3072,896]{1,0:T(8,128)(2,1)S(1)}, bf16[3072,896]{1,0:T(8,128)(2,1)}, u32[]{:S(2)}) copy-start(bf16[3072,896]{1,0:T(8,128)(2,1)} %all-gather.4.cloned.1.call-done) | copy-start | bytes 16515076
  127.7 4.8 %copy-start.3 = (bf16[1,7168,128]{2,1,0:T(8,128)(2,1)S(1)}, bf16[1,7168,128]{2,1,0:T(8,128)(2,1)}, u32[]{:S(2)}) copy-start(bf16[1,7168,128]{2,1,0:T(8,128)(2,1)} %param.9) | copy-start | bytes 5505028
Sparse Core Ops, SparseCore 0:
  76.7 50.9 all-gather.3

commit v2 on v1

v2 whole, which is shorter than its diff:
```python
import functools

import jax
import jax.numpy as jnp
from jax import lax
from jax.experimental import pallas as pl
from jax.experimental.pallas import tpu as pltpu
from jax.sharding import Mesh
from jax.sharding import PartitionSpec as P

SLOT = 3
LANE = 128
LOCAL = ("x", "core")
AXES = ("node", "x", "core")
BF16 = jnp.bfloat16
F32 = jnp.float32
PARAMS = pltpu.CompilerParams(vmem_limit_bytes=40 * 2**20)
VMEM = pl.BlockSpec(memory_space=pltpu.VMEM)


def rows_of(tiles):
    return -(-tiles * SLOT // 2) * 2


def send_kernel(n_local, sel_ref, tok_ref, out_ref, held):
    experts = sel_ref.shape[0] // SLOT
    cut = tok_ref.shape[1] // n_local
    tiles = cut // LANE
    rows = rows_of(tiles)
    for k in range(n_local):
        part = tok_ref[:, k * cut : (k + 1) * cut]
        val = jnp.dot(sel_ref[...], part, preferred_element_type=F32)
        for t in range(tiles):
            for s in range(SLOT):
                at = pl.ds(k * rows + t * SLOT + s, experts, stride=n_local * rows)
                held[at, :] = val[s * experts : (s + 1) * experts, t * LANE : (t + 1) * LANE]
        for r in range(SLOT * tiles, rows):
            held[pl.ds(k * rows + r, experts, stride=n_local * rows), :] = jnp.zeros((experts, LANE), F32)
    out_ref[...] = held[...].astype(BF16)


def send(sel, tokens, n_local):
    shape = (sel.shape[0] // SLOT * n_local * rows_of(tokens.shape[1] // (n_local * LANE)), LANE)
    return pl.pallas_call(
        functools.partial(send_kernel, n_local),
        out_shape=jax.ShapeDtypeStruct(shape, BF16),
        in_specs=[VMEM, VMEM],
        out_specs=VMEM,
        scratch_shapes=[pltpu.VMEM(shape, F32)],
        compiler_params=PARAMS,
        name="send",
    )(sel, tokens)


def pack_kernel(tiles, column_ref, msg_ref, out_ref, held):
    rows = rows_of(tiles)
    devices = msg_ref.shape[0] // rows
    cap = column_ref.shape[0]
    held[...] = msg_ref[...].astype(F32)
    total = jnp.zeros(out_ref.shape, F32)
    for s in range(SLOT):
        flat = [held[pl.ds(t * SLOT + s, devices, stride=rows), :] for t in range(tiles)]
        flat = jnp.concatenate(flat, axis=1).astype(BF16)
        slot = lax.broadcasted_iota(jnp.int32, (cap, devices), 1) * SLOT + s
        hot = (slot == column_ref[...]).astype(F32).astype(BF16)
        total = total + jnp.dot(hot, flat, preferred_element_type=F32)
    out_ref[...] = total.astype(BF16)


def pack(column, msg, tiles):
    return pl.pallas_call(
        functools.partial(pack_kernel, tiles),
        out_shape=jax.ShapeDtypeStruct((column.shape[0], tiles * LANE), BF16),
        in_specs=[VMEM, VMEM],
        out_specs=VMEM,
        scratch_shapes=[pltpu.VMEM(msg.shape, F32)],
        compiler_params=PARAMS,
        name="pack",
    )(column, msg)


def expand_kernel(rows_ref, gate_ref, up_ref, out_ref, total):
    k = pl.program_id(0)
    width = rows_ref.shape[2]

    @pl.when(k == 0)
    def _():
        total[...] = jnp.zeros_like(total)

    at = pl.ds(pl.multiple_of(k * width, LANE), width)
    both = jnp.concatenate([gate_ref[at, :], up_ref[at, :]], axis=1)
    total[...] += jnp.dot(rows_ref[0], both, preferred_element_type=F32)

    @pl.when(k == pl.num_programs(0) - 1)
    def _():
        units = gate_ref.shape[1]
        gate, up = total[:, :units], total[:, units:]
        out_ref[...] = (gate / (1.0 + jnp.exp(-gate)) * up).astype(BF16)


def expand(gathered, gate_mat, up_mat):
    n, cap, width = gathered.shape
    units = gate_mat.shape[1]
    return pl.pallas_call(
        expand_kernel,
        grid=(n,),
        out_shape=jax.ShapeDtypeStruct((cap, units), BF16),
        in_specs=[pl.BlockSpec((1, cap, width), lambda k: (k, 0, 0)), VMEM, VMEM],
        out_specs=pl.BlockSpec((cap, units), lambda k: (0, 0)),
        scratch_shapes=[pltpu.VMEM((cap, 2 * units), F32)],
        compiler_params=PARAMS,
        name="expand",
    )(gathered, gate_mat, up_mat)


def down_kernel(n_hidden, weight_ref, column_ref, *refs):
    hidden_refs, down_refs, (out_ref, held) = refs[:n_hidden], refs[n_hidden:-2], refs[-2:]
    width = down_refs[0].shape[1]
    cap = weight_ref.shape[0]
    tiles = width // LANE
    rows = rows_of(tiles)
    devices = out_ref.shape[0] // rows
    hidden = []
    for ref in hidden_refs:
        hidden += [ref[...]] if len(ref.shape) == 2 else [ref[k] for k in range(ref.shape[0])]
    hidden = jnp.concatenate(hidden, axis=1)
    mat = jnp.concatenate([ref[...] for ref in down_refs], axis=0)
    answer = weight_ref[...] * jnp.dot(hidden, mat, preferred_element_type=F32)
    answer = answer.astype(BF16)
    for s in range(SLOT):
        slot = lax.broadcasted_iota(jnp.int32, (devices, cap), 0) * SLOT + s
        hot = (slot == column_ref[...]).astype(F32).astype(BF16)
        val = jnp.dot(hot, answer, preferred_element_type=F32)
        for t in range(tiles):
            held[pl.ds(t * SLOT + s, devices, stride=rows), :] = val[:, t * LANE : (t + 1) * LANE]
    for r in range(SLOT * tiles, rows):
        held[pl.ds(r, devices, stride=rows), :] = jnp.zeros((devices, LANE), F32)
    out_ref[...] = held[...].astype(BF16)


def down(hidden, down_blocks, weight, column, devices):
    shape = (devices * rows_of(down_blocks[0].shape[1] // LANE), LANE)
    return pl.pallas_call(
        functools.partial(down_kernel, len(hidden)),
        out_shape=jax.ShapeDtypeStruct(shape, BF16),
        in_specs=[VMEM] * (2 + len(hidden) + len(down_blocks)),
        out_specs=VMEM,
        scratch_shapes=[pltpu.VMEM(shape, F32)],
        compiler_params=PARAMS,
        name="down",
    )(weight, column, *hidden, *down_blocks)


def place_kernel(n_local, sel_ref, msg_ref, out_ref, held):
    experts = sel_ref.shape[0] // SLOT
    tiles = out_ref.shape[1] // (n_local * LANE)
    rows = rows_of(tiles)
    held[...] = msg_ref[...].astype(F32)
    for k in range(n_local):
        val = []
        for s in range(SLOT):
            at = [pl.ds(k * rows + t * SLOT + s, experts, stride=n_local * rows) for t in range(tiles)]
            val.append(jnp.concatenate([held[a, :] for a in at], axis=1))
        val = jnp.concatenate(val, axis=0).astype(BF16)
        mixed = lax.dot_general(sel_ref[...], val, (((0,), (0,)), ((), ())), preferred_element_type=F32)
        out_ref[:, k * tiles * LANE : (k + 1) * tiles * LANE] = mixed.astype(BF16)


def place(sel, msg, n_local, width):
    return pl.pallas_call(
        functools.partial(place_kernel, n_local),
        out_shape=jax.ShapeDtypeStruct((sel.shape[1], width), BF16),
        in_specs=[VMEM, VMEM],
        out_specs=VMEM,
        scratch_shapes=[pltpu.VMEM(msg.shape, F32)],
        compiler_params=PARAMS,
        name="place",
    )(sel, msg)


def exchange(msg, devices):
    parts = msg.reshape(devices, -1, 2, LANE)
    return lax.all_to_all(parts, AXES, split_axis=0, concat_axis=0, tiled=True).reshape(msg.shape)


def sent(value, dx, flip):
    nx, nc = lax.axis_size("x"), lax.axis_size("core")
    pairs = []
    for x in range(nx):
        for c in range(nc):
            pairs.append((x * nc + c, (x + dx) % nx * nc + (c + flip) % nc))
    return lax.ppermute(value, LOCAL, pairs)


def shards(tokens, w_gate, w_up, w_down, chosen, counts, gates):
    tok_dev, width = tokens.shape
    n_node = lax.axis_size("node")
    nx, nc = lax.axis_size("x"), lax.axis_size("core")
    n_local = nx * nc
    devices = n_node * n_local
    experts, cap = chosen.shape
    cut = width // n_local
    tiles = cut // LANE
    expert = lax.axis_index("node")
    at_x, at_core = lax.axis_index("x"), lax.axis_index("core")
    myself = expert * n_local + at_x * nc + at_core

    place_at = jnp.arange(cap, dtype=jnp.int32)[None, :]
    rest = (place_at < counts[:, None]) & (chosen // tok_dev == myself)
    position = chosen % tok_dev
    token = jnp.arange(tok_dev, dtype=jnp.int32)[None, :]
    sel = []
    for _ in range(SLOT):
        first = jnp.min(jnp.where(rest, place_at, cap), axis=1)
        hit = place_at == first[:, None]
        token_slot = jnp.sum(jnp.where(hit, position, 0), axis=1)
        sel.append((token == token_slot[:, None]) & (first < cap)[:, None])
        rest = rest & ~hit
    sel = jnp.concatenate(sel, axis=0).astype(BF16)

    outgoing = send(sel, tokens, n_local)
    arrived = exchange(outgoing, devices)

    mat, _ = lax.optimization_barrier((w_down, outgoing))
    down_blocks = []
    for flip in range(nc):
        for dx in range(nx):
            to = (at_x + dx) % nx * nc + (at_core + flip) % nc
            block = lax.dynamic_slice(mat[0], (0, to * cut), (mat.shape[1], cut))
            down_blocks.append(sent(block, dx, flip) if dx or flip else block)

    picked = lax.dynamic_index_in_dim(chosen, expert, 0, keepdims=False)
    count = lax.dynamic_index_in_dim(counts, expert, 0, keepdims=False)
    weight = lax.dynamic_index_in_dim(gates, expert, 0, keepdims=False)
    entry = jnp.arange(cap, dtype=jnp.int32)
    holder = picked // tok_dev
    before = (holder[:, None] == holder[None, :]) & (entry[None, :] < entry[:, None])
    column = holder * SLOT + jnp.sum(before.astype(jnp.int32), axis=1)
    column = jnp.where(entry < count, column, -1)

    arrived, *down_blocks = lax.optimization_barrier((arrived, *down_blocks))
    compact = pack(column[:, None], arrived, tiles)
    gathered = lax.all_gather(compact, LOCAL, axis=0, tiled=False)
    hidden = expand(gathered, w_gate[0], w_up[0])

    near = [sent(hidden, dx, 0) for dx in range(1, nx)]
    other = sent(hidden, 0, 1)
    others = sent(jnp.stack(near), 0, 1)
    groups = [hidden, *near, other, others]

    back = down(groups, down_blocks, weight[:, None], column[None, :], devices)
    returned = exchange(back, devices)
    return place(sel, returned, n_local, width)


def solution(mesh):
    split = Mesh(mesh.devices.reshape(mesh.shape["node"], 4, 2), AXES)
    in_specs = (
        P(AXES, None),
        P("node", None, LOCAL),
        P("node", None, LOCAL),
        P("node", LOCAL, None),
        P(),
        P(),
        P(),
    )
    return jax.shard_map(
        shards, mesh=split, in_specs=in_specs, out_specs=P(AXES, None), check_vma=False
    )
```

time: 228 us -> 193 us (0.85)
  waiting for transfers between devices: 76.4 us -> 55.3 us
  blocking collectives: 70.1 us -> 51 us
  starting transfers between devices: 21.3 us -> 39.5 us
  matrix products: 16.9 us -> 0 us
  local copies, waits for them, and re-layouts: 25.3 us -> 12.1 us
  Pallas kernels: 0 us -> 12.9 us
  other arithmetic: 3.48 us -> 8.32 us
    all_to_all x2 -> x1, waiting for transfers between devices: 39.3 us -> 0.01 us  [exchange(): lax.all_to_all(parts, AXES, split_axis=0, concat_axis=0, tiled=True)]
    ppermute x0 -> x12, starting transfers between devices: none -> 23.8 us  [sent(): return lax.ppermute(value, LOCAL, pairs)]
    dot_general x6 -> x0, matrix products: 16.9 us -> none  [the longest x1 4.34 us: shards(): jnp.dot(spread, answer, preferred_element_type=jnp.float32).astype(BF16)]
    ppermute x0 -> x12, waiting for transfers between devices: none -> 16 us  [sent(): return lax.ppermute(value, LOCAL, pairs)]
    all_gather x1 -> x0, blocking collectives: 15.7 us -> none  [shards(): groups = lax.all_gather(hidden, LOCAL, axis=0, tiled=False)]
    reshape x4 -> x0, local copies, waits for them, and re-layouts: 13.1 us -> none  [the longest x1 4.81 us: shards(): returned.reshape(experts, n_local, SLOT, cut).transpose(0, 2, 1, 3)]
    pallas_call x0 -> x5, Pallas kernels: none -> 12.9 us  [the longest x1 3.22 us: down(): pl.pallas_call(functools.partial(down_kernel, len(hidden)), out_shape=jax...]
    transpose x3 -> x0, local copies, waits for them, and re-layouts: 5.83 us -> none  [the longest x1 3.83 us: shards(): down_parts = w_down[0].reshape(-1, n_local, cut).transpose(1, 0, 2)]
  transfers between devices with their start and end apart: 3 -> 14, of which waited for: 2 -> 6; matrix products, arithmetic and copies ran while one was open for 7% -> 6% of each run, Pallas kernels for 0% -> 0%
where the time goes in v2:
time: 193 us
  waiting for transfers between devices  55.3 us (29%)
  blocking collectives  51 us (26%)
  starting transfers between devices  39.5 us (20%)
  between operations  13.7 us (7%)
  Pallas kernels  12.9 us (7%)
  local copies, waits for them, and re-layouts  12.1 us (6%)
  other arithmetic  8.32 us (4%)
    all_to_all x1, blocking collectives, exchange(): lax.all_to_all(parts, AXES, split_axis=0, concat_axis=0, tiled=True)  51 us
    all_gather x1, waiting for transfers between devices, shards(): gathered = lax.all_gather(compact, LOCAL, axis=0, tiled=False)  39.3 us
    ppermute x12, starting transfers between devices, sent(): return lax.ppermute(value, LOCAL, pairs)  23.8 us
    ppermute x12, waiting for transfers between devices, sent(): return lax.ppermute(value, LOCAL, pairs)  16 us
    all_to_all x1, starting transfers between devices, exchange(): lax.all_to_all(parts, AXES, split_axis=0, concat_axis=0, tiled=True)  15.7 us
    unnamed x32, local copies, waits for them, and re-layouts  7.95 us
  transfers between devices with their start and end apart: 14, of which 6 were waited for; matrix products, arithmetic and copies ran while one was open for 6% of the time, Pallas kernels for 0%

profile of v2, /device:TPU:1, one launch (start us, length us, event | category | flops | bytes accessed | tf_op | source)
XLA Modules:
  0.0 192.9 jit_solution(1464553082438735108)
XLA Ops:
  8.4 1.5 copy-done.2
  9.9 2.3 %send.1 = bf16[5632,128]{1,0:T(8,128)(2,1)} custom-call(bf16[96,128]{1,0:T(8,128)(2,1)S(1)} %add_convert_fusion.sel_ref, bf16[128,7168]{1,0:T(8,128)(2,1)S(1)} %copy-done.2), custom_call_target="tpu_custom_call" | custom-call | tf_op jit(solution)/shard_map/send/pallas_call | solution.py:44
  12.1 15.7 %all-to-all-start = ((bf16[256,11,2,128]{3,2,1,0:T(2,128)(2,1)}), bf16[256,11,2,128]{3,2,1,0:T(2,128)(2,1)S(1)}, u32[]{:S(2)}, u32[]{:S(2)}) async-start(bf16[256,11,2,128]{3,2,1,0:T(2,128)(2,1)} %bitcast.3), calls=%async_computation | async-start | bytes 2883584 | tf_op jit(solution)/shard_map/all_to_all | solution.py:183
  29.2 1.4 collective-permute-start
  30.6 2.4 %collective-permute-start.1 = (bf16[128,896]{1,0:T(8,128)(2,1)}, bf16[128,896]{1,0:T(8,128)(2,1)}, u32[]{:S(2)}, u32[]{:S(2)}) collective-permute-start(bf16[128,896]{1,0:T(8,128)(2,1)} %get-tuple-element.39), channel_id=1, source_target_pairs={{0,4},{1,5},{2,6},{3,7},{4,0},{5,1},{6,2},{7,3},{8,12},{9,13},{10,... | collective-permute-start | bytes 688136 | tf_op jit(solution)/shard_map/ppermute | solution.py:192
  35.5 1.9 fusion.22
  38.0 1.3 dynamic_slice.53
  39.3 1.5 copy.14
  41.7 12.1 %collective-permute-start.5 = (bf16[128,896]{1,0:T(8,128)(2,1)}, bf16[128,896]{1,0:T(8,128)(2,1)S(1)}, u32[]{:S(2)}, u32[]{:S(2)}) collective-permute-start(bf16[128,896]{1,0:T(8,128)(2,1)} %get-tuple-element.35), channel_id=1, source_target_pairs={{0,5},{1,4},{2,7},{3,6},{4,1},{5,0},{6,3},{7,2},{8,13},{9,12},{10,... | collective-permute-start | bytes 688136 | tf_op jit(solution)/shard_map/ppermute | solution.py:192
  53.8 2.4 %fusion.4.column_ref = s32[384,1]{1,0:T(8,128)} fusion(s32[384]{0:T(512)S(1)} %convert_reduce_fusion, s32[384,1]{1,0:T(8,128)} %copy.14, s32[]{:T(128)} %bitcast.1), kind=kLoop, calls=%fused_computation.19 | loop fusion | flops 7296 | bytes 4612 | tf_op jit(solution)/shard_map/jit(_where)/select_n | solution.py:239
  56.3 2.5 %collective-permute-done.4.refs_11_ = bf16[128,896]{1,0:T(8,128)(2,1)} collective-permute-done((bf16[128,896]{1,0:T(8,128)(2,1)}, bf16[128,896]{1,0:T(8,128)(2,1)}, u32[]{:S(2)}, u32[]{:S(2)}) %collective-permute-start.4) | collective-permute-done | bytes 229408 | tf_op jit(solution)/shard_map/ppermute | solution.py:192
  58.8 8.2 %collective-permute-done.5.refs_12_ = bf16[128,896]{1,0:T(8,128)(2,1)S(1)} collective-permute-done((bf16[128,896]{1,0:T(8,128)(2,1)}, bf16[128,896]{1,0:T(8,128)(2,1)S(1)}, u32[]{:S(2)}, u32[]{:S(2)}) %collective-permute-start.5) | collective-permute-done | bytes 229408 | tf_op jit(solution)/shard_map/ppermute | solution.py:192
  69.3 1.8 pack.1
  71.2 39.3 %all-gather.3.cloned.1.call-done = bf16[3072,896]{1,0:T(8,128)(2,1)} async-done(((bf16[384,896]{1,0:T(8,128)(2,1)}), bf16[3072,896]{1,0:T(8,128)(2,1)}) %all-gather.3.cloned.1.call-update) | async-done | bytes 5505040 | tf_op jit(solution)/shard_map/all_gather | solution.py:243
  110.5 2.6 %copy-done.1 = bf16[3072,896]{1,0:T(8,128)(2,1)S(1)} copy-done((bf16[3072,896]{1,0:T(8,128)(2,1)S(1)}, bf16[3072,896]{1,0:T(8,128)(2,1)}, u32[]{:S(2)}) %copy-start.1) | copy-done | bytes 5505048
  113.1 1.5 copy-done.4
  114.6 3.2 %expand.1.refs_0_ = bf16[384,128]{1,0:T(8,128)(2,1)S(1)} custom-call(bf16[8,384,896]{2,1,0:T(8,128)(2,1)S(1)} %bitcast.34, bf16[7168,128]{1,0:T(8,128)(2,1)S(1)} %bitcast.35, bf16[7168,128]{1,0:T(8,128)(2,1)S(1)} %bitcast.36), custom_call_target="tpu_custom_call" | custom-call | tf_op jit(solution)/shard_map/expand/pallas_call | solution.py:104
  118.1 1.5 collective-permute-start.8
  119.6 1.8 collective-permute-start.9
  121.4 4.0 %collective-permute-done.7.refs_1_ = bf16[384,128]{1,0:T(8,128)(2,1)S(1)} collective-permute-done((bf16[384,128]{1,0:T(8,128)(2,1)S(1)}, bf16[384,128]{1,0:T(8,128)(2,1)S(1)}, u32[]{:S(2)}, u32[]{:S(2)}) %collective-permute-start.7) | collective-permute-done | bytes 98336 | tf_op jit(solution)/shard_map/ppermute | solution.py:192
  125.6 1.7 collective-permute-start.11
  129.3 3.2 %down.1 = bf16[5632,128]{1,0:T(8,128)(2,1)S(1)} custom-call(f32[384,1]{1,0:T(8,128)S(1)} %copy.19.weight_ref, s32[1,384]{1,0:T(1,128)S(1)} %compare_select_fusion.column_ref, bf16[384,128]{1,0:T(8,128)(2,1)S(1)} %expand.1.refs_0_, bf16[384,128]{1,0:T(8,128)(2,1)S(1)} %collective-permute-done.7.refs_1_, bf16[384,128]{1,0:T(8,128)(2,1)S(1)} %collective-permute-done.8.refs_2_, ...), custom_call_target="tpu_custom_call" | custom-call | tf_op jit(solution)/shard_map/down/pallas_call | solution.py:143
  132.6 51.0 %all_to_all.10 = bf16[256,11,2,128]{3,2,1,0:T(2,128)(2,1)S(1)} all-to-all(bf16[256,11,2,128]{3,2,1,0:T(2,128)(2,1)S(1)} %bitcast.31), channel_id=1, replica_groups=mesh['node'=32,'x'=4,'core'=2] {'node','x','core'}, dimensions={0} | all-to-all | bytes 2883584 | tf_op jit(solution)/shard_map/all_to_all | solution.py:183
  183.6 2.4 %place.1 = bf16[128,7168]{1,0:T(8,128)(2,1)} custom-call(bf16[96,128]{1,0:T(8,128)(2,1)S(1)} %copy-done.11, bf16[5632,128]{1,0:T(8,128)(2,1)S(1)} %bitcast.33), custom_call_target="tpu_custom_call" | custom-call | tf_op jit(solution)/shard_map/place/pallas_call | solution.py:170
  (64 shorter events, 12.1 us)
Async XLA Ops:
  6.5 121.5 %copy-start = (f32[32,384]{1,0:T(8,128)S(1)}, f32[32,384]{1,0:T(8,128)}, u32[]{:S(2)}) copy-start(f32[32,384]{1,0:T(8,128)} %param.13) | copy-start | bytes 147460
  12.1 15.8 %copy-start.12 = (bf16[1,128,7168]{2,1,0:T(8,128)(2,1)S(1)}, bf16[1,128,7168]{2,1,0:T(8,128)(2,1)}, u32[]{:S(2)}) copy-start(bf16[1,128,7168]{2,1,0:T(8,128)(2,1)} %param.10) | copy-start | bytes 5505028
  12.1 56.2 %all-to-all-start = ((bf16[256,11,2,128]{3,2,1,0:T(2,128)(2,1)}), bf16[256,11,2,128]{3,2,1,0:T(2,128)(2,1)S(1)}, u32[]{:S(2)}, u32[]{:S(2)}) async-start(bf16[256,11,2,128]{3,2,1,0:T(2,128)(2,1)} %bitcast.3), calls=%async_computation | async-start | bytes 2883584 | tf_op jit(solution)/shard_map/all_to_all | solution.py:183
  27.8 82.7 %all-gather.3.cloned.1.call-start = ((), (), s32[]{:S(2)}) async-start(), calls=%async_computation.2 | async-start | bytes 6193152 | tf_op jit(solution)/shard_map/all_gather | solution.py:243
  29.2 81.3 %copy-start.3 = (bf16[1,7168,128]{2,1,0:T(8,128)(2,1)S(1)}, bf16[1,7168,128]{2,1,0:T(8,128)(2,1)}, u32[]{:S(2)}) copy-start(bf16[1,7168,128]{2,1,0:T(8,128)(2,1)} %param.8) | copy-start | bytes 5505028
  29.2 12.5 %collective-permute-start = (bf16[128,896]{1,0:T(8,128)(2,1)}, bf16[128,896]{1,0:T(8,128)(2,1)}, u32[]{:S(2)}, u32[]{:S(2)}) collective-permute-start(bf16[128,896]{1,0:T(8,128)(2,1)} %get-tuple-element.40), channel_id=1, source_target_pairs={{0,2},{1,3},{2,4},{3,5},{4,6},{5,7},{6,0},{7,1},{8,10},{9,11},{10,... | collective-permute-start | bytes 688136 | tf_op jit(solution)/shard_map/ppermute | solution.py:192
  30.6 23.3 %collective-permute-start.1 = (bf16[128,896]{1,0:T(8,128)(2,1)}, bf16[128,896]{1,0:T(8,128)(2,1)}, u32[]{:S(2)}, u32[]{:S(2)}) collective-permute-start(bf16[128,896]{1,0:T(8,128)(2,1)} %get-tuple-element.39), channel_id=1, source_target_pairs={{0,4},{1,5},{2,6},{3,7},{4,0},{5,1},{6,2},{7,3},{8,12},{9,13},{10,... | collective-permute-start | bytes 688136 | tf_op jit(solution)/shard_map/ppermute | solution.py:192
  33.0 23.3 %collective-permute-start.2 = (bf16[128,896]{1,0:T(8,128)(2,1)}, bf16[128,896]{1,0:T(8,128)(2,1)}, u32[]{:S(2)}, u32[]{:S(2)}) collective-permute-start(bf16[128,896]{1,0:T(8,128)(2,1)} %get-tuple-element.38), channel_id=1, source_target_pairs={{0,6},{1,7},{2,0},{3,1},{4,2},{5,3},{6,4},{7,5},{8,14},{9,15},{10,... | collective-permute-start | bytes 688136 | tf_op jit(solution)/shard_map/ppermute | solution.py:192
  34.1 22.1 %collective-permute-start.3 = (bf16[128,896]{1,0:T(8,128)(2,1)}, bf16[128,896]{1,0:T(8,128)(2,1)}, u32[]{:S(2)}, u32[]{:S(2)}) collective-permute-start(bf16[128,896]{1,0:T(8,128)(2,1)} %get-tuple-element.37), channel_id=1, source_target_pairs={{0,1},{1,0},{2,3},{3,2},{4,5},{5,4},{6,7},{7,6},{8,9},{9,8},{10,11... | collective-permute-start | bytes 688136 | tf_op jit(solution)/shard_map/ppermute | solution.py:192
  35.3 23.4 %collective-permute-start.4 = (bf16[128,896]{1,0:T(8,128)(2,1)}, bf16[128,896]{1,0:T(8,128)(2,1)}, u32[]{:S(2)}, u32[]{:S(2)}) collective-permute-start(bf16[128,896]{1,0:T(8,128)(2,1)} %get-tuple-element.36), channel_id=1, source_target_pairs={{0,3},{1,2},{2,5},{3,4},{4,7},{5,6},{6,1},{7,0},{8,11},{9,10},{10,... | collective-permute-start | bytes 688136 | tf_op jit(solution)/shard_map/ppermute | solution.py:192
  41.7 25.2 %copy-start.13 = (s32[384]{0:T(512)}, s32[384]{0:T(512)S(1)}, u32[]{:S(2)}) copy-start(s32[384]{0:T(512)S(1)} %convert_reduce_fusion) | copy-start | bytes 4612
  41.7 25.2 %collective-permute-start.5 = (bf16[128,896]{1,0:T(8,128)(2,1)}, bf16[128,896]{1,0:T(8,128)(2,1)S(1)}, u32[]{:S(2)}, u32[]{:S(2)}) collective-permute-start(bf16[128,896]{1,0:T(8,128)(2,1)} %get-tuple-element.35), channel_id=1, source_target_pairs={{0,5},{1,4},{2,7},{3,6},{4,1},{5,0},{6,3},{7,2},{8,13},{9,12},{10,... | collective-permute-start | bytes 688136 | tf_op jit(solution)/shard_map/ppermute | solution.py:192
  53.8 13.8 %collective-permute-start.6 = (bf16[128,896]{1,0:T(8,128)(2,1)}, bf16[128,896]{1,0:T(8,128)(2,1)S(1)}, u32[]{:S(2)}, u32[]{:S(2)}) collective-permute-start(bf16[128,896]{1,0:T(8,128)(2,1)} %get-tuple-element.34), channel_id=1, source_target_pairs={{0,7},{1,6},{2,1},{3,0},{4,3},{5,2},{6,5},{7,4},{8,15},{9,14},{10,... | collective-permute-start | bytes 688136 | tf_op jit(solution)/shard_map/ppermute | solution.py:192
  110.5 2.6 %copy-start.1 = (bf16[3072,896]{1,0:T(8,128)(2,1)S(1)}, bf16[3072,896]{1,0:T(8,128)(2,1)}, u32[]{:S(2)}) copy-start(bf16[3072,896]{1,0:T(8,128)(2,1)} %all-gather.3.cloned.1.call-done) | copy-start | bytes 16515076
  114.6 12.7 %copy-start.14 = (s32[384]{0:T(512)S(1)}, s32[384]{0:T(512)}, u32[]{:S(2)}) copy-start(s32[384]{0:T(512)} %copy-done.13) | copy-start | bytes 4612
  114.6 12.7 %copy-start.15 = (s32[1,384]{1,0:T(1,128)S(1)}, s32[1,384]{1,0:T(1,128)}, u32[]{:S(2)}) copy-start(s32[1,384]{1,0:T(1,128)} %get-tuple-element.29) | copy-start | bytes 4612
  114.6 14.8 %copy-start.7 = (bf16[128,896]{1,0:T(8,128)(2,1)S(1)}, bf16[128,896]{1,0:T(8,128)(2,1)}, u32[]{:S(2)}) copy-start(bf16[128,896]{1,0:T(8,128)(2,1)} %copy-done.6) | copy-start | bytes 688132
  114.6 14.8 %copy-start.9 = (bf16[128,896]{1,0:T(8,128)(2,1)S(1)}, bf16[128,896]{1,0:T(8,128)(2,1)}, u32[]{:S(2)}) copy-start(bf16[128,896]{1,0:T(8,128)(2,1)} %copy-done.8) | copy-start | bytes 688132
  117.8 7.6 %collective-permute-start.7 = (bf16[384,128]{1,0:T(8,128)(2,1)S(1)}, bf16[384,128]{1,0:T(8,128)(2,1)S(1)}, u32[]{:S(2)}, u32[]{:S(2)}) collective-permute-start(bf16[384,128]{1,0:T(8,128)(2,1)S(1)} %expand.1.refs_0_), channel_id=1, source_target_pairs={{0,2},{1,3},{2,4},{3,5},{4,6},{5,7},{6,0},{7,1},{8,10},{9,11},{10,... | collective-permute-start | bytes 294920 | tf_op jit(solution)/shard_map/ppermute | solution.py:192
  118.1 7.3 %collective-permute-start.8 = (bf16[384,128]{1,0:T(8,128)(2,1)S(1)}, bf16[384,128]{1,0:T(8,128)(2,1)S(1)}, u32[]{:S(2)}, u32[]{:S(2)}) collective-permute-start(bf16[384,128]{1,0:T(8,128)(2,1)S(1)} %expand.1.refs_0_), channel_id=1, source_target_pairs={{0,4},{1,5},{2,6},{3,7},{4,0},{5,1},{6,2},{7,3},{8,12},{9,13},{10,... | collective-permute-start | bytes 294920 | tf_op jit(solution)/shard_map/ppermute | solution.py:192
  119.6 6.0 %collective-permute-start.9 = (bf16[384,128]{1,0:T(8,128)(2,1)S(1)}, bf16[384,128]{1,0:T(8,128)(2,1)S(1)}, u32[]{:S(2)}, u32[]{:S(2)}) collective-permute-start(bf16[384,128]{1,0:T(8,128)(2,1)S(1)} %expand.1.refs_0_), channel_id=1, source_target_pairs={{0,6},{1,7},{2,0},{3,1},{4,2},{5,3},{6,4},{7,5},{8,14},{9,15},{10,... | collective-permute-start | bytes 294920 | tf_op jit(solution)/shard_map/ppermute | solution.py:192
  125.6 3.7 %collective-permute-start.11 = (bf16[3,384,128]{2,1,0:T(8,128)(2,1)S(1)}, bf16[3,384,128]{2,1,0:T(8,128)(2,1)S(1)}, u32[]{:S(2)}, u32[]{:S(2)}) collective-permute-start(bf16[3,384,128]{2,1,0:T(8,128)(2,1)S(1)} %pad_maximum_fusion), channel_id=1, source_target_pairs={{0,1},{1,0},{2,3},{3,2},{4,5},{5,4},{6,7},{7,6},{8,9},{9,8},{10,11... | collective-permute-start | bytes 884744 | tf_op jit(solution)/shard_map/ppermute | solution.py:192
  127.9 1.4 collective-permute-start.10
  132.6 51.1 %copy-start.11 = (bf16[96,128]{1,0:T(8,128)(2,1)S(1)}, bf16[96,128]{1,0:T(8,128)(2,1)}, u32[]{:S(2)}) copy-start(bf16[96,128]{1,0:T(8,128)(2,1)} %copy-done.10) | copy-start | bytes 73732
  (6 other events, 7.6 us)
Sparse Core Ops, SparseCore 0:
  71.3 39.1 all-gather.2

commit v3 on v2

--- a/solution.py
+++ b/solution.py
@@ -12,9 +12,10 @@
 LANE = 128
 LOCAL = ("x", "core")
 AXES = ("node", "x", "core")
+PARTS = (7,)
 BF16 = jnp.bfloat16
 F32 = jnp.float32
-PARAMS = pltpu.CompilerParams(vmem_limit_bytes=40 * 2**20)
+PARAMS = pltpu.CompilerParams(vmem_limit_bytes=24 * 2**20)
 VMEM = pl.BlockSpec(memory_space=pltpu.VMEM)
 
 
@@ -22,31 +23,36 @@
     return -(-tiles * SLOT // 2) * 2
 
 
-def send_kernel(n_local, sel_ref, tok_ref, out_ref, held):
+def send_kernel(parts, sel_ref, tok_ref, *refs):
+    outs, held = refs[: len(parts)], refs[len(parts) :]
     experts = sel_ref.shape[0] // SLOT
-    cut = tok_ref.shape[1] // n_local
-    tiles = cut // LANE
-    rows = rows_of(tiles)
+    cut = sum(parts) * LANE
+    n_local = tok_ref.shape[1] // cut
     for k in range(n_local):
-        part = tok_ref[:, k * cut : (k + 1) * cut]
-        val = jnp.dot(sel_ref[...], part, preferred_element_type=F32)
-        for t in range(tiles):
-            for s in range(SLOT):
-                at = pl.ds(k * rows + t * SLOT + s, experts, stride=n_local * rows)
-                held[at, :] = val[s * experts : (s + 1) * experts, t * LANE : (t + 1) * LANE]
-        for r in range(SLOT * tiles, rows):
-            held[pl.ds(k * rows + r, experts, stride=n_local * rows), :] = jnp.zeros((experts, LANE), F32)
-    out_ref[...] = held[...].astype(BF16)
-
-
-def send(sel, tokens, n_local):
-    shape = (sel.shape[0] // SLOT * n_local * rows_of(tokens.shape[1] // (n_local * LANE)), LANE)
-    return pl.pallas_call(
-        functools.partial(send_kernel, n_local),
-        out_shape=jax.ShapeDtypeStruct(shape, BF16),
+        val = jnp.dot(sel_ref[...], tok_ref[:, k * cut : (k + 1) * cut], preferred_element_type=F32)
+        first = 0
+        for tiles, ref in zip(parts, held):
+            rows = rows_of(tiles)
+            for t in range(tiles):
+                lanes = slice((first + t) * LANE, (first + t + 1) * LANE)
+                for s in range(SLOT):
+                    at = pl.ds(k * rows + t * SLOT + s, experts, stride=n_local * rows)
+                    ref[at, :] = val[s * experts : (s + 1) * experts, lanes]
+            for r in range(SLOT * tiles, rows):
+                ref[pl.ds(k * rows + r, experts, stride=n_local * rows), :] = jnp.zeros((experts, LANE), F32)
+            first += tiles
+    for out, ref in zip(outs, held):
+        out[...] = ref[...].astype(BF16)
+
+
+def send(sel, tokens, parts, devices):
+    shapes = [(devices * rows_of(tiles), LANE) for tiles in parts]
+    return pl.pallas_call(
+        functools.partial(send_kernel, parts),
+        out_shape=[jax.ShapeDtypeStruct(shape, BF16) for shape in shapes],
         in_specs=[VMEM, VMEM],
-        out_specs=VMEM,
-        scratch_shapes=[pltpu.VMEM(shape, F32)],
+        out_specs=[VMEM] * len(parts),
+        scratch_shapes=[pltpu.VMEM(shape, F32) for shape in shapes],
         compiler_params=PARAMS,
         name="send",
     )(sel, tokens)
@@ -79,38 +85,38 @@
     )(column, msg)
 
 
-def expand_kernel(rows_ref, gate_ref, up_ref, out_ref, total):
-    k = pl.program_id(0)
-    width = rows_ref.shape[2]
-
-    @pl.when(k == 0)
-    def _():
-        total[...] = jnp.zeros_like(total)
-
-    at = pl.ds(pl.multiple_of(k * width, LANE), width)
-    both = jnp.concatenate([gate_ref[at, :], up_ref[at, :]], axis=1)
-    total[...] += jnp.dot(rows_ref[0], both, preferred_element_type=F32)
-
-    @pl.when(k == pl.num_programs(0) - 1)
-    def _():
+def expand_kernel(n_blocks, opening, last, place_ref, gate_ref, up_ref, *refs):
+    blocks, out_ref = refs[:n_blocks], refs[-1]
+    total = None if opening else refs[n_blocks][...]
+    for n, ref in enumerate(blocks):
+        at = pl.ds(pl.multiple_of(place_ref[n], LANE), ref.shape[1])
+        both = jnp.concatenate([gate_ref[at, :], up_ref[at, :]], axis=1)
+        val = jnp.dot(ref[...], both, preferred_element_type=F32)
+        total = val if total is None else total + val
+    if last:
         units = gate_ref.shape[1]
         gate, up = total[:, :units], total[:, units:]
         out_ref[...] = (gate / (1.0 + jnp.exp(-gate)) * up).astype(BF16)
-
-
-def expand(gathered, gate_mat, up_mat):
-    n, cap, width = gathered.shape
+    else:
+        out_ref[...] = total
+
+
+def expand(total, blocks, places, gate_mat, up_mat, last):
+    cap = blocks[0].shape[0]
     units = gate_mat.shape[1]
-    return pl.pallas_call(
-        expand_kernel,
-        grid=(n,),
-        out_shape=jax.ShapeDtypeStruct((cap, units), BF16),
-        in_specs=[pl.BlockSpec((1, cap, width), lambda k: (k, 0, 0)), VMEM, VMEM],
-        out_specs=pl.BlockSpec((cap, units), lambda k: (0, 0)),
-        scratch_shapes=[pltpu.VMEM((cap, 2 * units), F32)],
-        compiler_params=PARAMS,
+    opening = total is None
+    shape = jax.ShapeDtypeStruct((cap, units), BF16) if last else jax.ShapeDtypeStruct((cap, 2 * units), F32)
+    smem = pl.BlockSpec(memory_space=pltpu.SMEM)
+    flops = 4 * cap * units * sum(block.shape[1] for block in blocks)
+    return pl.pallas_call(
+        functools.partial(expand_kernel, len(blocks), opening, last),
+        out_shape=shape,
+        in_specs=[smem] + [VMEM] * (2 + len(blocks) + (not opening)),
+        out_specs=VMEM,
+        compiler_params=PARAMS,
+        cost_estimate=pl.CostEstimate(flops=flops, bytes_accessed=flops // 512, transcendentals=0),
         name="expand",
-    )(gathered, gate_mat, up_mat)
+    )(jnp.stack(places), gate_mat, up_mat, *blocks, *([] if opening else [total]))
 
 
 def down_kernel(n_hidden, weight_ref, column_ref, *refs):
@@ -192,6 +198,15 @@
     return lax.ppermute(value, LOCAL, pairs)
 
 
+def forwarded(fore, aft):
+    nx = lax.axis_size("x")
+    pairs = []
+    for x in range(nx):
+        pairs.append((2 * x, (x + 1) % nx * 2))
+        pairs.append((2 * x + 1, (x - 1) % nx * 2 + 1))
+    return lax.ppermute(jnp.where(lax.axis_index("core") == 0, fore, aft), LOCAL, pairs)
+
+
 def shards(tokens, w_gate, w_up, w_down, chosen, counts, gates):
     tok_dev, width = tokens.shape
     n_node = lax.axis_size("node")
@@ -200,7 +215,6 @@
     devices = n_node * n_local
     experts, cap = chosen.shape
     cut = width // n_local
-    tiles = cut // LANE
     expert = lax.axis_index("node")
     at_x, at_core = lax.axis_index("x"), lax.axis_index("core")
     myself = expert * n_local + at_x * nc + at_core
@@ -218,10 +232,10 @@
         rest = rest & ~hit
     sel = jnp.concatenate(sel, axis=0).astype(BF16)
 
-    outgoing = send(sel, tokens, n_local)
-    arrived = exchange(outgoing, devices)
-
-    mat, _ = lax.optimization_barrier((w_down, outgoing))
+    outgoing = send(sel, tokens, PARTS, devices)
+    arrived = [exchange(msg, devices) for msg in outgoing]
+
+    mat, _ = lax.optimization_barrier((w_down, outgoing[0]))
     down_blocks = []
     for flip in range(nc):
         for dx in range(nx):
@@ -238,10 +252,28 @@
     column = holder * SLOT + jnp.sum(before.astype(jnp.int32), axis=1)
     column = jnp.where(entry < count, column, -1)
 
-    arrived, *down_blocks = lax.optimization_barrier((arrived, *down_blocks))
-    compact = pack(column[:, None], arrived, tiles)
-    gathered = lax.all_gather(compact, LOCAL, axis=0, tiled=False)
-    hidden = expand(gathered, w_gate[0], w_up[0])
+    arrived[-1], *down_blocks = lax.optimization_barrier((arrived[-1], *down_blocks))
+    total = None
+    first = 0
+    for n, (msg, tiles) in enumerate(zip(arrived, PARTS)):
+        own = pack(column[:, None], msg, tiles)
+        fore, aft, other = sent(own, 1, 0), sent(own, -1, 0), sent(own, 0, 1)
+        far = forwarded(fore, aft)
+        stages = [
+            [(own, 0, 0), (other, 0, 1)],
+            [(fore, 1, 0), (aft, -1, 0), (sent(fore, 0, 1), 1, 1), (sent(aft, 0, 1), -1, 1)],
+            [(far, 2, 0)],
+            [(sent(far, 0, 1), 2, 1)],
+        ]
+        for m, stage in enumerate(stages):
+            places = []
+            for _, dx, flip in stage:
+                source = (at_x - dx) % nx * nc + (at_core + flip) % nc
+                places.append(source * cut + first * LANE)
+            last = n == len(PARTS) - 1 and m == len(stages) - 1
+            total = expand(total, [block for block, _, _ in stage], places, w_gate[0], w_up[0], last)
+        first += tiles
+    hidden = total
 
     near = [sent(hidden, dx, 0) for dx in range(1, nx)]
     other = sent(hidden, 0, 1)

time: 193 us -> 173 us (0.90)
  waiting for transfers between devices: 55.3 us -> 38.8 us
  between operations: 13.7 us -> 0.43 us
  starting transfers between devices: 39.5 us -> 49.6 us
  Pallas kernels: 12.9 us -> 15.6 us
  other arithmetic: 8.32 us -> 5.68 us
    all_gather x1 -> x0, waiting for transfers between devices: 39.3 us -> none  [shards(): gathered = lax.all_gather(compact, LOCAL, axis=0, tiled=False)]
    ppermute x12 -> x18, waiting for transfers between devices: 16 us -> 31.4 us  [sent(): return lax.ppermute(value, LOCAL, pairs)]
    ppermute x12 -> x18, starting transfers between devices: 23.8 us -> 31.5 us  [sent(): return lax.ppermute(value, LOCAL, pairs)]
    ppermute x0 -> x1, waiting for transfers between devices: none -> 7.37 us  [forwarded(): lax.ppermute(jnp.where(lax.axis_index('core') == 0, fore, aft), LOCAL, pa...]
    pallas_call x2 -> x5, Pallas kernels: 5.44 us -> 9.5 us  [the longest x4 7.23 us: expand(): pl.pallas_call(functools.partial(expand_kernel, len(blocks), opening, las...]
    ppermute x0 -> x1, starting transfers between devices: none -> 2.51 us  [forwarded(): lax.ppermute(jnp.where(lax.axis_index('core') == 0, fore, aft), LOCAL, pa...]
    unnamed x32 -> x50, local copies, waits for them, and re-layouts: 7.95 us -> 9.99 us
  transfers between devices with their start and end apart: 14 -> 20, of which waited for: 6 -> 8; matrix products, arithmetic and copies ran while one was open for 6% -> 4% of each run, Pallas kernels for 0% -> 3%
where the time goes in v3:
time: 173 us
  blocking collectives  50 us (29%)
  starting transfers between devices  49.6 us (29%)
  waiting for transfers between devices  38.8 us (22%)
  Pallas kernels  15.6 us (9%)
  local copies, waits for them, and re-layouts  12.7 us (7%)
  other arithmetic  5.68 us (3%)
    all_to_all x1, blocking collectives, exchange(): lax.all_to_all(parts, AXES, split_axis=0, concat_axis=0, tiled=True)  50 us
    ppermute x18, starting transfers between devices, sent(): return lax.ppermute(value, LOCAL, pairs)  31.5 us
    ppermute x18, waiting for transfers between devices, sent(): return lax.ppermute(value, LOCAL, pairs)  31.4 us
    all_to_all x1, starting transfers between devices, exchange(): lax.all_to_all(parts, AXES, split_axis=0, concat_axis=0, tiled=True)  15.7 us
    unnamed x50, local copies, waits for them, and re-layouts  9.99 us
    ppermute x1, waiting for transfers between devices, forwarded(): lax.ppermute(jnp.where(lax.axis_index('core') == 0, fore, aft), LOCAL, pa...  7.37 us
    pallas_call x4, Pallas kernels, expand(): pl.pallas_call(functools.partial(expand_kernel, len(blocks), opening, las...  7.23 us
  transfers between devices with their start and end apart: 20, of which 8 were waited for; matrix products, arithmetic and copies ran while one was open for 4% of the time, Pallas kernels for 3%

profile of v3, /device:TPU:1, one launch (start us, length us, event | category | flops | bytes accessed | tf_op | source)
XLA Modules:
  0.0 172.8 jit_solution(8582546368544583183)
XLA Ops:
  1.8 1.5 copy-done.3
  3.3 2.3 %send.1 = bf16[5632,128]{1,0:T(8,128)(2,1)} custom-call(bf16[96,128]{1,0:T(8,128)(2,1)S(1)} %add_convert_fusion.sel_ref, bf16[128,7168]{1,0:T(8,128)(2,1)S(1)} %copy-done.3), custom_call_target="tpu_custom_call" | custom-call | tf_op jit(solution)/shard_map/send/pallas_call | solution.py:50
  5.6 15.7 %all-to-all-start = ((bf16[256,11,2,128]{3,2,1,0:T(2,128)(2,1)}), bf16[256,11,2,128]{3,2,1,0:T(2,128)(2,1)S(1)}, u32[]{:S(2)}, u32[]{:S(2)}) async-start(bf16[256,11,2,128]{3,2,1,0:T(2,128)(2,1)} %bitcast.6), calls=%async_computation | async-start | bytes 2883584 | tf_op jit(solution)/shard_map/all_to_all | solution.py:189
  24.0 2.4 %collective-permute-start.1 = (bf16[128,896]{1,0:T(8,128)(2,1)}, bf16[128,896]{1,0:T(8,128)(2,1)S(1)}, u32[]{:S(2)}, u32[]{:S(2)}) collective-permute-start(bf16[128,896]{1,0:T(8,128)(2,1)} %get-tuple-element.39), channel_id=1, source_target_pairs={{0,4},{1,5},{2,6},{3,7},{4,0},{5,1},{6,2},{7,3},{8,12},{9,13},{10,... | collective-permute-start | bytes 688136 | tf_op jit(solution)/shard_map/ppermute | solution.py:198
  31.9 15.2 %collective-permute-start.5 = (bf16[128,896]{1,0:T(8,128)(2,1)}, bf16[128,896]{1,0:T(8,128)(2,1)S(1)}, u32[]{:S(2)}, u32[]{:S(2)}) collective-permute-start(bf16[128,896]{1,0:T(8,128)(2,1)} %get-tuple-element.35), channel_id=1, source_target_pairs={{0,5},{1,4},{2,7},{3,6},{4,1},{5,0},{6,3},{7,2},{8,13},{9,12},{10,... | collective-permute-start | bytes 688136 | tf_op jit(solution)/shard_map/ppermute | solution.py:198
  50.7 1.5 collective-permute-done.4.refs_11_
  52.9 7.5 %collective-permute-done.5.refs_12_ = bf16[128,896]{1,0:T(8,128)(2,1)S(1)} collective-permute-done((bf16[128,896]{1,0:T(8,128)(2,1)}, bf16[128,896]{1,0:T(8,128)(2,1)S(1)}, u32[]{:S(2)}, u32[]{:S(2)}) %collective-permute-start.5) | collective-permute-done | bytes 229408 | tf_op jit(solution)/shard_map/ppermute | solution.py:198
  62.7 1.8 %pack.1.refs_0_ = bf16[384,896]{1,0:T(8,128)(2,1)} custom-call(s32[384,1]{1,0:T(8,128)S(1)} %copy-done.4, bf16[5632,128]{1,0:T(8,128)(2,1)S(1)} %bitcast.47), custom_call_target="tpu_custom_call" | custom-call | tf_op jit(solution)/shard_map/pack/pallas_call | solution.py:77
  64.7 2.6 %collective-permute-start.8 = (bf16[384,896]{1,0:T(8,128)(2,1)}, bf16[384,896]{1,0:T(8,128)(2,1)S(1)}, u32[]{:S(2)}, u32[]{:S(2)}) collective-permute-start(bf16[384,896]{1,0:T(8,128)(2,1)} %pack.1.refs_0_), channel_id=1, source_target_pairs={{0,6},{1,7},{2,0},{3,1},{4,2},{5,3},{6,4},{7,5},{8,14},{9,15},{10,... | collective-permute-start | bytes 2064392 | tf_op jit(solution)/shard_map/ppermute | solution.py:198
  67.2 15.9 %collective-permute-done.7.refs_0_ = bf16[384,896]{1,0:T(8,128)(2,1)S(1)} collective-permute-done((bf16[384,896]{1,0:T(8,128)(2,1)}, bf16[384,896]{1,0:T(8,128)(2,1)S(1)}, u32[]{:S(2)}, u32[]{:S(2)}) %collective-permute-start.7) | collective-permute-done | bytes 688160 | tf_op jit(solution)/shard_map/ppermute | solution.py:198
  83.2 2.5 %collective-permute-start.9 = (bf16[384,896]{1,0:T(8,128)(2,1)S(1)}, bf16[384,896]{1,0:T(8,128)(2,1)}, u32[]{:S(2)}, u32[]{:S(2)}) collective-permute-start(bf16[384,896]{1,0:T(8,128)(2,1)S(1)} %broadcast_select_fusion), channel_id=1, source_target_pairs={{0,2},{1,7},{2,4},{3,1},{4,6},{5,3},{6,0},{7,5},{8,10},{9,15},{10,... | collective-permute-start | bytes 2064392 | tf_op jit(solution)/shard_map/ppermute | solution.py:207
  86.2 7.4 %collective-permute-done.9.refs_0_ = bf16[384,896]{1,0:T(8,128)(2,1)} collective-permute-done((bf16[384,896]{1,0:T(8,128)(2,1)S(1)}, bf16[384,896]{1,0:T(8,128)(2,1)}, u32[]{:S(2)}, u32[]{:S(2)}) %collective-permute-start.9) | collective-permute-done | bytes 688160 | tf_op jit(solution)/shard_map/ppermute | solution.py:207
  93.6 2.7 %collective-permute-start.10 = (bf16[384,896]{1,0:T(8,128)(2,1)}, bf16[384,896]{1,0:T(8,128)(2,1)}, u32[]{:S(2)}, u32[]{:S(2)}) collective-permute-start(bf16[384,896]{1,0:T(8,128)(2,1)} %collective-permute-done.9.refs_0_), channel_id=1, source_target_pairs={{0,1},{1,0},{2,3},{3,2},{4,5},{5,4},{6,7},{7,6},{8,9},{9,8},{10,11... | collective-permute-start | bytes 2064392 | tf_op jit(solution)/shard_map/ppermute | solution.py:198
  96.4 1.5 copy-done.2
  97.9 1.9 %expand.4.refs_4_ = f32[384,256]{1,0:T(8,128)S(1)} custom-call(s32[2]{0:T(128)S(1)} %pad_add_fusion.1.place_ref, bf16[7168,128]{1,0:T(8,128)(2,1)S(1)} %bitcast.38, bf16[7168,128]{1,0:T(8,128)(2,1)S(1)} %bitcast.42, bf16[384,896]{1,0:T(8,128)(2,1)} %pack.1.refs_0_, bf16[384,896]{1,0:T(8,128)(2,1)} %collective-permute-done.13.refs_1_), custom_call_target="tpu_custom_call" | custom-call | flops 352321536 | bytes 688128 | tf_op jit(solution)/shard_map/expand/pallas_call | solution.py:111
  99.8 2.3 %expand.5.refs_1_ = f32[384,256]{1,0:T(8,128)S(1)} custom-call(s32[4]{0:T(128)S(1)} %pad_add_fusion.place_ref, bf16[7168,128]{1,0:T(8,128)(2,1)S(1)} %bitcast.39, bf16[7168,128]{1,0:T(8,128)(2,1)S(1)} %bitcast.43, bf16[384,896]{1,0:T(8,128)(2,1)S(1)} %collective-permute-done.7.refs_0_, bf16[384,896]{1,0:T(8,128)(2,1)S(1)} %collective-permute-done.8.refs_1_, ...), custom_call_target="tpu_custom_call" | custom-call | flops 704643072 | bytes 1376256 | tf_op jit(solution)/shard_map/expand/pallas_call | solution.py:111
  102.1 1.5 expand.6.refs_1_
  103.7 1.6 expand.7.refs_0_
  105.4 2.6 %collective-permute-start.15 = (bf16[384,128]{1,0:T(8,128)(2,1)S(1)}, bf16[384,128]{1,0:T(8,128)(2,1)S(1)}, u32[]{:S(2)}, u32[]{:S(2)}) collective-permute-start(bf16[384,128]{1,0:T(8,128)(2,1)S(1)} %expand.7.refs_0_), channel_id=1, source_target_pairs={{0,4},{1,5},{2,6},{3,7},{4,0},{5,1},{6,2},{7,3},{8,12},{9,13},{10,... | collective-permute-start | bytes 294920 | tf_op jit(solution)/shard_map/ppermute | solution.py:198
  108.0 3.0 %collective-permute-done.14.refs_1_ = bf16[384,128]{1,0:T(8,128)(2,1)S(1)} collective-permute-done((bf16[384,128]{1,0:T(8,128)(2,1)S(1)}, bf16[384,128]{1,0:T(8,128)(2,1)S(1)}, u32[]{:S(2)}, u32[]{:S(2)}) %collective-permute-start.14) | collective-permute-done | bytes 98336 | tf_op jit(solution)/shard_map/ppermute | solution.py:198
  111.0 2.0 %collective-permute-done.15.refs_2_ = bf16[384,128]{1,0:T(8,128)(2,1)S(1)} collective-permute-done((bf16[384,128]{1,0:T(8,128)(2,1)S(1)}, bf16[384,128]{1,0:T(8,128)(2,1)S(1)}, u32[]{:S(2)}, u32[]{:S(2)}) %collective-permute-start.15) | collective-permute-done | bytes 98336 | tf_op jit(solution)/shard_map/ppermute | solution.py:198
  118.6 1.9 %down.1 = bf16[5632,128]{1,0:T(8,128)(2,1)S(1)} custom-call(f32[384,1]{1,0:T(8,128)S(1)} %copy.19.weight_ref, s32[1,384]{1,0:T(1,128)S(1)} %compare_select_fusion.column_ref, bf16[384,128]{1,0:T(8,128)(2,1)S(1)} %expand.7.refs_0_, bf16[384,128]{1,0:T(8,128)(2,1)S(1)} %collective-permute-done.14.refs_1_, ...), custom_call_target="tpu_custom_call" | custom-call | tf_op jit(solution)/shard_map/down/pallas_call | solution.py:149
  120.5 50.0 %all_to_all.10 = bf16[256,11,2,128]{3,2,1,0:T(2,128)(2,1)S(1)} all-to-all(bf16[256,11,2,128]{3,2,1,0:T(2,128)(2,1)S(1)} %bitcast.46), channel_id=1, replica_groups=mesh['node'=32,'x'=4,'core'=2] {'node','x','core'}, dimensions={0} | all-to-all | bytes 2883584 | tf_op jit(solution)/shard_map/all_to_all | solution.py:189
  170.4 2.4 %place.1 = bf16[128,7168]{1,0:T(8,128)(2,1)} custom-call(bf16[96,128]{1,0:T(8,128)(2,1)S(1)} %copy-done.20, bf16[5632,128]{1,0:T(8,128)(2,1)S(1)} %bitcast.48), custom_call_target="tpu_custom_call" | custom-call | tf_op jit(solution)/shard_map/place/pallas_call | solution.py:176
  (99 shorter events, 22.9 us)
Async XLA Ops:
  0.0 115.4 %copy-start = (f32[32,384]{1,0:T(8,128)S(1)}, f32[32,384]{1,0:T(8,128)}, u32[]{:S(2)}) copy-start(f32[32,384]{1,0:T(8,128)} %param.13) | copy-start | bytes 147460
  5.6 56.2 %all-to-all-start = ((bf16[256,11,2,128]{3,2,1,0:T(2,128)(2,1)}), bf16[256,11,2,128]{3,2,1,0:T(2,128)(2,1)S(1)}, u32[]{:S(2)}, u32[]{:S(2)}) async-start(bf16[256,11,2,128]{3,2,1,0:T(2,128)(2,1)} %bitcast.6), calls=%async_computation | async-start | bytes 2883584 | tf_op jit(solution)/shard_map/all_to_all | solution.py:189
  22.6 9.3 %collective-permute-start = (bf16[128,896]{1,0:T(8,128)(2,1)}, bf16[128,896]{1,0:T(8,128)(2,1)S(1)}, u32[]{:S(2)}, u32[]{:S(2)}) collective-permute-start(bf16[128,896]{1,0:T(8,128)(2,1)} %get-tuple-element.40), channel_id=1, source_target_pairs={{0,2},{1,3},{2,4},{3,5},{4,6},{5,7},{6,0},{7,1},{8,10},{9,11},{10,... | collective-permute-start | bytes 688136 | tf_op jit(solution)/shard_map/ppermute | solution.py:198
  24.0 23.2 %collective-permute-start.1 = (bf16[128,896]{1,0:T(8,128)(2,1)}, bf16[128,896]{1,0:T(8,128)(2,1)S(1)}, u32[]{:S(2)}, u32[]{:S(2)}) collective-permute-start(bf16[128,896]{1,0:T(8,128)(2,1)} %get-tuple-element.39), channel_id=1, source_target_pairs={{0,4},{1,5},{2,6},{3,7},{4,0},{5,1},{6,2},{7,3},{8,12},{9,13},{10,... | collective-permute-start | bytes 688136 | tf_op jit(solution)/shard_map/ppermute | solution.py:198
  26.4 22.9 %collective-permute-start.2 = (bf16[128,896]{1,0:T(8,128)(2,1)}, bf16[128,896]{1,0:T(8,128)(2,1)S(1)}, u32[]{:S(2)}, u32[]{:S(2)}) collective-permute-start(bf16[128,896]{1,0:T(8,128)(2,1)} %get-tuple-element.38), channel_id=1, source_target_pairs={{0,6},{1,7},{2,0},{3,1},{4,2},{5,3},{6,4},{7,5},{8,14},{9,15},{10,... | collective-permute-start | bytes 688136 | tf_op jit(solution)/shard_map/ppermute | solution.py:198
  27.6 22.4 %collective-permute-start.3 = (bf16[128,896]{1,0:T(8,128)(2,1)}, bf16[128,896]{1,0:T(8,128)(2,1)S(1)}, u32[]{:S(2)}, u32[]{:S(2)}) collective-permute-start(bf16[128,896]{1,0:T(8,128)(2,1)} %get-tuple-element.37), channel_id=1, source_target_pairs={{0,1},{1,0},{2,3},{3,2},{4,5},{5,4},{6,7},{7,6},{8,9},{9,8},{10,11... | collective-permute-start | bytes 688136 | tf_op jit(solution)/shard_map/ppermute | solution.py:198
  28.8 23.4 %collective-permute-start.4 = (bf16[128,896]{1,0:T(8,128)(2,1)}, bf16[128,896]{1,0:T(8,128)(2,1)S(1)}, u32[]{:S(2)}, u32[]{:S(2)}) collective-permute-start(bf16[128,896]{1,0:T(8,128)(2,1)} %get-tuple-element.36), channel_id=1, source_target_pairs={{0,3},{1,2},{2,5},{3,4},{4,7},{5,6},{6,1},{7,0},{8,11},{9,10},{10,... | collective-permute-start | bytes 688136 | tf_op jit(solution)/shard_map/ppermute | solution.py:198
  31.9 29.9 %copy-start.5 = (bf16[128,896]{1,0:T(8,128)(2,1)}, bf16[128,896]{1,0:T(8,128)(2,1)S(1)}, u32[]{:S(2)}) copy-start(bf16[128,896]{1,0:T(8,128)(2,1)S(1)} %collective-permute-done.refs_7_) | copy-start | bytes 688132
  31.9 28.5 %collective-permute-start.5 = (bf16[128,896]{1,0:T(8,128)(2,1)}, bf16[128,896]{1,0:T(8,128)(2,1)S(1)}, u32[]{:S(2)}, u32[]{:S(2)}) collective-permute-start(bf16[128,896]{1,0:T(8,128)(2,1)} %get-tuple-element.35), channel_id=1, source_target_pairs={{0,5},{1,4},{2,7},{3,6},{4,1},{5,0},{6,3},{7,2},{8,13},{9,12},{10,... | collective-permute-start | bytes 688136 | tf_op jit(solution)/shard_map/ppermute | solution.py:198
  47.8 13.3 %collective-permute-start.6 = (bf16[128,896]{1,0:T(8,128)(2,1)}, bf16[128,896]{1,0:T(8,128)(2,1)S(1)}, u32[]{:S(2)}, u32[]{:S(2)}) collective-permute-start(bf16[128,896]{1,0:T(8,128)(2,1)} %get-tuple-element.34), channel_id=1, source_target_pairs={{0,7},{1,6},{2,1},{3,0},{4,3},{5,2},{6,5},{7,4},{8,15},{9,14},{10,... | collective-permute-start | bytes 688136 | tf_op jit(solution)/shard_map/ppermute | solution.py:198
  62.7 33.7 %copy-start.1 = (bf16[1,7168,128]{2,1,0:T(8,128)(2,1)S(1)}, bf16[1,7168,128]{2,1,0:T(8,128)(2,1)}, u32[]{:S(2)}) copy-start(bf16[1,7168,128]{2,1,0:T(8,128)(2,1)} %param.8) | copy-start | bytes 5505028
  64.6 18.6 %collective-permute-start.7 = (bf16[384,896]{1,0:T(8,128)(2,1)}, bf16[384,896]{1,0:T(8,128)(2,1)S(1)}, u32[]{:S(2)}, u32[]{:S(2)}) collective-permute-start(bf16[384,896]{1,0:T(8,128)(2,1)} %pack.1.refs_0_), channel_id=1, source_target_pairs={{0,2},{1,3},{2,4},{3,5},{4,6},{5,7},{6,0},{7,1},{8,10},{9,11},{10,... | collective-permute-start | bytes 2064392 | tf_op jit(solution)/shard_map/ppermute | solution.py:198
  64.7 18.5 %collective-permute-start.8 = (bf16[384,896]{1,0:T(8,128)(2,1)}, bf16[384,896]{1,0:T(8,128)(2,1)S(1)}, u32[]{:S(2)}, u32[]{:S(2)}) collective-permute-start(bf16[384,896]{1,0:T(8,128)(2,1)} %pack.1.refs_0_), channel_id=1, source_target_pairs={{0,6},{1,7},{2,0},{3,1},{4,2},{5,3},{6,4},{7,5},{8,14},{9,15},{10,... | collective-permute-start | bytes 2064392 | tf_op jit(solution)/shard_map/ppermute | solution.py:198
  83.2 10.4 %collective-permute-start.9 = (bf16[384,896]{1,0:T(8,128)(2,1)S(1)}, bf16[384,896]{1,0:T(8,128)(2,1)}, u32[]{:S(2)}, u32[]{:S(2)}) collective-permute-start(bf16[384,896]{1,0:T(8,128)(2,1)S(1)} %broadcast_select_fusion), channel_id=1, source_target_pairs={{0,2},{1,7},{2,4},{3,1},{4,6},{5,3},{6,0},{7,5},{8,10},{9,15},{10,... | collective-permute-start | bytes 2064392 | tf_op jit(solution)/shard_map/ppermute | solution.py:207
  85.7 10.7 %collective-permute-start.13 = (bf16[384,896]{1,0:T(8,128)(2,1)}, bf16[384,896]{1,0:T(8,128)(2,1)}, u32[]{:S(2)}, u32[]{:S(2)}) collective-permute-start(bf16[384,896]{1,0:T(8,128)(2,1)} %pack.1.refs_0_), channel_id=1, source_target_pairs={{0,1},{1,0},{2,3},{3,2},{4,5},{5,4},{6,7},{7,6},{8,9},{9,8},{10,11... | collective-permute-start | bytes 2064392 | tf_op jit(solution)/shard_map/ppermute | solution.py:198
  85.7 14.1 %collective-permute-start.11 = (bf16[384,896]{1,0:T(8,128)(2,1)S(1)}, bf16[384,896]{1,0:T(8,128)(2,1)}, u32[]{:S(2)}, u32[]{:S(2)}) collective-permute-start(bf16[384,896]{1,0:T(8,128)(2,1)S(1)} %collective-permute-done.7.refs_0_), channel_id=1, source_target_pairs={{0,1},{1,0},{2,3},{3,2},{4,5},{5,4},{6,7},{7,6},{8,9},{9,8},{10,11... | collective-permute-start | bytes 2064392 | tf_op jit(solution)/shard_map/ppermute | solution.py:198
  86.2 13.6 %collective-permute-start.12 = (bf16[384,896]{1,0:T(8,128)(2,1)S(1)}, bf16[384,896]{1,0:T(8,128)(2,1)}, u32[]{:S(2)}, u32[]{:S(2)}) collective-permute-start(bf16[384,896]{1,0:T(8,128)(2,1)S(1)} %collective-permute-done.8.refs_1_), channel_id=1, source_target_pairs={{0,1},{1,0},{2,3},{3,2},{4,5},{5,4},{6,7},{7,6},{8,9},{9,8},{10,11... | collective-permute-start | bytes 2064392 | tf_op jit(solution)/shard_map/ppermute | solution.py:198
  93.6 10.0 %collective-permute-start.10 = (bf16[384,896]{1,0:T(8,128)(2,1)}, bf16[384,896]{1,0:T(8,128)(2,1)}, u32[]{:S(2)}, u32[]{:S(2)}) collective-permute-start(bf16[384,896]{1,0:T(8,128)(2,1)} %collective-permute-done.9.refs_0_), channel_id=1, source_target_pairs={{0,1},{1,0},{2,3},{3,2},{4,5},{5,4},{6,7},{7,6},{8,9},{9,8},{10,11... | collective-permute-start | bytes 2064392 | tf_op jit(solution)/shard_map/ppermute | solution.py:198
  105.3 5.7 %collective-permute-start.14 = (bf16[384,128]{1,0:T(8,128)(2,1)S(1)}, bf16[384,128]{1,0:T(8,128)(2,1)S(1)}, u32[]{:S(2)}, u32[]{:S(2)}) collective-permute-start(bf16[384,128]{1,0:T(8,128)(2,1)S(1)} %expand.7.refs_0_), channel_id=1, source_target_pairs={{0,2},{1,3},{2,4},{3,5},{4,6},{5,7},{6,0},{7,1},{8,10},{9,11},{10,... | collective-permute-start | bytes 294920 | tf_op jit(solution)/shard_map/ppermute | solution.py:198
  105.4 7.7 %collective-permute-start.15 = (bf16[384,128]{1,0:T(8,128)(2,1)S(1)}, bf16[384,128]{1,0:T(8,128)(2,1)S(1)}, u32[]{:S(2)}, u32[]{:S(2)}) collective-permute-start(bf16[384,128]{1,0:T(8,128)(2,1)S(1)} %expand.7.refs_0_), channel_id=1, source_target_pairs={{0,4},{1,5},{2,6},{3,7},{4,0},{5,1},{6,2},{7,3},{8,12},{9,13},{10,... | collective-permute-start | bytes 294920 | tf_op jit(solution)/shard_map/ppermute | solution.py:198
  108.0 5.4 %collective-permute-start.16 = (bf16[384,128]{1,0:T(8,128)(2,1)S(1)}, bf16[384,128]{1,0:T(8,128)(2,1)S(1)}, u32[]{:S(2)}, u32[]{:S(2)}) collective-permute-start(bf16[384,128]{1,0:T(8,128)(2,1)S(1)} %expand.7.refs_0_), channel_id=1, source_target_pairs={{0,6},{1,7},{2,0},{3,1},{4,2},{5,3},{6,4},{7,5},{8,14},{9,15},{10,... | collective-permute-start | bytes 294920 | tf_op jit(solution)/shard_map/ppermute | solution.py:198
  113.4 3.2 %collective-permute-start.18 = (bf16[3,384,128]{2,1,0:T(8,128)(2,1)S(1)}, bf16[3,384,128]{2,1,0:T(8,128)(2,1)S(1)}, u32[]{:S(2)}, u32[]{:S(2)}) collective-permute-start(bf16[3,384,128]{2,1,0:T(8,128)(2,1)S(1)} %pad_maximum_fusion), channel_id=1, source_target_pairs={{0,1},{1,0},{2,3},{3,2},{4,5},{5,4},{6,7},{7,6},{8,9},{9,8},{10,11... | collective-permute-start | bytes 884744 | tf_op jit(solution)/shard_map/ppermute | solution.py:198
  115.3 1.4 collective-permute-start.17
  120.4 50.0 %copy-start.20 = (bf16[96,128]{1,0:T(8,128)(2,1)S(1)}, bf16[96,128]{1,0:T(8,128)(2,1)}, u32[]{:S(2)}) copy-start(bf16[96,128]{1,0:T(8,128)(2,1)} %copy-done.19) | copy-start | bytes 73732
  (21 other events, 143.6 us)

commit v4 on v3

--- a/solution.py
+++ b/solution.py
@@ -15,7 +15,7 @@
 PARTS = (7,)
 BF16 = jnp.bfloat16
 F32 = jnp.float32
-PARAMS = pltpu.CompilerParams(vmem_limit_bytes=24 * 2**20)
+PARAMS = pltpu.CompilerParams(vmem_limit_bytes=14 * 2**20)
 VMEM = pl.BlockSpec(memory_space=pltpu.VMEM)
 
 
@@ -257,21 +257,23 @@
     first = 0
     for n, (msg, tiles) in enumerate(zip(arrived, PARTS)):
         own = pack(column[:, None], msg, tiles)
-        fore, aft, other = sent(own, 1, 0), sent(own, -1, 0), sent(own, 0, 1)
-        far = forwarded(fore, aft)
-        stages = [
-            [(own, 0, 0), (other, 0, 1)],
-            [(fore, 1, 0), (aft, -1, 0), (sent(fore, 0, 1), 1, 1), (sent(aft, 0, 1), -1, 1)],
-            [(far, 2, 0)],
-            [(sent(far, 0, 1), 2, 1)],
-        ]
-        for m, stage in enumerate(stages):
+
+        def add(total, blocks, last=False):
             places = []
-            for _, dx, flip in stage:
+            for _, dx, flip in blocks:
                 source = (at_x - dx) % nx * nc + (at_core + flip) % nc
                 places.append(source * cut + first * LANE)
-            last = n == len(PARTS) - 1 and m == len(stages) - 1
-            total = expand(total, [block for block, _, _ in stage], places, w_gate[0], w_up[0], last)
+            return expand(total, [block for block, _, _ in blocks], places, w_gate[0], w_up[0], last)
+
+        fore, aft = sent(own, 1, 0), sent(own, -1, 0)
+        total = add(total, [(own, 0, 0), (sent(own, 0, 1), 0, 1)])
+        fore, aft, total = lax.optimization_barrier((fore, aft, total))
+        far = forwarded(fore, aft)
+        near = [(fore, 1, 0), (aft, -1, 0), (sent(fore, 0, 1), 1, 1), (sent(aft, 0, 1), -1, 1)]
+        total = add(total, near)
+        far, total = lax.optimization_barrier((far, total))
+        total = add(total, [(far, 2, 0)])
+        total = add(total, [(sent(far, 0, 1), 2, 1)], last=n == len(PARTS) - 1)
         first += tiles
     hidden = total
 

time: 173 us -> 171 us (0.988)
  waiting for transfers between devices: 38.8 us -> 30.4 us
  local copies, waits for them, and re-layouts: 12.7 us -> 16.9 us
  other arithmetic: 5.68 us -> 9.34 us
  starting transfers between devices: 49.6 us -> 47.4 us
    ppermute x1, waiting for transfers between devices: 7.37 us -> 2.58 us  [forwarded(): lax.ppermute(jnp.where(lax.axis_index('core') == 0, fore, aft), LOCAL, pa...]
    ppermute x18, waiting for transfers between devices: 31.4 us -> 27.8 us  [sent(): return lax.ppermute(value, LOCAL, pairs)]
    unnamed x50 -> x42, local copies, waits for them, and re-layouts: 9.99 us -> 12.7 us
    ppermute x18, starting transfers between devices: 31.5 us -> 29.1 us  [sent(): return lax.ppermute(value, LOCAL, pairs)]
  transfers between devices with their start and end apart: 20 -> 20, of which waited for: 8 -> 8; matrix products, arithmetic and copies ran while one was open for 4% -> 7% of each run, Pallas kernels for 3% -> 3%
where the time goes in v4:
time: 171 us; the launch traced here: 170 us
  blocking collectives  50.4 us (29%)
  starting transfers between devices  47.4 us (28%)
  waiting for transfers between devices  30.4 us (18%)
  local copies, waits for them, and re-layouts  16.9 us (10%)
  Pallas kernels  15.7 us (9%)
  other arithmetic  9.34 us (5%)
    all_to_all x1, blocking collectives, exchange(): lax.all_to_all(parts, AXES, split_axis=0, concat_axis=0, tiled=True)  50.4 us
    ppermute x18, starting transfers between devices, sent(): return lax.ppermute(value, LOCAL, pairs)  29.1 us
    ppermute x18, waiting for transfers between devices, sent(): return lax.ppermute(value, LOCAL, pairs)  27.8 us
    all_to_all x1, starting transfers between devices, exchange(): lax.all_to_all(parts, AXES, split_axis=0, concat_axis=0, tiled=True)  15.7 us
    unnamed x42, local copies, waits for them, and re-layouts  12.7 us
    pallas_call x4, Pallas kernels, expand(): pl.pallas_call(functools.partial(expand_kernel, len(blocks), opening, las...  6.02 us
  transfers between devices with their start and end apart: 20, of which 8 were waited for; matrix products, arithmetic and copies ran while one was open for 7% of the time, Pallas kernels for 3%

profile of v4, /device:TPU:1, one launch (start us, length us, event | category | flops | bytes accessed | tf_op | source)
XLA Modules:
  0.0 170.4 jit_solution(11329039237771040564)
XLA Ops:
  3.3 2.3 %send.1 = bf16[5632,128]{1,0:T(8,128)(2,1)} custom-call(bf16[96,128]{1,0:T(8,128)(2,1)S(1)} %add_convert_fusion.sel_ref, bf16[128,7168]{1,0:T(8,128)(2,1)S(1)} %copy-done.5), custom_call_target="tpu_custom_call" | custom-call | tf_op jit(solution)/shard_map/send/pallas_call | solution.py:50
  5.6 15.7 %all-to-all-start = ((bf16[256,11,2,128]{3,2,1,0:T(2,128)(2,1)}), bf16[256,11,2,128]{3,2,1,0:T(2,128)(2,1)S(1)}, u32[]{:S(2)}, u32[]{:S(2)}) async-start(bf16[256,11,2,128]{3,2,1,0:T(2,128)(2,1)} %bitcast.6), calls=%async_computation | async-start | bytes 2883584 | tf_op jit(solution)/shard_map/all_to_all | solution.py:189
  24.0 2.4 %collective-permute-start.1 = (bf16[128,896]{1,0:T(8,128)(2,1)}, bf16[128,896]{1,0:T(8,128)(2,1)}, u32[]{:S(2)}, u32[]{:S(2)}) collective-permute-start(bf16[128,896]{1,0:T(8,128)(2,1)} %get-tuple-element.49), channel_id=1, source_target_pairs={{0,4},{1,5},{2,6},{3,7},{4,0},{5,1},{6,2},{7,3},{8,12},{9,13},{10,... | collective-permute-start | bytes 688136 | tf_op jit(solution)/shard_map/ppermute | solution.py:198
  29.0 1.9 %fusion.22 = (s32[384]{0:T(512)}, s32[1,384]{1,0:T(1,128)}, s32[384,1]{0,1:T(1,128)}, s32[384]{0:T(512)S(1)}) fusion(s32[32,384]{1,0:T(8,128)} %param.11, s32[]{:T(128)S(6)} %select_n.197), kind=kLoop, calls=%fused_computation.77 | loop fusion | flops 5760 | bytes 7684 | tf_op jit(solution)/shard_map/jit(floor_divide)/jit(_where)/select_n | solution.py:250
  35.2 12.2 %collective-permute-start.5 = (bf16[128,896]{1,0:T(8,128)(2,1)}, bf16[128,896]{1,0:T(8,128)(2,1)S(1)}, u32[]{:S(2)}, u32[]{:S(2)}) collective-permute-start(bf16[128,896]{1,0:T(8,128)(2,1)} %get-tuple-element.45), channel_id=1, source_target_pairs={{0,5},{1,4},{2,7},{3,6},{4,1},{5,0},{6,3},{7,2},{8,13},{9,12},{10,... | collective-permute-start | bytes 688136 | tf_op jit(solution)/shard_map/ppermute | solution.py:198
  47.3 2.4 %fusion.4.column_ref = s32[384,1]{1,0:T(8,128)} fusion(s32[384]{0:T(512)S(1)} %convert_reduce_fusion, s32[384,1]{1,0:T(8,128)} %copy.14, s32[]{:T(128)} %bitcast.1), kind=kLoop, calls=%fused_computation.20 | loop fusion | flops 7296 | bytes 4612 | tf_op jit(solution)/shard_map/jit(_where)/select_n | solution.py:253
  49.7 2.5 %collective-permute-done.4.refs_11_ = bf16[128,896]{1,0:T(8,128)(2,1)} collective-permute-done((bf16[128,896]{1,0:T(8,128)(2,1)}, bf16[128,896]{1,0:T(8,128)(2,1)}, u32[]{:S(2)}, u32[]{:S(2)}) %collective-permute-start.4) | collective-permute-done | bytes 229408 | tf_op jit(solution)/shard_map/ppermute | solution.py:198
  52.2 8.2 %collective-permute-done.5.refs_12_ = bf16[128,896]{1,0:T(8,128)(2,1)S(1)} collective-permute-done((bf16[128,896]{1,0:T(8,128)(2,1)}, bf16[128,896]{1,0:T(8,128)(2,1)S(1)}, u32[]{:S(2)}, u32[]{:S(2)}) %collective-permute-start.5) | collective-permute-done | bytes 229408 | tf_op jit(solution)/shard_map/ppermute | solution.py:198
  62.7 1.8 %pack.1.refs_0_ = bf16[384,896]{1,0:T(8,128)(2,1)} custom-call(s32[384,1]{1,0:T(8,128)S(1)} %copy-done.10, bf16[5632,128]{1,0:T(8,128)(2,1)S(1)} %bitcast.47), custom_call_target="tpu_custom_call" | custom-call | tf_op jit(solution)/shard_map/pack/pallas_call | solution.py:77
  64.7 2.5 %collective-permute-start.8 = (bf16[384,896]{1,0:T(8,128)(2,1)}, bf16[384,896]{1,0:T(8,128)(2,1)S(1)}, u32[]{:S(2)}, u32[]{:S(2)}) collective-permute-start(bf16[384,896]{1,0:T(8,128)(2,1)} %pack.1.refs_0_), channel_id=1, source_target_pairs={{0,6},{1,7},{2,0},{3,1},{4,2},{5,3},{6,4},{7,5},{8,14},{9,15},{10,... | collective-permute-start | bytes 2064392 | tf_op jit(solution)/shard_map/ppermute | solution.py:198
  67.3 1.5 copy-done.2
  68.8 1.9 %expand.4.refs_4_ = f32[384,256]{1,0:T(8,128)S(1)} custom-call(s32[2]{0:T(128)S(1)} %pad_add_fusion.place_ref, bf16[7168,128]{1,0:T(8,128)(2,1)S(1)} %bitcast.38, bf16[7168,128]{1,0:T(8,128)(2,1)S(1)} %bitcast.42, bf16[384,896]{1,0:T(8,128)(2,1)} %pack.1.refs_0_, bf16[384,896]{1,0:T(8,128)(2,1)} %collective-permute-done.9.refs_1_), custom_call_target="tpu_custom_call" | custom-call | flops 352321536 | bytes 688128 | tf_op jit(solution)/shard_map/expand/pallas_call | solution.py:111
  71.4 11.0 %collective-permute-done.7.refs_0_ = bf16[384,896]{1,0:T(8,128)(2,1)S(1)} collective-permute-done((bf16[384,896]{1,0:T(8,128)(2,1)}, bf16[384,896]{1,0:T(8,128)(2,1)S(1)}, u32[]{:S(2)}, u32[]{:S(2)}) %collective-permute-start.7) | collective-permute-done | bytes 688160 | tf_op jit(solution)/shard_map/ppermute | solution.py:198
  84.8 2.7 %collective-permute-start.10 = (bf16[384,896]{1,0:T(8,128)(2,1)}, bf16[384,896]{1,0:T(8,128)(2,1)}, u32[]{:S(2)}, u32[]{:S(2)}) collective-permute-start(bf16[384,896]{1,0:T(8,128)(2,1)} %broadcast_select_fusion), channel_id=1, source_target_pairs={{0,2},{1,7},{2,4},{3,1},{4,6},{5,3},{6,0},{7,5},{8,10},{9,15},{10,... | collective-permute-start | bytes 2064392 | tf_op jit(solution)/shard_map/ppermute | solution.py:207
  90.0 2.3 %expand.5.refs_1_ = f32[384,256]{1,0:T(8,128)S(1)} custom-call(s32[4]{0:T(128)S(1)} %pad_add_fusion.1.place_ref, bf16[7168,128]{1,0:T(8,128)(2,1)S(1)} %bitcast.39, bf16[7168,128]{1,0:T(8,128)(2,1)S(1)} %bitcast.43, bf16[384,896]{1,0:T(8,128)(2,1)S(1)} %collective-permute-done.7.refs_0_, bf16[384,896]{1,0:T(8,128)(2,1)S(1)} %collective-permute-done.8.refs_1_, ...), custom_call_target="tpu_custom_call" | custom-call | flops 704643072 | bytes 1376256 | tf_op jit(solution)/shard_map/expand/pallas_call | solution.py:111
  93.1 2.6 %collective-permute-done.10.refs_0_ = bf16[384,896]{1,0:T(8,128)(2,1)} collective-permute-done((bf16[384,896]{1,0:T(8,128)(2,1)}, bf16[384,896]{1,0:T(8,128)(2,1)}, u32[]{:S(2)}, u32[]{:S(2)}) %collective-permute-start.10) | collective-permute-done | bytes 688160 | tf_op jit(solution)/shard_map/ppermute | solution.py:207
  95.6 2.1 %collective-permute-start.13 = (bf16[384,896]{1,0:T(8,128)(2,1)}, bf16[384,896]{1,0:T(8,128)(2,1)S(1)}, u32[]{:S(2)}, u32[]{:S(2)}) collective-permute-start(bf16[384,896]{1,0:T(8,128)(2,1)} %collective-permute-done.10.refs_0_), channel_id=1, source_target_pairs={{0,1},{1,0},{2,3},{3,2},{4,5},{5,4},{6,7},{7,6},{8,9},{9,8},{10,11... | collective-permute-start | bytes 2064392 | tf_op jit(solution)/shard_map/ppermute | solution.py:198
  97.7 1.5 copy-done.4
  102.2 2.6 %collective-permute-start.15 = (bf16[384,128]{1,0:T(8,128)(2,1)S(1)}, bf16[384,128]{1,0:T(8,128)(2,1)S(1)}, u32[]{:S(2)}, u32[]{:S(2)}) collective-permute-start(bf16[384,128]{1,0:T(8,128)(2,1)S(1)} %expand.7.refs_0_), channel_id=1, source_target_pairs={{0,4},{1,5},{2,6},{3,7},{4,0},{5,1},{6,2},{7,3},{8,12},{9,13},{10,... | collective-permute-start | bytes 294920 | tf_op jit(solution)/shard_map/ppermute | solution.py:198
  105.3 2.7 %collective-permute-done.14.refs_1_ = bf16[384,128]{1,0:T(8,128)(2,1)S(1)} collective-permute-done((bf16[384,128]{1,0:T(8,128)(2,1)S(1)}, bf16[384,128]{1,0:T(8,128)(2,1)S(1)}, u32[]{:S(2)}, u32[]{:S(2)}) %collective-permute-start.14) | collective-permute-done | bytes 98336 | tf_op jit(solution)/shard_map/ppermute | solution.py:198
  107.9 1.9 %collective-permute-done.15.refs_2_ = bf16[384,128]{1,0:T(8,128)(2,1)S(1)} collective-permute-done((bf16[384,128]{1,0:T(8,128)(2,1)S(1)}, bf16[384,128]{1,0:T(8,128)(2,1)S(1)}, u32[]{:S(2)}, u32[]{:S(2)}) %collective-permute-start.15) | collective-permute-done | bytes 98336 | tf_op jit(solution)/shard_map/ppermute | solution.py:198
  114.4 3.2 %down.1 = bf16[5632,128]{1,0:T(8,128)(2,1)S(1)} custom-call(f32[384,1]{1,0:T(8,128)S(1)} %copy.19.weight_ref, s32[1,384]{1,0:T(1,128)S(1)} %compare_select_fusion.column_ref, bf16[384,128]{1,0:T(8,128)(2,1)S(1)} %expand.7.refs_0_, bf16[384,128]{1,0:T(8,128)(2,1)S(1)} %collective-permute-done.14.refs_1_, ...), custom_call_target="tpu_custom_call" | custom-call | tf_op jit(solution)/shard_map/down/pallas_call | solution.py:149
  117.7 50.4 %all_to_all.10 = bf16[256,11,2,128]{3,2,1,0:T(2,128)(2,1)S(1)} all-to-all(bf16[256,11,2,128]{3,2,1,0:T(2,128)(2,1)S(1)} %bitcast.46), channel_id=1, replica_groups=mesh['node'=32,'x'=4,'core'=2] {'node','x','core'}, dimensions={0} | all-to-all | bytes 2883584 | tf_op jit(solution)/shard_map/all_to_all | solution.py:189
  168.0 2.4 %place.1 = bf16[128,7168]{1,0:T(8,128)(2,1)} custom-call(bf16[96,128]{1,0:T(8,128)(2,1)S(1)} %copy-done.16, bf16[5632,128]{1,0:T(8,128)(2,1)S(1)} %bitcast.48), custom_call_target="tpu_custom_call" | custom-call | tf_op jit(solution)/shard_map/place/pallas_call | solution.py:176
  (91 shorter events, 29.6 us)
Async XLA Ops:
  0.0 112.2 %copy-start = (f32[32,384]{1,0:T(8,128)S(1)}, f32[32,384]{1,0:T(8,128)}, u32[]{:S(2)}) copy-start(f32[32,384]{1,0:T(8,128)} %param.13) | copy-start | bytes 147460
  5.6 56.2 %all-to-all-start = ((bf16[256,11,2,128]{3,2,1,0:T(2,128)(2,1)}), bf16[256,11,2,128]{3,2,1,0:T(2,128)(2,1)S(1)}, u32[]{:S(2)}, u32[]{:S(2)}) async-start(bf16[256,11,2,128]{3,2,1,0:T(2,128)(2,1)} %bitcast.6), calls=%async_computation | async-start | bytes 2883584 | tf_op jit(solution)/shard_map/all_to_all | solution.py:189
  22.6 44.7 %copy-start.1 = (bf16[1,7168,128]{2,1,0:T(8,128)(2,1)S(1)}, bf16[1,7168,128]{2,1,0:T(8,128)(2,1)}, u32[]{:S(2)}) copy-start(bf16[1,7168,128]{2,1,0:T(8,128)(2,1)} %param.8) | copy-start | bytes 5505028
  22.6 12.5 %collective-permute-start = (bf16[128,896]{1,0:T(8,128)(2,1)}, bf16[128,896]{1,0:T(8,128)(2,1)}, u32[]{:S(2)}, u32[]{:S(2)}) collective-permute-start(bf16[128,896]{1,0:T(8,128)(2,1)} %get-tuple-element.50), channel_id=1, source_target_pairs={{0,2},{1,3},{2,4},{3,5},{4,6},{5,7},{6,0},{7,1},{8,10},{9,11},{10,... | collective-permute-start | bytes 688136 | tf_op jit(solution)/shard_map/ppermute | solution.py:198
  24.0 23.3 %collective-permute-start.1 = (bf16[128,896]{1,0:T(8,128)(2,1)}, bf16[128,896]{1,0:T(8,128)(2,1)}, u32[]{:S(2)}, u32[]{:S(2)}) collective-permute-start(bf16[128,896]{1,0:T(8,128)(2,1)} %get-tuple-element.49), channel_id=1, source_target_pairs={{0,4},{1,5},{2,6},{3,7},{4,0},{5,1},{6,2},{7,3},{8,12},{9,13},{10,... | collective-permute-start | bytes 688136 | tf_op jit(solution)/shard_map/ppermute | solution.py:198
  26.4 23.3 %collective-permute-start.2 = (bf16[128,896]{1,0:T(8,128)(2,1)}, bf16[128,896]{1,0:T(8,128)(2,1)}, u32[]{:S(2)}, u32[]{:S(2)}) collective-permute-start(bf16[128,896]{1,0:T(8,128)(2,1)} %get-tuple-element.48), channel_id=1, source_target_pairs={{0,6},{1,7},{2,0},{3,1},{4,2},{5,3},{6,4},{7,5},{8,14},{9,15},{10,... | collective-permute-start | bytes 688136 | tf_op jit(solution)/shard_map/ppermute | solution.py:198
  27.6 22.1 %collective-permute-start.3 = (bf16[128,896]{1,0:T(8,128)(2,1)}, bf16[128,896]{1,0:T(8,128)(2,1)}, u32[]{:S(2)}, u32[]{:S(2)}) collective-permute-start(bf16[128,896]{1,0:T(8,128)(2,1)} %get-tuple-element.47), channel_id=1, source_target_pairs={{0,1},{1,0},{2,3},{3,2},{4,5},{5,4},{6,7},{7,6},{8,9},{9,8},{10,11... | collective-permute-start | bytes 688136 | tf_op jit(solution)/shard_map/ppermute | solution.py:198
  28.8 23.4 %collective-permute-start.4 = (bf16[128,896]{1,0:T(8,128)(2,1)}, bf16[128,896]{1,0:T(8,128)(2,1)}, u32[]{:S(2)}, u32[]{:S(2)}) collective-permute-start(bf16[128,896]{1,0:T(8,128)(2,1)} %get-tuple-element.46), channel_id=1, source_target_pairs={{0,3},{1,2},{2,5},{3,4},{4,7},{5,6},{6,1},{7,0},{8,11},{9,10},{10,... | collective-permute-start | bytes 688136 | tf_op jit(solution)/shard_map/ppermute | solution.py:198
  35.1 25.3 %copy-start.18 = (s32[384]{0:T(512)}, s32[384]{0:T(512)S(1)}, u32[]{:S(2)}) copy-start(s32[384]{0:T(512)S(1)} %convert_reduce_fusion) | copy-start | bytes 4612
  35.2 25.2 %collective-permute-start.5 = (bf16[128,896]{1,0:T(8,128)(2,1)}, bf16[128,896]{1,0:T(8,128)(2,1)S(1)}, u32[]{:S(2)}, u32[]{:S(2)}) collective-permute-start(bf16[128,896]{1,0:T(8,128)(2,1)} %get-tuple-element.45), channel_id=1, source_target_pairs={{0,5},{1,4},{2,7},{3,6},{4,1},{5,0},{6,3},{7,2},{8,13},{9,12},{10,... | collective-permute-start | bytes 688136 | tf_op jit(solution)/shard_map/ppermute | solution.py:198
  47.3 13.8 %collective-permute-start.6 = (bf16[128,896]{1,0:T(8,128)(2,1)}, bf16[128,896]{1,0:T(8,128)(2,1)S(1)}, u32[]{:S(2)}, u32[]{:S(2)}) collective-permute-start(bf16[128,896]{1,0:T(8,128)(2,1)} %get-tuple-element.44), channel_id=1, source_target_pairs={{0,7},{1,6},{2,1},{3,0},{4,3},{5,2},{6,5},{7,4},{8,15},{9,14},{10,... | collective-permute-start | bytes 688136 | tf_op jit(solution)/shard_map/ppermute | solution.py:198
  64.6 2.8 %collective-permute-start.9 = (bf16[384,896]{1,0:T(8,128)(2,1)}, bf16[384,896]{1,0:T(8,128)(2,1)}, u32[]{:S(2)}, u32[]{:S(2)}) collective-permute-start(bf16[384,896]{1,0:T(8,128)(2,1)} %pack.1.refs_0_), channel_id=1, source_target_pairs={{0,1},{1,0},{2,3},{3,2},{4,5},{5,4},{6,7},{7,6},{8,9},{9,8},{10,11... | collective-permute-start | bytes 2064392 | tf_op jit(solution)/shard_map/ppermute | solution.py:198
  64.6 17.9 %collective-permute-start.7 = (bf16[384,896]{1,0:T(8,128)(2,1)}, bf16[384,896]{1,0:T(8,128)(2,1)S(1)}, u32[]{:S(2)}, u32[]{:S(2)}) collective-permute-start(bf16[384,896]{1,0:T(8,128)(2,1)} %pack.1.refs_0_), channel_id=1, source_target_pairs={{0,2},{1,3},{2,4},{3,5},{4,6},{5,7},{6,0},{7,1},{8,10},{9,11},{10,... | collective-permute-start | bytes 2064392 | tf_op jit(solution)/shard_map/ppermute | solution.py:198
  64.7 17.7 %collective-permute-start.8 = (bf16[384,896]{1,0:T(8,128)(2,1)}, bf16[384,896]{1,0:T(8,128)(2,1)S(1)}, u32[]{:S(2)}, u32[]{:S(2)}) collective-permute-start(bf16[384,896]{1,0:T(8,128)(2,1)} %pack.1.refs_0_), channel_id=1, source_target_pairs={{0,6},{1,7},{2,0},{3,1},{4,2},{5,3},{6,4},{7,5},{8,14},{9,15},{10,... | collective-permute-start | bytes 2064392 | tf_op jit(solution)/shard_map/ppermute | solution.py:198
  82.5 5.0 %collective-permute-start.11 = (bf16[384,896]{1,0:T(8,128)(2,1)S(1)}, bf16[384,896]{1,0:T(8,128)(2,1)}, u32[]{:S(2)}, u32[]{:S(2)}) collective-permute-start(bf16[384,896]{1,0:T(8,128)(2,1)S(1)} %collective-permute-done.7.refs_0_), channel_id=1, source_target_pairs={{0,1},{1,0},{2,3},{3,2},{4,5},{5,4},{6,7},{7,6},{8,9},{9,8},{10,11... | collective-permute-start | bytes 2064392 | tf_op jit(solution)/shard_map/ppermute | solution.py:198
  83.8 3.7 %collective-permute-start.12 = (bf16[384,896]{1,0:T(8,128)(2,1)S(1)}, bf16[384,896]{1,0:T(8,128)(2,1)}, u32[]{:S(2)}, u32[]{:S(2)}) collective-permute-start(bf16[384,896]{1,0:T(8,128)(2,1)S(1)} %collective-permute-done.8.refs_1_), channel_id=1, source_target_pairs={{0,1},{1,0},{2,3},{3,2},{4,5},{5,4},{6,7},{7,6},{8,9},{9,8},{10,11... | collective-permute-start | bytes 2064392 | tf_op jit(solution)/shard_map/ppermute | solution.py:198
  84.8 10.9 %collective-permute-start.10 = (bf16[384,896]{1,0:T(8,128)(2,1)}, bf16[384,896]{1,0:T(8,128)(2,1)}, u32[]{:S(2)}, u32[]{:S(2)}) collective-permute-start(bf16[384,896]{1,0:T(8,128)(2,1)} %broadcast_select_fusion), channel_id=1, source_target_pairs={{0,2},{1,7},{2,4},{3,1},{4,6},{5,3},{6,0},{7,5},{8,10},{9,15},{10,... | collective-permute-start | bytes 2064392 | tf_op jit(solution)/shard_map/ppermute | solution.py:207
  95.6 6.1 %collective-permute-start.13 = (bf16[384,896]{1,0:T(8,128)(2,1)}, bf16[384,896]{1,0:T(8,128)(2,1)S(1)}, u32[]{:S(2)}, u32[]{:S(2)}) collective-permute-start(bf16[384,896]{1,0:T(8,128)(2,1)} %collective-permute-done.10.refs_0_), channel_id=1, source_target_pairs={{0,1},{1,0},{2,3},{3,2},{4,5},{5,4},{6,7},{7,6},{8,9},{9,8},{10,11... | collective-permute-start | bytes 2064392 | tf_op jit(solution)/shard_map/ppermute | solution.py:198
  102.1 5.8 %collective-permute-start.14 = (bf16[384,128]{1,0:T(8,128)(2,1)S(1)}, bf16[384,128]{1,0:T(8,128)(2,1)S(1)}, u32[]{:S(2)}, u32[]{:S(2)}) collective-permute-start(bf16[384,128]{1,0:T(8,128)(2,1)S(1)} %expand.7.refs_0_), channel_id=1, source_target_pairs={{0,2},{1,3},{2,4},{3,5},{4,6},{5,7},{6,0},{7,1},{8,10},{9,11},{10,... | collective-permute-start | bytes 294920 | tf_op jit(solution)/shard_map/ppermute | solution.py:198
  102.2 7.6 %collective-permute-start.15 = (bf16[384,128]{1,0:T(8,128)(2,1)S(1)}, bf16[384,128]{1,0:T(8,128)(2,1)S(1)}, u32[]{:S(2)}, u32[]{:S(2)}) collective-permute-start(bf16[384,128]{1,0:T(8,128)(2,1)S(1)} %expand.7.refs_0_), channel_id=1, source_target_pairs={{0,4},{1,5},{2,6},{3,7},{4,0},{5,1},{6,2},{7,3},{8,12},{9,13},{10,... | collective-permute-start | bytes 294920 | tf_op jit(solution)/shard_map/ppermute | solution.py:198
  104.9 5.4 %collective-permute-start.16 = (bf16[384,128]{1,0:T(8,128)(2,1)S(1)}, bf16[384,128]{1,0:T(8,128)(2,1)S(1)}, u32[]{:S(2)}, u32[]{:S(2)}) collective-permute-start(bf16[384,128]{1,0:T(8,128)(2,1)S(1)} %expand.7.refs_0_), channel_id=1, source_target_pairs={{0,6},{1,7},{2,0},{3,1},{4,2},{5,3},{6,4},{7,5},{8,14},{9,15},{10,... | collective-permute-start | bytes 294920 | tf_op jit(solution)/shard_map/ppermute | solution.py:198
  110.3 3.2 %collective-permute-start.18 = (bf16[3,384,128]{2,1,0:T(8,128)(2,1)S(1)}, bf16[3,384,128]{2,1,0:T(8,128)(2,1)S(1)}, u32[]{:S(2)}, u32[]{:S(2)}) collective-permute-start(bf16[3,384,128]{2,1,0:T(8,128)(2,1)S(1)} %pad_maximum_fusion), channel_id=1, source_target_pairs={{0,1},{1,0},{2,3},{3,2},{4,5},{5,4},{6,7},{7,6},{8,9},{9,8},{10,11... | collective-permute-start | bytes 884744 | tf_op jit(solution)/shard_map/ppermute | solution.py:198
  112.1 1.4 collective-permute-start.17
  117.7 50.4 %copy-start.16 = (bf16[96,128]{1,0:T(8,128)(2,1)S(1)}, bf16[96,128]{1,0:T(8,128)(2,1)}, u32[]{:S(2)}) copy-start(bf16[96,128]{1,0:T(8,128)(2,1)} %copy-done.15) | copy-start | bytes 73732
  (17 other events, 62.0 us)

commit v5 on v4

--- a/solution.py
+++ b/solution.py
@@ -12,11 +12,13 @@
 LANE = 128
 LOCAL = ("x", "core")
 AXES = ("node", "x", "core")
-PARTS = (7,)
+PARTS = (5, 2)
 BF16 = jnp.bfloat16
 F32 = jnp.float32
 PARAMS = pltpu.CompilerParams(vmem_limit_bytes=14 * 2**20)
+WIDE = pltpu.CompilerParams(vmem_limit_bytes=56 * 2**20)
 VMEM = pl.BlockSpec(memory_space=pltpu.VMEM)
+HBM = pl.BlockSpec(memory_space=pltpu.HBM)
 
 
 def rows_of(tiles):
@@ -24,12 +26,18 @@
 
 
 def send_kernel(parts, sel_ref, tok_ref, *refs):
-    outs, held = refs[: len(parts)], refs[len(parts) :]
+    outs, held, tok, sems = refs[: len(parts)], refs[len(parts) : -2], refs[-2], refs[-1]
     experts = sel_ref.shape[0] // SLOT
     cut = sum(parts) * LANE
     n_local = tok_ref.shape[1] // cut
+    copies = []
     for k in range(n_local):
-        val = jnp.dot(sel_ref[...], tok_ref[:, k * cut : (k + 1) * cut], preferred_element_type=F32)
+        lanes = pl.ds(k * cut, cut)
+        copies.append(pltpu.make_async_copy(tok_ref.at[:, lanes], tok.at[:, lanes], sems.at[k]))
+        copies[-1].start()
+    for k in range(n_local):
+        copies[k].wait()
+        val = jnp.dot(sel_ref[...], tok[:, k * cut : (k + 1) * cut], preferred_element_type=F32)
         first = 0
         for tiles, ref in zip(parts, held):
             rows = rows_of(tiles)
@@ -47,13 +55,15 @@
 
 def send(sel, tokens, parts, devices):
     shapes = [(devices * rows_of(tiles), LANE) for tiles in parts]
+    scratch = [pltpu.VMEM(shape, F32) for shape in shapes]
+    scratch += [pltpu.VMEM(tokens.shape, BF16), pltpu.SemaphoreType.DMA((devices * SLOT // sel.shape[0],))]
     return pl.pallas_call(
         functools.partial(send_kernel, parts),
         out_shape=[jax.ShapeDtypeStruct(shape, BF16) for shape in shapes],
-        in_specs=[VMEM, VMEM],
+        in_specs=[VMEM, HBM],
         out_specs=[VMEM] * len(parts),
-        scratch_shapes=[pltpu.VMEM(shape, F32) for shape in shapes],
-        compiler_params=PARAMS,
+        scratch_shapes=scratch,
+        compiler_params=WIDE,
         name="send",
     )(sel, tokens)
 
@@ -86,34 +96,54 @@
 
 
 def expand_kernel(n_blocks, opening, last, place_ref, gate_ref, up_ref, *refs):
-    blocks, out_ref = refs[:n_blocks], refs[-1]
+    blocks, (out_ref, rows, mats, sems) = refs[:n_blocks], refs[-4:]
+    cap, width = rows.shape[1:]
+    units = gate_ref.shape[1]
+    each = len(rows) // n_blocks
+    copies = []
+    for n in range(len(rows)):
+        at = pl.ds(pl.multiple_of(place_ref[n], LANE), width)
+        took = blocks[n // each].at[pl.ds(n % each * cap, cap), :]
+        copies.append(
+            [
+                pltpu.make_async_copy(gate_ref.at[at, :], mats.at[n, :, pl.ds(0, units)], sems.at[n, 0]),
+                pltpu.make_async_copy(up_ref.at[at, :], mats.at[n, :, pl.ds(units, units)], sems.at[n, 1]),
+                pltpu.make_async_copy(took, rows.at[n], sems.at[n, 2]),
+            ]
+        )
+        for copy in copies[-1]:
+            copy.start()
     total = None if opening else refs[n_blocks][...]
-    for n, ref in enumerate(blocks):
-        at = pl.ds(pl.multiple_of(place_ref[n], LANE), ref.shape[1])
-        both = jnp.concatenate([gate_ref[at, :], up_ref[at, :]], axis=1)
-        val = jnp.dot(ref[...], both, preferred_element_type=F32)
+    for n in range(len(rows)):
+        for copy in copies[n]:
+            copy.wait()
+        val = jnp.dot(rows[n], mats[n], preferred_element_type=F32)
         total = val if total is None else total + val
     if last:
-        units = gate_ref.shape[1]
         gate, up = total[:, :units], total[:, units:]
         out_ref[...] = (gate / (1.0 + jnp.exp(-gate)) * up).astype(BF16)
     else:
         out_ref[...] = total
 
 
-def expand(total, blocks, places, gate_mat, up_mat, last):
-    cap = blocks[0].shape[0]
-    units = gate_mat.shape[1]
+def expand(total, blocks, places, cap, gate_mat, up_mat, last):
+    width, units = blocks[0].shape[1], gate_mat.shape[1]
+    n = len(places)
     opening = total is None
     shape = jax.ShapeDtypeStruct((cap, units), BF16) if last else jax.ShapeDtypeStruct((cap, 2 * units), F32)
     smem = pl.BlockSpec(memory_space=pltpu.SMEM)
-    flops = 4 * cap * units * sum(block.shape[1] for block in blocks)
+    flops = 4 * cap * units * width * n
     return pl.pallas_call(
         functools.partial(expand_kernel, len(blocks), opening, last),
         out_shape=shape,
-        in_specs=[smem] + [VMEM] * (2 + len(blocks) + (not opening)),
+        in_specs=[smem] + [HBM] * (2 + len(blocks)) + [VMEM] * (not opening),
         out_specs=VMEM,
-        compiler_params=PARAMS,
+        scratch_shapes=[
+            pltpu.VMEM((n, cap, width), BF16),
+            pltpu.VMEM((n, width, 2 * units), BF16),
+            pltpu.SemaphoreType.DMA((n, 3)),
+        ],
+        compiler_params=WIDE,
         cost_estimate=pl.CostEstimate(flops=flops, bytes_accessed=flops // 512, transcendentals=0),
         name="expand",
     )(jnp.stack(places), gate_mat, up_mat, *blocks, *([] if opening else [total]))
@@ -121,7 +151,7 @@
 
 def down_kernel(n_hidden, weight_ref, column_ref, *refs):
     hidden_refs, down_refs, (out_ref, held) = refs[:n_hidden], refs[n_hidden:-2], refs[-2:]
-    width = down_refs[0].shape[1]
+    width = down_refs[0].shape[2]
     cap = weight_ref.shape[0]
     tiles = width // LANE
     rows = rows_of(tiles)
@@ -130,7 +160,7 @@
     for ref in hidden_refs:
         hidden += [ref[...]] if len(ref.shape) == 2 else [ref[k] for k in range(ref.shape[0])]
     hidden = jnp.concatenate(hidden, axis=1)
-    mat = jnp.concatenate([ref[...] for ref in down_refs], axis=0)
+    mat = jnp.concatenate([ref[flip] for flip in range(2) for ref in down_refs], axis=0)
     answer = weight_ref[...] * jnp.dot(hidden, mat, preferred_element_type=F32)
     answer = answer.astype(BF16)
     for s in range(SLOT):
@@ -145,7 +175,7 @@
 
 
 def down(hidden, down_blocks, weight, column, devices):
-    shape = (devices * rows_of(down_blocks[0].shape[1] // LANE), LANE)
+    shape = (devices * rows_of(down_blocks[0].shape[2] // LANE), LANE)
     return pl.pallas_call(
         functools.partial(down_kernel, len(hidden)),
         out_shape=jax.ShapeDtypeStruct(shape, BF16),
@@ -233,15 +263,17 @@
     sel = jnp.concatenate(sel, axis=0).astype(BF16)
 
     outgoing = send(sel, tokens, PARTS, devices)
-    arrived = [exchange(msg, devices) for msg in outgoing]
+    arrived = exchange(outgoing[0], devices)
 
     mat, _ = lax.optimization_barrier((w_down, outgoing[0]))
-    down_blocks = []
-    for flip in range(nc):
-        for dx in range(nx):
-            to = (at_x + dx) % nx * nc + (at_core + flip) % nc
-            block = lax.dynamic_slice(mat[0], (0, to * cut), (mat.shape[1], cut))
-            down_blocks.append(sent(block, dx, flip) if dx or flip else block)
+
+    def columns(core):
+        at = [(x * nc + core) * cut for x in range(nx)]
+        return jnp.stack([lax.dynamic_slice(mat[0], (0, start), (mat.shape[1], cut)) for start in at])
+
+    pair = jnp.stack([columns(at_core), sent(columns(1 - at_core), 0, 1)], axis=1)
+    down_blocks = [lax.dynamic_index_in_dim(pair, (at_x + dx) % nx, 0, keepdims=False) for dx in range(nx)]
+    down_blocks = [sent(block, dx, 0) if dx else block for dx, block in enumerate(down_blocks)]
 
     picked = lax.dynamic_index_in_dim(chosen, expert, 0, keepdims=False)
     count = lax.dynamic_index_in_dim(counts, expert, 0, keepdims=False)
@@ -252,30 +284,31 @@
     column = holder * SLOT + jnp.sum(before.astype(jnp.int32), axis=1)
     column = jnp.where(entry < count, column, -1)
 
-    arrived[-1], *down_blocks = lax.optimization_barrier((arrived[-1], *down_blocks))
-    total = None
-    first = 0
-    for n, (msg, tiles) in enumerate(zip(arrived, PARTS)):
-        own = pack(column[:, None], msg, tiles)
-
-        def add(total, blocks, last=False):
-            places = []
-            for _, dx, flip in blocks:
-                source = (at_x - dx) % nx * nc + (at_core + flip) % nc
-                places.append(source * cut + first * LANE)
-            return expand(total, [block for block, _, _ in blocks], places, w_gate[0], w_up[0], last)
-
-        fore, aft = sent(own, 1, 0), sent(own, -1, 0)
-        total = add(total, [(own, 0, 0), (sent(own, 0, 1), 0, 1)])
-        fore, aft, total = lax.optimization_barrier((fore, aft, total))
-        far = forwarded(fore, aft)
-        near = [(fore, 1, 0), (aft, -1, 0), (sent(fore, 0, 1), 1, 1), (sent(aft, 0, 1), -1, 1)]
-        total = add(total, near)
-        far, total = lax.optimization_barrier((far, total))
-        total = add(total, [(far, 2, 0)])
-        total = add(total, [(sent(far, 0, 1), 2, 1)], last=n == len(PARTS) - 1)
-        first += tiles
-    hidden = total
+    head, tail = PARTS
+    arrived, down_blocks[1], down_blocks[3] = lax.optimization_barrier((arrived, down_blocks[1], down_blocks[3]))
+    own = pack(column[:, None], arrived, head)
+    message, own = lax.optimization_barrier((outgoing[1], own))
+    gathered = lax.all_gather(own, LOCAL, axis=0, tiled=True)
+    message = exchange(message, devices)
+    message, down_blocks[2] = lax.optimization_barrier((message, down_blocks[2]))
+    own = pack(column[:, None], message, tail)
+
+    def places(sources, first):
+        return [jnp.int32(source * cut + first * LANE) for source in sources]
+
+    def source(dx, flip):
+        return (at_x - dx) % nx * nc + (at_core + flip) % nc
+
+    def add(total, blocks, at, last=False):
+        return expand(total, blocks, at, cap, w_gate[0], w_up[0], last)
+
+    fore, aft, other = sent(own, 1, 0), sent(own, -1, 0), sent(own, 0, 1)
+    far = forwarded(fore, aft)
+    total = add(None, [gathered], places(range(n_local), 0))
+    far, total = lax.optimization_barrier((far, total))
+    blocks = [own, other, fore, sent(fore, 0, 1), aft, sent(aft, 0, 1), far, sent(far, 0, 1)]
+    at = places([source(dx, flip) for dx in (0, 1, -1, 2) for flip in range(nc)], head)
+    hidden = add(total, blocks, at, last=True)
 
     near = [sent(hidden, dx, 0) for dx in range(1, nx)]
     other = sent(hidden, 0, 1)

time: 171 us -> 199 us (1.16)
  waiting for transfers between devices: 30.4 us -> 57.6 us
  between operations: 0.35 us -> 13.7 us
  local copies, waits for them, and re-layouts: 16.9 us -> 4.99 us
  Pallas kernels: 15.7 us -> 22.2 us
  starting transfers between devices: 47.4 us -> 43.3 us
    ppermute x18 -> x15, waiting for transfers between devices: 27.8 us -> 55.6 us  [sent(): return lax.ppermute(value, LOCAL, pairs)]
    ppermute x18 -> x15, starting transfers between devices: 29.1 us -> 17.1 us  [sent(): return lax.ppermute(value, LOCAL, pairs)]
    unnamed x42 -> x24, local copies, waits for them, and re-layouts: 12.7 us -> 1.71 us
    all_to_all x1 -> x2, starting transfers between devices: 15.7 us -> 24.6 us  [exchange(): lax.all_to_all(parts, AXES, split_axis=0, concat_axis=0, tiled=True)]
    pallas_call x4 -> x2, Pallas kernels: 6.02 us -> 10 us  [expand(): pl.pallas_call(functools.partial(expand_kernel, len(blocks), opening, las...]
    pallas_call x1, Pallas kernels: 2.27 us -> 5.71 us  [send(): pl.pallas_call(functools.partial(send_kernel, parts), out_shape=[jax.Shap...]
    ppermute x1, waiting for transfers between devices: 2.58 us -> 0.01 us  [forwarded(): lax.ppermute(jnp.where(lax.axis_index('core') == 0, fore, aft), LOCAL, pa...]
    squeeze x0 -> x1, other arithmetic: none -> 2.48 us  [shards(): lax.dynamic_index_in_dim(pair, (at_x + dx) % nx, 0, keepdims=False)]
  transfers between devices with their start and end apart: 20 -> 19, of which waited for: 8 -> 10; matrix products, arithmetic and copies ran while one was open for 7% -> 5% of each run, Pallas kernels for 3% -> 3%
where the time goes in v5:
time: 199 us
  waiting for transfers between devices  57.6 us (29%)
  blocking collectives  48.6 us (24%)
  starting transfers between devices  43.3 us (22%)
  Pallas kernels  22.2 us (11%)
  between operations  13.7 us (7%)
  other arithmetic  8.2 us (4%)
  local copies, waits for them, and re-layouts  4.99 us (3%)
    ppermute x15, waiting for transfers between devices, sent(): return lax.ppermute(value, LOCAL, pairs)  55.6 us
    all_to_all x1, blocking collectives, exchange(): lax.all_to_all(parts, AXES, split_axis=0, concat_axis=0, tiled=True)  48.6 us
    all_to_all x2, starting transfers between devices, exchange(): lax.all_to_all(parts, AXES, split_axis=0, concat_axis=0, tiled=True)  24.6 us
    ppermute x15, starting transfers between devices, sent(): return lax.ppermute(value, LOCAL, pairs)  17.1 us
    pallas_call x2, Pallas kernels, expand(): pl.pallas_call(functools.partial(expand_kernel, len(blocks), opening, las...  10 us
    pallas_call x1, Pallas kernels, send(): pl.pallas_call(functools.partial(send_kernel, parts), out_shape=[jax.Shap...  5.71 us
  transfers between devices with their start and end apart: 19, of which 10 were waited for; matrix products, arithmetic and copies ran while one was open for 5% of the time, Pallas kernels for 3%

profile of v5, /device:TPU:1, one launch (start us, length us, event | category | flops | bytes accessed | tf_op | source)
XLA Modules:
  0.0 198.7 jit_solution(5353197639534060835)
XLA Ops:
  9.0 5.7 %send.1 = (bf16[4096,128]{1,0:T(8,128)(2,1)}, bf16[1536,128]{1,0:T(8,128)(2,1)}) custom-call(bf16[96,128]{1,0:T(8,128)(2,1)} %add_convert_fusion.sel_ref, bf16[128,7168]{1,0:T(8,128)(2,1)} %tok_ref.1), custom_call_target="tpu_custom_call" | custom-call | tf_op jit(solution)/shard_map/send/pallas_call | solution.py:60
  14.7 15.7 %all-to-all-start = ((bf16[256,8,2,128]{3,2,1,0:T(2,128)(2,1)}), bf16[256,8,2,128]{3,2,1,0:T(2,128)(2,1)S(1)}, u32[]{:S(2)}, u32[]{:S(2)}) async-start(bf16[256,8,2,128]{3,2,1,0:T(2,128)(2,1)} %bitcast.46), calls=%async_computation | async-start | bytes 2097152 | tf_op jit(solution)/shard_map/all_to_all | solution.py:219
  30.4 1.7 constant_dynamic-slice_fusion.3
  32.3 2.2 %collective-permute-start = (bf16[4,128,896]{2,1,0:T(8,128)(2,1)S(1)}, bf16[4,128,896]{2,1,0:T(8,128)(2,1)}, u32[]{:S(2)}, u32[]{:S(2)}) collective-permute-start(bf16[4,128,896]{2,1,0:T(8,128)(2,1)S(1)} %pad_maximum_fusion), channel_id=1, source_target_pairs={{0,1},{1,0},{2,3},{3,2},{4,5},{5,4},{6,7},{7,6},{8,9},{9,8},{10,11... | collective-permute-start | bytes 2752520 | tf_op jit(solution)/shard_map/ppermute | solution.py:228
  36.8 2.5 %fusion.2 = (bf16[2,128,896]{2,1,0:T(8,128)(2,1)S(1)}, bf16[2,128,896]{2,1,0:T(8,128)(2,1)}, bf16[2,128,896]{2,1,0:T(8,128)(2,1)}, bf16[2,128,896]{2,1,0:T(8,128)(2,1)S(1)}) fusion(s32[]{:T(128)S(6)} %select_n.213, bf16[4,1,128,896]{3,2,0,1:T(8,128)(2,1)S(1)} %maximum_bitcast_fusion, bf16[4,1,128,896]{3,2,0,1:T(8,128)(2,1)} %bitcast.16, s32[]{:T(128)S(6)} %select_n.206, ...), kind=kLoop, calls=%fused_computation.14 | loop fusion | flops 917504 | bytes 3670032 | tf_op jit(solution)/shard_map/jit(dynamic_index_in_dim)/squeeze | solution.py:275
  39.2 2.7 %collective-permute-start.2 = (bf16[2,128,896]{2,1,0:T(8,128)(2,1)}, bf16[2,128,896]{2,1,0:T(8,128)(2,1)S(1)}, u32[]{:S(2)}, u32[]{:S(2)}) collective-permute-start(bf16[2,128,896]{2,1,0:T(8,128)(2,1)} %get-tuple-element.40), channel_id=1, source_target_pairs={{0,6},{1,7},{2,0},{3,1},{4,2},{5,3},{6,4},{7,5},{8,14},{9,15},{10,... | collective-permute-start | bytes 1376264 | tf_op jit(solution)/shard_map/ppermute | solution.py:228
  43.8 15.1 %collective-permute-done.1.refs_7_ = bf16[2,128,896]{2,1,0:T(8,128)(2,1)S(1)} collective-permute-done((bf16[2,128,896]{2,1,0:T(8,128)(2,1)}, bf16[2,128,896]{2,1,0:T(8,128)(2,1)S(1)}, u32[]{:S(2)}, u32[]{:S(2)}) %collective-permute-start.1) | collective-permute-done | bytes 458784 | tf_op jit(solution)/shard_map/ppermute | solution.py:228
  58.9 2.0 %all-to-all-done = bf16[256,8,2,128]{3,2,1,0:T(2,128)(2,1)S(1)} async-done(((bf16[256,8,2,128]{3,2,1,0:T(2,128)(2,1)}), bf16[256,8,2,128]{3,2,1,0:T(2,128)(2,1)S(1)}, u32[]{:S(2)}, u32[]{:S(2)}) %all-to-all-start) | async-done | bytes 1048608 | tf_op jit(solution)/shard_map/all_to_all | solution.py:219
  60.9 1.8 pack.2
  62.7 8.9 %all-to-all-start.1 = ((bf16[256,3,2,128]{3,2,1,0:T(2,128)(2,1)}), bf16[256,3,2,128]{3,2,1,0:T(2,128)(2,1)S(1)}, u32[]{:S(2)}, u32[]{:S(2)}) async-start(bf16[256,3,2,128]{3,2,1,0:T(2,128)(2,1)} %bitcast.47), calls=%async_computation.1 | async-start | bytes 786432 | tf_op jit(solution)/shard_map/all_to_all | solution.py:219
  71.6 3.0 %collective-permute-start.3 = (bf16[2,128,896]{2,1,0:T(8,128)(2,1)S(1)}, bf16[2,128,896]{2,1,0:T(8,128)(2,1)S(1)}, u32[]{:S(2)}, u32[]{:S(2)}) collective-permute-start(bf16[2,128,896]{2,1,0:T(8,128)(2,1)S(1)} %get-tuple-element.41), channel_id=1, source_target_pairs={{0,4},{1,5},{2,6},{3,7},{4,0},{5,1},{6,2},{7,3},{8,12},{9,13},{10,... | collective-permute-start | bytes 1376264 | tf_op jit(solution)/shard_map/ppermute | solution.py:228
  74.6 22.9 %collective-permute-done.3.refs_8_ = bf16[2,128,896]{2,1,0:T(8,128)(2,1)S(1)} collective-permute-done((bf16[2,128,896]{2,1,0:T(8,128)(2,1)S(1)}, bf16[2,128,896]{2,1,0:T(8,128)(2,1)S(1)}, u32[]{:S(2)}, u32[]{:S(2)}) %collective-permute-start.3) | collective-permute-done | bytes 458784 | tf_op jit(solution)/shard_map/ppermute | solution.py:228
  98.0 3.3 %collective-permute-start.7 = (bf16[384,256]{1,0:T(8,128)(2,1)S(1)}, bf16[384,256]{1,0:T(8,128)(2,1)S(1)}, u32[]{:S(2)}, u32[]{:S(2)}) collective-permute-start(bf16[384,256]{1,0:T(8,128)(2,1)S(1)} %pack.3.refs_0_), channel_id=1, source_target_pairs={{0,6},{1,7},{2,0},{3,1},{4,2},{5,3},{6,4},{7,5},{8,14},{9,15},{10,... | collective-permute-start | bytes 589832 | tf_op jit(solution)/shard_map/ppermute | solution.py:228
  101.3 6.5 %collective-permute-done.7.refs_4_ = bf16[384,256]{1,0:T(8,128)(2,1)S(1)} collective-permute-done((bf16[384,256]{1,0:T(8,128)(2,1)S(1)}, bf16[384,256]{1,0:T(8,128)(2,1)S(1)}, u32[]{:S(2)}, u32[]{:S(2)}) %collective-permute-start.7) | collective-permute-done | bytes 196640 | tf_op jit(solution)/shard_map/ppermute | solution.py:228
  107.8 1.6 collective-permute-start.9
  110.0 1.4 collective-permute-start.4
  111.9 5.8 %expand.2.refs_8_ = f32[384,256]{1,0:T(8,128)} custom-call(s32[8]{0:T(128)} %iota_multiply_fusion.place_ref, bf16[7168,128]{1,0:T(8,128)(2,1)} %bitcast.42, bf16[7168,128]{1,0:T(8,128)(2,1)} %bitcast.44, bf16[3072,640]{1,0:T(8,128)(2,1)} %all-gather.2.cloned.1.call-done.refs_0_), custom_call_target="tpu_custom_call" | custom-call | flops 1006632960 | bytes 1966080 | tf_op jit(solution)/shard_map/expand/pallas_call | solution.py:136
  120.1 4.2 %expand.3.refs_0_ = bf16[384,128]{1,0:T(8,128)(2,1)} custom-call(s32[8]{0:T(128)} %stack.70.place_ref, bf16[7168,128]{1,0:T(8,128)(2,1)} %bitcast.43, bf16[7168,128]{1,0:T(8,128)(2,1)} %bitcast.45, bf16[384,256]{1,0:T(8,128)(2,1)} %copy-done.1, bf16[384,256]{1,0:T(8,128)(2,1)} %copy-done.7, bf16[384,256]{1,0:T(8,128)(2,1)} %copy-done.5, ...), custom_call_target="tpu_custom_call" | custom-call | flops 402653184 | bytes 786432 | tf_op jit(solution)/shard_map/expand/pallas_call | solution.py:136
  124.3 2.3 %collective-permute-start.13 = (bf16[384,128]{1,0:T(8,128)(2,1)}, bf16[384,128]{1,0:T(8,128)(2,1)S(1)}, u32[]{:S(2)}, u32[]{:S(2)}) collective-permute-start(bf16[384,128]{1,0:T(8,128)(2,1)} %expand.3.refs_0_), channel_id=1, source_target_pairs={{0,6},{1,7},{2,0},{3,1},{4,2},{5,3},{6,4},{7,5},{8,14},{9,15},{10,... | collective-permute-start | bytes 294920 | tf_op jit(solution)/shard_map/ppermute | solution.py:228
  127.3 3.6 %collective-permute-done.13.refs_3_ = bf16[384,128]{1,0:T(8,128)(2,1)S(1)} collective-permute-done((bf16[384,128]{1,0:T(8,128)(2,1)}, bf16[384,128]{1,0:T(8,128)(2,1)S(1)}, u32[]{:S(2)}, u32[]{:S(2)}) %collective-permute-start.13) | collective-permute-done | bytes 98336 | tf_op jit(solution)/shard_map/ppermute | solution.py:228
  131.9 3.1 %collective-permute-done.11.refs_1_ = bf16[384,128]{1,0:T(8,128)(2,1)S(1)} collective-permute-done((bf16[384,128]{1,0:T(8,128)(2,1)}, bf16[384,128]{1,0:T(8,128)(2,1)S(1)}, u32[]{:S(2)}, u32[]{:S(2)}) %collective-permute-start.11) | collective-permute-done | bytes 98336 | tf_op jit(solution)/shard_map/ppermute | solution.py:228
  138.9 1.9 down.1
  140.8 48.6 %all_to_all.15 = bf16[256,11,2,128]{3,2,1,0:T(2,128)(2,1)S(1)} all-to-all(bf16[256,11,2,128]{3,2,1,0:T(2,128)(2,1)S(1)} %bitcast.35), channel_id=1, replica_groups=mesh['node'=32,'x'=4,'core'=2] {'node','x','core'}, dimensions={0} | all-to-all | bytes 2883584 | tf_op jit(solution)/shard_map/all_to_all | solution.py:219
  189.5 2.4 %place.1 = bf16[128,7168]{1,0:T(8,128)(2,1)} custom-call(bf16[96,128]{1,0:T(8,128)(2,1)S(1)} %copy-done.3, bf16[5632,128]{1,0:T(8,128)(2,1)S(1)} %bitcast.36), custom_call_target="tpu_custom_call" | custom-call | tf_op jit(solution)/shard_map/place/pallas_call | solution.py:206
  (74 shorter events, 16.0 us)
Async XLA Ops:
  6.5 130.0 %copy-start = (f32[32,384]{1,0:T(8,128)S(1)}, f32[32,384]{1,0:T(8,128)}, u32[]{:S(2)}) copy-start(f32[32,384]{1,0:T(8,128)} %param.13) | copy-start | bytes 147460
  14.7 46.2 %all-to-all-start = ((bf16[256,8,2,128]{3,2,1,0:T(2,128)(2,1)}), bf16[256,8,2,128]{3,2,1,0:T(2,128)(2,1)S(1)}, u32[]{:S(2)}, u32[]{:S(2)}) async-start(bf16[256,8,2,128]{3,2,1,0:T(2,128)(2,1)} %bitcast.46), calls=%async_computation | async-start | bytes 2097152 | tf_op jit(solution)/shard_map/all_to_all | solution.py:219
  30.4 81.6 %all-gather.2.cloned.1.call-start = ((), (), s32[]{:S(2)}) async-start(), calls=%async_computation.3 | async-start | bytes 4423680 | tf_op jit(solution)/shard_map/all_gather | solution.py:291
  32.3 4.5 %collective-permute-start = (bf16[4,128,896]{2,1,0:T(8,128)(2,1)S(1)}, bf16[4,128,896]{2,1,0:T(8,128)(2,1)}, u32[]{:S(2)}, u32[]{:S(2)}) collective-permute-start(bf16[4,128,896]{2,1,0:T(8,128)(2,1)S(1)} %pad_maximum_fusion), channel_id=1, source_target_pairs={{0,1},{1,0},{2,3},{3,2},{4,5},{5,4},{6,7},{7,6},{8,9},{9,8},{10,11... | collective-permute-start | bytes 2752520 | tf_op jit(solution)/shard_map/ppermute | solution.py:228
  39.2 19.6 %collective-permute-start.1 = (bf16[2,128,896]{2,1,0:T(8,128)(2,1)}, bf16[2,128,896]{2,1,0:T(8,128)(2,1)S(1)}, u32[]{:S(2)}, u32[]{:S(2)}) collective-permute-start(bf16[2,128,896]{2,1,0:T(8,128)(2,1)} %get-tuple-element.39), channel_id=1, source_target_pairs={{0,2},{1,3},{2,4},{3,5},{4,6},{5,7},{6,0},{7,1},{8,10},{9,11},{10,... | collective-permute-start | bytes 1376264 | tf_op jit(solution)/shard_map/ppermute | solution.py:228
  39.2 19.6 %collective-permute-start.2 = (bf16[2,128,896]{2,1,0:T(8,128)(2,1)}, bf16[2,128,896]{2,1,0:T(8,128)(2,1)S(1)}, u32[]{:S(2)}, u32[]{:S(2)}) collective-permute-start(bf16[2,128,896]{2,1,0:T(8,128)(2,1)} %get-tuple-element.40), channel_id=1, source_target_pairs={{0,6},{1,7},{2,0},{3,1},{4,2},{5,3},{6,4},{7,5},{8,14},{9,15},{10,... | collective-permute-start | bytes 1376264 | tf_op jit(solution)/shard_map/ppermute | solution.py:228
  62.7 34.9 %all-to-all-start.1 = ((bf16[256,3,2,128]{3,2,1,0:T(2,128)(2,1)}), bf16[256,3,2,128]{3,2,1,0:T(2,128)(2,1)S(1)}, u32[]{:S(2)}, u32[]{:S(2)}) async-start(bf16[256,3,2,128]{3,2,1,0:T(2,128)(2,1)} %bitcast.47), calls=%async_computation.1 | async-start | bytes 786432 | tf_op jit(solution)/shard_map/all_to_all | solution.py:219
  71.6 25.9 %collective-permute-start.3 = (bf16[2,128,896]{2,1,0:T(8,128)(2,1)S(1)}, bf16[2,128,896]{2,1,0:T(8,128)(2,1)S(1)}, u32[]{:S(2)}, u32[]{:S(2)}) collective-permute-start(bf16[2,128,896]{2,1,0:T(8,128)(2,1)S(1)} %get-tuple-element.41), channel_id=1, source_target_pairs={{0,4},{1,5},{2,6},{3,7},{4,0},{5,1},{6,2},{7,3},{8,12},{9,13},{10,... | collective-permute-start | bytes 1376264 | tf_op jit(solution)/shard_map/ppermute | solution.py:228
  98.0 19.8 %copy-start.1 = (bf16[384,256]{1,0:T(8,128)(2,1)}, bf16[384,256]{1,0:T(8,128)(2,1)S(1)}, u32[]{:S(2)}) copy-start(bf16[384,256]{1,0:T(8,128)(2,1)S(1)} %pack.3.refs_0_) | copy-start | bytes 589828
  98.0 9.8 %collective-permute-start.7 = (bf16[384,256]{1,0:T(8,128)(2,1)S(1)}, bf16[384,256]{1,0:T(8,128)(2,1)S(1)}, u32[]{:S(2)}, u32[]{:S(2)}) collective-permute-start(bf16[384,256]{1,0:T(8,128)(2,1)S(1)} %pack.3.refs_0_), channel_id=1, source_target_pairs={{0,6},{1,7},{2,0},{3,1},{4,2},{5,3},{6,4},{7,5},{8,14},{9,15},{10,... | collective-permute-start | bytes 589832 | tf_op jit(solution)/shard_map/ppermute | solution.py:228
  101.3 6.5 %collective-permute-start.5 = (bf16[384,256]{1,0:T(8,128)(2,1)S(1)}, bf16[384,256]{1,0:T(8,128)(2,1)S(1)}, u32[]{:S(2)}, u32[]{:S(2)}) collective-permute-start(bf16[384,256]{1,0:T(8,128)(2,1)S(1)} %pack.3.refs_0_), channel_id=1, source_target_pairs={{0,2},{1,3},{2,4},{3,5},{4,6},{5,7},{6,0},{7,1},{8,10},{9,11},{10,... | collective-permute-start | bytes 589832 | tf_op jit(solution)/shard_map/ppermute | solution.py:228
  107.8 10.0 %copy-start.4 = (bf16[384,256]{1,0:T(8,128)(2,1)}, bf16[384,256]{1,0:T(8,128)(2,1)S(1)}, u32[]{:S(2)}) copy-start(bf16[384,256]{1,0:T(8,128)(2,1)S(1)} %collective-permute-done.7.refs_4_) | copy-start | bytes 589828
  107.8 10.0 %copy-start.5 = (bf16[384,256]{1,0:T(8,128)(2,1)}, bf16[384,256]{1,0:T(8,128)(2,1)S(1)}, u32[]{:S(2)}) copy-start(bf16[384,256]{1,0:T(8,128)(2,1)S(1)} %collective-permute-done.5.refs_2_) | copy-start | bytes 589828
  107.8 10.0 %collective-permute-start.9 = (bf16[384,256]{1,0:T(8,128)(2,1)S(1)}, bf16[384,256]{1,0:T(8,128)(2,1)S(1)}, u32[]{:S(2)}, u32[]{:S(2)}) collective-permute-start(bf16[384,256]{1,0:T(8,128)(2,1)S(1)} %broadcast_select_fusion), channel_id=1, source_target_pairs={{0,2},{1,7},{2,4},{3,1},{4,6},{5,3},{6,0},{7,5},{8,10},{9,15},{10,... | collective-permute-start | bytes 589832 | tf_op jit(solution)/shard_map/ppermute | solution.py:237
  110.0 8.6 %collective-permute-start.4 = (bf16[384,256]{1,0:T(8,128)(2,1)S(1)}, bf16[384,256]{1,0:T(8,128)(2,1)S(1)}, u32[]{:S(2)}, u32[]{:S(2)}) collective-permute-start(bf16[384,256]{1,0:T(8,128)(2,1)S(1)} %pack.3.refs_0_), channel_id=1, source_target_pairs={{0,1},{1,0},{2,3},{3,2},{4,5},{5,4},{6,7},{7,6},{8,9},{9,8},{10,11... | collective-permute-start | bytes 589832 | tf_op jit(solution)/shard_map/ppermute | solution.py:228
  111.4 7.2 %collective-permute-start.8 = (bf16[384,256]{1,0:T(8,128)(2,1)S(1)}, bf16[384,256]{1,0:T(8,128)(2,1)S(1)}, u32[]{:S(2)}, u32[]{:S(2)}) collective-permute-start(bf16[384,256]{1,0:T(8,128)(2,1)S(1)} %collective-permute-done.7.refs_4_), channel_id=1, source_target_pairs={{0,1},{1,0},{2,3},{3,2},{4,5},{5,4},{6,7},{7,6},{8,9},{9,8},{10,11... | collective-permute-start | bytes 589832 | tf_op jit(solution)/shard_map/ppermute | solution.py:228
  111.4 7.2 %collective-permute-start.6 = (bf16[384,256]{1,0:T(8,128)(2,1)S(1)}, bf16[384,256]{1,0:T(8,128)(2,1)S(1)}, u32[]{:S(2)}, u32[]{:S(2)}) collective-permute-start(bf16[384,256]{1,0:T(8,128)(2,1)S(1)} %collective-permute-done.5.refs_2_), channel_id=1, source_target_pairs={{0,1},{1,0},{2,3},{3,2},{4,5},{5,4},{6,7},{7,6},{8,9},{9,8},{10,11... | collective-permute-start | bytes 589832 | tf_op jit(solution)/shard_map/ppermute | solution.py:228
  117.8 1.5 collective-permute-start.10
  124.3 6.6 %collective-permute-start.13 = (bf16[384,128]{1,0:T(8,128)(2,1)}, bf16[384,128]{1,0:T(8,128)(2,1)S(1)}, u32[]{:S(2)}, u32[]{:S(2)}) collective-permute-start(bf16[384,128]{1,0:T(8,128)(2,1)} %expand.3.refs_0_), channel_id=1, source_target_pairs={{0,6},{1,7},{2,0},{3,1},{4,2},{5,3},{6,4},{7,5},{8,14},{9,15},{10,... | collective-permute-start | bytes 294920 | tf_op jit(solution)/shard_map/ppermute | solution.py:228
  126.7 5.3 %collective-permute-start.12 = (bf16[384,128]{1,0:T(8,128)(2,1)}, bf16[384,128]{1,0:T(8,128)(2,1)S(1)}, u32[]{:S(2)}, u32[]{:S(2)}) collective-permute-start(bf16[384,128]{1,0:T(8,128)(2,1)} %expand.3.refs_0_), channel_id=1, source_target_pairs={{0,4},{1,5},{2,6},{3,7},{4,0},{5,1},{6,2},{7,3},{8,12},{9,13},{10,... | collective-permute-start | bytes 294920 | tf_op jit(solution)/shard_map/ppermute | solution.py:228
  127.0 8.0 %collective-permute-start.11 = (bf16[384,128]{1,0:T(8,128)(2,1)}, bf16[384,128]{1,0:T(8,128)(2,1)S(1)}, u32[]{:S(2)}, u32[]{:S(2)}) collective-permute-start(bf16[384,128]{1,0:T(8,128)(2,1)} %expand.3.refs_0_), channel_id=1, source_target_pairs={{0,2},{1,3},{2,4},{3,5},{4,6},{5,7},{6,0},{7,1},{8,10},{9,11},{10,... | collective-permute-start | bytes 294920 | tf_op jit(solution)/shard_map/ppermute | solution.py:228
  135.0 3.0 %collective-permute-start.15 = (bf16[3,384,128]{2,1,0:T(8,128)(2,1)S(1)}, bf16[3,384,128]{2,1,0:T(8,128)(2,1)S(1)}, u32[]{:S(2)}, u32[]{:S(2)}) collective-permute-start(bf16[3,384,128]{2,1,0:T(8,128)(2,1)S(1)} %pad_maximum_fusion.1), channel_id=1, source_target_pairs={{0,1},{1,0},{2,3},{3,2},{4,5},{5,4},{6,7},{7,6},{8,9},{9,8},{10,11... | collective-permute-start | bytes 884744 | tf_op jit(solution)/shard_map/ppermute | solution.py:228
  136.5 1.6 collective-permute-start.14
  140.8 48.6 %copy-start.3 = (bf16[96,128]{1,0:T(8,128)(2,1)S(1)}, bf16[96,128]{1,0:T(8,128)(2,1)}, u32[]{:S(2)}) copy-start(bf16[96,128]{1,0:T(8,128)(2,1)} %add_convert_fusion.sel_ref) | copy-start | bytes 73732
  (7 other events, 10.6 us)
Sparse Core Ops, SparseCore 0:
  62.8 45.1 all-gather.1

commit v6 on v4

--- a/solution.py
+++ b/solution.py
@@ -85,43 +85,42 @@
     )(column, msg)
 
 
-def expand_kernel(n_blocks, opening, last, place_ref, gate_ref, up_ref, *refs):
-    blocks, out_ref = refs[:n_blocks], refs[-1]
-    total = None if opening else refs[n_blocks][...]
+def expand_kernel(uses, opening, last, place_ref, *refs):
+    blocks, mats, out_ref = refs[: len(uses)], refs[len(uses) : len(uses) + max(uses) + 1], refs[-1]
+    total = None if opening else refs[-2][...]
     for n, ref in enumerate(blocks):
         at = pl.ds(pl.multiple_of(place_ref[n], LANE), ref.shape[1])
-        both = jnp.concatenate([gate_ref[at, :], up_ref[at, :]], axis=1)
-        val = jnp.dot(ref[...], both, preferred_element_type=F32)
+        val = jnp.dot(ref[...], mats[uses[n]][at, :], preferred_element_type=F32)
         total = val if total is None else total + val
     if last:
-        units = gate_ref.shape[1]
+        units = out_ref.shape[1]
         gate, up = total[:, :units], total[:, units:]
         out_ref[...] = (gate / (1.0 + jnp.exp(-gate)) * up).astype(BF16)
     else:
         out_ref[...] = total
 
 
-def expand(total, blocks, places, gate_mat, up_mat, last):
+def expand(total, blocks, uses, places, mats, last=False):
     cap = blocks[0].shape[0]
-    units = gate_mat.shape[1]
+    both = mats[0].shape[1]
     opening = total is None
-    shape = jax.ShapeDtypeStruct((cap, units), BF16) if last else jax.ShapeDtypeStruct((cap, 2 * units), F32)
+    shape = jax.ShapeDtypeStruct((cap, both // 2), BF16) if last else jax.ShapeDtypeStruct((cap, both), F32)
     smem = pl.BlockSpec(memory_space=pltpu.SMEM)
-    flops = 4 * cap * units * sum(block.shape[1] for block in blocks)
-    return pl.pallas_call(
-        functools.partial(expand_kernel, len(blocks), opening, last),
+    flops = 2 * cap * both * sum(block.shape[1] for block in blocks)
+    return pl.pallas_call(
+        functools.partial(expand_kernel, uses, opening, last),
         out_shape=shape,
-        in_specs=[smem] + [VMEM] * (2 + len(blocks) + (not opening)),
+        in_specs=[smem] + [VMEM] * (len(blocks) + len(mats) + (not opening)),
         out_specs=VMEM,
         compiler_params=PARAMS,
         cost_estimate=pl.CostEstimate(flops=flops, bytes_accessed=flops // 512, transcendentals=0),
         name="expand",
-    )(jnp.stack(places), gate_mat, up_mat, *blocks, *([] if opening else [total]))
+    )(places, *blocks, *mats, *([] if opening else [total]))
 
 
 def down_kernel(n_hidden, weight_ref, column_ref, *refs):
     hidden_refs, down_refs, (out_ref, held) = refs[:n_hidden], refs[n_hidden:-2], refs[-2:]
-    width = down_refs[0].shape[1]
+    width = down_refs[0].shape[2]
     cap = weight_ref.shape[0]
     tiles = width // LANE
     rows = rows_of(tiles)
@@ -130,7 +129,7 @@
     for ref in hidden_refs:
         hidden += [ref[...]] if len(ref.shape) == 2 else [ref[k] for k in range(ref.shape[0])]
     hidden = jnp.concatenate(hidden, axis=1)
-    mat = jnp.concatenate([ref[...] for ref in down_refs], axis=0)
+    mat = jnp.concatenate([ref[flip] for flip in range(2) for ref in down_refs], axis=0)
     answer = weight_ref[...] * jnp.dot(hidden, mat, preferred_element_type=F32)
     answer = answer.astype(BF16)
     for s in range(SLOT):
@@ -145,7 +144,7 @@
 
 
 def down(hidden, down_blocks, weight, column, devices):
-    shape = (devices * rows_of(down_blocks[0].shape[1] // LANE), LANE)
+    shape = (devices * rows_of(down_blocks[0].shape[2] // LANE), LANE)
     return pl.pallas_call(
         functools.partial(down_kernel, len(hidden)),
         out_shape=jax.ShapeDtypeStruct(shape, BF16),
@@ -233,15 +232,23 @@
     sel = jnp.concatenate(sel, axis=0).astype(BF16)
 
     outgoing = send(sel, tokens, PARTS, devices)
-    arrived = [exchange(msg, devices) for msg in outgoing]
-
-    mat, _ = lax.optimization_barrier((w_down, outgoing[0]))
-    down_blocks = []
-    for flip in range(nc):
-        for dx in range(nx):
-            to = (at_x + dx) % nx * nc + (at_core + flip) % nc
-            block = lax.dynamic_slice(mat[0], (0, to * cut), (mat.shape[1], cut))
-            down_blocks.append(sent(block, dx, flip) if dx or flip else block)
+    arrived = exchange(outgoing[0], devices)
+
+    mat, gate_mat, up_mat, _ = lax.optimization_barrier((w_down[0], w_gate[0], w_up[0], outgoing[0]))
+
+    def columns(core):
+        at = [(x * nc + core) * cut for x in range(nx)]
+        return jnp.stack([lax.dynamic_slice(mat, (0, start), (mat.shape[0], cut)) for start in at])
+
+    pair = jnp.stack([columns(at_core), sent(columns(1 - at_core), 0, 1)], axis=1)
+    down_blocks = [lax.dynamic_index_in_dim(pair, (at_x + dx) % nx, 0, keepdims=False) for dx in range(nx)]
+    down_blocks = [sent(block, dx, 0) if dx else block for dx, block in enumerate(down_blocks)]
+
+    pieces = []
+    for dx in range(nx):
+        at = ((at_x - dx) % nx * nc * cut, 0)
+        size = (nc * cut, gate_mat.shape[1])
+        pieces.append(jnp.concatenate([lax.dynamic_slice(m, at, size) for m in (gate_mat, up_mat)], axis=1))
 
     picked = lax.dynamic_index_in_dim(chosen, expert, 0, keepdims=False)
     count = lax.dynamic_index_in_dim(counts, expert, 0, keepdims=False)
@@ -252,30 +259,19 @@
     column = holder * SLOT + jnp.sum(before.astype(jnp.int32), axis=1)
     column = jnp.where(entry < count, column, -1)
 
-    arrived[-1], *down_blocks = lax.optimization_barrier((arrived[-1], *down_blocks))
-    total = None
-    first = 0
-    for n, (msg, tiles) in enumerate(zip(arrived, PARTS)):
-        own = pack(column[:, None], msg, tiles)
-
-        def add(total, blocks, last=False):
-            places = []
-            for _, dx, flip in blocks:
-                source = (at_x - dx) % nx * nc + (at_core + flip) % nc
-                places.append(source * cut + first * LANE)
-            return expand(total, [block for block, _, _ in blocks], places, w_gate[0], w_up[0], last)
-
-        fore, aft = sent(own, 1, 0), sent(own, -1, 0)
-        total = add(total, [(own, 0, 0), (sent(own, 0, 1), 0, 1)])
-        fore, aft, total = lax.optimization_barrier((fore, aft, total))
-        far = forwarded(fore, aft)
-        near = [(fore, 1, 0), (aft, -1, 0), (sent(fore, 0, 1), 1, 1), (sent(aft, 0, 1), -1, 1)]
-        total = add(total, near)
-        far, total = lax.optimization_barrier((far, total))
-        total = add(total, [(far, 2, 0)])
-        total = add(total, [(sent(far, 0, 1), 2, 1)], last=n == len(PARTS) - 1)
-        first += tiles
-    hidden = total
+    arrived, down_blocks, pieces = lax.optimization_barrier((arrived, down_blocks, pieces))
+    own = pack(column[:, None], arrived, *PARTS)
+    here, there = at_core * cut, (1 - at_core) * cut
+    fore, aft = sent(own, 1, 0), sent(own, -1, 0)
+    total = expand(None, [own, sent(own, 0, 1)], (0, 0), jnp.stack([here, there]), pieces[:1])
+    fore, aft, total = lax.optimization_barrier((fore, aft, total))
+    far = forwarded(fore, aft)
+    near = [fore, sent(fore, 0, 1), aft, sent(aft, 0, 1)]
+    at = jnp.stack([here, there, here, there])
+    total = expand(total, near, (0, 0, 1, 1), at, [pieces[1], pieces[-1]])
+    far, total = lax.optimization_barrier((far, total))
+    total = expand(total, [far], (0,), jnp.stack([here]), pieces[2:3])
+    hidden = expand(total, [sent(far, 0, 1)], (0,), jnp.stack([there]), pieces[2:3], last=True)
 
     near = [sent(hidden, dx, 0) for dx in range(1, nx)]
     other = sent(hidden, 0, 1)

time: 171 us -> 178 us (1.041)
  waiting for transfers between devices: 30.4 us -> 52.7 us
  starting transfers between devices: 47.4 us -> 34.3 us
  Pallas kernels: 15.7 us -> 13.5 us
  other arithmetic: 9.34 us -> 11.5 us
  blocking collectives: 50.4 us -> 48.6 us
    ppermute x18 -> x15, waiting for transfers between devices: 27.8 us -> 47.2 us  [sent(): return lax.ppermute(value, LOCAL, pairs)]
    ppermute x18 -> x15, starting transfers between devices: 29.1 us -> 15.9 us  [sent(): return lax.ppermute(value, LOCAL, pairs)]
    ppermute x1, waiting for transfers between devices: 2.58 us -> 5.49 us  [forwarded(): lax.ppermute(jnp.where(lax.axis_index('core') == 0, fore, aft), LOCAL, pa...]
    dynamic_slice x1 -> x2, local copies, waits for them, and re-layouts: 1.25 us -> 3.92 us  [shards(): lax.dynamic_slice(m, at, size)]
    unnamed x42 -> x58, local copies, waits for them, and re-layouts: 12.7 us -> 10.1 us
    squeeze x0 -> x1, other arithmetic: none -> 2.35 us  [shards(): lax.dynamic_index_in_dim(pair, (at_x + dx) % nx, 0, keepdims=False)]
    concatenate x0 -> x4, other arithmetic: none -> 2.28 us  [shards(): jnp.concatenate([lax.dynamic_slice(m, at, size) for m in (gate_mat, up_ma...]
  transfers between devices with their start and end apart: 20 -> 17, of which waited for: 8 -> 8; matrix products, arithmetic and copies ran while one was open for 7% -> 9% of each run, Pallas kernels for 3% -> 3%
where the time goes in v6:
time: 178 us
  waiting for transfers between devices  52.7 us (30%)
  blocking collectives  48.6 us (27%)
  starting transfers between devices  34.3 us (19%)
  local copies, waits for them, and re-layouts  16.7 us (9%)
  Pallas kernels  13.5 us (8%)
  other arithmetic  11.5 us (6%)
    all_to_all x1, blocking collectives, exchange(): lax.all_to_all(parts, AXES, split_axis=0, concat_axis=0, tiled=True)  48.6 us
    ppermute x15, waiting for transfers between devices, sent(): return lax.ppermute(value, LOCAL, pairs)  47.2 us
    ppermute x15, starting transfers between devices, sent(): return lax.ppermute(value, LOCAL, pairs)  15.9 us
    all_to_all x1, starting transfers between devices, exchange(): lax.all_to_all(parts, AXES, split_axis=0, concat_axis=0, tiled=True)  15.7 us
    unnamed x58, local copies, waits for them, and re-layouts  10.1 us
    ppermute x1, waiting for transfers between devices, forwarded(): lax.ppermute(jnp.where(lax.axis_index('core') == 0, fore, aft), LOCAL, pa...  5.49 us
    pallas_call x4, Pallas kernels, expand(): pl.pallas_call(functools.partial(expand_kernel, uses, opening, last), out...  5.06 us
    dynamic_slice x2, local copies, waits for them, and re-layouts, shards(): lax.dynamic_slice(m, at, size)  3.92 us
  transfers between devices with their start and end apart: 17, of which 8 were waited for; matrix products, arithmetic and copies ran while one was open for 9% of the time, Pallas kernels for 3%

profile of v6, /device:TPU:1, one launch (start us, length us, event | category | flops | bytes accessed | tf_op | source)
XLA Modules:
  0.0 177.6 jit_solution(534302699162423056)
XLA Ops:
  1.8 1.5 copy-done.4
  3.3 2.3 %send.1 = bf16[5632,128]{1,0:T(8,128)(2,1)} custom-call(bf16[96,128]{1,0:T(8,128)(2,1)S(1)} %add_convert_fusion.sel_ref, bf16[128,7168]{1,0:T(8,128)(2,1)S(1)} %copy-done.4), custom_call_target="tpu_custom_call" | custom-call | tf_op jit(solution)/shard_map/send/pallas_call | solution.py:50
  5.6 15.7 %all-to-all-start = ((bf16[256,11,2,128]{3,2,1,0:T(2,128)(2,1)}), bf16[256,11,2,128]{3,2,1,0:T(2,128)(2,1)S(1)}, u32[]{:S(2)}, u32[]{:S(2)}) async-start(bf16[256,11,2,128]{3,2,1,0:T(2,128)(2,1)} %bitcast.4), calls=%async_computation | async-start | bytes 2883584 | tf_op jit(solution)/shard_map/all_to_all | solution.py:188
  23.4 2.1 %collective-permute-start = (bf16[4,128,896]{2,1,0:T(8,128)(2,1)}, bf16[4,128,896]{2,1,0:T(8,128)(2,1)}, u32[]{:S(2)}, u32[]{:S(2)}) collective-permute-start(bf16[4,128,896]{2,1,0:T(8,128)(2,1)} %pad_maximum_fusion), channel_id=1, source_target_pairs={{0,1},{1,0},{2,3},{3,2},{4,5},{5,4},{6,7},{7,6},{8,9},{9,8},{10,11... | collective-permute-start | bytes 2752520 | tf_op jit(solution)/shard_map/ppermute | solution.py:197
  26.4 2.6 %constant_dynamic-slice_fusion.1 = (bf16[1792,128]{1,0:T(8,128)(2,1)}, bf16[1792,128]{1,0:T(8,128)(2,1)}, bf16[1792,128]{1,0:T(8,128)(2,1)S(1)}, bf16[1792,128]{1,0:T(8,128)(2,1)S(1)}) fusion(bf16[7168,128]{1,0:T(8,128)(2,1)} %bitcast.50, s32[]{:T(128)S(6)} %select_n.205, s32[]{:T(128)S(6)} %select_n.203, s32[]{:T(128)S(6)} %select_n.201, s32[]{:T(128)S(6)} %select_n.199), kind=kLoop, calls=%fused_computation.78 | loop fusion | bytes 3670032 | tf_op jit(solution)/shard_map/dynamic_slice | solution.py:251
  34.5 2.3 %fusion.2 = (bf16[2,128,896]{2,1,0:T(8,128)(2,1)S(1)}, bf16[2,128,896]{2,1,0:T(8,128)(2,1)}, bf16[2,128,896]{2,1,0:T(8,128)(2,1)S(1)}, bf16[2,128,896]{2,1,0:T(8,128)(2,1)S(1)}) fusion(s32[]{:T(128)S(6)} %select_n.198, bf16[4,1,128,896]{3,2,1,0:T(8,128)(2,1)S(1)} %maximum_bitcast_fusion, bf16[4,1,128,896]{3,2,1,0:T(8,128)(2,1)} %bitcast.18, ...), kind=kLoop, calls=%fused_computation.19 | loop fusion | flops 917504 | bytes 3670032 | tf_op jit(solution)/shard_map/jit(dynamic_index_in_dim)/squeeze | solution.py:244
  36.9 2.0 %collective-permute-start.2 = (bf16[2,128,896]{2,1,0:T(8,128)(2,1)S(1)}, bf16[2,128,896]{2,1,0:T(8,128)(2,1)S(1)}, u32[]{:S(2)}, u32[]{:S(2)}) collective-permute-start(bf16[2,128,896]{2,1,0:T(8,128)(2,1)S(1)} %get-tuple-element.59), channel_id=1, source_target_pairs={{0,4},{1,5},{2,6},{3,7},{4,0},{5,1},{6,2},{7,3},{8,12},{9,13},{10,... | collective-permute-start | bytes 1376264 | tf_op jit(solution)/shard_map/ppermute | solution.py:197
  41.9 25.9 %collective-permute-done.1.refs_7_ = bf16[2,128,896]{2,1,0:T(8,128)(2,1)S(1)} collective-permute-done((bf16[2,128,896]{2,1,0:T(8,128)(2,1)S(1)}, bf16[2,128,896]{2,1,0:T(8,128)(2,1)S(1)}, u32[]{:S(2)}, u32[]{:S(2)}) %collective-permute-start.1) | collective-permute-done | bytes 458784 | tf_op jit(solution)/shard_map/ppermute | solution.py:197
  70.2 1.8 %pack.1.refs_0_ = bf16[384,896]{1,0:T(8,128)(2,1)} custom-call(s32[384,1]{1,0:T(8,128)S(1)} %fusion.12.column_ref, bf16[5632,128]{1,0:T(8,128)(2,1)S(1)} %bitcast.45), custom_call_target="tpu_custom_call" | custom-call | tf_op jit(solution)/shard_map/pack/pallas_call | solution.py:77
  72.6 2.7 %collective-permute-start.5 = (bf16[384,896]{1,0:T(8,128)(2,1)}, bf16[384,896]{1,0:T(8,128)(2,1)}, u32[]{:S(2)}, u32[]{:S(2)}) collective-permute-start(bf16[384,896]{1,0:T(8,128)(2,1)} %pack.1.refs_0_), channel_id=1, source_target_pairs={{0,6},{1,7},{2,0},{3,1},{4,2},{5,3},{6,4},{7,5},{8,14},{9,15},{10,... | collective-permute-start | bytes 2064392 | tf_op jit(solution)/shard_map/ppermute | solution.py:197
  75.3 2.0 %expand.4.refs_6_ = f32[384,256]{1,0:T(8,128)S(1)} custom-call(s32[2]{0:T(128)S(1)} %pad_add_fusion.place_ref, bf16[384,896]{1,0:T(8,128)(2,1)} %pack.1.refs_0_, bf16[384,896]{1,0:T(8,128)(2,1)} %collective-permute-done.6.refs_1_, bf16[1792,256]{1,0:T(8,128)(2,1)S(1)} %pad_maximum_fusion.1.refs_2_), custom_call_target="tpu_custom_call" | custom-call | flops 352321536 | bytes 688128 | tf_op jit(solution)/shard_map/expand/pallas_call | solution.py:110
  77.4 13.8 %collective-permute-done.4.refs_0_ = bf16[384,896]{1,0:T(8,128)(2,1)} collective-permute-done((bf16[384,896]{1,0:T(8,128)(2,1)}, bf16[384,896]{1,0:T(8,128)(2,1)}, u32[]{:S(2)}, u32[]{:S(2)}) %collective-permute-start.4) | collective-permute-done | bytes 688160 | tf_op jit(solution)/shard_map/ppermute | solution.py:197
  93.1 2.8 %collective-permute-start.7 = (bf16[384,896]{1,0:T(8,128)(2,1)S(1)}, bf16[384,896]{1,0:T(8,128)(2,1)S(1)}, u32[]{:S(2)}, u32[]{:S(2)}) collective-permute-start(bf16[384,896]{1,0:T(8,128)(2,1)S(1)} %broadcast_select_fusion), channel_id=1, source_target_pairs={{0,2},{1,7},{2,4},{3,1},{4,6},{5,3},{6,0},{7,5},{8,10},{9,15},{10,... | collective-permute-start | bytes 2064392 | tf_op jit(solution)/shard_map/ppermute | solution.py:206
  96.0 2.3 %expand.5.refs_2_ = f32[384,256]{1,0:T(8,128)S(1)} custom-call(s32[4]{0:T(128)S(1)} %pad_add_fusion.1.place_ref, bf16[384,896]{1,0:T(8,128)(2,1)} %collective-permute-done.4.refs_0_, bf16[384,896]{1,0:T(8,128)(2,1)S(1)} %collective-permute-done.8.refs_1_, bf16[384,896]{1,0:T(8,128)(2,1)} %collective-permute-done.5.refs_2_, ...), custom_call_target="tpu_custom_call" | custom-call | flops 704643072 | bytes 1376256 | tf_op jit(solution)/shard_map/expand/pallas_call | solution.py:110
  98.3 5.5 %collective-permute-done.7.refs_0_ = bf16[384,896]{1,0:T(8,128)(2,1)S(1)} collective-permute-done((bf16[384,896]{1,0:T(8,128)(2,1)S(1)}, bf16[384,896]{1,0:T(8,128)(2,1)S(1)}, u32[]{:S(2)}, u32[]{:S(2)}) %collective-permute-start.7) | collective-permute-done | bytes 688160 | tf_op jit(solution)/shard_map/ppermute | solution.py:206
  103.8 2.1 %collective-permute-start.10 = (bf16[384,896]{1,0:T(8,128)(2,1)S(1)}, bf16[384,896]{1,0:T(8,128)(2,1)S(1)}, u32[]{:S(2)}, u32[]{:S(2)}) collective-permute-start(bf16[384,896]{1,0:T(8,128)(2,1)S(1)} %collective-permute-done.7.refs_0_), channel_id=1, source_target_pairs={{0,1},{1,0},{2,3},{3,2},{4,5},{5,4},{6,7},{7,6},{8,9},{9,8},{10,11... | collective-permute-start | bytes 2064392 | tf_op jit(solution)/shard_map/ppermute | solution.py:197
  106.3 1.4 collective-permute-done.10.refs_0_
  108.1 2.6 %collective-permute-start.12 = (bf16[384,128]{1,0:T(8,128)(2,1)S(1)}, bf16[384,128]{1,0:T(8,128)(2,1)S(1)}, u32[]{:S(2)}, u32[]{:S(2)}) collective-permute-start(bf16[384,128]{1,0:T(8,128)(2,1)S(1)} %expand.7.refs_0_), channel_id=1, source_target_pairs={{0,4},{1,5},{2,6},{3,7},{4,0},{5,1},{6,2},{7,3},{8,12},{9,13},{10,... | collective-permute-start | bytes 294920 | tf_op jit(solution)/shard_map/ppermute | solution.py:197
  110.8 2.6 %collective-permute-done.11.refs_1_ = bf16[384,128]{1,0:T(8,128)(2,1)S(1)} collective-permute-done((bf16[384,128]{1,0:T(8,128)(2,1)S(1)}, bf16[384,128]{1,0:T(8,128)(2,1)S(1)}, u32[]{:S(2)}, u32[]{:S(2)}) %collective-permute-start.11) | collective-permute-done | bytes 98336 | tf_op jit(solution)/shard_map/ppermute | solution.py:197
  113.4 2.1 %collective-permute-done.12.refs_2_ = bf16[384,128]{1,0:T(8,128)(2,1)S(1)} collective-permute-done((bf16[384,128]{1,0:T(8,128)(2,1)S(1)}, bf16[384,128]{1,0:T(8,128)(2,1)S(1)}, u32[]{:S(2)}, u32[]{:S(2)}) %collective-permute-start.12) | collective-permute-done | bytes 98336 | tf_op jit(solution)/shard_map/ppermute | solution.py:197
  115.8 1.6 collective-permute-start.15
  124.7 1.9 %down.1 = bf16[5632,128]{1,0:T(8,128)(2,1)S(1)} custom-call(f32[384,1]{1,0:T(8,128)S(1)} %copy.19.weight_ref, s32[1,384]{1,0:T(1,128)S(1)} %compare_select_fusion.column_ref, bf16[384,128]{1,0:T(8,128)(2,1)S(1)} %expand.7.refs_0_, bf16[384,128]{1,0:T(8,128)(2,1)S(1)} %collective-permute-done.11.refs_1_, ...), custom_call_target="tpu_custom_call" | custom-call | tf_op jit(solution)/shard_map/down/pallas_call | solution.py:148
  126.6 48.6 %all_to_all.10 = bf16[256,11,2,128]{3,2,1,0:T(2,128)(2,1)S(1)} all-to-all(bf16[256,11,2,128]{3,2,1,0:T(2,128)(2,1)S(1)} %bitcast.44), channel_id=1, replica_groups=mesh['node'=32,'x'=4,'core'=2] {'node','x','core'}, dimensions={0} | all-to-all | bytes 2883584 | tf_op jit(solution)/shard_map/all_to_all | solution.py:188
  175.2 2.4 %place.1 = bf16[128,7168]{1,0:T(8,128)(2,1)} custom-call(bf16[96,128]{1,0:T(8,128)(2,1)S(1)} %add_convert_fusion.sel_ref, bf16[5632,128]{1,0:T(8,128)(2,1)S(1)} %bitcast.46), custom_call_target="tpu_custom_call" | custom-call | tf_op jit(solution)/shard_map/place/pallas_call | solution.py:175
  (110 shorter events, 26.8 us)
Async XLA Ops:
  0.0 118.2 %copy-start = (f32[32,384]{1,0:T(8,128)S(1)}, f32[32,384]{1,0:T(8,128)}, u32[]{:S(2)}) copy-start(f32[32,384]{1,0:T(8,128)} %param.13) | copy-start | bytes 147460
  5.6 15.7 %copy-start.22 = (bf16[1,128,7168]{2,1,0:T(8,128)(2,1)S(1)}, bf16[1,128,7168]{2,1,0:T(8,128)(2,1)}, u32[]{:S(2)}) copy-start(bf16[1,128,7168]{2,1,0:T(8,128)(2,1)} %param.10) | copy-start | bytes 5505028
  5.6 64.6 %all-to-all-start = ((bf16[256,11,2,128]{3,2,1,0:T(2,128)(2,1)}), bf16[256,11,2,128]{3,2,1,0:T(2,128)(2,1)S(1)}, u32[]{:S(2)}, u32[]{:S(2)}) async-start(bf16[256,11,2,128]{3,2,1,0:T(2,128)(2,1)} %bitcast.4), calls=%async_computation | async-start | bytes 2883584 | tf_op jit(solution)/shard_map/all_to_all | solution.py:188
  23.4 11.0 %collective-permute-start = (bf16[4,128,896]{2,1,0:T(8,128)(2,1)}, bf16[4,128,896]{2,1,0:T(8,128)(2,1)}, u32[]{:S(2)}, u32[]{:S(2)}) collective-permute-start(bf16[4,128,896]{2,1,0:T(8,128)(2,1)} %pad_maximum_fusion), channel_id=1, source_target_pairs={{0,1},{1,0},{2,3},{3,2},{4,5},{5,4},{6,7},{7,6},{8,9},{9,8},{10,11... | collective-permute-start | bytes 2752520 | tf_op jit(solution)/shard_map/ppermute | solution.py:197
  34.5 6.4 %copy-start.15 = (bf16[1792,128]{1,0:T(8,128)(2,1)S(1)}, bf16[1792,128]{1,0:T(8,128)(2,1)}, u32[]{:S(2)}) copy-start(bf16[1792,128]{1,0:T(8,128)(2,1)} %get-tuple-element.48) | copy-start | bytes 1376260
  36.9 30.9 %collective-permute-start.1 = (bf16[2,128,896]{2,1,0:T(8,128)(2,1)S(1)}, bf16[2,128,896]{2,1,0:T(8,128)(2,1)S(1)}, u32[]{:S(2)}, u32[]{:S(2)}) collective-permute-start(bf16[2,128,896]{2,1,0:T(8,128)(2,1)S(1)} %get-tuple-element.58), channel_id=1, source_target_pairs={{0,2},{1,3},{2,4},{3,5},{4,6},{5,7},{6,0},{7,1},{8,10},{9,11},{10,... | collective-permute-start | bytes 1376264 | tf_op jit(solution)/shard_map/ppermute | solution.py:197
  36.9 31.7 %collective-permute-start.2 = (bf16[2,128,896]{2,1,0:T(8,128)(2,1)S(1)}, bf16[2,128,896]{2,1,0:T(8,128)(2,1)S(1)}, u32[]{:S(2)}, u32[]{:S(2)}) collective-permute-start(bf16[2,128,896]{2,1,0:T(8,128)(2,1)S(1)} %get-tuple-element.59), channel_id=1, source_target_pairs={{0,4},{1,5},{2,6},{3,7},{4,0},{5,1},{6,2},{7,3},{8,12},{9,13},{10,... | collective-permute-start | bytes 1376264 | tf_op jit(solution)/shard_map/ppermute | solution.py:197
  38.9 30.5 %collective-permute-start.3 = (bf16[2,128,896]{2,1,0:T(8,128)(2,1)S(1)}, bf16[2,128,896]{2,1,0:T(8,128)(2,1)S(1)}, u32[]{:S(2)}, u32[]{:S(2)}) collective-permute-start(bf16[2,128,896]{2,1,0:T(8,128)(2,1)S(1)} %get-tuple-element.56), channel_id=1, source_target_pairs={{0,6},{1,7},{2,0},{3,1},{4,2},{5,3},{6,4},{7,5},{8,14},{9,15},{10,... | collective-permute-start | bytes 1376264 | tf_op jit(solution)/shard_map/ppermute | solution.py:197
  72.0 3.3 %collective-permute-start.6 = (bf16[384,896]{1,0:T(8,128)(2,1)}, bf16[384,896]{1,0:T(8,128)(2,1)}, u32[]{:S(2)}, u32[]{:S(2)}) collective-permute-start(bf16[384,896]{1,0:T(8,128)(2,1)} %pack.1.refs_0_), channel_id=1, source_target_pairs={{0,1},{1,0},{2,3},{3,2},{4,5},{5,4},{6,7},{7,6},{8,9},{9,8},{10,11... | collective-permute-start | bytes 2064392 | tf_op jit(solution)/shard_map/ppermute | solution.py:197
  72.6 18.6 %collective-permute-start.4 = (bf16[384,896]{1,0:T(8,128)(2,1)}, bf16[384,896]{1,0:T(8,128)(2,1)}, u32[]{:S(2)}, u32[]{:S(2)}) collective-permute-start(bf16[384,896]{1,0:T(8,128)(2,1)} %pack.1.refs_0_), channel_id=1, source_target_pairs={{0,2},{1,3},{2,4},{3,5},{4,6},{5,7},{6,0},{7,1},{8,10},{9,11},{10,... | collective-permute-start | bytes 2064392 | tf_op jit(solution)/shard_map/ppermute | solution.py:197
  72.6 18.6 %collective-permute-start.5 = (bf16[384,896]{1,0:T(8,128)(2,1)}, bf16[384,896]{1,0:T(8,128)(2,1)}, u32[]{:S(2)}, u32[]{:S(2)}) collective-permute-start(bf16[384,896]{1,0:T(8,128)(2,1)} %pack.1.refs_0_), channel_id=1, source_target_pairs={{0,6},{1,7},{2,0},{3,1},{4,2},{5,3},{6,4},{7,5},{8,14},{9,15},{10,... | collective-permute-start | bytes 2064392 | tf_op jit(solution)/shard_map/ppermute | solution.py:197
  75.3 20.6 %copy-start.1 = (bf16[1792,256]{1,0:T(8,128)(2,1)S(1)}, bf16[1792,256]{1,0:T(8,128)(2,1)}, u32[]{:S(2)}) copy-start(bf16[1792,256]{1,0:T(8,128)(2,1)} %pad_maximum_fusion.2.refs_4_) | copy-start | bytes 2752516
  75.3 20.7 %copy-start.2 = (bf16[1792,256]{1,0:T(8,128)(2,1)S(1)}, bf16[1792,256]{1,0:T(8,128)(2,1)}, u32[]{:S(2)}) copy-start(bf16[1792,256]{1,0:T(8,128)(2,1)} %pad_maximum_fusion.4.refs_5_) | copy-start | bytes 2752516
  91.2 4.8 %collective-permute-start.8 = (bf16[384,896]{1,0:T(8,128)(2,1)}, bf16[384,896]{1,0:T(8,128)(2,1)S(1)}, u32[]{:S(2)}, u32[]{:S(2)}) collective-permute-start(bf16[384,896]{1,0:T(8,128)(2,1)} %collective-permute-done.4.refs_0_), channel_id=1, source_target_pairs={{0,1},{1,0},{2,3},{3,2},{4,5},{5,4},{6,7},{7,6},{8,9},{9,8},{10,11... | collective-permute-start | bytes 2064392 | tf_op jit(solution)/shard_map/ppermute | solution.py:197
  92.0 4.0 %collective-permute-start.9 = (bf16[384,896]{1,0:T(8,128)(2,1)}, bf16[384,896]{1,0:T(8,128)(2,1)S(1)}, u32[]{:S(2)}, u32[]{:S(2)}) collective-permute-start(bf16[384,896]{1,0:T(8,128)(2,1)} %collective-permute-done.5.refs_2_), channel_id=1, source_target_pairs={{0,1},{1,0},{2,3},{3,2},{4,5},{5,4},{6,7},{7,6},{8,9},{9,8},{10,11... | collective-permute-start | bytes 2064392 | tf_op jit(solution)/shard_map/ppermute | solution.py:197
  93.1 10.6 %collective-permute-start.7 = (bf16[384,896]{1,0:T(8,128)(2,1)S(1)}, bf16[384,896]{1,0:T(8,128)(2,1)S(1)}, u32[]{:S(2)}, u32[]{:S(2)}) collective-permute-start(bf16[384,896]{1,0:T(8,128)(2,1)S(1)} %broadcast_select_fusion), channel_id=1, source_target_pairs={{0,2},{1,7},{2,4},{3,1},{4,6},{5,3},{6,0},{7,5},{8,10},{9,15},{10,... | collective-permute-start | bytes 2064392 | tf_op jit(solution)/shard_map/ppermute | solution.py:206
  103.8 3.9 %collective-permute-start.10 = (bf16[384,896]{1,0:T(8,128)(2,1)S(1)}, bf16[384,896]{1,0:T(8,128)(2,1)S(1)}, u32[]{:S(2)}, u32[]{:S(2)}) collective-permute-start(bf16[384,896]{1,0:T(8,128)(2,1)S(1)} %collective-permute-done.7.refs_0_), channel_id=1, source_target_pairs={{0,1},{1,0},{2,3},{3,2},{4,5},{5,4},{6,7},{7,6},{8,9},{9,8},{10,11... | collective-permute-start | bytes 2064392 | tf_op jit(solution)/shard_map/ppermute | solution.py:197
  106.3 14.6 %copy-start.3 = (bf16[2,128,896]{2,1,0:T(8,128)(2,1)S(1)}, bf16[2,128,896]{2,1,0:T(8,128)(2,1)}, u32[]{:S(2)}) copy-start(bf16[2,128,896]{2,1,0:T(8,128)(2,1)} %get-tuple-element.35.refs_6_) | copy-start | bytes 1376260
  106.3 14.6 %copy-start.6 = (bf16[2,128,896]{2,1,0:T(8,128)(2,1)S(1)}, bf16[2,128,896]{2,1,0:T(8,128)(2,1)}, u32[]{:S(2)}) copy-start(bf16[2,128,896]{2,1,0:T(8,128)(2,1)} %copy-done.5) | copy-start | bytes 1376260
  108.0 5.3 %collective-permute-start.11 = (bf16[384,128]{1,0:T(8,128)(2,1)S(1)}, bf16[384,128]{1,0:T(8,128)(2,1)S(1)}, u32[]{:S(2)}, u32[]{:S(2)}) collective-permute-start(bf16[384,128]{1,0:T(8,128)(2,1)S(1)} %expand.7.refs_0_), channel_id=1, source_target_pairs={{0,2},{1,3},{2,4},{3,5},{4,6},{5,7},{6,0},{7,1},{8,10},{9,11},{10,... | collective-permute-start | bytes 294920 | tf_op jit(solution)/shard_map/ppermute | solution.py:197
  108.1 7.3 %collective-permute-start.12 = (bf16[384,128]{1,0:T(8,128)(2,1)S(1)}, bf16[384,128]{1,0:T(8,128)(2,1)S(1)}, u32[]{:S(2)}, u32[]{:S(2)}) collective-permute-start(bf16[384,128]{1,0:T(8,128)(2,1)S(1)} %expand.7.refs_0_), channel_id=1, source_target_pairs={{0,4},{1,5},{2,6},{3,7},{4,0},{5,1},{6,2},{7,3},{8,12},{9,13},{10,... | collective-permute-start | bytes 294920 | tf_op jit(solution)/shard_map/ppermute | solution.py:197
  110.8 5.0 %collective-permute-start.13 = (bf16[384,128]{1,0:T(8,128)(2,1)S(1)}, bf16[384,128]{1,0:T(8,128)(2,1)S(1)}, u32[]{:S(2)}, u32[]{:S(2)}) collective-permute-start(bf16[384,128]{1,0:T(8,128)(2,1)S(1)} %expand.7.refs_0_), channel_id=1, source_target_pairs={{0,6},{1,7},{2,0},{3,1},{4,2},{5,3},{6,4},{7,5},{8,14},{9,15},{10,... | collective-permute-start | bytes 294920 | tf_op jit(solution)/shard_map/ppermute | solution.py:197
  115.8 4.3 %collective-permute-start.15 = (bf16[3,384,128]{2,1,0:T(8,128)(2,1)S(1)}, bf16[3,384,128]{2,1,0:T(8,128)(2,1)S(1)}, u32[]{:S(2)}, u32[]{:S(2)}) collective-permute-start(bf16[3,384,128]{2,1,0:T(8,128)(2,1)S(1)} %pad_maximum_fusion.5), channel_id=1, source_target_pairs={{0,1},{1,0},{2,3},{3,2},{4,5},{5,4},{6,7},{7,6},{8,9},{9,8},{10,11... | collective-permute-start | bytes 884744 | tf_op jit(solution)/shard_map/ppermute | solution.py:197
  118.1 1.4 collective-permute-start.14
  (22 other events, 42.4 us)

commit v7 on v6

--- a/solution.py
+++ b/solution.py
@@ -118,7 +118,7 @@
     )(places, *blocks, *mats, *([] if opening else [total]))
 
 
-def down_kernel(n_hidden, weight_ref, column_ref, *refs):
+def down_kernel(n_hidden, order, weight_ref, column_ref, *refs):
     hidden_refs, down_refs, (out_ref, held) = refs[:n_hidden], refs[n_hidden:-2], refs[-2:]
     width = down_refs[0].shape[2]
     cap = weight_ref.shape[0]
@@ -129,7 +129,7 @@
     for ref in hidden_refs:
         hidden += [ref[...]] if len(ref.shape) == 2 else [ref[k] for k in range(ref.shape[0])]
     hidden = jnp.concatenate(hidden, axis=1)
-    mat = jnp.concatenate([ref[flip] for flip in range(2) for ref in down_refs], axis=0)
+    mat = jnp.concatenate([down_refs[at][block] for at, block in order], axis=0)
     answer = weight_ref[...] * jnp.dot(hidden, mat, preferred_element_type=F32)
     answer = answer.astype(BF16)
     for s in range(SLOT):
@@ -143,10 +143,10 @@
     out_ref[...] = held[...].astype(BF16)
 
 
-def down(hidden, down_blocks, weight, column, devices):
+def down(hidden, down_blocks, order, weight, column, devices):
     shape = (devices * rows_of(down_blocks[0].shape[2] // LANE), LANE)
     return pl.pallas_call(
-        functools.partial(down_kernel, len(hidden)),
+        functools.partial(down_kernel, len(hidden), order),
         out_shape=jax.ShapeDtypeStruct(shape, BF16),
         in_specs=[VMEM] * (2 + len(hidden) + len(down_blocks)),
         out_specs=VMEM,
@@ -235,14 +235,15 @@
     arrived = exchange(outgoing[0], devices)
 
     mat, gate_mat, up_mat, _ = lax.optimization_barrier((w_down[0], w_gate[0], w_up[0], outgoing[0]))
-
-    def columns(core):
-        at = [(x * nc + core) * cut for x in range(nx)]
-        return jnp.stack([lax.dynamic_slice(mat, (0, start), (mat.shape[0], cut)) for start in at])
-
-    pair = jnp.stack([columns(at_core), sent(columns(1 - at_core), 0, 1)], axis=1)
-    down_blocks = [lax.dynamic_index_in_dim(pair, (at_x + dx) % nx, 0, keepdims=False) for dx in range(nx)]
-    down_blocks = [sent(block, dx, 0) if dx else block for dx, block in enumerate(down_blocks)]
+    def block_to(dx, flip):
+        to = (at_x + dx) % nx * nc + (at_core + flip) % nc
+        return lax.dynamic_slice(mat, (0, to * cut), (mat.shape[0], cut))
+
+    across = sent(jnp.stack([block_to(0, 1), block_to(2, 1)]), 0, 1)
+    near_blocks = [sent(block_to(dx, flip)[None], dx, flip) for dx in (1, 3) for flip in range(nc)]
+    far_blocks = sent(jnp.stack([block_to(2, 0), across[1]]), 2, 0)
+    down_blocks = [block_to(0, 0)[None], across, *near_blocks, far_blocks]
+    order = ((0, 0), (2, 0), (6, 0), (4, 0), (1, 0), (3, 0), (6, 1), (5, 0))
 
     pieces = []
     for dx in range(nx):
@@ -259,7 +260,7 @@
     column = holder * SLOT + jnp.sum(before.astype(jnp.int32), axis=1)
     column = jnp.where(entry < count, column, -1)
 
-    arrived, down_blocks, pieces = lax.optimization_barrier((arrived, down_blocks, pieces))
+    arrived, pieces, down_blocks = lax.optimization_barrier((arrived, pieces, down_blocks))
     own = pack(column[:, None], arrived, *PARTS)
     here, there = at_core * cut, (1 - at_core) * cut
     fore, aft = sent(own, 1, 0), sent(own, -1, 0)
@@ -278,7 +279,7 @@
     others = sent(jnp.stack(near), 0, 1)
     groups = [hidden, *near, other, others]
 
-    back = down(groups, down_blocks, weight[:, None], column[None, :], devices)
+    back = down(groups, down_blocks, order, weight[:, None], column[None, :], devices)
     returned = exchange(back, devices)
     return place(sel, returned, n_local, width)
 

time: 178 us -> 167 us (0.938)
  local copies, waits for them, and re-layouts: 16.7 us -> 9.5 us
  waiting for transfers between devices: 52.7 us -> 48.2 us
  other arithmetic: 11.5 us -> 8.76 us
    unnamed x58 -> x36, local copies, waits for them, and re-layouts: 10.1 us -> 4.37 us
    ppermute x15 -> x17, waiting for transfers between devices: 47.2 us -> 42.1 us  [sent(): return lax.ppermute(value, LOCAL, pairs)]
    squeeze x1 -> x0, other arithmetic: 2.35 us -> none  [shards(): lax.dynamic_index_in_dim(pair, (at_x + dx) % nx, 0, keepdims=False)]
    ppermute x15 -> x17, starting transfers between devices: 15.9 us -> 18 us  [sent(): return lax.ppermute(value, LOCAL, pairs)]
    dynamic_slice x2, local copies, waits for them, and re-layouts: 3.92 us -> 1.82 us  [shards(): lax.dynamic_slice(m, at, size)]
  transfers between devices with their start and end apart: 17 -> 19, of which waited for: 8 -> 10; matrix products, arithmetic and copies ran while one was open for 9% -> 7% of each run, Pallas kernels for 3% -> 2%
where the time goes in v7:
time: 167 us; the launch traced here: 166 us
  blocking collectives  49.5 us (30%)
  waiting for transfers between devices  48.2 us (29%)
  starting transfers between devices  36 us (22%)
  Pallas kernels  13.9 us (8%)
  local copies, waits for them, and re-layouts  9.5 us (6%)
  other arithmetic  8.76 us (5%)
    all_to_all x1, blocking collectives, exchange(): lax.all_to_all(parts, AXES, split_axis=0, concat_axis=0, tiled=True)  49.5 us
    ppermute x17, waiting for transfers between devices, sent(): return lax.ppermute(value, LOCAL, pairs)  42.1 us
    ppermute x17, starting transfers between devices, sent(): return lax.ppermute(value, LOCAL, pairs)  18 us
    all_to_all x1, starting transfers between devices, exchange(): lax.all_to_all(parts, AXES, split_axis=0, concat_axis=0, tiled=True)  15.7 us
    ppermute x1, waiting for transfers between devices, forwarded(): lax.ppermute(jnp.where(lax.axis_index('core') == 0, fore, aft), LOCAL, pa...  6.1 us
    unnamed x36, local copies, waits for them, and re-layouts  4.37 us
    pallas_call x4, Pallas kernels, expand(): pl.pallas_call(functools.partial(expand_kernel, uses, opening, last), out...  4.27 us
  transfers between devices with their start and end apart: 19, of which 10 were waited for; matrix products, arithmetic and copies ran while one was open for 7% of the time, Pallas kernels for 2%

profile of v7, /device:TPU:1, one launch (start us, length us, event | category | flops | bytes accessed | tf_op | source)
XLA Modules:
  0.0 166.3 jit_solution(11274793737694942011)
XLA Ops:
  1.8 1.5 copy-done.3
  3.3 2.3 %send.1 = bf16[5632,128]{1,0:T(8,128)(2,1)} custom-call(bf16[96,128]{1,0:T(8,128)(2,1)S(1)} %add_convert_fusion.sel_ref, bf16[128,7168]{1,0:T(8,128)(2,1)S(1)} %copy-done.3), custom_call_target="tpu_custom_call" | custom-call | tf_op jit(solution)/shard_map/send/pallas_call | solution.py:50
  5.6 15.7 %all-to-all-start = ((bf16[256,11,2,128]{3,2,1,0:T(2,128)(2,1)}), bf16[256,11,2,128]{3,2,1,0:T(2,128)(2,1)S(1)}, u32[]{:S(2)}, u32[]{:S(2)}) async-start(bf16[256,11,2,128]{3,2,1,0:T(2,128)(2,1)} %bitcast.4), calls=%async_computation | async-start | bytes 2883584 | tf_op jit(solution)/shard_map/all_to_all | solution.py:188
  23.3 2.1 %collective-permute-start = (bf16[2,128,896]{2,1,0:T(8,128)(2,1)}, bf16[2,128,896]{2,1,0:T(8,128)(2,1)S(1)}, u32[]{:S(2)}, u32[]{:S(2)}) collective-permute-start(bf16[2,128,896]{2,1,0:T(8,128)(2,1)} %pad_maximum_fusion.4), channel_id=1, source_target_pairs={{0,1},{1,0},{2,3},{3,2},{4,5},{5,4},{6,7},{7,6},{8,9},{9,8},{10,11... | collective-permute-start | bytes 1376264 | tf_op jit(solution)/shard_map/ppermute | solution.py:197
  26.5 1.6 collective-permute-start.3
  28.1 2.0 %collective-permute-start.4 = (bf16[1,128,896]{2,1,0:T(8,128)(2,1)}, bf16[1,128,896]{2,1,0:T(8,128)(2,1)}, u32[]{:S(2)}, u32[]{:S(2)}) collective-permute-start(bf16[1,128,896]{2,1,0:T(8,128)(2,1)} %get-tuple-element.55), channel_id=1, source_target_pairs={{0,7},{1,6},{2,1},{3,0},{4,3},{5,2},{6,5},{7,4},{8,15},{9,14},{10,... | collective-permute-start | bytes 688136 | tf_op jit(solution)/shard_map/ppermute | solution.py:197
  33.8 1.7 %constant_dynamic-slice_fusion.1 = (bf16[1792,128]{1,0:T(8,128)(2,1)S(1)}, bf16[1792,128]{1,0:T(8,128)(2,1)S(1)}, bf16[1792,128]{1,0:T(8,128)(2,1)S(1)}, bf16[1792,128]{1,0:T(8,128)(2,1)S(1)}) fusion(bf16[7168,128]{1,0:T(8,128)(2,1)} %bitcast.39, s32[]{:T(128)S(6)} %select_n.205, s32[]{:T(128)S(6)} %select_n.203, s32[]{:T(128)S(6)} %select_n.201, ...), kind=kLoop, calls=%fused_computation.64 | loop fusion | bytes 3670032 | tf_op jit(solution)/shard_map/dynamic_slice | solution.py:252
  39.2 1.4 fusion.4.column_ref
  40.6 20.7 %collective-permute-done.2.refs_9_ = bf16[1,128,896]{2,1,0:T(8,128)(2,1)} collective-permute-done((bf16[1,128,896]{2,1,0:T(8,128)(2,1)}, bf16[1,128,896]{2,1,0:T(8,128)(2,1)}, u32[]{:S(2)}, u32[]{:S(2)}) %collective-permute-start.2) | collective-permute-done | bytes 229408 | tf_op jit(solution)/shard_map/ppermute | solution.py:197
  63.0 1.8 %pack.1.refs_0_ = bf16[384,896]{1,0:T(8,128)(2,1)} custom-call(s32[384,1]{1,0:T(8,128)S(1)} %copy-done.6, bf16[5632,128]{1,0:T(8,128)(2,1)S(1)} %bitcast.33), custom_call_target="tpu_custom_call" | custom-call | tf_op jit(solution)/shard_map/pack/pallas_call | solution.py:77
  65.3 1.6 collective-permute-start.6
  68.0 2.0 %expand.4.refs_6_ = f32[384,256]{1,0:T(8,128)S(1)} custom-call(s32[2]{0:T(128)S(1)} %pad_add_fusion.place_ref, bf16[384,896]{1,0:T(8,128)(2,1)} %pack.1.refs_0_, bf16[384,896]{1,0:T(8,128)(2,1)} %collective-permute-done.8.refs_1_, bf16[1792,256]{1,0:T(8,128)(2,1)S(1)} %pad_maximum_fusion.refs_2_), custom_call_target="tpu_custom_call" | custom-call | flops 352321536 | bytes 688128 | tf_op jit(solution)/shard_map/expand/pallas_call | solution.py:110
  70.0 13.5 %collective-permute-done.6.refs_0_ = bf16[384,896]{1,0:T(8,128)(2,1)S(1)} collective-permute-done((bf16[384,896]{1,0:T(8,128)(2,1)}, bf16[384,896]{1,0:T(8,128)(2,1)S(1)}, u32[]{:S(2)}, u32[]{:S(2)}) %collective-permute-start.6) | collective-permute-done | bytes 688160 | tf_op jit(solution)/shard_map/ppermute | solution.py:197
  85.0 2.4 %collective-permute-start.9 = (bf16[384,896]{1,0:T(8,128)(2,1)S(1)}, bf16[384,896]{1,0:T(8,128)(2,1)S(1)}, u32[]{:S(2)}, u32[]{:S(2)}) collective-permute-start(bf16[384,896]{1,0:T(8,128)(2,1)S(1)} %broadcast_select_fusion), channel_id=1, source_target_pairs={{0,2},{1,7},{2,4},{3,1},{4,6},{5,3},{6,0},{7,5},{8,10},{9,15},{10,... | collective-permute-start | bytes 2064392 | tf_op jit(solution)/shard_map/ppermute | solution.py:206
  87.6 1.5 expand.5.refs_2_
  89.1 6.1 %collective-permute-done.9.refs_0_ = bf16[384,896]{1,0:T(8,128)(2,1)S(1)} collective-permute-done((bf16[384,896]{1,0:T(8,128)(2,1)S(1)}, bf16[384,896]{1,0:T(8,128)(2,1)S(1)}, u32[]{:S(2)}, u32[]{:S(2)}) %collective-permute-start.9) | collective-permute-done | bytes 688160 | tf_op jit(solution)/shard_map/ppermute | solution.py:206
  95.3 2.4 %collective-permute-start.12 = (bf16[384,896]{1,0:T(8,128)(2,1)S(1)}, bf16[384,896]{1,0:T(8,128)(2,1)S(1)}, u32[]{:S(2)}, u32[]{:S(2)}) collective-permute-start(bf16[384,896]{1,0:T(8,128)(2,1)S(1)} %collective-permute-done.9.refs_0_), channel_id=1, source_target_pairs={{0,1},{1,0},{2,3},{3,2},{4,5},{5,4},{6,7},{7,6},{8,9},{9,8},{10,11... | collective-permute-start | bytes 2064392 | tf_op jit(solution)/shard_map/ppermute | solution.py:197
  98.1 1.4 collective-permute-done.12.refs_0_
  99.9 2.3 %collective-permute-start.14 = (bf16[384,128]{1,0:T(8,128)(2,1)S(1)}, bf16[384,128]{1,0:T(8,128)(2,1)S(1)}, u32[]{:S(2)}, u32[]{:S(2)}) collective-permute-start(bf16[384,128]{1,0:T(8,128)(2,1)S(1)} %expand.7.refs_0_), channel_id=1, source_target_pairs={{0,4},{1,5},{2,6},{3,7},{4,0},{5,1},{6,2},{7,3},{8,12},{9,13},{10,... | collective-permute-start | bytes 294920 | tf_op jit(solution)/shard_map/ppermute | solution.py:197
  102.6 2.9 %collective-permute-done.13.refs_1_ = bf16[384,128]{1,0:T(8,128)(2,1)S(1)} collective-permute-done((bf16[384,128]{1,0:T(8,128)(2,1)S(1)}, bf16[384,128]{1,0:T(8,128)(2,1)S(1)}, u32[]{:S(2)}, u32[]{:S(2)}) %collective-permute-start.13) | collective-permute-done | bytes 98336 | tf_op jit(solution)/shard_map/ppermute | solution.py:197
  107.6 1.6 collective-permute-start.17
  111.2 3.1 %down.1 = bf16[5632,128]{1,0:T(8,128)(2,1)S(1)} custom-call(f32[384,1]{1,0:T(8,128)S(1)} %copy.19.weight_ref, s32[1,384]{1,0:T(1,128)S(1)} %compare_select_fusion.column_ref, bf16[384,128]{1,0:T(8,128)(2,1)S(1)} %expand.7.refs_0_, bf16[384,128]{1,0:T(8,128)(2,1)S(1)} %collective-permute-done.13.refs_1_, ...), custom_call_target="tpu_custom_call" | custom-call | tf_op jit(solution)/shard_map/down/pallas_call | solution.py:148
  114.4 49.5 %all_to_all.10 = bf16[256,11,2,128]{3,2,1,0:T(2,128)(2,1)S(1)} all-to-all(bf16[256,11,2,128]{3,2,1,0:T(2,128)(2,1)S(1)} %bitcast.35), channel_id=1, replica_groups=mesh['node'=32,'x'=4,'core'=2] {'node','x','core'}, dimensions={0} | all-to-all | bytes 2883584 | tf_op jit(solution)/shard_map/all_to_all | solution.py:188
  163.8 2.4 %place.1 = bf16[128,7168]{1,0:T(8,128)(2,1)} custom-call(bf16[96,128]{1,0:T(8,128)(2,1)S(1)} %copy-done.10, bf16[5632,128]{1,0:T(8,128)(2,1)S(1)} %bitcast.34), custom_call_target="tpu_custom_call" | custom-call | tf_op jit(solution)/shard_map/place/pallas_call | solution.py:175
  (92 shorter events, 22.4 us)
Async XLA Ops:
  0.0 109.9 %copy-start = (f32[32,384]{1,0:T(8,128)S(1)}, f32[32,384]{1,0:T(8,128)}, u32[]{:S(2)}) copy-start(f32[32,384]{1,0:T(8,128)} %param.13) | copy-start | bytes 147460
  5.6 15.8 %copy-start.12 = (bf16[1,128,7168]{2,1,0:T(8,128)(2,1)S(1)}, bf16[1,128,7168]{2,1,0:T(8,128)(2,1)}, u32[]{:S(2)}) copy-start(bf16[1,128,7168]{2,1,0:T(8,128)(2,1)} %param.10) | copy-start | bytes 5505028
  5.6 56.5 %all-to-all-start = ((bf16[256,11,2,128]{3,2,1,0:T(2,128)(2,1)}), bf16[256,11,2,128]{3,2,1,0:T(2,128)(2,1)S(1)}, u32[]{:S(2)}, u32[]{:S(2)}) async-start(bf16[256,11,2,128]{3,2,1,0:T(2,128)(2,1)} %bitcast.4), calls=%async_computation | async-start | bytes 2883584 | tf_op jit(solution)/shard_map/all_to_all | solution.py:188
  23.3 14.9 %collective-permute-start = (bf16[2,128,896]{2,1,0:T(8,128)(2,1)}, bf16[2,128,896]{2,1,0:T(8,128)(2,1)S(1)}, u32[]{:S(2)}, u32[]{:S(2)}) collective-permute-start(bf16[2,128,896]{2,1,0:T(8,128)(2,1)} %pad_maximum_fusion.4), channel_id=1, source_target_pairs={{0,1},{1,0},{2,3},{3,2},{4,5},{5,4},{6,7},{7,6},{8,9},{9,8},{10,11... | collective-permute-start | bytes 1376264 | tf_op jit(solution)/shard_map/ppermute | solution.py:197
  25.4 15.2 %collective-permute-start.1 = (bf16[1,128,896]{2,1,0:T(8,128)(2,1)}, bf16[1,128,896]{2,1,0:T(8,128)(2,1)}, u32[]{:S(2)}, u32[]{:S(2)}) collective-permute-start(bf16[1,128,896]{2,1,0:T(8,128)(2,1)} %get-tuple-element.58), channel_id=1, source_target_pairs={{0,2},{1,3},{2,4},{3,5},{4,6},{5,7},{6,0},{7,1},{8,10},{9,11},{10,... | collective-permute-start | bytes 688136 | tf_op jit(solution)/shard_map/ppermute | solution.py:197
  25.4 35.9 %collective-permute-start.2 = (bf16[1,128,896]{2,1,0:T(8,128)(2,1)}, bf16[1,128,896]{2,1,0:T(8,128)(2,1)}, u32[]{:S(2)}, u32[]{:S(2)}) collective-permute-start(bf16[1,128,896]{2,1,0:T(8,128)(2,1)} %get-tuple-element.57), channel_id=1, source_target_pairs={{0,3},{1,2},{2,5},{3,4},{4,7},{5,6},{6,1},{7,0},{8,11},{9,10},{10,... | collective-permute-start | bytes 688136 | tf_op jit(solution)/shard_map/ppermute | solution.py:197
  26.5 34.8 %collective-permute-start.3 = (bf16[1,128,896]{2,1,0:T(8,128)(2,1)}, bf16[1,128,896]{2,1,0:T(8,128)(2,1)}, u32[]{:S(2)}, u32[]{:S(2)}) collective-permute-start(bf16[1,128,896]{2,1,0:T(8,128)(2,1)} %get-tuple-element.56), channel_id=1, source_target_pairs={{0,6},{1,7},{2,0},{3,1},{4,2},{5,3},{6,4},{7,5},{8,14},{9,15},{10,... | collective-permute-start | bytes 688136 | tf_op jit(solution)/shard_map/ppermute | solution.py:197
  28.1 33.2 %collective-permute-start.4 = (bf16[1,128,896]{2,1,0:T(8,128)(2,1)}, bf16[1,128,896]{2,1,0:T(8,128)(2,1)}, u32[]{:S(2)}, u32[]{:S(2)}) collective-permute-start(bf16[1,128,896]{2,1,0:T(8,128)(2,1)} %get-tuple-element.55), channel_id=1, source_target_pairs={{0,7},{1,6},{2,1},{3,0},{4,3},{5,2},{6,5},{7,4},{8,15},{9,14},{10,... | collective-permute-start | bytes 688136 | tf_op jit(solution)/shard_map/ppermute | solution.py:197
  38.2 23.1 %collective-permute-start.5 = (bf16[2,128,896]{2,1,0:T(8,128)(2,1)S(1)}, bf16[2,128,896]{2,1,0:T(8,128)(2,1)S(1)}, u32[]{:S(2)}, u32[]{:S(2)}) collective-permute-start(bf16[2,128,896]{2,1,0:T(8,128)(2,1)S(1)} %pad_maximum_fusion.5), channel_id=1, source_target_pairs={{0,4},{1,5},{2,6},{3,7},{4,0},{5,1},{6,2},{7,3},{8,12},{9,13},{10,... | collective-permute-start | bytes 1376264 | tf_op jit(solution)/shard_map/ppermute | solution.py:197
  64.9 3.1 %collective-permute-start.8 = (bf16[384,896]{1,0:T(8,128)(2,1)}, bf16[384,896]{1,0:T(8,128)(2,1)}, u32[]{:S(2)}, u32[]{:S(2)}) collective-permute-start(bf16[384,896]{1,0:T(8,128)(2,1)} %pack.1.refs_0_), channel_id=1, source_target_pairs={{0,1},{1,0},{2,3},{3,2},{4,5},{5,4},{6,7},{7,6},{8,9},{9,8},{10,11... | collective-permute-start | bytes 2064392 | tf_op jit(solution)/shard_map/ppermute | solution.py:197
  65.3 18.3 %collective-permute-start.6 = (bf16[384,896]{1,0:T(8,128)(2,1)}, bf16[384,896]{1,0:T(8,128)(2,1)S(1)}, u32[]{:S(2)}, u32[]{:S(2)}) collective-permute-start(bf16[384,896]{1,0:T(8,128)(2,1)} %pack.1.refs_0_), channel_id=1, source_target_pairs={{0,2},{1,3},{2,4},{3,5},{4,6},{5,7},{6,0},{7,1},{8,10},{9,11},{10,... | collective-permute-start | bytes 2064392 | tf_op jit(solution)/shard_map/ppermute | solution.py:197
  66.8 17.0 %collective-permute-start.7 = (bf16[384,896]{1,0:T(8,128)(2,1)}, bf16[384,896]{1,0:T(8,128)(2,1)S(1)}, u32[]{:S(2)}, u32[]{:S(2)}) collective-permute-start(bf16[384,896]{1,0:T(8,128)(2,1)} %pack.1.refs_0_), channel_id=1, source_target_pairs={{0,6},{1,7},{2,0},{3,1},{4,2},{5,3},{6,4},{7,5},{8,14},{9,15},{10,... | collective-permute-start | bytes 2064392 | tf_op jit(solution)/shard_map/ppermute | solution.py:197
  68.0 19.6 %copy-start.1 = (bf16[1792,256]{1,0:T(8,128)(2,1)S(1)}, bf16[1792,256]{1,0:T(8,128)(2,1)}, u32[]{:S(2)}) copy-start(bf16[1792,256]{1,0:T(8,128)(2,1)} %pad_maximum_fusion.3.refs_5_) | copy-start | bytes 2752516
  68.0 19.6 %copy-start.2 = (bf16[1792,256]{1,0:T(8,128)(2,1)S(1)}, bf16[1792,256]{1,0:T(8,128)(2,1)}, u32[]{:S(2)}) copy-start(bf16[1792,256]{1,0:T(8,128)(2,1)} %pad_maximum_fusion.1.refs_4_) | copy-start | bytes 2752516
  83.8 3.7 %collective-permute-start.10 = (bf16[384,896]{1,0:T(8,128)(2,1)S(1)}, bf16[384,896]{1,0:T(8,128)(2,1)S(1)}, u32[]{:S(2)}, u32[]{:S(2)}) collective-permute-start(bf16[384,896]{1,0:T(8,128)(2,1)S(1)} %collective-permute-done.6.refs_0_), channel_id=1, source_target_pairs={{0,1},{1,0},{2,3},{3,2},{4,5},{5,4},{6,7},{7,6},{8,9},{9,8},{10,11... | collective-permute-start | bytes 2064392 | tf_op jit(solution)/shard_map/ppermute | solution.py:197
  84.9 2.8 %collective-permute-start.11 = (bf16[384,896]{1,0:T(8,128)(2,1)S(1)}, bf16[384,896]{1,0:T(8,128)(2,1)S(1)}, u32[]{:S(2)}, u32[]{:S(2)}) collective-permute-start(bf16[384,896]{1,0:T(8,128)(2,1)S(1)} %collective-permute-done.7.refs_2_), channel_id=1, source_target_pairs={{0,1},{1,0},{2,3},{3,2},{4,5},{5,4},{6,7},{7,6},{8,9},{9,8},{10,11... | collective-permute-start | bytes 2064392 | tf_op jit(solution)/shard_map/ppermute | solution.py:197
  85.0 10.3 %collective-permute-start.9 = (bf16[384,896]{1,0:T(8,128)(2,1)S(1)}, bf16[384,896]{1,0:T(8,128)(2,1)S(1)}, u32[]{:S(2)}, u32[]{:S(2)}) collective-permute-start(bf16[384,896]{1,0:T(8,128)(2,1)S(1)} %broadcast_select_fusion), channel_id=1, source_target_pairs={{0,2},{1,7},{2,4},{3,1},{4,6},{5,3},{6,0},{7,5},{8,10},{9,15},{10,... | collective-permute-start | bytes 2064392 | tf_op jit(solution)/shard_map/ppermute | solution.py:206
  95.3 4.2 %collective-permute-start.12 = (bf16[384,896]{1,0:T(8,128)(2,1)S(1)}, bf16[384,896]{1,0:T(8,128)(2,1)S(1)}, u32[]{:S(2)}, u32[]{:S(2)}) collective-permute-start(bf16[384,896]{1,0:T(8,128)(2,1)S(1)} %collective-permute-done.9.refs_0_), channel_id=1, source_target_pairs={{0,1},{1,0},{2,3},{3,2},{4,5},{5,4},{6,7},{7,6},{8,9},{9,8},{10,11... | collective-permute-start | bytes 2064392 | tf_op jit(solution)/shard_map/ppermute | solution.py:197
  99.9 5.7 %collective-permute-start.13 = (bf16[384,128]{1,0:T(8,128)(2,1)S(1)}, bf16[384,128]{1,0:T(8,128)(2,1)S(1)}, u32[]{:S(2)}, u32[]{:S(2)}) collective-permute-start(bf16[384,128]{1,0:T(8,128)(2,1)S(1)} %expand.7.refs_0_), channel_id=1, source_target_pairs={{0,2},{1,3},{2,4},{3,5},{4,6},{5,7},{6,0},{7,1},{8,10},{9,11},{10,... | collective-permute-start | bytes 294920 | tf_op jit(solution)/shard_map/ppermute | solution.py:197
  99.9 6.9 %collective-permute-start.14 = (bf16[384,128]{1,0:T(8,128)(2,1)S(1)}, bf16[384,128]{1,0:T(8,128)(2,1)S(1)}, u32[]{:S(2)}, u32[]{:S(2)}) collective-permute-start(bf16[384,128]{1,0:T(8,128)(2,1)S(1)} %expand.7.refs_0_), channel_id=1, source_target_pairs={{0,4},{1,5},{2,6},{3,7},{4,0},{5,1},{6,2},{7,3},{8,12},{9,13},{10,... | collective-permute-start | bytes 294920 | tf_op jit(solution)/shard_map/ppermute | solution.py:197
  102.2 5.4 %collective-permute-start.15 = (bf16[384,128]{1,0:T(8,128)(2,1)S(1)}, bf16[384,128]{1,0:T(8,128)(2,1)S(1)}, u32[]{:S(2)}, u32[]{:S(2)}) collective-permute-start(bf16[384,128]{1,0:T(8,128)(2,1)S(1)} %expand.7.refs_0_), channel_id=1, source_target_pairs={{0,6},{1,7},{2,0},{3,1},{4,2},{5,3},{6,4},{7,5},{8,14},{9,15},{10,... | collective-permute-start | bytes 294920 | tf_op jit(solution)/shard_map/ppermute | solution.py:197
  107.6 3.6 %collective-permute-start.17 = (bf16[3,384,128]{2,1,0:T(8,128)(2,1)S(1)}, bf16[3,384,128]{2,1,0:T(8,128)(2,1)S(1)}, u32[]{:S(2)}, u32[]{:S(2)}) collective-permute-start(bf16[3,384,128]{2,1,0:T(8,128)(2,1)S(1)} %pad_maximum_fusion.6), channel_id=1, source_target_pairs={{0,1},{1,0},{2,3},{3,2},{4,5},{5,4},{6,7},{7,6},{8,9},{9,8},{10,11... | collective-permute-start | bytes 884744 | tf_op jit(solution)/shard_map/ppermute | solution.py:197
  109.8 1.4 collective-permute-start.16
  114.3 49.5 %copy-start.10 = (bf16[96,128]{1,0:T(8,128)(2,1)S(1)}, bf16[96,128]{1,0:T(8,128)(2,1)}, u32[]{:S(2)}) copy-start(bf16[96,128]{1,0:T(8,128)(2,1)} %copy-done.9) | copy-start | bytes 73732
  (13 other events, 64.3 us)

commit v8 on v7

--- a/solution.py
+++ b/solution.py
@@ -58,7 +58,7 @@
     )(sel, tokens)
 
 
-def pack_kernel(tiles, column_ref, msg_ref, out_ref, held):
+def pack_kernel(tiles, column_ref, msg_ref, out_ref, top_ref, bottom_ref, held):
     rows = rows_of(tiles)
     devices = msg_ref.shape[0] // rows
     cap = column_ref.shape[0]
@@ -70,27 +70,35 @@
         slot = lax.broadcasted_iota(jnp.int32, (cap, devices), 1) * SLOT + s
         hot = (slot == column_ref[...]).astype(F32).astype(BF16)
         total = total + jnp.dot(hot, flat, preferred_element_type=F32)
-    out_ref[...] = total.astype(BF16)
+    rounded = total.astype(BF16)
+    out_ref[...] = rounded
+    top_ref[...] = rounded[: cap // 2]
+    bottom_ref[...] = rounded[cap // 2 :]
 
 
 def pack(column, msg, tiles):
+    cap, width = column.shape[0], tiles * LANE
+    shapes = [(cap, width), (cap // 2, width), (cap // 2, width)]
     return pl.pallas_call(
         functools.partial(pack_kernel, tiles),
-        out_shape=jax.ShapeDtypeStruct((column.shape[0], tiles * LANE), BF16),
+        out_shape=[jax.ShapeDtypeStruct(shape, BF16) for shape in shapes],
         in_specs=[VMEM, VMEM],
-        out_specs=VMEM,
+        out_specs=[VMEM] * 3,
         scratch_shapes=[pltpu.VMEM(msg.shape, F32)],
         compiler_params=PARAMS,
         name="pack",
     )(column, msg)
 
 
-def expand_kernel(uses, opening, last, place_ref, *refs):
-    blocks, mats, out_ref = refs[: len(uses)], refs[len(uses) : len(uses) + max(uses) + 1], refs[-1]
+def expand_kernel(uses, pieces, opening, last, place_ref, *refs):
+    n_refs = len(uses) * pieces
+    blocks, mats, out_ref = refs[:n_refs], refs[n_refs : n_refs + max(uses) + 1], refs[-1]
+    width = blocks[0].shape[1]
     total = None if opening else refs[-2][...]
-    for n, ref in enumerate(blocks):
-        at = pl.ds(pl.multiple_of(place_ref[n], LANE), ref.shape[1])
-        val = jnp.dot(ref[...], mats[uses[n]][at, :], preferred_element_type=F32)
+    for n, use in enumerate(uses):
+        mat = mats[use][pl.ds(pl.multiple_of(place_ref[n], LANE), width), :]
+        val = [jnp.dot(ref[...], mat, preferred_element_type=F32) for ref in blocks[n * pieces : (n + 1) * pieces]]
+        val = jnp.concatenate(val, axis=0)
         total = val if total is None else total + val
     if last:
         units = out_ref.shape[1]
@@ -101,21 +109,23 @@
 
 
 def expand(total, blocks, uses, places, mats, last=False):
-    cap = blocks[0].shape[0]
+    pieces = len(blocks[0])
+    flat = [part for block in blocks for part in block]
+    cap = sum(part.shape[0] for part in blocks[0])
     both = mats[0].shape[1]
     opening = total is None
     shape = jax.ShapeDtypeStruct((cap, both // 2), BF16) if last else jax.ShapeDtypeStruct((cap, both), F32)
     smem = pl.BlockSpec(memory_space=pltpu.SMEM)
-    flops = 2 * cap * both * sum(block.shape[1] for block in blocks)
-    return pl.pallas_call(
-        functools.partial(expand_kernel, uses, opening, last),
+    flops = 2 * cap * both * flat[0].shape[1] * len(blocks)
+    return pl.pallas_call(
+        functools.partial(expand_kernel, uses, pieces, opening, last),
         out_shape=shape,
-        in_specs=[smem] + [VMEM] * (len(blocks) + len(mats) + (not opening)),
+        in_specs=[smem] + [VMEM] * (len(flat) + len(mats) + (not opening)),
         out_specs=VMEM,
         compiler_params=PARAMS,
         cost_estimate=pl.CostEstimate(flops=flops, bytes_accessed=flops // 512, transcendentals=0),
         name="expand",
-    )(places, *blocks, *mats, *([] if opening else [total]))
+    )(places, *flat, *mats, *([] if opening else [total]))
 
 
 def down_kernel(n_hidden, order, weight_ref, column_ref, *refs):
@@ -197,15 +207,6 @@
     return lax.ppermute(value, LOCAL, pairs)
 
 
-def forwarded(fore, aft):
-    nx = lax.axis_size("x")
-    pairs = []
-    for x in range(nx):
-        pairs.append((2 * x, (x + 1) % nx * 2))
-        pairs.append((2 * x + 1, (x - 1) % nx * 2 + 1))
-    return lax.ppermute(jnp.where(lax.axis_index("core") == 0, fore, aft), LOCAL, pairs)
-
-
 def shards(tokens, w_gate, w_up, w_down, chosen, counts, gates):
     tok_dev, width = tokens.shape
     n_node = lax.axis_size("node")
@@ -261,18 +262,21 @@
     column = jnp.where(entry < count, column, -1)
 
     arrived, pieces, down_blocks = lax.optimization_barrier((arrived, pieces, down_blocks))
-    own = pack(column[:, None], arrived, *PARTS)
+    own, top, bottom = pack(column[:, None], arrived, *PARTS)
     here, there = at_core * cut, (1 - at_core) * cut
-    fore, aft = sent(own, 1, 0), sent(own, -1, 0)
-    total = expand(None, [own, sent(own, 0, 1)], (0, 0), jnp.stack([here, there]), pieces[:1])
-    fore, aft, total = lax.optimization_barrier((fore, aft, total))
-    far = forwarded(fore, aft)
-    near = [fore, sent(fore, 0, 1), aft, sent(aft, 0, 1)]
+    fore_top, aft_bottom = sent(top, 1, 0), sent(bottom, -1, 0)
+    other, top, bottom = lax.optimization_barrier((sent(own, 0, 1), top, bottom))
+    fore_bottom, aft_top = sent(bottom, 1, 0), sent(top, -1, 0)
+    total = expand(None, [[own], [other]], (0, 0), jnp.stack([here, there]), pieces[:1])
+    fore_top, aft_bottom, total = lax.optimization_barrier((fore_top, aft_bottom, total))
+    far = [sent(fore_top, 1, 0), sent(aft_bottom, -1, 0)]
+    fore, aft = [fore_top, fore_bottom], [aft_top, aft_bottom]
+    near = [fore, [sent(part, 0, 1) for part in fore], aft, [sent(part, 0, 1) for part in aft]]
     at = jnp.stack([here, there, here, there])
     total = expand(total, near, (0, 0, 1, 1), at, [pieces[1], pieces[-1]])
-    far, total = lax.optimization_barrier((far, total))
     total = expand(total, [far], (0,), jnp.stack([here]), pieces[2:3])
-    hidden = expand(total, [sent(far, 0, 1)], (0,), jnp.stack([there]), pieces[2:3], last=True)
+    far = [sent(part, 0, 1) for part in far]
+    hidden = expand(total, [far], (0,), jnp.stack([there]), pieces[2:3], last=True)
 
     near = [sent(hidden, dx, 0) for dx in range(1, nx)]
     other = sent(hidden, 0, 1)

time: 167 us -> 170 us (1.018)
  starting transfers between devices: 36 us -> 40.6 us
  waiting for transfers between devices: 48.2 us -> 43.7 us
  local copies, waits for them, and re-layouts: 9.5 us -> 11.8 us
    ppermute x17 -> x24, starting transfers between devices: 18 us -> 25 us  [sent(): return lax.ppermute(value, LOCAL, pairs)]
    ppermute x1 -> x0, waiting for transfers between devices: 6.1 us -> none  [forwarded(): lax.ppermute(jnp.where(lax.axis_index('core') == 0, fore, aft), LOCAL, pa...]
    ppermute x1 -> x0, starting transfers between devices: 2.41 us -> none  [forwarded(): lax.ppermute(jnp.where(lax.axis_index('core') == 0, fore, aft), LOCAL, pa...]
    unnamed x36, local copies, waits for them, and re-layouts: 4.37 us -> 6.57 us
    ppermute x17 -> x24, waiting for transfers between devices: 42.1 us -> 43.7 us  [sent(): return lax.ppermute(value, LOCAL, pairs)]
  transfers between devices with their start and end apart: 19 -> 25, of which waited for: 10 -> 8; matrix products, arithmetic and copies ran while one was open for 7% -> 7% of each run, Pallas kernels for 2% -> 3%
where the time goes in v8:
time: 170 us; the launch traced here: 169 us
  blocking collectives  49.5 us (29%)
  waiting for transfers between devices  43.7 us (26%)
  starting transfers between devices  40.6 us (24%)
  Pallas kernels  14.6 us (9%)
  local copies, waits for them, and re-layouts  11.8 us (7%)
  other arithmetic  8.81 us (5%)
    all_to_all x1, blocking collectives, exchange(): lax.all_to_all(parts, AXES, split_axis=0, concat_axis=0, tiled=True)  49.5 us
    ppermute x24, waiting for transfers between devices, sent(): return lax.ppermute(value, LOCAL, pairs)  43.7 us
    ppermute x24, starting transfers between devices, sent(): return lax.ppermute(value, LOCAL, pairs)  25 us
    all_to_all x1, starting transfers between devices, exchange(): lax.all_to_all(parts, AXES, split_axis=0, concat_axis=0, tiled=True)  15.7 us
    unnamed x36, local copies, waits for them, and re-layouts  6.57 us
    pallas_call x4, Pallas kernels, expand(): pl.pallas_call(functools.partial(expand_kernel, uses, pieces, opening, la...  4.75 us
  transfers between devices with their start and end apart: 25, of which 8 were waited for; matrix products, arithmetic and copies ran while one was open for 7% of the time, Pallas kernels for 3%

profile of v8, /device:TPU:1, one launch (start us, length us, event | category | flops | bytes accessed | tf_op | source)
XLA Modules:
  0.0 169.4 jit_solution(18037307307744689212)
XLA Ops:
  1.8 1.5 copy-done.3
  3.3 2.3 %send.1 = bf16[5632,128]{1,0:T(8,128)(2,1)} custom-call(bf16[96,128]{1,0:T(8,128)(2,1)S(1)} %add_convert_fusion.sel_ref, bf16[128,7168]{1,0:T(8,128)(2,1)S(1)} %copy-done.3), custom_call_target="tpu_custom_call" | custom-call | tf_op jit(solution)/shard_map/send/pallas_call | solution.py:50
  5.6 15.7 %all-to-all-start = ((bf16[256,11,2,128]{3,2,1,0:T(2,128)(2,1)}), bf16[256,11,2,128]{3,2,1,0:T(2,128)(2,1)S(1)}, u32[]{:S(2)}, u32[]{:S(2)}) async-start(bf16[256,11,2,128]{3,2,1,0:T(2,128)(2,1)} %bitcast.4), calls=%async_computation | async-start | bytes 2883584 | tf_op jit(solution)/shard_map/all_to_all | solution.py:198
  23.3 2.1 %collective-permute-start = (bf16[2,128,896]{2,1,0:T(8,128)(2,1)}, bf16[2,128,896]{2,1,0:T(8,128)(2,1)S(1)}, u32[]{:S(2)}, u32[]{:S(2)}) collective-permute-start(bf16[2,128,896]{2,1,0:T(8,128)(2,1)} %pad_maximum_fusion.4), channel_id=1, source_target_pairs={{0,1},{1,0},{2,3},{3,2},{4,5},{5,4},{6,7},{7,6},{8,9},{9,8},{10,11... | collective-permute-start | bytes 1376264 | tf_op jit(solution)/shard_map/ppermute | solution.py:207
  26.6 1.6 collective-permute-start.3
  28.1 2.0 %collective-permute-start.4 = (bf16[1,128,896]{2,1,0:T(8,128)(2,1)}, bf16[1,128,896]{2,1,0:T(8,128)(2,1)}, u32[]{:S(2)}, u32[]{:S(2)}) collective-permute-start(bf16[1,128,896]{2,1,0:T(8,128)(2,1)} %get-tuple-element.63), channel_id=1, source_target_pairs={{0,7},{1,6},{2,1},{3,0},{4,3},{5,2},{6,5},{7,4},{8,15},{9,14},{10,... | collective-permute-start | bytes 688136 | tf_op jit(solution)/shard_map/ppermute | solution.py:207
  30.1 1.3 dynamic_slice.61
  33.8 1.7 %constant_dynamic-slice_fusion.1 = (bf16[1792,128]{1,0:T(8,128)(2,1)S(1)}, bf16[1792,128]{1,0:T(8,128)(2,1)S(1)}, bf16[1792,128]{1,0:T(8,128)(2,1)S(1)}, bf16[1792,128]{1,0:T(8,128)(2,1)S(1)}) fusion(bf16[7168,128]{1,0:T(8,128)(2,1)} %bitcast.39, s32[]{:T(128)S(6)} %select_n.196, s32[]{:T(128)S(6)} %select_n.194, s32[]{:T(128)S(6)} %select_n.192, ...), kind=kLoop, calls=%fused_computation.63 | loop fusion | bytes 3670032 | tf_op jit(solution)/shard_map/dynamic_slice | solution.py:253
  39.3 1.5 fusion.4.column_ref
  40.8 20.6 %collective-permute-done.2.refs_9_ = bf16[1,128,896]{2,1,0:T(8,128)(2,1)} collective-permute-done((bf16[1,128,896]{2,1,0:T(8,128)(2,1)}, bf16[1,128,896]{2,1,0:T(8,128)(2,1)}, u32[]{:S(2)}, u32[]{:S(2)}) %collective-permute-start.2) | collective-permute-done | bytes 229408 | tf_op jit(solution)/shard_map/ppermute | solution.py:207
  63.1 2.0 %pack.1 = (bf16[384,896]{1,0:T(8,128)(2,1)}, bf16[192,896]{1,0:T(8,128)(2,1)}, bf16[192,896]{1,0:T(8,128)(2,1)}) custom-call(s32[384,1]{1,0:T(8,128)S(1)} %copy-done.6, bf16[5632,128]{1,0:T(8,128)(2,1)S(1)} %bitcast.33), custom_call_target="tpu_custom_call" | custom-call | tf_op jit(solution)/shard_map/pack/pallas_call | solution.py:82
  65.5 1.6 collective-permute-start.6
  68.3 1.9 %expand.4.refs_10_ = f32[384,256]{1,0:T(8,128)S(1)} custom-call(s32[2]{0:T(128)S(1)} %pad_add_fusion.place_ref, bf16[384,896]{1,0:T(8,128)(2,1)} %get-tuple-element.35.refs_0_, bf16[384,896]{1,0:T(8,128)(2,1)} %collective-permute-done.8.refs_1_, bf16[1792,256]{1,0:T(8,128)(2,1)S(1)} %pad_maximum_fusion.refs_2_), custom_call_target="tpu_custom_call" | custom-call | flops 352321536 | bytes 688128 | tf_op jit(solution)/shard_map/expand/pallas_call | solution.py:120
  70.1 6.4 %collective-permute-done.6.refs_0_ = bf16[192,896]{1,0:T(8,128)(2,1)} collective-permute-done((bf16[192,896]{1,0:T(8,128)(2,1)}, bf16[192,896]{1,0:T(8,128)(2,1)}, u32[]{:S(2)}, u32[]{:S(2)}) %collective-permute-start.6) | collective-permute-done | bytes 344096 | tf_op jit(solution)/shard_map/ppermute | solution.py:207
  77.9 2.7 %collective-permute-start.16 = (bf16[192,896]{1,0:T(8,128)(2,1)}, bf16[192,896]{1,0:T(8,128)(2,1)S(1)}, u32[]{:S(2)}, u32[]{:S(2)}) collective-permute-start(bf16[192,896]{1,0:T(8,128)(2,1)} %get-tuple-element.42), channel_id=1, source_target_pairs={{0,6},{1,7},{2,0},{3,1},{4,2},{5,3},{6,4},{7,5},{8,14},{9,15},{10,... | collective-permute-start | bytes 1032200 | tf_op jit(solution)/shard_map/ppermute | solution.py:207
  80.5 2.7 %collective-permute-start.11 = (bf16[192,896]{1,0:T(8,128)(2,1)}, bf16[192,896]{1,0:T(8,128)(2,1)S(1)}, u32[]{:S(2)}, u32[]{:S(2)}) collective-permute-start(bf16[192,896]{1,0:T(8,128)(2,1)} %collective-permute-done.7.refs_5_), channel_id=1, source_target_pairs={{0,6},{1,7},{2,0},{3,1},{4,2},{5,3},{6,4},{7,5},{8,14},{9,15},{10,... | collective-permute-start | bytes 1032200 | tf_op jit(solution)/shard_map/ppermute | solution.py:207
  84.3 4.6 %collective-permute-done.13.refs_1_ = bf16[192,896]{1,0:T(8,128)(2,1)S(1)} collective-permute-done((bf16[192,896]{1,0:T(8,128)(2,1)}, bf16[192,896]{1,0:T(8,128)(2,1)S(1)}, u32[]{:S(2)}, u32[]{:S(2)}) %collective-permute-start.13) | collective-permute-done | bytes 344096 | tf_op jit(solution)/shard_map/ppermute | solution.py:207
  90.1 6.2 %collective-permute-done.9.refs_0_ = bf16[192,896]{1,0:T(8,128)(2,1)S(1)} collective-permute-done((bf16[192,896]{1,0:T(8,128)(2,1)}, bf16[192,896]{1,0:T(8,128)(2,1)S(1)}, u32[]{:S(2)}, u32[]{:S(2)}) %collective-permute-start.9) | collective-permute-done | bytes 344096 | tf_op jit(solution)/shard_map/ppermute | solution.py:207
  98.4 2.1 %expand.5.refs_3_ = f32[384,256]{1,0:T(8,128)S(1)} custom-call(s32[4]{0:T(128)S(1)} %pad_add_fusion.1.place_ref, bf16[192,896]{1,0:T(8,128)(2,1)} %collective-permute-done.6.refs_0_, bf16[192,896]{1,0:T(8,128)(2,1)S(1)} %collective-permute-done.13.refs_1_, bf16[192,896]{1,0:T(8,128)(2,1)S(1)} %collective-permute-done.14.refs_2_, ...), custom_call_target="tpu_custom_call" | custom-call | flops 704643072 | bytes 1376256 | tf_op jit(solution)/shard_map/expand/pallas_call | solution.py:120
  101.9 3.3 %collective-permute-start.20 = (bf16[384,128]{1,0:T(8,128)(2,1)S(1)}, bf16[384,128]{1,0:T(8,128)(2,1)S(1)}, u32[]{:S(2)}, u32[]{:S(2)}) collective-permute-start(bf16[384,128]{1,0:T(8,128)(2,1)S(1)} %expand.7.refs_0_), channel_id=1, source_target_pairs={{0,4},{1,5},{2,6},{3,7},{4,0},{5,1},{6,2},{7,3},{8,12},{9,13},{10,... | collective-permute-start | bytes 294920 | tf_op jit(solution)/shard_map/ppermute | solution.py:207
  106.5 3.8 %collective-permute-done.20.refs_2_ = bf16[384,128]{1,0:T(8,128)(2,1)S(1)} collective-permute-done((bf16[384,128]{1,0:T(8,128)(2,1)S(1)}, bf16[384,128]{1,0:T(8,128)(2,1)S(1)}, u32[]{:S(2)}, u32[]{:S(2)}) %collective-permute-start.20) | collective-permute-done | bytes 98336 | tf_op jit(solution)/shard_map/ppermute | solution.py:207
  114.3 3.1 %down.1 = bf16[5632,128]{1,0:T(8,128)(2,1)S(1)} custom-call(f32[384,1]{1,0:T(8,128)S(1)} %copy.19.weight_ref, s32[1,384]{1,0:T(1,128)S(1)} %compare_select_fusion.column_ref, bf16[384,128]{1,0:T(8,128)(2,1)S(1)} %expand.7.refs_0_, bf16[384,128]{1,0:T(8,128)(2,1)S(1)} %collective-permute-done.19.refs_1_, ...), custom_call_target="tpu_custom_call" | custom-call | tf_op jit(solution)/shard_map/down/pallas_call | solution.py:158
  117.5 49.5 %all_to_all.10 = bf16[256,11,2,128]{3,2,1,0:T(2,128)(2,1)S(1)} all-to-all(bf16[256,11,2,128]{3,2,1,0:T(2,128)(2,1)S(1)} %bitcast.35), channel_id=1, replica_groups=mesh['node'=32,'x'=4,'core'=2] {'node','x','core'}, dimensions={0} | all-to-all | bytes 2883584 | tf_op jit(solution)/shard_map/all_to_all | solution.py:198
  167.0 2.4 %place.1 = bf16[128,7168]{1,0:T(8,128)(2,1)} custom-call(bf16[96,128]{1,0:T(8,128)(2,1)S(1)} %copy-done.10, bf16[5632,128]{1,0:T(8,128)(2,1)S(1)} %bitcast.34), custom_call_target="tpu_custom_call" | custom-call | tf_op jit(solution)/shard_map/place/pallas_call | solution.py:185
  (103 shorter events, 26.5 us)
Async XLA Ops:
  5.6 56.6 %all-to-all-start = ((bf16[256,11,2,128]{3,2,1,0:T(2,128)(2,1)}), bf16[256,11,2,128]{3,2,1,0:T(2,128)(2,1)S(1)}, u32[]{:S(2)}, u32[]{:S(2)}) async-start(bf16[256,11,2,128]{3,2,1,0:T(2,128)(2,1)} %bitcast.4), calls=%async_computation | async-start | bytes 2883584 | tf_op jit(solution)/shard_map/all_to_all | solution.py:198
  23.3 14.9 %collective-permute-start = (bf16[2,128,896]{2,1,0:T(8,128)(2,1)}, bf16[2,128,896]{2,1,0:T(8,128)(2,1)S(1)}, u32[]{:S(2)}, u32[]{:S(2)}) collective-permute-start(bf16[2,128,896]{2,1,0:T(8,128)(2,1)} %pad_maximum_fusion.4), channel_id=1, source_target_pairs={{0,1},{1,0},{2,3},{3,2},{4,5},{5,4},{6,7},{7,6},{8,9},{9,8},{10,11... | collective-permute-start | bytes 1376264 | tf_op jit(solution)/shard_map/ppermute | solution.py:207
  25.4 15.3 %collective-permute-start.1 = (bf16[1,128,896]{2,1,0:T(8,128)(2,1)}, bf16[1,128,896]{2,1,0:T(8,128)(2,1)}, u32[]{:S(2)}, u32[]{:S(2)}) collective-permute-start(bf16[1,128,896]{2,1,0:T(8,128)(2,1)} %get-tuple-element.66), channel_id=1, source_target_pairs={{0,2},{1,3},{2,4},{3,5},{4,6},{5,7},{6,0},{7,1},{8,10},{9,11},{10,... | collective-permute-start | bytes 688136 | tf_op jit(solution)/shard_map/ppermute | solution.py:207
  25.4 35.9 %collective-permute-start.2 = (bf16[1,128,896]{2,1,0:T(8,128)(2,1)}, bf16[1,128,896]{2,1,0:T(8,128)(2,1)}, u32[]{:S(2)}, u32[]{:S(2)}) collective-permute-start(bf16[1,128,896]{2,1,0:T(8,128)(2,1)} %get-tuple-element.65), channel_id=1, source_target_pairs={{0,3},{1,2},{2,5},{3,4},{4,7},{5,6},{6,1},{7,0},{8,11},{9,10},{10,... | collective-permute-start | bytes 688136 | tf_op jit(solution)/shard_map/ppermute | solution.py:207
  26.6 34.8 %collective-permute-start.3 = (bf16[1,128,896]{2,1,0:T(8,128)(2,1)}, bf16[1,128,896]{2,1,0:T(8,128)(2,1)}, u32[]{:S(2)}, u32[]{:S(2)}) collective-permute-start(bf16[1,128,896]{2,1,0:T(8,128)(2,1)} %get-tuple-element.64), channel_id=1, source_target_pairs={{0,6},{1,7},{2,0},{3,1},{4,2},{5,3},{6,4},{7,5},{8,14},{9,15},{10,... | collective-permute-start | bytes 688136 | tf_op jit(solution)/shard_map/ppermute | solution.py:207
  28.1 33.2 %collective-permute-start.4 = (bf16[1,128,896]{2,1,0:T(8,128)(2,1)}, bf16[1,128,896]{2,1,0:T(8,128)(2,1)}, u32[]{:S(2)}, u32[]{:S(2)}) collective-permute-start(bf16[1,128,896]{2,1,0:T(8,128)(2,1)} %get-tuple-element.63), channel_id=1, source_target_pairs={{0,7},{1,6},{2,1},{3,0},{4,3},{5,2},{6,5},{7,4},{8,15},{9,14},{10,... | collective-permute-start | bytes 688136 | tf_op jit(solution)/shard_map/ppermute | solution.py:207
  38.3 23.1 %collective-permute-start.5 = (bf16[2,128,896]{2,1,0:T(8,128)(2,1)S(1)}, bf16[2,128,896]{2,1,0:T(8,128)(2,1)S(1)}, u32[]{:S(2)}, u32[]{:S(2)}) collective-permute-start(bf16[2,128,896]{2,1,0:T(8,128)(2,1)S(1)} %pad_maximum_fusion.5), channel_id=1, source_target_pairs={{0,4},{1,5},{2,6},{3,7},{4,0},{5,1},{6,2},{7,3},{8,12},{9,13},{10,... | collective-permute-start | bytes 1376264 | tf_op jit(solution)/shard_map/ppermute | solution.py:207
  65.1 3.1 %collective-permute-start.8 = (bf16[384,896]{1,0:T(8,128)(2,1)}, bf16[384,896]{1,0:T(8,128)(2,1)}, u32[]{:S(2)}, u32[]{:S(2)}) collective-permute-start(bf16[384,896]{1,0:T(8,128)(2,1)} %get-tuple-element.35.refs_0_), channel_id=1, source_target_pairs={{0,1},{1,0},{2,3},{3,2},{4,5},{5,4},{6,7},{7,6},{8,9},{9,8},{10,11... | collective-permute-start | bytes 2064392 | tf_op jit(solution)/shard_map/ppermute | solution.py:207
  65.5 11.1 %collective-permute-start.6 = (bf16[192,896]{1,0:T(8,128)(2,1)}, bf16[192,896]{1,0:T(8,128)(2,1)}, u32[]{:S(2)}, u32[]{:S(2)}) collective-permute-start(bf16[192,896]{1,0:T(8,128)(2,1)} %get-tuple-element.42), channel_id=1, source_target_pairs={{0,2},{1,3},{2,4},{3,5},{4,6},{5,7},{6,0},{7,1},{8,10},{9,11},{10,... | collective-permute-start | bytes 1032200 | tf_op jit(solution)/shard_map/ppermute | solution.py:207
  67.1 9.7 %collective-permute-start.7 = (bf16[192,896]{1,0:T(8,128)(2,1)}, bf16[192,896]{1,0:T(8,128)(2,1)}, u32[]{:S(2)}, u32[]{:S(2)}) collective-permute-start(bf16[192,896]{1,0:T(8,128)(2,1)} %get-tuple-element.41), channel_id=1, source_target_pairs={{0,6},{1,7},{2,0},{3,1},{4,2},{5,3},{6,4},{7,5},{8,14},{9,15},{10,... | collective-permute-start | bytes 1032200 | tf_op jit(solution)/shard_map/ppermute | solution.py:207
  76.7 6.5 %collective-permute-start.14 = (bf16[192,896]{1,0:T(8,128)(2,1)}, bf16[192,896]{1,0:T(8,128)(2,1)S(1)}, u32[]{:S(2)}, u32[]{:S(2)}) collective-permute-start(bf16[192,896]{1,0:T(8,128)(2,1)} %collective-permute-done.6.refs_0_), channel_id=1, source_target_pairs={{0,1},{1,0},{2,3},{3,2},{4,5},{5,4},{6,7},{7,6},{8,9},{9,8},{10,11... | collective-permute-start | bytes 1032200 | tf_op jit(solution)/shard_map/ppermute | solution.py:207
  77.8 11.1 %collective-permute-start.13 = (bf16[192,896]{1,0:T(8,128)(2,1)}, bf16[192,896]{1,0:T(8,128)(2,1)S(1)}, u32[]{:S(2)}, u32[]{:S(2)}) collective-permute-start(bf16[192,896]{1,0:T(8,128)(2,1)} %get-tuple-element.41), channel_id=1, source_target_pairs={{0,2},{1,3},{2,4},{3,5},{4,6},{5,7},{6,0},{7,1},{8,10},{9,11},{10,... | collective-permute-start | bytes 1032200 | tf_op jit(solution)/shard_map/ppermute | solution.py:207
  77.9 12.3 %collective-permute-start.16 = (bf16[192,896]{1,0:T(8,128)(2,1)}, bf16[192,896]{1,0:T(8,128)(2,1)S(1)}, u32[]{:S(2)}, u32[]{:S(2)}) collective-permute-start(bf16[192,896]{1,0:T(8,128)(2,1)} %get-tuple-element.42), channel_id=1, source_target_pairs={{0,6},{1,7},{2,0},{3,1},{4,2},{5,3},{6,4},{7,5},{8,14},{9,15},{10,... | collective-permute-start | bytes 1032200 | tf_op jit(solution)/shard_map/ppermute | solution.py:207
  80.5 15.8 %collective-permute-start.9 = (bf16[192,896]{1,0:T(8,128)(2,1)}, bf16[192,896]{1,0:T(8,128)(2,1)S(1)}, u32[]{:S(2)}, u32[]{:S(2)}) collective-permute-start(bf16[192,896]{1,0:T(8,128)(2,1)} %collective-permute-done.6.refs_0_), channel_id=1, source_target_pairs={{0,2},{1,3},{2,4},{3,5},{4,6},{5,7},{6,0},{7,1},{8,10},{9,11},{10,... | collective-permute-start | bytes 1032200 | tf_op jit(solution)/shard_map/ppermute | solution.py:207
  80.5 16.6 %collective-permute-start.11 = (bf16[192,896]{1,0:T(8,128)(2,1)}, bf16[192,896]{1,0:T(8,128)(2,1)S(1)}, u32[]{:S(2)}, u32[]{:S(2)}) collective-permute-start(bf16[192,896]{1,0:T(8,128)(2,1)} %collective-permute-done.7.refs_5_), channel_id=1, source_target_pairs={{0,6},{1,7},{2,0},{3,1},{4,2},{5,3},{6,4},{7,5},{8,14},{9,15},{10,... | collective-permute-start | bytes 1032200 | tf_op jit(solution)/shard_map/ppermute | solution.py:207
  83.2 14.0 %collective-permute-start.18 = (bf16[192,896]{1,0:T(8,128)(2,1)}, bf16[192,896]{1,0:T(8,128)(2,1)S(1)}, u32[]{:S(2)}, u32[]{:S(2)}) collective-permute-start(bf16[192,896]{1,0:T(8,128)(2,1)} %collective-permute-done.7.refs_5_), channel_id=1, source_target_pairs={{0,1},{1,0},{2,3},{3,2},{4,5},{5,4},{6,7},{7,6},{8,9},{9,8},{10,11... | collective-permute-start | bytes 1032200 | tf_op jit(solution)/shard_map/ppermute | solution.py:207
  89.0 8.2 %collective-permute-start.15 = (bf16[192,896]{1,0:T(8,128)(2,1)S(1)}, bf16[192,896]{1,0:T(8,128)(2,1)S(1)}, u32[]{:S(2)}, u32[]{:S(2)}) collective-permute-start(bf16[192,896]{1,0:T(8,128)(2,1)S(1)} %collective-permute-done.13.refs_1_), channel_id=1, source_target_pairs={{0,1},{1,0},{2,3},{3,2},{4,5},{5,4},{6,7},{7,6},{8,9},{9,8},{10,11... | collective-permute-start | bytes 1032200 | tf_op jit(solution)/shard_map/ppermute | solution.py:207
  90.1 7.1 %collective-permute-start.17 = (bf16[192,896]{1,0:T(8,128)(2,1)S(1)}, bf16[192,896]{1,0:T(8,128)(2,1)S(1)}, u32[]{:S(2)}, u32[]{:S(2)}) collective-permute-start(bf16[192,896]{1,0:T(8,128)(2,1)S(1)} %collective-permute-done.16.refs_4_), channel_id=1, source_target_pairs={{0,1},{1,0},{2,3},{3,2},{4,5},{5,4},{6,7},{7,6},{8,9},{9,8},{10,11... | collective-permute-start | bytes 1032200 | tf_op jit(solution)/shard_map/ppermute | solution.py:207
  96.3 4.6 %collective-permute-start.10 = (bf16[192,896]{1,0:T(8,128)(2,1)S(1)}, bf16[192,896]{1,0:T(8,128)(2,1)S(1)}, u32[]{:S(2)}, u32[]{:S(2)}) collective-permute-start(bf16[192,896]{1,0:T(8,128)(2,1)S(1)} %collective-permute-done.9.refs_0_), channel_id=1, source_target_pairs={{0,1},{1,0},{2,3},{3,2},{4,5},{5,4},{6,7},{7,6},{8,9},{9,8},{10,11... | collective-permute-start | bytes 1032200 | tf_op jit(solution)/shard_map/ppermute | solution.py:207
  97.1 3.8 %collective-permute-start.12 = (bf16[192,896]{1,0:T(8,128)(2,1)S(1)}, bf16[192,896]{1,0:T(8,128)(2,1)S(1)}, u32[]{:S(2)}, u32[]{:S(2)}) collective-permute-start(bf16[192,896]{1,0:T(8,128)(2,1)S(1)} %collective-permute-done.11.refs_1_), channel_id=1, source_target_pairs={{0,1},{1,0},{2,3},{3,2},{4,5},{5,4},{6,7},{7,6},{8,9},{9,8},{10,11... | collective-permute-start | bytes 1032200 | tf_op jit(solution)/shard_map/ppermute | solution.py:207
  101.4 5.1 %collective-permute-start.19 = (bf16[384,128]{1,0:T(8,128)(2,1)S(1)}, bf16[384,128]{1,0:T(8,128)(2,1)S(1)}, u32[]{:S(2)}, u32[]{:S(2)}) collective-permute-start(bf16[384,128]{1,0:T(8,128)(2,1)S(1)} %expand.7.refs_0_), channel_id=1, source_target_pairs={{0,2},{1,3},{2,4},{3,5},{4,6},{5,7},{6,0},{7,1},{8,10},{9,11},{10,... | collective-permute-start | bytes 294920 | tf_op jit(solution)/shard_map/ppermute | solution.py:207
  101.9 8.4 %collective-permute-start.20 = (bf16[384,128]{1,0:T(8,128)(2,1)S(1)}, bf16[384,128]{1,0:T(8,128)(2,1)S(1)}, u32[]{:S(2)}, u32[]{:S(2)}) collective-permute-start(bf16[384,128]{1,0:T(8,128)(2,1)S(1)} %expand.7.refs_0_), channel_id=1, source_target_pairs={{0,4},{1,5},{2,6},{3,7},{4,0},{5,1},{6,2},{7,3},{8,12},{9,13},{10,... | collective-permute-start | bytes 294920 | tf_op jit(solution)/shard_map/ppermute | solution.py:207
  105.3 5.1 %collective-permute-start.21 = (bf16[384,128]{1,0:T(8,128)(2,1)S(1)}, bf16[384,128]{1,0:T(8,128)(2,1)S(1)}, u32[]{:S(2)}, u32[]{:S(2)}) collective-permute-start(bf16[384,128]{1,0:T(8,128)(2,1)S(1)} %expand.7.refs_0_), channel_id=1, source_target_pairs={{0,6},{1,7},{2,0},{3,1},{4,2},{5,3},{6,4},{7,5},{8,14},{9,15},{10,... | collective-permute-start | bytes 294920 | tf_op jit(solution)/shard_map/ppermute | solution.py:207
  110.4 2.9 %collective-permute-start.23 = (bf16[3,384,128]{2,1,0:T(8,128)(2,1)S(1)}, bf16[3,384,128]{2,1,0:T(8,128)(2,1)S(1)}, u32[]{:S(2)}, u32[]{:S(2)}) collective-permute-start(bf16[3,384,128]{2,1,0:T(8,128)(2,1)S(1)} %pad_maximum_fusion.6), channel_id=1, source_target_pairs={{0,1},{1,0},{2,3},{3,2},{4,5},{5,4},{6,7},{7,6},{8,9},{9,8},{10,11... | collective-permute-start | bytes 884744 | tf_op jit(solution)/shard_map/ppermute | solution.py:207
  (19 other events, 262.1 us)

commit v9 on v7

--- a/solution.py
+++ b/solution.py
@@ -12,63 +12,87 @@
 LANE = 128
 LOCAL = ("x", "core")
 AXES = ("node", "x", "core")
-PARTS = (7,)
 BF16 = jnp.bfloat16
 F32 = jnp.float32
 PARAMS = pltpu.CompilerParams(vmem_limit_bytes=14 * 2**20)
+WIDE = pltpu.CompilerParams(vmem_limit_bytes=56 * 2**20)
 VMEM = pl.BlockSpec(memory_space=pltpu.VMEM)
+HBM = pl.BlockSpec(memory_space=pltpu.HBM)
 
 
 def rows_of(tiles):
     return -(-tiles * SLOT // 2) * 2
 
 
-def send_kernel(parts, sel_ref, tok_ref, *refs):
-    outs, held = refs[: len(parts)], refs[len(parts) :]
-    experts = sel_ref.shape[0] // SLOT
-    cut = sum(parts) * LANE
-    n_local = tok_ref.shape[1] // cut
+def send_kernel(n_local, me_ref, counts_ref, chosen_ref, tok_ref, out_ref, sel_ref, held, tok, sems):
+    tok_dev, width = tok_ref.shape
+    experts, cap = chosen_ref.shape
+    step = tok_dev // sems.shape[0]
+    copies = []
+    for n in range(sems.shape[0]):
+        part = pl.ds(n * step, step)
+        copies.append(pltpu.make_async_copy(tok_ref.at[part, :], tok.at[part, :], sems.at[n]))
+        copies[-1].start()
+
+    place_at = lax.broadcasted_iota(jnp.int32, (experts, cap), 1)
+    token = lax.broadcasted_iota(jnp.int32, (experts, tok_dev), 1)
+    position = chosen_ref[...] - me_ref[0] * tok_dev
+    rest = (place_at < counts_ref[...]) & (position >= 0) & (position < tok_dev)
+    for s in range(SLOT):
+        first = jnp.min(jnp.where(rest, place_at, cap), axis=1, keepdims=True)
+        hit = place_at == first
+        slot = jnp.sum(jnp.where(hit, position, 0), axis=1, keepdims=True)
+        chose = (token == slot) & (first < cap)
+        sel_ref[s * experts : (s + 1) * experts, :] = chose.astype(F32).astype(BF16)
+        rest = rest & jnp.logical_not(hit)
+
+    for copy in copies:
+        copy.wait()
+    cut = width // n_local
+    tiles = cut // LANE
+    rows = rows_of(tiles)
     for k in range(n_local):
-        val = jnp.dot(sel_ref[...], tok_ref[:, k * cut : (k + 1) * cut], preferred_element_type=F32)
-        first = 0
-        for tiles, ref in zip(parts, held):
-            rows = rows_of(tiles)
-            for t in range(tiles):
-                lanes = slice((first + t) * LANE, (first + t + 1) * LANE)
-                for s in range(SLOT):
-                    at = pl.ds(k * rows + t * SLOT + s, experts, stride=n_local * rows)
-                    ref[at, :] = val[s * experts : (s + 1) * experts, lanes]
-            for r in range(SLOT * tiles, rows):
-                ref[pl.ds(k * rows + r, experts, stride=n_local * rows), :] = jnp.zeros((experts, LANE), F32)
-            first += tiles
-    for out, ref in zip(outs, held):
-        out[...] = ref[...].astype(BF16)
-
-
-def send(sel, tokens, parts, devices):
-    shapes = [(devices * rows_of(tiles), LANE) for tiles in parts]
-    return pl.pallas_call(
-        functools.partial(send_kernel, parts),
-        out_shape=[jax.ShapeDtypeStruct(shape, BF16) for shape in shapes],
-        in_specs=[VMEM, VMEM],
-        out_specs=[VMEM] * len(parts),
-        scratch_shapes=[pltpu.VMEM(shape, F32) for shape in shapes],
-        compiler_params=PARAMS,
+        val = jnp.dot(sel_ref[...], tok[:, k * cut : (k + 1) * cut], preferred_element_type=F32)
+        for t in range(tiles):
+            for s in range(SLOT):
+                at = pl.ds(k * rows + t * SLOT + s, experts, stride=n_local * rows)
+                held[at, :] = val[s * experts : (s + 1) * experts, t * LANE : (t + 1) * LANE]
+        for r in range(SLOT * tiles, rows):
+            held[pl.ds(k * rows + r, experts, stride=n_local * rows), :] = jnp.zeros((experts, LANE), F32)
+    out_ref[...] = held[...].astype(BF16)
+
+
+def send(me, counts, chosen, tokens, n_local):
+    tok_dev, width = tokens.shape
+    experts = chosen.shape[0]
+    shape = (experts * n_local * rows_of(width // (n_local * LANE)), LANE)
+    return pl.pallas_call(
+        functools.partial(send_kernel, n_local),
+        out_shape=[jax.ShapeDtypeStruct(shape, BF16), jax.ShapeDtypeStruct((SLOT * experts, tok_dev), BF16)],
+        in_specs=[pl.BlockSpec(memory_space=pltpu.SMEM), VMEM, VMEM, HBM],
+        out_specs=[VMEM, VMEM],
+        scratch_shapes=[
+            pltpu.VMEM(shape, F32),
+            pltpu.VMEM(tokens.shape, BF16),
+            pltpu.SemaphoreType.DMA((4,)),
+        ],
+        compiler_params=WIDE,
         name="send",
-    )(sel, tokens)
+    )(me[None], counts[:, None], chosen, tokens)
 
 
 def pack_kernel(tiles, column_ref, msg_ref, out_ref, held):
     rows = rows_of(tiles)
     devices = msg_ref.shape[0] // rows
-    cap = column_ref.shape[0]
+    cap = column_ref.shape[1]
+    column = jnp.broadcast_to(column_ref[...].astype(F32), (LANE, cap)).T[:, :1].astype(jnp.int32)
     held[...] = msg_ref[...].astype(F32)
     total = jnp.zeros(out_ref.shape, F32)
     for s in range(SLOT):
         flat = [held[pl.ds(t * SLOT + s, devices, stride=rows), :] for t in range(tiles)]
         flat = jnp.concatenate(flat, axis=1).astype(BF16)
         slot = lax.broadcasted_iota(jnp.int32, (cap, devices), 1) * SLOT + s
-        hot = (slot == column_ref[...]).astype(F32).astype(BF16)
+        hot = (slot == column).astype(F32).astype(BF16)
         total = total + jnp.dot(hot, flat, preferred_element_type=F32)
     out_ref[...] = total.astype(BF16)
 
@@ -76,7 +100,7 @@
 def pack(column, msg, tiles):
     return pl.pallas_call(
         functools.partial(pack_kernel, tiles),
-        out_shape=jax.ShapeDtypeStruct((column.shape[0], tiles * LANE), BF16),
+        out_shape=jax.ShapeDtypeStruct((column.shape[1], tiles * LANE), BF16),
         in_specs=[VMEM, VMEM],
         out_specs=VMEM,
         scratch_shapes=[pltpu.VMEM(msg.shape, F32)],
@@ -218,23 +242,10 @@
     at_x, at_core = lax.axis_index("x"), lax.axis_index("core")
     myself = expert * n_local + at_x * nc + at_core
 
-    place_at = jnp.arange(cap, dtype=jnp.int32)[None, :]
-    rest = (place_at < counts[:, None]) & (chosen // tok_dev == myself)
-    position = chosen % tok_dev
-    token = jnp.arange(tok_dev, dtype=jnp.int32)[None, :]
-    sel = []
-    for _ in range(SLOT):
-        first = jnp.min(jnp.where(rest, place_at, cap), axis=1)
-        hit = place_at == first[:, None]
-        token_slot = jnp.sum(jnp.where(hit, position, 0), axis=1)
-        sel.append((token == token_slot[:, None]) & (first < cap)[:, None])
-        rest = rest & ~hit
-    sel = jnp.concatenate(sel, axis=0).astype(BF16)
-
-    outgoing = send(sel, tokens, PARTS, devices)
-    arrived = exchange(outgoing[0], devices)
-
-    mat, gate_mat, up_mat, _ = lax.optimization_barrier((w_down[0], w_gate[0], w_up[0], outgoing[0]))
+    outgoing, sel = send(myself, counts, chosen, tokens, n_local)
+    arrived = exchange(outgoing, devices)
+
+    mat, gate_mat, up_mat, _ = lax.optimization_barrier((w_down[0], w_gate[0], w_up[0], outgoing))
     def block_to(dx, flip):
         to = (at_x + dx) % nx * nc + (at_core + flip) % nc
         return lax.dynamic_slice(mat, (0, to * cut), (mat.shape[0], cut))
@@ -261,7 +272,7 @@
     column = jnp.where(entry < count, column, -1)
 
     arrived, pieces, down_blocks = lax.optimization_barrier((arrived, pieces, down_blocks))
-    own = pack(column[:, None], arrived, *PARTS)
+    own = pack(column[None, :], arrived, cut // LANE)
     here, there = at_core * cut, (1 - at_core) * cut
     fore, aft = sent(own, 1, 0), sent(own, -1, 0)
     total = expand(None, [own, sent(own, 0, 1)], (0, 0), jnp.stack([here, there]), pieces[:1])

time: 167 us -> 167 us (level)
  other arithmetic: 8.76 us -> 5.71 us
  Pallas kernels: 13.9 us -> 16.5 us
  waiting for transfers between devices: 48.2 us -> 50 us
    unnamed x36 -> x22, local copies, waits for them, and re-layouts: 4.37 us -> 1.5 us
    pallas_call x1, Pallas kernels: 2.27 us -> 4.58 us  [send(): pl.pallas_call(functools.partial(send_kernel, n_local), out_shape=[jax.Sh...]
    ppermute x17, waiting for transfers between devices: 42.1 us -> 43.9 us  [sent(): return lax.ppermute(value, LOCAL, pairs)]
where the time goes in v9:
time: 167 us; the launch traced here: 166 us
  waiting for transfers between devices  50 us (30%)
  blocking collectives  49.7 us (30%)
  starting transfers between devices  36 us (22%)
  Pallas kernels  16.5 us (10%)
  local copies, waits for them, and re-layouts  7.99 us (5%)
  other arithmetic  5.71 us (3%)
    all_to_all x1, blocking collectives, exchange(): lax.all_to_all(parts, AXES, split_axis=0, concat_axis=0, tiled=True)  49.7 us
    ppermute x17, waiting for transfers between devices, sent(): return lax.ppermute(value, LOCAL, pairs)  43.9 us
    ppermute x17, starting transfers between devices, sent(): return lax.ppermute(value, LOCAL, pairs)  17.9 us
    all_to_all x1, starting transfers between devices, exchange(): lax.all_to_all(parts, AXES, split_axis=0, concat_axis=0, tiled=True)  15.7 us
    ppermute x1, waiting for transfers between devices, forwarded(): lax.ppermute(jnp.where(lax.axis_index('core') == 0, fore, aft), LOCAL, pa...  6.1 us
    pallas_call x1, Pallas kernels, send(): pl.pallas_call(functools.partial(send_kernel, n_local), out_shape=[jax.Sh...  4.58 us
    pallas_call x4, Pallas kernels, expand(): pl.pallas_call(functools.partial(expand_kernel, uses, opening, last), out...  4.27 us
  transfers between devices with their start and end apart: 19, of which 10 were waited for; matrix products, arithmetic and copies ran while one was open for 7% of the time, Pallas kernels for 2%

profile of v9, /device:TPU:1, one launch (start us, length us, event | category | flops | bytes accessed | tf_op | source)
XLA Modules:
  0.0 166.3 jit_solution(3667878022864720332)
XLA Ops:
  0.0 1.3 copy.11.counts_ref
  1.3 4.6 %send.1 = (bf16[5632,128]{1,0:T(8,128)(2,1)}, bf16[96,128]{1,0:T(8,128)(2,1)}) custom-call(s32[1]{0:T(128)} %bitcast.me_ref, s32[32,1]{1,0:T(8,128)} %copy.11.counts_ref, s32[32,384]{1,0:T(8,128)} %chosen_ref.1, bf16[128,7168]{1,0:T(8,128)(2,1)} %tok_ref.1), custom_call_target="tpu_custom_call" | custom-call | tf_op jit(solution)/shard_map/send/pallas_call | solution.py:69
  5.9 15.7 %all-to-all-start = ((bf16[256,11,2,128]{3,2,1,0:T(2,128)(2,1)}), bf16[256,11,2,128]{3,2,1,0:T(2,128)(2,1)S(1)}, u32[]{:S(2)}, u32[]{:S(2)}) async-start(bf16[256,11,2,128]{3,2,1,0:T(2,128)(2,1)} %bitcast.42), calls=%async_computation | async-start | bytes 2883584 | tf_op jit(solution)/shard_map/all_to_all | solution.py:212
  23.7 2.1 %collective-permute-start = (bf16[2,128,896]{2,1,0:T(8,128)(2,1)}, bf16[2,128,896]{2,1,0:T(8,128)(2,1)}, u32[]{:S(2)}, u32[]{:S(2)}) collective-permute-start(bf16[2,128,896]{2,1,0:T(8,128)(2,1)} %pad_maximum_fusion.4), channel_id=1, source_target_pairs={{0,1},{1,0},{2,3},{3,2},{4,5},{5,4},{6,7},{7,6},{8,9},{9,8},{10,11... | collective-permute-start | bytes 1376264 | tf_op jit(solution)/shard_map/ppermute | solution.py:221
  26.9 1.6 collective-permute-start.3
  28.5 2.0 %collective-permute-start.4 = (bf16[1,128,896]{2,1,0:T(8,128)(2,1)}, bf16[1,128,896]{2,1,0:T(8,128)(2,1)}, u32[]{:S(2)}, u32[]{:S(2)}) collective-permute-start(bf16[1,128,896]{2,1,0:T(8,128)(2,1)} %get-tuple-element.52), channel_id=1, source_target_pairs={{0,7},{1,6},{2,1},{3,0},{4,3},{5,2},{6,5},{7,4},{8,15},{9,14},{10,... | collective-permute-start | bytes 688136 | tf_op jit(solution)/shard_map/ppermute | solution.py:221
  31.3 2.3 %constant_dynamic-slice_fusion = (bf16[1792,128]{1,0:T(8,128)(2,1)S(1)}, bf16[1792,128]{1,0:T(8,128)(2,1)S(1)}, bf16[1792,128]{1,0:T(8,128)(2,1)S(1)}, bf16[1792...) fusion(bf16[7168,128]{1,0:T(8,128)(2,1)} %bitcast.40, ...), kind=kLoop, calls=%fused_computation.21 | loop fusion | bytes 7340048 | tf_op jit(solution)/shard_map/dynamic_slice | solution.py:263
  39.2 22.5 %collective-permute-done.2.refs_9_ = bf16[1,128,896]{2,1,0:T(8,128)(2,1)} collective-permute-done((bf16[1,128,896]{2,1,0:T(8,128)(2,1)}, bf16[1,128,896]{2,1,0:T(8,128)(2,1)}, u32[]{:S(2)}, u32[]{:S(2)}) %collective-permute-start.2) | collective-permute-done | bytes 229408 | tf_op jit(solution)/shard_map/ppermute | solution.py:221
  63.2 2.0 %pack.1.refs_0_ = bf16[384,896]{1,0:T(8,128)(2,1)} custom-call(s32[1,384]{1,0:T(1,128)S(1)} %copy-done.6, bf16[5632,128]{1,0:T(8,128)(2,1)S(1)} %bitcast.33), custom_call_target="tpu_custom_call" | custom-call | tf_op jit(solution)/shard_map/pack/pallas_call | solution.py:101
  65.6 1.6 collective-permute-start.6
  68.3 2.0 %expand.4.refs_6_ = f32[384,256]{1,0:T(8,128)S(1)} custom-call(s32[2]{0:T(128)S(1)} %pad_add_fusion.place_ref, bf16[384,896]{1,0:T(8,128)(2,1)} %pack.1.refs_0_, bf16[384,896]{1,0:T(8,128)(2,1)} %collective-permute-done.8.refs_1_, bf16[1792,256]{1,0:T(8,128)(2,1)S(1)} %pad_maximum_fusion.refs_2_), custom_call_target="tpu_custom_call" | custom-call | flops 352321536 | bytes 688128 | tf_op jit(solution)/shard_map/expand/pallas_call | solution.py:134
  70.4 13.5 %collective-permute-done.6.refs_0_ = bf16[384,896]{1,0:T(8,128)(2,1)S(1)} collective-permute-done((bf16[384,896]{1,0:T(8,128)(2,1)}, bf16[384,896]{1,0:T(8,128)(2,1)S(1)}, u32[]{:S(2)}, u32[]{:S(2)}) %collective-permute-start.6) | collective-permute-done | bytes 688160 | tf_op jit(solution)/shard_map/ppermute | solution.py:221
  85.3 2.4 %collective-permute-start.9 = (bf16[384,896]{1,0:T(8,128)(2,1)S(1)}, bf16[384,896]{1,0:T(8,128)(2,1)S(1)}, u32[]{:S(2)}, u32[]{:S(2)}) collective-permute-start(bf16[384,896]{1,0:T(8,128)(2,1)S(1)} %broadcast_select_fusion), channel_id=1, source_target_pairs={{0,2},{1,7},{2,4},{3,1},{4,6},{5,3},{6,0},{7,5},{8,10},{9,15},{10,... | collective-permute-start | bytes 2064392 | tf_op jit(solution)/shard_map/ppermute | solution.py:230
  88.0 1.5 expand.5.refs_2_
  89.5 6.1 %collective-permute-done.9.refs_0_ = bf16[384,896]{1,0:T(8,128)(2,1)S(1)} collective-permute-done((bf16[384,896]{1,0:T(8,128)(2,1)S(1)}, bf16[384,896]{1,0:T(8,128)(2,1)S(1)}, u32[]{:S(2)}, u32[]{:S(2)}) %collective-permute-start.9) | collective-permute-done | bytes 688160 | tf_op jit(solution)/shard_map/ppermute | solution.py:230
  95.6 2.4 %collective-permute-start.12 = (bf16[384,896]{1,0:T(8,128)(2,1)S(1)}, bf16[384,896]{1,0:T(8,128)(2,1)S(1)}, u32[]{:S(2)}, u32[]{:S(2)}) collective-permute-start(bf16[384,896]{1,0:T(8,128)(2,1)S(1)} %collective-permute-done.9.refs_0_), channel_id=1, source_target_pairs={{0,1},{1,0},{2,3},{3,2},{4,5},{5,4},{6,7},{7,6},{8,9},{9,8},{10,11... | collective-permute-start | bytes 2064392 | tf_op jit(solution)/shard_map/ppermute | solution.py:221
  98.4 1.4 collective-permute-done.12.refs_0_
  100.3 2.3 %collective-permute-start.14 = (bf16[384,128]{1,0:T(8,128)(2,1)S(1)}, bf16[384,128]{1,0:T(8,128)(2,1)S(1)}, u32[]{:S(2)}, u32[]{:S(2)}) collective-permute-start(bf16[384,128]{1,0:T(8,128)(2,1)S(1)} %expand.7.refs_0_), channel_id=1, source_target_pairs={{0,4},{1,5},{2,6},{3,7},{4,0},{5,1},{6,2},{7,3},{8,12},{9,13},{10,... | collective-permute-start | bytes 294920 | tf_op jit(solution)/shard_map/ppermute | solution.py:221
  102.9 2.9 %collective-permute-done.13.refs_1_ = bf16[384,128]{1,0:T(8,128)(2,1)S(1)} collective-permute-done((bf16[384,128]{1,0:T(8,128)(2,1)S(1)}, bf16[384,128]{1,0:T(8,128)(2,1)S(1)}, u32[]{:S(2)}, u32[]{:S(2)}) %collective-permute-start.13) | collective-permute-done | bytes 98336 | tf_op jit(solution)/shard_map/ppermute | solution.py:221
  105.8 1.4 collective-permute-done.14.refs_2_
  108.0 1.6 collective-permute-start.17
  110.9 3.2 %down.1 = bf16[5632,128]{1,0:T(8,128)(2,1)S(1)} custom-call(f32[384,1]{1,0:T(8,128)S(1)} %copy.12.weight_ref, s32[1,384]{1,0:T(1,128)S(1)} %copy-done.7, bf16[384,128]{1,0:T(8,128)(2,1)S(1)} %expand.7.refs_0_, bf16[384,128]{1,0:T(8,128)(2,1)S(1)} %collective-permute-done.13.refs_1_, bf16[384,128]{1,0:T(8,128)(2,1)S(1)} %collective-permute-done.14.refs_2_, ...), custom_call_target="tpu_custom_call" | custom-call | tf_op jit(solution)/shard_map/down/pallas_call | solution.py:172
  114.1 49.7 %all_to_all.10 = bf16[256,11,2,128]{3,2,1,0:T(2,128)(2,1)S(1)} all-to-all(bf16[256,11,2,128]{3,2,1,0:T(2,128)(2,1)S(1)} %bitcast.35), channel_id=1, replica_groups=mesh['node'=32,'x'=4,'core'=2] {'node','x','core'}, dimensions={0} | all-to-all | bytes 2883584 | tf_op jit(solution)/shard_map/all_to_all | solution.py:212
  163.8 2.4 %place.1 = bf16[128,7168]{1,0:T(8,128)(2,1)} custom-call(bf16[96,128]{1,0:T(8,128)(2,1)S(1)} %copy-done.5, bf16[5632,128]{1,0:T(8,128)(2,1)S(1)} %bitcast.34), custom_call_target="tpu_custom_call" | custom-call | tf_op jit(solution)/shard_map/place/pallas_call | solution.py:199
  (66 shorter events, 17.4 us)
Async XLA Ops:
  0.0 109.6 %copy-start = (f32[32,384]{1,0:T(8,128)S(1)}, f32[32,384]{1,0:T(8,128)}, u32[]{:S(2)}) copy-start(f32[32,384]{1,0:T(8,128)} %param.13) | copy-start | bytes 147460
  5.9 15.8 %copy-start.8 = (bf16[1,128,7168]{2,1,0:T(8,128)(2,1)S(1)}, bf16[1,128,7168]{2,1,0:T(8,128)(2,1)}, u32[]{:S(2)}) copy-start(bf16[1,128,7168]{2,1,0:T(8,128)(2,1)} %param.10) | copy-start | bytes 5505028
  5.9 56.6 %all-to-all-start = ((bf16[256,11,2,128]{3,2,1,0:T(2,128)(2,1)}), bf16[256,11,2,128]{3,2,1,0:T(2,128)(2,1)S(1)}, u32[]{:S(2)}, u32[]{:S(2)}) async-start(bf16[256,11,2,128]{3,2,1,0:T(2,128)(2,1)} %bitcast.42), calls=%async_computation | async-start | bytes 2883584 | tf_op jit(solution)/shard_map/all_to_all | solution.py:212
  23.7 12.2 %collective-permute-start = (bf16[2,128,896]{2,1,0:T(8,128)(2,1)}, bf16[2,128,896]{2,1,0:T(8,128)(2,1)}, u32[]{:S(2)}, u32[]{:S(2)}) collective-permute-start(bf16[2,128,896]{2,1,0:T(8,128)(2,1)} %pad_maximum_fusion.4), channel_id=1, source_target_pairs={{0,1},{1,0},{2,3},{3,2},{4,5},{5,4},{6,7},{7,6},{8,9},{9,8},{10,11... | collective-permute-start | bytes 1376264 | tf_op jit(solution)/shard_map/ppermute | solution.py:221
  25.8 13.4 %collective-permute-start.1 = (bf16[1,128,896]{2,1,0:T(8,128)(2,1)}, bf16[1,128,896]{2,1,0:T(8,128)(2,1)}, u32[]{:S(2)}, u32[]{:S(2)}) collective-permute-start(bf16[1,128,896]{2,1,0:T(8,128)(2,1)} %get-tuple-element.55), channel_id=1, source_target_pairs={{0,2},{1,3},{2,4},{3,5},{4,6},{5,7},{6,0},{7,1},{8,10},{9,11},{10,... | collective-permute-start | bytes 688136 | tf_op jit(solution)/shard_map/ppermute | solution.py:221
  25.8 35.9 %collective-permute-start.2 = (bf16[1,128,896]{2,1,0:T(8,128)(2,1)}, bf16[1,128,896]{2,1,0:T(8,128)(2,1)}, u32[]{:S(2)}, u32[]{:S(2)}) collective-permute-start(bf16[1,128,896]{2,1,0:T(8,128)(2,1)} %get-tuple-element.54), channel_id=1, source_target_pairs={{0,3},{1,2},{2,5},{3,4},{4,7},{5,6},{6,1},{7,0},{8,11},{9,10},{10,... | collective-permute-start | bytes 688136 | tf_op jit(solution)/shard_map/ppermute | solution.py:221
  26.9 34.8 %collective-permute-start.3 = (bf16[1,128,896]{2,1,0:T(8,128)(2,1)}, bf16[1,128,896]{2,1,0:T(8,128)(2,1)}, u32[]{:S(2)}, u32[]{:S(2)}) collective-permute-start(bf16[1,128,896]{2,1,0:T(8,128)(2,1)} %get-tuple-element.53), channel_id=1, source_target_pairs={{0,6},{1,7},{2,0},{3,1},{4,2},{5,3},{6,4},{7,5},{8,14},{9,15},{10,... | collective-permute-start | bytes 688136 | tf_op jit(solution)/shard_map/ppermute | solution.py:221
  28.5 33.2 %collective-permute-start.4 = (bf16[1,128,896]{2,1,0:T(8,128)(2,1)}, bf16[1,128,896]{2,1,0:T(8,128)(2,1)}, u32[]{:S(2)}, u32[]{:S(2)}) collective-permute-start(bf16[1,128,896]{2,1,0:T(8,128)(2,1)} %get-tuple-element.52), channel_id=1, source_target_pairs={{0,7},{1,6},{2,1},{3,0},{4,3},{5,2},{6,5},{7,4},{8,15},{9,14},{10,... | collective-permute-start | bytes 688136 | tf_op jit(solution)/shard_map/ppermute | solution.py:221
  36.9 24.8 %collective-permute-start.5 = (bf16[2,128,896]{2,1,0:T(8,128)(2,1)S(1)}, bf16[2,128,896]{2,1,0:T(8,128)(2,1)S(1)}, u32[]{:S(2)}, u32[]{:S(2)}) collective-permute-start(bf16[2,128,896]{2,1,0:T(8,128)(2,1)S(1)} %pad_maximum_fusion.5), channel_id=1, source_target_pairs={{0,4},{1,5},{2,6},{3,7},{4,0},{5,1},{6,2},{7,3},{8,12},{9,13},{10,... | collective-permute-start | bytes 1376264 | tf_op jit(solution)/shard_map/ppermute | solution.py:221
  65.2 3.1 %collective-permute-start.8 = (bf16[384,896]{1,0:T(8,128)(2,1)}, bf16[384,896]{1,0:T(8,128)(2,1)}, u32[]{:S(2)}, u32[]{:S(2)}) collective-permute-start(bf16[384,896]{1,0:T(8,128)(2,1)} %pack.1.refs_0_), channel_id=1, source_target_pairs={{0,1},{1,0},{2,3},{3,2},{4,5},{5,4},{6,7},{7,6},{8,9},{9,8},{10,11... | collective-permute-start | bytes 2064392 | tf_op jit(solution)/shard_map/ppermute | solution.py:221
  65.6 18.3 %collective-permute-start.6 = (bf16[384,896]{1,0:T(8,128)(2,1)}, bf16[384,896]{1,0:T(8,128)(2,1)S(1)}, u32[]{:S(2)}, u32[]{:S(2)}) collective-permute-start(bf16[384,896]{1,0:T(8,128)(2,1)} %pack.1.refs_0_), channel_id=1, source_target_pairs={{0,2},{1,3},{2,4},{3,5},{4,6},{5,7},{6,0},{7,1},{8,10},{9,11},{10,... | collective-permute-start | bytes 2064392 | tf_op jit(solution)/shard_map/ppermute | solution.py:221
  67.1 17.0 %collective-permute-start.7 = (bf16[384,896]{1,0:T(8,128)(2,1)}, bf16[384,896]{1,0:T(8,128)(2,1)S(1)}, u32[]{:S(2)}, u32[]{:S(2)}) collective-permute-start(bf16[384,896]{1,0:T(8,128)(2,1)} %pack.1.refs_0_), channel_id=1, source_target_pairs={{0,6},{1,7},{2,0},{3,1},{4,2},{5,3},{6,4},{7,5},{8,14},{9,15},{10,... | collective-permute-start | bytes 2064392 | tf_op jit(solution)/shard_map/ppermute | solution.py:221
  68.3 19.6 %copy-start.1 = (bf16[1792,256]{1,0:T(8,128)(2,1)S(1)}, bf16[1792,256]{1,0:T(8,128)(2,1)}, u32[]{:S(2)}) copy-start(bf16[1792,256]{1,0:T(8,128)(2,1)} %pad_maximum_fusion.3.refs_5_) | copy-start | bytes 2752516
  68.3 19.6 %copy-start.2 = (bf16[1792,256]{1,0:T(8,128)(2,1)S(1)}, bf16[1792,256]{1,0:T(8,128)(2,1)}, u32[]{:S(2)}) copy-start(bf16[1792,256]{1,0:T(8,128)(2,1)} %pad_maximum_fusion.1.refs_4_) | copy-start | bytes 2752516
  84.1 3.7 %collective-permute-start.10 = (bf16[384,896]{1,0:T(8,128)(2,1)S(1)}, bf16[384,896]{1,0:T(8,128)(2,1)S(1)}, u32[]{:S(2)}, u32[]{:S(2)}) collective-permute-start(bf16[384,896]{1,0:T(8,128)(2,1)S(1)} %collective-permute-done.6.refs_0_), channel_id=1, source_target_pairs={{0,1},{1,0},{2,3},{3,2},{4,5},{5,4},{6,7},{7,6},{8,9},{9,8},{10,11... | collective-permute-start | bytes 2064392 | tf_op jit(solution)/shard_map/ppermute | solution.py:221
  85.2 2.8 %collective-permute-start.11 = (bf16[384,896]{1,0:T(8,128)(2,1)S(1)}, bf16[384,896]{1,0:T(8,128)(2,1)S(1)}, u32[]{:S(2)}, u32[]{:S(2)}) collective-permute-start(bf16[384,896]{1,0:T(8,128)(2,1)S(1)} %collective-permute-done.7.refs_2_), channel_id=1, source_target_pairs={{0,1},{1,0},{2,3},{3,2},{4,5},{5,4},{6,7},{7,6},{8,9},{9,8},{10,11... | collective-permute-start | bytes 2064392 | tf_op jit(solution)/shard_map/ppermute | solution.py:221
  85.3 10.3 %collective-permute-start.9 = (bf16[384,896]{1,0:T(8,128)(2,1)S(1)}, bf16[384,896]{1,0:T(8,128)(2,1)S(1)}, u32[]{:S(2)}, u32[]{:S(2)}) collective-permute-start(bf16[384,896]{1,0:T(8,128)(2,1)S(1)} %broadcast_select_fusion), channel_id=1, source_target_pairs={{0,2},{1,7},{2,4},{3,1},{4,6},{5,3},{6,0},{7,5},{8,10},{9,15},{10,... | collective-permute-start | bytes 2064392 | tf_op jit(solution)/shard_map/ppermute | solution.py:230
  95.6 4.2 %collective-permute-start.12 = (bf16[384,896]{1,0:T(8,128)(2,1)S(1)}, bf16[384,896]{1,0:T(8,128)(2,1)S(1)}, u32[]{:S(2)}, u32[]{:S(2)}) collective-permute-start(bf16[384,896]{1,0:T(8,128)(2,1)S(1)} %collective-permute-done.9.refs_0_), channel_id=1, source_target_pairs={{0,1},{1,0},{2,3},{3,2},{4,5},{5,4},{6,7},{7,6},{8,9},{9,8},{10,11... | collective-permute-start | bytes 2064392 | tf_op jit(solution)/shard_map/ppermute | solution.py:221
  100.2 5.7 %collective-permute-start.13 = (bf16[384,128]{1,0:T(8,128)(2,1)S(1)}, bf16[384,128]{1,0:T(8,128)(2,1)S(1)}, u32[]{:S(2)}, u32[]{:S(2)}) collective-permute-start(bf16[384,128]{1,0:T(8,128)(2,1)S(1)} %expand.7.refs_0_), channel_id=1, source_target_pairs={{0,2},{1,3},{2,4},{3,5},{4,6},{5,7},{6,0},{7,1},{8,10},{9,11},{10,... | collective-permute-start | bytes 294920 | tf_op jit(solution)/shard_map/ppermute | solution.py:221
  100.3 6.9 %collective-permute-start.14 = (bf16[384,128]{1,0:T(8,128)(2,1)S(1)}, bf16[384,128]{1,0:T(8,128)(2,1)S(1)}, u32[]{:S(2)}, u32[]{:S(2)}) collective-permute-start(bf16[384,128]{1,0:T(8,128)(2,1)S(1)} %expand.7.refs_0_), channel_id=1, source_target_pairs={{0,4},{1,5},{2,6},{3,7},{4,0},{5,1},{6,2},{7,3},{8,12},{9,13},{10,... | collective-permute-start | bytes 294920 | tf_op jit(solution)/shard_map/ppermute | solution.py:221
  102.6 5.4 %collective-permute-start.15 = (bf16[384,128]{1,0:T(8,128)(2,1)S(1)}, bf16[384,128]{1,0:T(8,128)(2,1)S(1)}, u32[]{:S(2)}, u32[]{:S(2)}) collective-permute-start(bf16[384,128]{1,0:T(8,128)(2,1)S(1)} %expand.7.refs_0_), channel_id=1, source_target_pairs={{0,6},{1,7},{2,0},{3,1},{4,2},{5,3},{6,4},{7,5},{8,14},{9,15},{10,... | collective-permute-start | bytes 294920 | tf_op jit(solution)/shard_map/ppermute | solution.py:221
  108.0 2.9 %collective-permute-start.17 = (bf16[3,384,128]{2,1,0:T(8,128)(2,1)S(1)}, bf16[3,384,128]{2,1,0:T(8,128)(2,1)S(1)}, u32[]{:S(2)}, u32[]{:S(2)}) collective-permute-start(bf16[3,384,128]{2,1,0:T(8,128)(2,1)S(1)} %pad_maximum_fusion.6), channel_id=1, source_target_pairs={{0,1},{1,0},{2,3},{3,2},{4,5},{5,4},{6,7},{7,6},{8,9},{9,8},{10,11... | collective-permute-start | bytes 884744 | tf_op jit(solution)/shard_map/ppermute | solution.py:221
  109.5 1.3 collective-permute-start.16
  114.1 49.7 %copy-start.5 = (bf16[96,128]{1,0:T(8,128)(2,1)S(1)}, bf16[96,128]{1,0:T(8,128)(2,1)}, u32[]{:S(2)}) copy-start(bf16[96,128]{1,0:T(8,128)(2,1)} %get-tuple-element.27.sel_ref) | copy-start | bytes 73732
  (6 other events, 30.1 us)

commit v10 on v9

--- a/solution.py
+++ b/solution.py
@@ -37,7 +37,10 @@
     place_at = lax.broadcasted_iota(jnp.int32, (experts, cap), 1)
     token = lax.broadcasted_iota(jnp.int32, (experts, tok_dev), 1)
     position = chosen_ref[...] - me_ref[0] * tok_dev
-    rest = (place_at < counts_ref[...]) & (position >= 0) & (position < tok_dev)
+    square = (experts, experts)
+    same = lax.broadcasted_iota(jnp.int32, square, 0) == lax.broadcasted_iota(jnp.int32, square, 1)
+    counts = jnp.sum(jnp.where(same, jnp.broadcast_to(counts_ref[...], square), 0), axis=1, keepdims=True)
+    rest = (place_at < counts) & (position >= 0) & (position < tok_dev)
     for s in range(SLOT):
         first = jnp.min(jnp.where(rest, place_at, cap), axis=1, keepdims=True)
         hit = place_at == first
@@ -78,7 +81,7 @@
         ],
         compiler_params=WIDE,
         name="send",
-    )(me[None], counts[:, None], chosen, tokens)
+    )(me[None], counts[None, :], chosen, tokens)
 
 
 def pack_kernel(tiles, column_ref, msg_ref, out_ref, held):
@@ -252,9 +255,10 @@
 
     across = sent(jnp.stack([block_to(0, 1), block_to(2, 1)]), 0, 1)
     near_blocks = [sent(block_to(dx, flip)[None], dx, flip) for dx in (1, 3) for flip in range(nc)]
-    far_blocks = sent(jnp.stack([block_to(2, 0), across[1]]), 2, 0)
-    down_blocks = [block_to(0, 0)[None], across, *near_blocks, far_blocks]
-    order = ((0, 0), (2, 0), (6, 0), (4, 0), (1, 0), (3, 0), (6, 1), (5, 0))
+    far_block = sent(across[1:], 2, 0)
+    down_blocks = [block_to(0, 0)[None], across, *near_blocks, far_block]
+    last_block = block_to(2, 0)[None]
+    order = ((0, 0), (2, 0), (7, 0), (4, 0), (1, 0), (3, 0), (6, 0), (5, 0))
 
     pieces = []
     for dx in range(nx):
@@ -286,6 +290,8 @@
     hidden = expand(total, [sent(far, 0, 1)], (0,), jnp.stack([there]), pieces[2:3], last=True)
 
     near = [sent(hidden, dx, 0) for dx in range(1, nx)]
+    near, last_block = lax.optimization_barrier((near, sent(last_block, 2, 0)))
+    down_blocks.append(last_block)
     other = sent(hidden, 0, 1)
     others = sent(jnp.stack(near), 0, 1)
     groups = [hidden, *near, other, others]

time: 167 us -> 162 us (0.970)
  blocking collectives: 49.7 us -> 45.4 us
  starting transfers between devices: 36 us -> 38.1 us
    ppermute x17 -> x18, waiting for transfers between devices: 43.9 us -> 39.4 us  [sent(): return lax.ppermute(value, LOCAL, pairs)]
    all_to_all x1, blocking collectives: 49.7 us -> 45.4 us  [exchange(): lax.all_to_all(parts, AXES, split_axis=0, concat_axis=0, tiled=True)]
    all_to_all x1, waiting for transfers between devices: 0.01 us -> 3.61 us  [exchange(): lax.all_to_all(parts, AXES, split_axis=0, concat_axis=0, tiled=True)]
    ppermute x17 -> x18, starting transfers between devices: 17.9 us -> 19.7 us  [sent(): return lax.ppermute(value, LOCAL, pairs)]
  transfers between devices with their start and end apart: 19 -> 20, of which waited for: 10 -> 9; matrix products, arithmetic and copies ran while one was open for 7% -> 7% of each run, Pallas kernels for 2% -> 3%
where the time goes in v10:
time: 162 us
  waiting for transfers between devices  49.3 us (30%)
  blocking collectives  45.4 us (28%)
  starting transfers between devices  38.1 us (24%)
  Pallas kernels  16.5 us (10%)
  local copies, waits for them, and re-layouts  6.48 us (4%)
  other arithmetic  5.56 us (3%)
    all_to_all x1, blocking collectives, exchange(): lax.all_to_all(parts, AXES, split_axis=0, concat_axis=0, tiled=True)  45.4 us
    ppermute x18, waiting for transfers between devices, sent(): return lax.ppermute(value, LOCAL, pairs)  39.4 us
    ppermute x18, starting transfers between devices, sent(): return lax.ppermute(value, LOCAL, pairs)  19.7 us
    all_to_all x1, starting transfers between devices, exchange(): lax.all_to_all(parts, AXES, split_axis=0, concat_axis=0, tiled=True)  15.7 us
    ppermute x1, waiting for transfers between devices, forwarded(): lax.ppermute(jnp.where(lax.axis_index('core') == 0, fore, aft), LOCAL, pa...  6.26 us
    pallas_call x1, Pallas kernels, send(): pl.pallas_call(functools.partial(send_kernel, n_local), out_shape=[jax.Sh...  4.59 us
    pallas_call x4, Pallas kernels, expand(): pl.pallas_call(functools.partial(expand_kernel, uses, opening, last), out...  4.28 us
    all_to_all x1, waiting for transfers between devices, exchange(): lax.all_to_all(parts, AXES, split_axis=0, concat_axis=0, tiled=True)  3.61 us
  transfers between devices with their start and end apart: 20, of which 9 were waited for; matrix products, arithmetic and copies ran while one was open for 7% of the time, Pallas kernels for 3%

profile of v10, /device:TPU:1, one launch (start us, length us, event | category | flops | bytes accessed | tf_op | source)
XLA Modules:
  0.0 161.6 jit_solution(15618917941741843214)
XLA Ops:
  0.0 4.6 %send.1 = (bf16[5632,128]{1,0:T(8,128)(2,1)}, bf16[96,128]{1,0:T(8,128)(2,1)}) custom-call(s32[1]{0:T(128)} %bitcast.me_ref, s32[1,32]{1,0:T(1,128)} %bitcast.43, s32[32,384]{1,0:T(8,128)} %chosen_ref.1, bf16[128,7168]{1,0:T(8,128)(2,1)} %tok_ref.1), custom_call_target="tpu_custom_call" | custom-call | tf_op jit(solution)/shard_map/send/pallas_call | solution.py:72
  4.6 15.7 %all-to-all-start = ((bf16[256,11,2,128]{3,2,1,0:T(2,128)(2,1)}), bf16[256,11,2,128]{3,2,1,0:T(2,128)(2,1)S(1)}, u32[]{:S(2)}, u32[]{:S(2)}) async-start(bf16[256,11,2,128]{3,2,1,0:T(2,128)(2,1)} %bitcast.42), calls=%async_computation | async-start | bytes 2883584 | tf_op jit(solution)/shard_map/all_to_all | solution.py:215
  22.3 2.1 %collective-permute-start = (bf16[2,128,896]{2,1,0:T(8,128)(2,1)}, bf16[2,128,896]{2,1,0:T(8,128)(2,1)}, u32[]{:S(2)}, u32[]{:S(2)}) collective-permute-start(bf16[2,128,896]{2,1,0:T(8,128)(2,1)} %pad_maximum_fusion.4), channel_id=1, source_target_pairs={{0,1},{1,0},{2,3},{3,2},{4,5},{5,4},{6,7},{7,6},{8,9},{9,8},{10,11... | collective-permute-start | bytes 1376264 | tf_op jit(solution)/shard_map/ppermute | solution.py:224
  25.6 1.6 collective-permute-start.3
  27.1 2.0 %collective-permute-start.4 = (bf16[1,128,896]{2,1,0:T(8,128)(2,1)}, bf16[1,128,896]{2,1,0:T(8,128)(2,1)}, u32[]{:S(2)}, u32[]{:S(2)}) collective-permute-start(bf16[1,128,896]{2,1,0:T(8,128)(2,1)} %get-tuple-element.60), channel_id=1, source_target_pairs={{0,7},{1,6},{2,1},{3,0},{4,3},{5,2},{6,5},{7,4},{8,15},{9,14},{10,... | collective-permute-start | bytes 688136 | tf_op jit(solution)/shard_map/ppermute | solution.py:224
  29.9 2.3 %constant_dynamic-slice_fusion = (bf16[1792,128]{1,0:T(8,128)(2,1)S(1)}, bf16[1792,128]{1,0:T(8,128)(2,1)S(1)}, bf16[1792,128]{1,0:T(8,128)(2,1)S(1)}, bf16[1792...) fusion(bf16[7168,128]{1,0:T(8,128)(2,1)} %bitcast.40, ...), kind=kLoop, calls=%fused_computation.20 | loop fusion | bytes 7340048 | tf_op jit(solution)/shard_map/dynamic_slice | solution.py:267
  37.7 17.2 %collective-permute-done.2.refs_9_ = bf16[1,128,896]{2,1,0:T(8,128)(2,1)} collective-permute-done((bf16[1,128,896]{2,1,0:T(8,128)(2,1)}, bf16[1,128,896]{2,1,0:T(8,128)(2,1)}, u32[]{:S(2)}, u32[]{:S(2)}) %collective-permute-start.2) | collective-permute-done | bytes 229408 | tf_op jit(solution)/shard_map/ppermute | solution.py:224
  55.6 3.6 %all-to-all-done = bf16[256,11,2,128]{3,2,1,0:T(2,128)(2,1)S(1)} async-done(((bf16[256,11,2,128]{3,2,1,0:T(2,128)(2,1)}), bf16[256,11,2,128]{3,2,1,0:T(2,128)(2,1)S(1)}, u32[]{:S(2)}, u32[]{:S(2)}) %all-to-all-start) | async-done | bytes 1441824 | tf_op jit(solution)/shard_map/all_to_all | solution.py:215
  59.8 2.0 %pack.1.refs_0_ = bf16[384,896]{1,0:T(8,128)(2,1)} custom-call(s32[1,384]{1,0:T(1,128)S(1)} %copy-done.6, bf16[5632,128]{1,0:T(8,128)(2,1)S(1)} %bitcast.33), custom_call_target="tpu_custom_call" | custom-call | tf_op jit(solution)/shard_map/pack/pallas_call | solution.py:104
  61.8 1.4 collective-permute-start.8
  63.5 2.4 %collective-permute-start.7 = (bf16[384,896]{1,0:T(8,128)(2,1)}, bf16[384,896]{1,0:T(8,128)(2,1)S(1)}, u32[]{:S(2)}, u32[]{:S(2)}) collective-permute-start(bf16[384,896]{1,0:T(8,128)(2,1)} %pack.1.refs_0_), channel_id=1, source_target_pairs={{0,6},{1,7},{2,0},{3,1},{4,2},{5,3},{6,4},{7,5},{8,14},{9,15},{10,... | collective-permute-start | bytes 2064392 | tf_op jit(solution)/shard_map/ppermute | solution.py:224
  66.0 2.0 %expand.4.refs_6_ = f32[384,256]{1,0:T(8,128)S(1)} custom-call(s32[2]{0:T(128)S(1)} %pad_add_fusion.place_ref, bf16[384,896]{1,0:T(8,128)(2,1)} %pack.1.refs_0_, bf16[384,896]{1,0:T(8,128)(2,1)} %collective-permute-done.8.refs_1_, bf16[1792,256]{1,0:T(8,128)(2,1)S(1)} %pad_maximum_fusion.refs_2_), custom_call_target="tpu_custom_call" | custom-call | flops 352321536 | bytes 688128 | tf_op jit(solution)/shard_map/expand/pallas_call | solution.py:137
  68.0 13.7 %collective-permute-done.6.refs_0_ = bf16[384,896]{1,0:T(8,128)(2,1)S(1)} collective-permute-done((bf16[384,896]{1,0:T(8,128)(2,1)}, bf16[384,896]{1,0:T(8,128)(2,1)S(1)}, u32[]{:S(2)}, u32[]{:S(2)}) %collective-permute-start.6) | collective-permute-done | bytes 688160 | tf_op jit(solution)/shard_map/ppermute | solution.py:224
  82.6 2.8 %collective-permute-start.9 = (bf16[384,896]{1,0:T(8,128)(2,1)S(1)}, bf16[384,896]{1,0:T(8,128)(2,1)S(1)}, u32[]{:S(2)}, u32[]{:S(2)}) collective-permute-start(bf16[384,896]{1,0:T(8,128)(2,1)S(1)} %broadcast_select_fusion), channel_id=1, source_target_pairs={{0,2},{1,7},{2,4},{3,1},{4,6},{5,3},{6,0},{7,5},{8,10},{9,15},{10,... | collective-permute-start | bytes 2064392 | tf_op jit(solution)/shard_map/ppermute | solution.py:233
  85.4 1.5 expand.5.refs_2_
  86.9 6.3 %collective-permute-done.9.refs_0_ = bf16[384,896]{1,0:T(8,128)(2,1)S(1)} collective-permute-done((bf16[384,896]{1,0:T(8,128)(2,1)S(1)}, bf16[384,896]{1,0:T(8,128)(2,1)S(1)}, u32[]{:S(2)}, u32[]{:S(2)}) %collective-permute-start.9) | collective-permute-done | bytes 688160 | tf_op jit(solution)/shard_map/ppermute | solution.py:233
  93.2 2.1 %collective-permute-start.12 = (bf16[384,896]{1,0:T(8,128)(2,1)S(1)}, bf16[384,896]{1,0:T(8,128)(2,1)S(1)}, u32[]{:S(2)}, u32[]{:S(2)}) collective-permute-start(bf16[384,896]{1,0:T(8,128)(2,1)S(1)} %collective-permute-done.9.refs_0_), channel_id=1, source_target_pairs={{0,1},{1,0},{2,3},{3,2},{4,5},{5,4},{6,7},{7,6},{8,9},{9,8},{10,11... | collective-permute-start | bytes 2064392 | tf_op jit(solution)/shard_map/ppermute | solution.py:224
  98.2 2.0 %collective-permute-start.14 = (bf16[384,128]{1,0:T(8,128)(2,1)S(1)}, bf16[384,128]{1,0:T(8,128)(2,1)S(1)}, u32[]{:S(2)}, u32[]{:S(2)}) collective-permute-start(bf16[384,128]{1,0:T(8,128)(2,1)S(1)} %expand.7.refs_0_), channel_id=1, source_target_pairs={{0,4},{1,5},{2,6},{3,7},{4,0},{5,1},{6,2},{7,3},{8,12},{9,13},{10,... | collective-permute-start | bytes 294920 | tf_op jit(solution)/shard_map/ppermute | solution.py:224
  101.2 2.9 %collective-permute-done.16.refs_13_ = bf16[1,128,896]{2,1,0:T(8,128)(2,1)S(1)} collective-permute-done((bf16[1,128,896]{2,1,0:T(8,128)(2,1)S(1)}, bf16[1,128,896]{2,1,0:T(8,128)(2,1)S(1)}, u32[]{:S(2)}, u32[]{:S(2)}) %collective-permute-start.16) | collective-permute-done | bytes 229408 | tf_op jit(solution)/shard_map/ppermute | solution.py:224
  104.1 2.6 %collective-permute-done.13.refs_1_ = bf16[384,128]{1,0:T(8,128)(2,1)S(1)} collective-permute-done((bf16[384,128]{1,0:T(8,128)(2,1)S(1)}, bf16[384,128]{1,0:T(8,128)(2,1)S(1)}, u32[]{:S(2)}, u32[]{:S(2)}) %collective-permute-start.13) | collective-permute-done | bytes 98336 | tf_op jit(solution)/shard_map/ppermute | solution.py:224
  106.7 1.6 collective-permute-done.14.refs_2_
  110.6 3.2 %down.1 = bf16[5632,128]{1,0:T(8,128)(2,1)S(1)} custom-call(f32[384,1]{1,0:T(8,128)S(1)} %copy.9.weight_ref, s32[1,384]{1,0:T(1,128)S(1)} %copy-done.7, bf16[384,128]{1,0:T(8,128)(2,1)S(1)} %expand.7.refs_0_, bf16[384,128]{1,0:T(8,128)(2,1)S(1)} %collective-permute-done.13.refs_1_, bf16[384,128]{1,0:T(8,128)(2,1)S(1)} %collective-permute-done.14.refs_2_, ...), custom_call_target="tpu_custom_call" | custom-call | tf_op jit(solution)/shard_map/down/pallas_call | solution.py:175
  113.8 45.4 %all_to_all.10 = bf16[256,11,2,128]{3,2,1,0:T(2,128)(2,1)S(1)} all-to-all(bf16[256,11,2,128]{3,2,1,0:T(2,128)(2,1)S(1)} %bitcast.35), channel_id=1, replica_groups=mesh['node'=32,'x'=4,'core'=2] {'node','x','core'}, dimensions={0} | all-to-all | bytes 2883584 | tf_op jit(solution)/shard_map/all_to_all | solution.py:215
  159.2 2.4 %place.1 = bf16[128,7168]{1,0:T(8,128)(2,1)} custom-call(bf16[96,128]{1,0:T(8,128)(2,1)S(1)} %copy-done.5, bf16[5632,128]{1,0:T(8,128)(2,1)S(1)} %bitcast.34), custom_call_target="tpu_custom_call" | custom-call | tf_op jit(solution)/shard_map/place/pallas_call | solution.py:202
  (66 shorter events, 18.1 us)
Async XLA Ops:
  0.0 109.3 %copy-start = (f32[32,384]{1,0:T(8,128)S(1)}, f32[32,384]{1,0:T(8,128)}, u32[]{:S(2)}) copy-start(f32[32,384]{1,0:T(8,128)} %param.13) | copy-start | bytes 147460
  4.6 54.6 %all-to-all-start = ((bf16[256,11,2,128]{3,2,1,0:T(2,128)(2,1)}), bf16[256,11,2,128]{3,2,1,0:T(2,128)(2,1)S(1)}, u32[]{:S(2)}, u32[]{:S(2)}) async-start(bf16[256,11,2,128]{3,2,1,0:T(2,128)(2,1)} %bitcast.42), calls=%async_computation | async-start | bytes 2883584 | tf_op jit(solution)/shard_map/all_to_all | solution.py:215
  22.3 12.2 %collective-permute-start = (bf16[2,128,896]{2,1,0:T(8,128)(2,1)}, bf16[2,128,896]{2,1,0:T(8,128)(2,1)}, u32[]{:S(2)}, u32[]{:S(2)}) collective-permute-start(bf16[2,128,896]{2,1,0:T(8,128)(2,1)} %pad_maximum_fusion.4), channel_id=1, source_target_pairs={{0,1},{1,0},{2,3},{3,2},{4,5},{5,4},{6,7},{7,6},{8,9},{9,8},{10,11... | collective-permute-start | bytes 1376264 | tf_op jit(solution)/shard_map/ppermute | solution.py:224
  24.4 13.2 %collective-permute-start.1 = (bf16[1,128,896]{2,1,0:T(8,128)(2,1)}, bf16[1,128,896]{2,1,0:T(8,128)(2,1)}, u32[]{:S(2)}, u32[]{:S(2)}) collective-permute-start(bf16[1,128,896]{2,1,0:T(8,128)(2,1)} %get-tuple-element.63), channel_id=1, source_target_pairs={{0,2},{1,3},{2,4},{3,5},{4,6},{5,7},{6,0},{7,1},{8,10},{9,11},{10,... | collective-permute-start | bytes 688136 | tf_op jit(solution)/shard_map/ppermute | solution.py:224
  24.5 30.4 %collective-permute-start.2 = (bf16[1,128,896]{2,1,0:T(8,128)(2,1)}, bf16[1,128,896]{2,1,0:T(8,128)(2,1)}, u32[]{:S(2)}, u32[]{:S(2)}) collective-permute-start(bf16[1,128,896]{2,1,0:T(8,128)(2,1)} %get-tuple-element.62), channel_id=1, source_target_pairs={{0,3},{1,2},{2,5},{3,4},{4,7},{5,6},{6,1},{7,0},{8,11},{9,10},{10,... | collective-permute-start | bytes 688136 | tf_op jit(solution)/shard_map/ppermute | solution.py:224
  25.6 29.3 %collective-permute-start.3 = (bf16[1,128,896]{2,1,0:T(8,128)(2,1)}, bf16[1,128,896]{2,1,0:T(8,128)(2,1)}, u32[]{:S(2)}, u32[]{:S(2)}) collective-permute-start(bf16[1,128,896]{2,1,0:T(8,128)(2,1)} %get-tuple-element.61), channel_id=1, source_target_pairs={{0,6},{1,7},{2,0},{3,1},{4,2},{5,3},{6,4},{7,5},{8,14},{9,15},{10,... | collective-permute-start | bytes 688136 | tf_op jit(solution)/shard_map/ppermute | solution.py:224
  27.1 27.7 %collective-permute-start.4 = (bf16[1,128,896]{2,1,0:T(8,128)(2,1)}, bf16[1,128,896]{2,1,0:T(8,128)(2,1)}, u32[]{:S(2)}, u32[]{:S(2)}) collective-permute-start(bf16[1,128,896]{2,1,0:T(8,128)(2,1)} %get-tuple-element.60), channel_id=1, source_target_pairs={{0,7},{1,6},{2,1},{3,0},{4,3},{5,2},{6,5},{7,4},{8,15},{9,14},{10,... | collective-permute-start | bytes 688136 | tf_op jit(solution)/shard_map/ppermute | solution.py:224
  35.4 19.4 %collective-permute-start.5 = (bf16[1,128,896]{2,1,0:T(8,128)(2,1)S(1)}, bf16[1,128,896]{2,1,0:T(8,128)(2,1)S(1)}, u32[]{:S(2)}, u32[]{:S(2)}) collective-permute-start(bf16[1,128,896]{2,1,0:T(8,128)(2,1)S(1)} %slice.4), channel_id=1, source_target_pairs={{0,4},{1,5},{2,6},{3,7},{4,0},{5,1},{6,2},{7,3},{8,12},{9,13},{10,... | collective-permute-start | bytes 688136 | tf_op jit(solution)/shard_map/ppermute | solution.py:224
  61.8 4.2 %collective-permute-start.8 = (bf16[384,896]{1,0:T(8,128)(2,1)}, bf16[384,896]{1,0:T(8,128)(2,1)}, u32[]{:S(2)}, u32[]{:S(2)}) collective-permute-start(bf16[384,896]{1,0:T(8,128)(2,1)} %pack.1.refs_0_), channel_id=1, source_target_pairs={{0,1},{1,0},{2,3},{3,2},{4,5},{5,4},{6,7},{7,6},{8,9},{9,8},{10,11... | collective-permute-start | bytes 2064392 | tf_op jit(solution)/shard_map/ppermute | solution.py:224
  63.2 18.5 %collective-permute-start.6 = (bf16[384,896]{1,0:T(8,128)(2,1)}, bf16[384,896]{1,0:T(8,128)(2,1)S(1)}, u32[]{:S(2)}, u32[]{:S(2)}) collective-permute-start(bf16[384,896]{1,0:T(8,128)(2,1)} %pack.1.refs_0_), channel_id=1, source_target_pairs={{0,2},{1,3},{2,4},{3,5},{4,6},{5,7},{6,0},{7,1},{8,10},{9,11},{10,... | collective-permute-start | bytes 2064392 | tf_op jit(solution)/shard_map/ppermute | solution.py:224
  63.5 18.2 %collective-permute-start.7 = (bf16[384,896]{1,0:T(8,128)(2,1)}, bf16[384,896]{1,0:T(8,128)(2,1)S(1)}, u32[]{:S(2)}, u32[]{:S(2)}) collective-permute-start(bf16[384,896]{1,0:T(8,128)(2,1)} %pack.1.refs_0_), channel_id=1, source_target_pairs={{0,6},{1,7},{2,0},{3,1},{4,2},{5,3},{6,4},{7,5},{8,14},{9,15},{10,... | collective-permute-start | bytes 2064392 | tf_op jit(solution)/shard_map/ppermute | solution.py:224
  66.0 19.4 %copy-start.1 = (bf16[1792,256]{1,0:T(8,128)(2,1)S(1)}, bf16[1792,256]{1,0:T(8,128)(2,1)}, u32[]{:S(2)}) copy-start(bf16[1792,256]{1,0:T(8,128)(2,1)} %pad_maximum_fusion.3.refs_5_) | copy-start | bytes 2752516
  66.0 19.5 %copy-start.2 = (bf16[1792,256]{1,0:T(8,128)(2,1)S(1)}, bf16[1792,256]{1,0:T(8,128)(2,1)}, u32[]{:S(2)}) copy-start(bf16[1792,256]{1,0:T(8,128)(2,1)} %pad_maximum_fusion.1.refs_4_) | copy-start | bytes 2752516
  81.7 3.7 %collective-permute-start.10 = (bf16[384,896]{1,0:T(8,128)(2,1)S(1)}, bf16[384,896]{1,0:T(8,128)(2,1)S(1)}, u32[]{:S(2)}, u32[]{:S(2)}) collective-permute-start(bf16[384,896]{1,0:T(8,128)(2,1)S(1)} %collective-permute-done.6.refs_0_), channel_id=1, source_target_pairs={{0,1},{1,0},{2,3},{3,2},{4,5},{5,4},{6,7},{7,6},{8,9},{9,8},{10,11... | collective-permute-start | bytes 2064392 | tf_op jit(solution)/shard_map/ppermute | solution.py:224
  82.5 2.9 %collective-permute-start.11 = (bf16[384,896]{1,0:T(8,128)(2,1)S(1)}, bf16[384,896]{1,0:T(8,128)(2,1)S(1)}, u32[]{:S(2)}, u32[]{:S(2)}) collective-permute-start(bf16[384,896]{1,0:T(8,128)(2,1)S(1)} %collective-permute-done.7.refs_2_), channel_id=1, source_target_pairs={{0,1},{1,0},{2,3},{3,2},{4,5},{5,4},{6,7},{7,6},{8,9},{9,8},{10,11... | collective-permute-start | bytes 2064392 | tf_op jit(solution)/shard_map/ppermute | solution.py:224
  82.6 10.6 %collective-permute-start.9 = (bf16[384,896]{1,0:T(8,128)(2,1)S(1)}, bf16[384,896]{1,0:T(8,128)(2,1)S(1)}, u32[]{:S(2)}, u32[]{:S(2)}) collective-permute-start(bf16[384,896]{1,0:T(8,128)(2,1)S(1)} %broadcast_select_fusion), channel_id=1, source_target_pairs={{0,2},{1,7},{2,4},{3,1},{4,6},{5,3},{6,0},{7,5},{8,10},{9,15},{10,... | collective-permute-start | bytes 2064392 | tf_op jit(solution)/shard_map/ppermute | solution.py:233
  93.2 3.9 %collective-permute-start.12 = (bf16[384,896]{1,0:T(8,128)(2,1)S(1)}, bf16[384,896]{1,0:T(8,128)(2,1)S(1)}, u32[]{:S(2)}, u32[]{:S(2)}) collective-permute-start(bf16[384,896]{1,0:T(8,128)(2,1)S(1)} %collective-permute-done.9.refs_0_), channel_id=1, source_target_pairs={{0,1},{1,0},{2,3},{3,2},{4,5},{5,4},{6,7},{7,6},{8,9},{9,8},{10,11... | collective-permute-start | bytes 2064392 | tf_op jit(solution)/shard_map/ppermute | solution.py:224
  95.3 8.8 %collective-permute-start.16 = (bf16[1,128,896]{2,1,0:T(8,128)(2,1)S(1)}, bf16[1,128,896]{2,1,0:T(8,128)(2,1)S(1)}, u32[]{:S(2)}, u32[]{:S(2)}) collective-permute-start(bf16[1,128,896]{2,1,0:T(8,128)(2,1)S(1)} %copy-done.9), channel_id=1, source_target_pairs={{0,4},{1,5},{2,6},{3,7},{4,0},{5,1},{6,2},{7,3},{8,12},{9,13},{10,... | collective-permute-start | bytes 688136 | tf_op jit(solution)/shard_map/ppermute | solution.py:224
  97.5 9.2 %collective-permute-start.13 = (bf16[384,128]{1,0:T(8,128)(2,1)S(1)}, bf16[384,128]{1,0:T(8,128)(2,1)S(1)}, u32[]{:S(2)}, u32[]{:S(2)}) collective-permute-start(bf16[384,128]{1,0:T(8,128)(2,1)S(1)} %expand.7.refs_0_), channel_id=1, source_target_pairs={{0,2},{1,3},{2,4},{3,5},{4,6},{5,7},{6,0},{7,1},{8,10},{9,11},{10,... | collective-permute-start | bytes 294920 | tf_op jit(solution)/shard_map/ppermute | solution.py:224
  98.2 10.1 %collective-permute-start.14 = (bf16[384,128]{1,0:T(8,128)(2,1)S(1)}, bf16[384,128]{1,0:T(8,128)(2,1)S(1)}, u32[]{:S(2)}, u32[]{:S(2)}) collective-permute-start(bf16[384,128]{1,0:T(8,128)(2,1)S(1)} %expand.7.refs_0_), channel_id=1, source_target_pairs={{0,4},{1,5},{2,6},{3,7},{4,0},{5,1},{6,2},{7,3},{8,12},{9,13},{10,... | collective-permute-start | bytes 294920 | tf_op jit(solution)/shard_map/ppermute | solution.py:224
  100.2 8.1 %collective-permute-start.15 = (bf16[384,128]{1,0:T(8,128)(2,1)S(1)}, bf16[384,128]{1,0:T(8,128)(2,1)S(1)}, u32[]{:S(2)}, u32[]{:S(2)}) collective-permute-start(bf16[384,128]{1,0:T(8,128)(2,1)S(1)} %expand.7.refs_0_), channel_id=1, source_target_pairs={{0,6},{1,7},{2,0},{3,1},{4,2},{5,3},{6,4},{7,5},{8,14},{9,15},{10,... | collective-permute-start | bytes 294920 | tf_op jit(solution)/shard_map/ppermute | solution.py:224
  108.3 2.2 %collective-permute-start.18 = (bf16[3,384,128]{2,1,0:T(8,128)(2,1)S(1)}, bf16[3,384,128]{2,1,0:T(8,128)(2,1)S(1)}, u32[]{:S(2)}, u32[]{:S(2)}) collective-permute-start(bf16[3,384,128]{2,1,0:T(8,128)(2,1)S(1)} %pad_maximum_fusion.5), channel_id=1, source_target_pairs={{0,1},{1,0},{2,3},{3,2},{4,5},{5,4},{6,7},{7,6},{8,9},{9,8},{10,11... | collective-permute-start | bytes 884744 | tf_op jit(solution)/shard_map/ppermute | solution.py:224
  109.2 1.3 collective-permute-start.17
  113.8 45.4 %copy-start.5 = (bf16[96,128]{1,0:T(8,128)(2,1)S(1)}, bf16[96,128]{1,0:T(8,128)(2,1)}, u32[]{:S(2)}) copy-start(bf16[96,128]{1,0:T(8,128)(2,1)} %get-tuple-element.31.sel_ref) | copy-start | bytes 73732
  (7 other events, 57.1 us)

commit v11 on v9

--- a/solution.py
+++ b/solution.py
@@ -37,7 +37,10 @@
     place_at = lax.broadcasted_iota(jnp.int32, (experts, cap), 1)
     token = lax.broadcasted_iota(jnp.int32, (experts, tok_dev), 1)
     position = chosen_ref[...] - me_ref[0] * tok_dev
-    rest = (place_at < counts_ref[...]) & (position >= 0) & (position < tok_dev)
+    square = (experts, experts)
+    same = lax.broadcasted_iota(jnp.int32, square, 0) == lax.broadcasted_iota(jnp.int32, square, 1)
+    counts = jnp.sum(jnp.where(same, jnp.broadcast_to(counts_ref[...], square), 0), axis=1, keepdims=True)
+    rest = (place_at < counts) & (position >= 0) & (position < tok_dev)
     for s in range(SLOT):
         first = jnp.min(jnp.where(rest, place_at, cap), axis=1, keepdims=True)
         hit = place_at == first
@@ -78,7 +81,7 @@
         ],
         compiler_params=WIDE,
         name="send",
-    )(me[None], counts[:, None], chosen, tokens)
+    )(me[None], counts[None, :], chosen, tokens)
 
 
 def pack_kernel(tiles, column_ref, msg_ref, out_ref, held):
@@ -271,8 +274,9 @@
     column = holder * SLOT + jnp.sum(before.astype(jnp.int32), axis=1)
     column = jnp.where(entry < count, column, -1)
 
-    arrived, pieces, down_blocks = lax.optimization_barrier((arrived, pieces, down_blocks))
+    arrived, pieces = lax.optimization_barrier((arrived, pieces))
     own = pack(column[None, :], arrived, cut // LANE)
+    own, down_blocks = lax.optimization_barrier((own, down_blocks))
     here, there = at_core * cut, (1 - at_core) * cut
     fore, aft = sent(own, 1, 0), sent(own, -1, 0)
     total = expand(None, [own, sent(own, 0, 1)], (0, 0), jnp.stack([here, there]), pieces[:1])

time: 167 us -> 162 us (0.970)
  local copies, waits for them, and re-layouts: 7.99 us -> 5.7 us
  blocking collectives: 49.7 us -> 47.5 us
  waiting for transfers between devices: 50 us -> 47.8 us
    ppermute x17, waiting for transfers between devices: 43.9 us -> 20.6 us  [sent(): return lax.ppermute(value, LOCAL, pairs)]
    all_to_all x1, waiting for transfers between devices: 0.01 us -> 21 us  [exchange(): lax.all_to_all(parts, AXES, split_axis=0, concat_axis=0, tiled=True)]
    all_to_all x1, blocking collectives: 49.7 us -> 47.5 us  [exchange(): lax.all_to_all(parts, AXES, split_axis=0, concat_axis=0, tiled=True)]
  transfers between devices with their start and end apart: 19 -> 19, of which waited for: 10 -> 8; matrix products, arithmetic and copies ran while one was open for 7% -> 7% of each run, Pallas kernels for 2% -> 4%
where the time goes in v11:
time: 162 us
  waiting for transfers between devices  47.8 us (30%)
  blocking collectives  47.5 us (29%)
  starting transfers between devices  37.4 us (23%)
  Pallas kernels  16.7 us (10%)
  other arithmetic  6.28 us (4%)
  local copies, waits for them, and re-layouts  5.7 us (4%)
    all_to_all x1, blocking collectives, exchange(): lax.all_to_all(parts, AXES, split_axis=0, concat_axis=0, tiled=True)  47.5 us
    all_to_all x1, waiting for transfers between devices, exchange(): lax.all_to_all(parts, AXES, split_axis=0, concat_axis=0, tiled=True)  21 us
    ppermute x17, waiting for transfers between devices, sent(): return lax.ppermute(value, LOCAL, pairs)  20.6 us
    ppermute x17, starting transfers between devices, sent(): return lax.ppermute(value, LOCAL, pairs)  19 us
    all_to_all x1, starting transfers between devices, exchange(): lax.all_to_all(parts, AXES, split_axis=0, concat_axis=0, tiled=True)  15.7 us
    ppermute x1, waiting for transfers between devices, forwarded(): lax.ppermute(jnp.where(lax.axis_index('core') == 0, fore, aft), LOCAL, pa...  6.26 us
    pallas_call x1, Pallas kernels, send(): pl.pallas_call(functools.partial(send_kernel, n_local), out_shape=[jax.Sh...  4.59 us
    pallas_call x4, Pallas kernels, expand(): pl.pallas_call(functools.partial(expand_kernel, uses, opening, last), out...  4.28 us
  transfers between devices with their start and end apart: 19, of which 8 were waited for; matrix products, arithmetic and copies ran while one was open for 7% of the time, Pallas kernels for 4%

profile of v11, /device:TPU:1, one launch (start us, length us, event | category | flops | bytes accessed | tf_op | source)
XLA Modules:
  0.0 161.7 jit_solution(10568260514722052960)
XLA Ops:
  0.0 4.6 %send.1 = (bf16[5632,128]{1,0:T(8,128)(2,1)}, bf16[96,128]{1,0:T(8,128)(2,1)}) custom-call(s32[1]{0:T(128)} %bitcast.me_ref, s32[1,32]{1,0:T(1,128)} %bitcast.43, s32[32,384]{1,0:T(8,128)} %chosen_ref.1, bf16[128,7168]{1,0:T(8,128)(2,1)} %tok_ref.1), custom_call_target="tpu_custom_call" | custom-call | tf_op jit(solution)/shard_map/send/pallas_call | solution.py:72
  4.6 15.7 %all-to-all-start = ((bf16[256,11,2,128]{3,2,1,0:T(2,128)(2,1)}), bf16[256,11,2,128]{3,2,1,0:T(2,128)(2,1)S(1)}, u32[]{:S(2)}, u32[]{:S(2)}) async-start(bf16[256,11,2,128]{3,2,1,0:T(2,128)(2,1)} %bitcast.42), calls=%async_computation | async-start | bytes 2883584 | tf_op jit(solution)/shard_map/all_to_all | solution.py:215
  22.3 2.1 %collective-permute-start = (bf16[2,128,896]{2,1,0:T(8,128)(2,1)}, bf16[2,128,896]{2,1,0:T(8,128)(2,1)}, u32[]{:S(2)}, u32[]{:S(2)}) collective-permute-start(bf16[2,128,896]{2,1,0:T(8,128)(2,1)} %pad_maximum_fusion.4), channel_id=1, source_target_pairs={{0,1},{1,0},{2,3},{3,2},{4,5},{5,4},{6,7},{7,6},{8,9},{9,8},{10,11... | collective-permute-start | bytes 1376264 | tf_op jit(solution)/shard_map/ppermute | solution.py:224
  25.6 1.6 collective-permute-start.3
  27.1 2.0 %collective-permute-start.4 = (bf16[1,128,896]{2,1,0:T(8,128)(2,1)}, bf16[1,128,896]{2,1,0:T(8,128)(2,1)}, u32[]{:S(2)}, u32[]{:S(2)}) collective-permute-start(bf16[1,128,896]{2,1,0:T(8,128)(2,1)} %get-tuple-element.54), channel_id=1, source_target_pairs={{0,7},{1,6},{2,1},{3,0},{4,3},{5,2},{6,5},{7,4},{8,15},{9,14},{10,... | collective-permute-start | bytes 688136 | tf_op jit(solution)/shard_map/ppermute | solution.py:224
  29.9 2.3 %constant_dynamic-slice_fusion = (bf16[1792,128]{1,0:T(8,128)(2,1)S(1)}, bf16[1792,128]{1,0:T(8,128)(2,1)S(1)}, bf16[1792,128]{1,0:T(8,128)(2,1)S(1)}, bf16[1792...) fusion(bf16[7168,128]{1,0:T(8,128)(2,1)} %bitcast.40, ...), kind=kLoop, calls=%fused_computation.21 | loop fusion | bytes 7340048 | tf_op jit(solution)/shard_map/dynamic_slice | solution.py:266
  38.2 21.0 %all-to-all-done = bf16[256,11,2,128]{3,2,1,0:T(2,128)(2,1)S(1)} async-done(((bf16[256,11,2,128]{3,2,1,0:T(2,128)(2,1)}), bf16[256,11,2,128]{3,2,1,0:T(2,128)(2,1)S(1)}, u32[]{:S(2)}, u32[]{:S(2)}) %all-to-all-start) | async-done | bytes 1441824 | tf_op jit(solution)/shard_map/all_to_all | solution.py:215
  59.9 2.0 %pack.1.refs_0_ = bf16[384,896]{1,0:T(8,128)(2,1)} custom-call(s32[1,384]{1,0:T(1,128)S(1)} %copy-done.4, bf16[5632,128]{1,0:T(8,128)(2,1)S(1)} %bitcast.33), custom_call_target="tpu_custom_call" | custom-call | tf_op jit(solution)/shard_map/pack/pallas_call | solution.py:104
  61.9 1.6 collective-permute-start.8
  63.6 2.5 %collective-permute-start.7 = (bf16[384,896]{1,0:T(8,128)(2,1)}, bf16[384,896]{1,0:T(8,128)(2,1)S(1)}, u32[]{:S(2)}, u32[]{:S(2)}) collective-permute-start(bf16[384,896]{1,0:T(8,128)(2,1)} %pack.1.refs_0_), channel_id=1, source_target_pairs={{0,6},{1,7},{2,0},{3,1},{4,2},{5,3},{6,4},{7,5},{8,14},{9,15},{10,... | collective-permute-start | bytes 2064392 | tf_op jit(solution)/shard_map/ppermute | solution.py:224
  66.2 2.0 %expand.4.refs_6_ = f32[384,256]{1,0:T(8,128)S(1)} custom-call(s32[2]{0:T(128)S(1)} %pad_add_fusion.place_ref, bf16[384,896]{1,0:T(8,128)(2,1)} %pack.1.refs_0_, bf16[384,896]{1,0:T(8,128)(2,1)} %collective-permute-done.8.refs_1_, bf16[1792,256]{1,0:T(8,128)(2,1)S(1)} %pad_maximum_fusion.refs_2_), custom_call_target="tpu_custom_call" | custom-call | flops 352321536 | bytes 688128 | tf_op jit(solution)/shard_map/expand/pallas_call | solution.py:137
  68.2 13.6 %collective-permute-done.6.refs_0_ = bf16[384,896]{1,0:T(8,128)(2,1)S(1)} collective-permute-done((bf16[384,896]{1,0:T(8,128)(2,1)}, bf16[384,896]{1,0:T(8,128)(2,1)S(1)}, u32[]{:S(2)}, u32[]{:S(2)}) %collective-permute-start.6) | collective-permute-done | bytes 688160 | tf_op jit(solution)/shard_map/ppermute | solution.py:224
  82.8 2.8 %collective-permute-start.9 = (bf16[384,896]{1,0:T(8,128)(2,1)S(1)}, bf16[384,896]{1,0:T(8,128)(2,1)S(1)}, u32[]{:S(2)}, u32[]{:S(2)}) collective-permute-start(bf16[384,896]{1,0:T(8,128)(2,1)S(1)} %broadcast_select_fusion), channel_id=1, source_target_pairs={{0,2},{1,7},{2,4},{3,1},{4,6},{5,3},{6,0},{7,5},{8,10},{9,15},{10,... | collective-permute-start | bytes 2064392 | tf_op jit(solution)/shard_map/ppermute | solution.py:233
  85.7 1.5 expand.5.refs_2_
  87.2 6.3 %collective-permute-done.9.refs_0_ = bf16[384,896]{1,0:T(8,128)(2,1)S(1)} collective-permute-done((bf16[384,896]{1,0:T(8,128)(2,1)S(1)}, bf16[384,896]{1,0:T(8,128)(2,1)S(1)}, u32[]{:S(2)}, u32[]{:S(2)}) %collective-permute-start.9) | collective-permute-done | bytes 688160 | tf_op jit(solution)/shard_map/ppermute | solution.py:233
  93.4 2.1 %collective-permute-start.12 = (bf16[384,896]{1,0:T(8,128)(2,1)S(1)}, bf16[384,896]{1,0:T(8,128)(2,1)S(1)}, u32[]{:S(2)}, u32[]{:S(2)}) collective-permute-start(bf16[384,896]{1,0:T(8,128)(2,1)S(1)} %collective-permute-done.9.refs_0_), channel_id=1, source_target_pairs={{0,1},{1,0},{2,3},{3,2},{4,5},{5,4},{6,7},{7,6},{8,9},{9,8},{10,11... | collective-permute-start | bytes 2064392 | tf_op jit(solution)/shard_map/ppermute | solution.py:224
  95.9 1.4 collective-permute-done.12.refs_0_
  97.8 2.6 %collective-permute-start.14 = (bf16[384,128]{1,0:T(8,128)(2,1)S(1)}, bf16[384,128]{1,0:T(8,128)(2,1)S(1)}, u32[]{:S(2)}, u32[]{:S(2)}) collective-permute-start(bf16[384,128]{1,0:T(8,128)(2,1)S(1)} %expand.7.refs_0_), channel_id=1, source_target_pairs={{0,4},{1,5},{2,6},{3,7},{4,0},{5,1},{6,2},{7,3},{8,12},{9,13},{10,... | collective-permute-start | bytes 294920 | tf_op jit(solution)/shard_map/ppermute | solution.py:224
  100.9 2.1 %collective-permute-done.13.refs_1_ = bf16[384,128]{1,0:T(8,128)(2,1)S(1)} collective-permute-done((bf16[384,128]{1,0:T(8,128)(2,1)S(1)}, bf16[384,128]{1,0:T(8,128)(2,1)S(1)}, u32[]{:S(2)}, u32[]{:S(2)}) %collective-permute-start.13) | collective-permute-done | bytes 98336 | tf_op jit(solution)/shard_map/ppermute | solution.py:224
  103.0 2.0 %collective-permute-done.14.refs_2_ = bf16[384,128]{1,0:T(8,128)(2,1)S(1)} collective-permute-done((bf16[384,128]{1,0:T(8,128)(2,1)S(1)}, bf16[384,128]{1,0:T(8,128)(2,1)S(1)}, u32[]{:S(2)}, u32[]{:S(2)}) %collective-permute-start.14) | collective-permute-done | bytes 98336 | tf_op jit(solution)/shard_map/ppermute | solution.py:224
  105.4 1.6 collective-permute-start.17
  108.4 3.4 %down.1 = bf16[5632,128]{1,0:T(8,128)(2,1)S(1)} custom-call(f32[384,1]{1,0:T(8,128)S(1)} %copy.9.weight_ref, s32[1,384]{1,0:T(1,128)S(1)} %copy-done.5, bf16[384,128]{1,0:T(8,128)(2,1)S(1)} %expand.7.refs_0_, bf16[384,128]{1,0:T(8,128)(2,1)S(1)} %collective-permute-done.13.refs_1_, bf16[384,128]{1,0:T(8,128)(2,1)S(1)} %collective-permute-done.14.refs_2_, ...), custom_call_target="tpu_custom_call" | custom-call | tf_op jit(solution)/shard_map/down/pallas_call | solution.py:175
  111.8 47.5 %all_to_all.10 = bf16[256,11,2,128]{3,2,1,0:T(2,128)(2,1)S(1)} all-to-all(bf16[256,11,2,128]{3,2,1,0:T(2,128)(2,1)S(1)} %bitcast.35), channel_id=1, replica_groups=mesh['node'=32,'x'=4,'core'=2] {'node','x','core'}, dimensions={0} | all-to-all | bytes 2883584 | tf_op jit(solution)/shard_map/all_to_all | solution.py:215
  159.3 2.4 %place.1 = bf16[128,7168]{1,0:T(8,128)(2,1)} custom-call(bf16[96,128]{1,0:T(8,128)(2,1)S(1)} %copy-done.3, bf16[5632,128]{1,0:T(8,128)(2,1)S(1)} %bitcast.34), custom_call_target="tpu_custom_call" | custom-call | tf_op jit(solution)/shard_map/place/pallas_call | solution.py:202
  (61 shorter events, 14.8 us)
Async XLA Ops:
  0.0 107.1 %copy-start = (f32[32,384]{1,0:T(8,128)S(1)}, f32[32,384]{1,0:T(8,128)}, u32[]{:S(2)}) copy-start(f32[32,384]{1,0:T(8,128)} %param.13) | copy-start | bytes 147460
  4.6 15.8 %copy-start.6 = (bf16[1,128,7168]{2,1,0:T(8,128)(2,1)S(1)}, bf16[1,128,7168]{2,1,0:T(8,128)(2,1)}, u32[]{:S(2)}) copy-start(bf16[1,128,7168]{2,1,0:T(8,128)(2,1)} %param.10) | copy-start | bytes 5505028
  4.6 54.6 %all-to-all-start = ((bf16[256,11,2,128]{3,2,1,0:T(2,128)(2,1)}), bf16[256,11,2,128]{3,2,1,0:T(2,128)(2,1)S(1)}, u32[]{:S(2)}, u32[]{:S(2)}) async-start(bf16[256,11,2,128]{3,2,1,0:T(2,128)(2,1)} %bitcast.42), calls=%async_computation | async-start | bytes 2883584 | tf_op jit(solution)/shard_map/all_to_all | solution.py:215
  22.3 12.2 %collective-permute-start = (bf16[2,128,896]{2,1,0:T(8,128)(2,1)}, bf16[2,128,896]{2,1,0:T(8,128)(2,1)}, u32[]{:S(2)}, u32[]{:S(2)}) collective-permute-start(bf16[2,128,896]{2,1,0:T(8,128)(2,1)} %pad_maximum_fusion.4), channel_id=1, source_target_pairs={{0,1},{1,0},{2,3},{3,2},{4,5},{5,4},{6,7},{7,6},{8,9},{9,8},{10,11... | collective-permute-start | bytes 1376264 | tf_op jit(solution)/shard_map/ppermute | solution.py:224
  24.4 37.4 %collective-permute-start.1 = (bf16[1,128,896]{2,1,0:T(8,128)(2,1)}, bf16[1,128,896]{2,1,0:T(8,128)(2,1)}, u32[]{:S(2)}, u32[]{:S(2)}) collective-permute-start(bf16[1,128,896]{2,1,0:T(8,128)(2,1)} %get-tuple-element.57), channel_id=1, source_target_pairs={{0,2},{1,3},{2,4},{3,5},{4,6},{5,7},{6,0},{7,1},{8,10},{9,11},{10,... | collective-permute-start | bytes 688136 | tf_op jit(solution)/shard_map/ppermute | solution.py:224
  24.5 37.4 %collective-permute-start.2 = (bf16[1,128,896]{2,1,0:T(8,128)(2,1)}, bf16[1,128,896]{2,1,0:T(8,128)(2,1)}, u32[]{:S(2)}, u32[]{:S(2)}) collective-permute-start(bf16[1,128,896]{2,1,0:T(8,128)(2,1)} %get-tuple-element.56), channel_id=1, source_target_pairs={{0,3},{1,2},{2,5},{3,4},{4,7},{5,6},{6,1},{7,0},{8,11},{9,10},{10,... | collective-permute-start | bytes 688136 | tf_op jit(solution)/shard_map/ppermute | solution.py:224
  25.6 36.3 %collective-permute-start.3 = (bf16[1,128,896]{2,1,0:T(8,128)(2,1)}, bf16[1,128,896]{2,1,0:T(8,128)(2,1)}, u32[]{:S(2)}, u32[]{:S(2)}) collective-permute-start(bf16[1,128,896]{2,1,0:T(8,128)(2,1)} %get-tuple-element.55), channel_id=1, source_target_pairs={{0,6},{1,7},{2,0},{3,1},{4,2},{5,3},{6,4},{7,5},{8,14},{9,15},{10,... | collective-permute-start | bytes 688136 | tf_op jit(solution)/shard_map/ppermute | solution.py:224
  27.1 34.7 %collective-permute-start.4 = (bf16[1,128,896]{2,1,0:T(8,128)(2,1)}, bf16[1,128,896]{2,1,0:T(8,128)(2,1)}, u32[]{:S(2)}, u32[]{:S(2)}) collective-permute-start(bf16[1,128,896]{2,1,0:T(8,128)(2,1)} %get-tuple-element.54), channel_id=1, source_target_pairs={{0,7},{1,6},{2,1},{3,0},{4,3},{5,2},{6,5},{7,4},{8,15},{9,14},{10,... | collective-permute-start | bytes 688136 | tf_op jit(solution)/shard_map/ppermute | solution.py:224
  36.3 25.6 %collective-permute-start.5 = (bf16[2,128,896]{2,1,0:T(8,128)(2,1)}, bf16[2,128,896]{2,1,0:T(8,128)(2,1)}, u32[]{:S(2)}, u32[]{:S(2)}) collective-permute-start(bf16[2,128,896]{2,1,0:T(8,128)(2,1)} %pad_maximum_fusion.5), channel_id=1, source_target_pairs={{0,4},{1,5},{2,6},{3,7},{4,0},{5,1},{6,2},{7,3},{8,12},{9,13},{10,... | collective-permute-start | bytes 1376264 | tf_op jit(solution)/shard_map/ppermute | solution.py:224
  61.9 4.3 %collective-permute-start.8 = (bf16[384,896]{1,0:T(8,128)(2,1)}, bf16[384,896]{1,0:T(8,128)(2,1)}, u32[]{:S(2)}, u32[]{:S(2)}) collective-permute-start(bf16[384,896]{1,0:T(8,128)(2,1)} %pack.1.refs_0_), channel_id=1, source_target_pairs={{0,1},{1,0},{2,3},{3,2},{4,5},{5,4},{6,7},{7,6},{8,9},{9,8},{10,11... | collective-permute-start | bytes 2064392 | tf_op jit(solution)/shard_map/ppermute | solution.py:224
  63.4 18.4 %collective-permute-start.6 = (bf16[384,896]{1,0:T(8,128)(2,1)}, bf16[384,896]{1,0:T(8,128)(2,1)S(1)}, u32[]{:S(2)}, u32[]{:S(2)}) collective-permute-start(bf16[384,896]{1,0:T(8,128)(2,1)} %pack.1.refs_0_), channel_id=1, source_target_pairs={{0,2},{1,3},{2,4},{3,5},{4,6},{5,7},{6,0},{7,1},{8,10},{9,11},{10,... | collective-permute-start | bytes 2064392 | tf_op jit(solution)/shard_map/ppermute | solution.py:224
  63.6 18.2 %collective-permute-start.7 = (bf16[384,896]{1,0:T(8,128)(2,1)}, bf16[384,896]{1,0:T(8,128)(2,1)S(1)}, u32[]{:S(2)}, u32[]{:S(2)}) collective-permute-start(bf16[384,896]{1,0:T(8,128)(2,1)} %pack.1.refs_0_), channel_id=1, source_target_pairs={{0,6},{1,7},{2,0},{3,1},{4,2},{5,3},{6,4},{7,5},{8,14},{9,15},{10,... | collective-permute-start | bytes 2064392 | tf_op jit(solution)/shard_map/ppermute | solution.py:224
  66.2 19.4 %copy-start.1 = (bf16[1792,256]{1,0:T(8,128)(2,1)S(1)}, bf16[1792,256]{1,0:T(8,128)(2,1)}, u32[]{:S(2)}) copy-start(bf16[1792,256]{1,0:T(8,128)(2,1)} %pad_maximum_fusion.3.refs_5_) | copy-start | bytes 2752516
  66.2 19.4 %copy-start.2 = (bf16[1792,256]{1,0:T(8,128)(2,1)S(1)}, bf16[1792,256]{1,0:T(8,128)(2,1)}, u32[]{:S(2)}) copy-start(bf16[1792,256]{1,0:T(8,128)(2,1)} %pad_maximum_fusion.1.refs_4_) | copy-start | bytes 2752516
  81.9 3.8 %collective-permute-start.10 = (bf16[384,896]{1,0:T(8,128)(2,1)S(1)}, bf16[384,896]{1,0:T(8,128)(2,1)S(1)}, u32[]{:S(2)}, u32[]{:S(2)}) collective-permute-start(bf16[384,896]{1,0:T(8,128)(2,1)S(1)} %collective-permute-done.6.refs_0_), channel_id=1, source_target_pairs={{0,1},{1,0},{2,3},{3,2},{4,5},{5,4},{6,7},{7,6},{8,9},{9,8},{10,11... | collective-permute-start | bytes 2064392 | tf_op jit(solution)/shard_map/ppermute | solution.py:224
  82.7 2.9 %collective-permute-start.11 = (bf16[384,896]{1,0:T(8,128)(2,1)S(1)}, bf16[384,896]{1,0:T(8,128)(2,1)S(1)}, u32[]{:S(2)}, u32[]{:S(2)}) collective-permute-start(bf16[384,896]{1,0:T(8,128)(2,1)S(1)} %collective-permute-done.7.refs_2_), channel_id=1, source_target_pairs={{0,1},{1,0},{2,3},{3,2},{4,5},{5,4},{6,7},{7,6},{8,9},{9,8},{10,11... | collective-permute-start | bytes 2064392 | tf_op jit(solution)/shard_map/ppermute | solution.py:224
  82.8 10.6 %collective-permute-start.9 = (bf16[384,896]{1,0:T(8,128)(2,1)S(1)}, bf16[384,896]{1,0:T(8,128)(2,1)S(1)}, u32[]{:S(2)}, u32[]{:S(2)}) collective-permute-start(bf16[384,896]{1,0:T(8,128)(2,1)S(1)} %broadcast_select_fusion), channel_id=1, source_target_pairs={{0,2},{1,7},{2,4},{3,1},{4,6},{5,3},{6,0},{7,5},{8,10},{9,15},{10,... | collective-permute-start | bytes 2064392 | tf_op jit(solution)/shard_map/ppermute | solution.py:233
  93.4 3.9 %collective-permute-start.12 = (bf16[384,896]{1,0:T(8,128)(2,1)S(1)}, bf16[384,896]{1,0:T(8,128)(2,1)S(1)}, u32[]{:S(2)}, u32[]{:S(2)}) collective-permute-start(bf16[384,896]{1,0:T(8,128)(2,1)S(1)} %collective-permute-done.9.refs_0_), channel_id=1, source_target_pairs={{0,1},{1,0},{2,3},{3,2},{4,5},{5,4},{6,7},{7,6},{8,9},{9,8},{10,11... | collective-permute-start | bytes 2064392 | tf_op jit(solution)/shard_map/ppermute | solution.py:224
  97.7 5.3 %collective-permute-start.13 = (bf16[384,128]{1,0:T(8,128)(2,1)S(1)}, bf16[384,128]{1,0:T(8,128)(2,1)S(1)}, u32[]{:S(2)}, u32[]{:S(2)}) collective-permute-start(bf16[384,128]{1,0:T(8,128)(2,1)S(1)} %expand.7.refs_0_), channel_id=1, source_target_pairs={{0,2},{1,3},{2,4},{3,5},{4,6},{5,7},{6,0},{7,1},{8,10},{9,11},{10,... | collective-permute-start | bytes 294920 | tf_op jit(solution)/shard_map/ppermute | solution.py:224
  97.8 7.3 %collective-permute-start.14 = (bf16[384,128]{1,0:T(8,128)(2,1)S(1)}, bf16[384,128]{1,0:T(8,128)(2,1)S(1)}, u32[]{:S(2)}, u32[]{:S(2)}) collective-permute-start(bf16[384,128]{1,0:T(8,128)(2,1)S(1)} %expand.7.refs_0_), channel_id=1, source_target_pairs={{0,4},{1,5},{2,6},{3,7},{4,0},{5,1},{6,2},{7,3},{8,12},{9,13},{10,... | collective-permute-start | bytes 294920 | tf_op jit(solution)/shard_map/ppermute | solution.py:224
  100.4 4.9 %collective-permute-start.15 = (bf16[384,128]{1,0:T(8,128)(2,1)S(1)}, bf16[384,128]{1,0:T(8,128)(2,1)S(1)}, u32[]{:S(2)}, u32[]{:S(2)}) collective-permute-start(bf16[384,128]{1,0:T(8,128)(2,1)S(1)} %expand.7.refs_0_), channel_id=1, source_target_pairs={{0,6},{1,7},{2,0},{3,1},{4,2},{5,3},{6,4},{7,5},{8,14},{9,15},{10,... | collective-permute-start | bytes 294920 | tf_op jit(solution)/shard_map/ppermute | solution.py:224
  105.4 3.0 %collective-permute-start.17 = (bf16[3,384,128]{2,1,0:T(8,128)(2,1)S(1)}, bf16[3,384,128]{2,1,0:T(8,128)(2,1)S(1)}, u32[]{:S(2)}, u32[]{:S(2)}) collective-permute-start(bf16[3,384,128]{2,1,0:T(8,128)(2,1)S(1)} %pad_maximum_fusion.6), channel_id=1, source_target_pairs={{0,1},{1,0},{2,3},{3,2},{4,5},{5,4},{6,7},{7,6},{8,9},{9,8},{10,11... | collective-permute-start | bytes 884744 | tf_op jit(solution)/shard_map/ppermute | solution.py:224
  107.0 1.3 collective-permute-start.16
  111.8 47.5 %copy-start.3 = (bf16[96,128]{1,0:T(8,128)(2,1)S(1)}, bf16[96,128]{1,0:T(8,128)(2,1)}, u32[]{:S(2)}) copy-start(bf16[96,128]{1,0:T(8,128)(2,1)} %get-tuple-element.28.sel_ref) | copy-start | bytes 73732
  (4 other events, 17.4 us)

commit v12 on v11

--- a/solution.py
+++ b/solution.py
@@ -183,28 +183,39 @@
     )(weight, column, *hidden, *down_blocks)
 
 
-def place_kernel(n_local, sel_ref, msg_ref, out_ref, held):
+def place_kernel(n_local, sel_ref, msg_ref, out_ref, held, mixed, sems):
     experts = sel_ref.shape[0] // SLOT
-    tiles = out_ref.shape[1] // (n_local * LANE)
+    cut = out_ref.shape[1] // n_local
+    tiles = cut // LANE
     rows = rows_of(tiles)
     held[...] = msg_ref[...].astype(F32)
+    each = n_local // sems.shape[0]
+    copies = []
     for k in range(n_local):
         val = []
         for s in range(SLOT):
             at = [pl.ds(k * rows + t * SLOT + s, experts, stride=n_local * rows) for t in range(tiles)]
             val.append(jnp.concatenate([held[a, :] for a in at], axis=1))
         val = jnp.concatenate(val, axis=0).astype(BF16)
-        mixed = lax.dot_general(sel_ref[...], val, (((0,), (0,)), ((), ())), preferred_element_type=F32)
-        out_ref[:, k * tiles * LANE : (k + 1) * tiles * LANE] = mixed.astype(BF16)
+        part = lax.dot_general(sel_ref[...], val, (((0,), (0,)), ((), ())), preferred_element_type=F32)
+        mixed[:, k * cut : (k + 1) * cut] = part.astype(BF16)
+        if k % each == each - 1:
+            n = k // each
+            lanes = pl.ds(n * each * cut, each * cut)
+            copies.append(pltpu.make_async_copy(mixed.at[:, lanes], out_ref.at[:, lanes], sems.at[n]))
+            copies[-1].start()
+    for copy in copies:
+        copy.wait()
 
 
 def place(sel, msg, n_local, width):
+    shape = (sel.shape[1], width)
     return pl.pallas_call(
         functools.partial(place_kernel, n_local),
-        out_shape=jax.ShapeDtypeStruct((sel.shape[1], width), BF16),
+        out_shape=jax.ShapeDtypeStruct(shape, BF16),
         in_specs=[VMEM, VMEM],
-        out_specs=VMEM,
-        scratch_shapes=[pltpu.VMEM(msg.shape, F32)],
+        out_specs=HBM,
+        scratch_shapes=[pltpu.VMEM(msg.shape, F32), pltpu.VMEM(shape, BF16), pltpu.SemaphoreType.DMA((4,))],
         compiler_params=PARAMS,
         name="place",
     )(sel, msg)

time: 162 us -> 162 us (level)
  no operation moved by 1% of the time
where the time goes in v12:
time: 162 us; the launch traced here: 161 us
  waiting for transfers between devices  47.8 us (30%)
  blocking collectives  47.5 us (29%)
  starting transfers between devices  37.4 us (23%)
  Pallas kernels  16.3 us (10%)
  other arithmetic  6.28 us (4%)
  local copies, waits for them, and re-layouts  5.7 us (4%)
    all_to_all x1, blocking collectives, exchange(): lax.all_to_all(parts, AXES, split_axis=0, concat_axis=0, tiled=True)  47.5 us
    all_to_all x1, waiting for transfers between devices, exchange(): lax.all_to_all(parts, AXES, split_axis=0, concat_axis=0, tiled=True)  21 us
    ppermute x17, waiting for transfers between devices, sent(): return lax.ppermute(value, LOCAL, pairs)  20.6 us
    ppermute x17, starting transfers between devices, sent(): return lax.ppermute(value, LOCAL, pairs)  19 us
    all_to_all x1, starting transfers between devices, exchange(): lax.all_to_all(parts, AXES, split_axis=0, concat_axis=0, tiled=True)  15.7 us
    ppermute x1, waiting for transfers between devices, forwarded(): lax.ppermute(jnp.where(lax.axis_index('core') == 0, fore, aft), LOCAL, pa...  6.26 us
    pallas_call x1, Pallas kernels, send(): pl.pallas_call(functools.partial(send_kernel, n_local), out_shape=[jax.Sh...  4.59 us
    pallas_call x4, Pallas kernels, expand(): pl.pallas_call(functools.partial(expand_kernel, uses, opening, last), out...  4.28 us
  transfers between devices with their start and end apart: 19, of which 8 were waited for; matrix products, arithmetic and copies ran while one was open for 7% of the time, Pallas kernels for 4%

profile of v12, /device:TPU:1, one launch (start us, length us, event | category | flops | bytes accessed | tf_op | source)
XLA Modules:
  0.0 161.4 jit_solution(9830212740159819579)
XLA Ops:
  0.0 4.6 %send.1 = (bf16[5632,128]{1,0:T(8,128)(2,1)}, bf16[96,128]{1,0:T(8,128)(2,1)}) custom-call(s32[1]{0:T(128)} %bitcast.me_ref, s32[1,32]{1,0:T(1,128)} %bitcast.43, s32[32,384]{1,0:T(8,128)} %chosen_ref.1, bf16[128,7168]{1,0:T(8,128)(2,1)} %tok_ref.1), custom_call_target="tpu_custom_call" | custom-call | tf_op jit(solution)/shard_map/send/pallas_call | solution.py:72
  4.6 15.7 %all-to-all-start = ((bf16[256,11,2,128]{3,2,1,0:T(2,128)(2,1)}), bf16[256,11,2,128]{3,2,1,0:T(2,128)(2,1)S(1)}, u32[]{:S(2)}, u32[]{:S(2)}) async-start(bf16[256,11,2,128]{3,2,1,0:T(2,128)(2,1)} %bitcast.42), calls=%async_computation | async-start | bytes 2883584 | tf_op jit(solution)/shard_map/all_to_all | solution.py:226
  22.3 2.1 %collective-permute-start = (bf16[2,128,896]{2,1,0:T(8,128)(2,1)}, bf16[2,128,896]{2,1,0:T(8,128)(2,1)}, u32[]{:S(2)}, u32[]{:S(2)}) collective-permute-start(bf16[2,128,896]{2,1,0:T(8,128)(2,1)} %pad_maximum_fusion.4), channel_id=1, source_target_pairs={{0,1},{1,0},{2,3},{3,2},{4,5},{5,4},{6,7},{7,6},{8,9},{9,8},{10,11... | collective-permute-start | bytes 1376264 | tf_op jit(solution)/shard_map/ppermute | solution.py:235
  25.6 1.6 collective-permute-start.3
  27.1 2.0 %collective-permute-start.4 = (bf16[1,128,896]{2,1,0:T(8,128)(2,1)}, bf16[1,128,896]{2,1,0:T(8,128)(2,1)}, u32[]{:S(2)}, u32[]{:S(2)}) collective-permute-start(bf16[1,128,896]{2,1,0:T(8,128)(2,1)} %get-tuple-element.54), channel_id=1, source_target_pairs={{0,7},{1,6},{2,1},{3,0},{4,3},{5,2},{6,5},{7,4},{8,15},{9,14},{10,... | collective-permute-start | bytes 688136 | tf_op jit(solution)/shard_map/ppermute | solution.py:235
  29.9 2.3 %constant_dynamic-slice_fusion = (bf16[1792,128]{1,0:T(8,128)(2,1)S(1)}, bf16[1792,128]{1,0:T(8,128)(2,1)S(1)}, bf16[1792,128]{1,0:T(8,128)(2,1)S(1)}, bf16[1792...) fusion(bf16[7168,128]{1,0:T(8,128)(2,1)} %bitcast.40, ...), kind=kLoop, calls=%fused_computation.21 | loop fusion | bytes 7340048 | tf_op jit(solution)/shard_map/dynamic_slice | solution.py:277
  38.2 21.0 %all-to-all-done = bf16[256,11,2,128]{3,2,1,0:T(2,128)(2,1)S(1)} async-done(((bf16[256,11,2,128]{3,2,1,0:T(2,128)(2,1)}), bf16[256,11,2,128]{3,2,1,0:T(2,128)(2,1)S(1)}, u32[]{:S(2)}, u32[]{:S(2)}) %all-to-all-start) | async-done | bytes 1441824 | tf_op jit(solution)/shard_map/all_to_all | solution.py:226
  59.9 2.0 %pack.1.refs_0_ = bf16[384,896]{1,0:T(8,128)(2,1)} custom-call(s32[1,384]{1,0:T(1,128)S(1)} %copy-done.4, bf16[5632,128]{1,0:T(8,128)(2,1)S(1)} %bitcast.33), custom_call_target="tpu_custom_call" | custom-call | tf_op jit(solution)/shard_map/pack/pallas_call | solution.py:104
  61.9 1.6 collective-permute-start.8
  63.6 2.5 %collective-permute-start.7 = (bf16[384,896]{1,0:T(8,128)(2,1)}, bf16[384,896]{1,0:T(8,128)(2,1)S(1)}, u32[]{:S(2)}, u32[]{:S(2)}) collective-permute-start(bf16[384,896]{1,0:T(8,128)(2,1)} %pack.1.refs_0_), channel_id=1, source_target_pairs={{0,6},{1,7},{2,0},{3,1},{4,2},{5,3},{6,4},{7,5},{8,14},{9,15},{10,... | collective-permute-start | bytes 2064392 | tf_op jit(solution)/shard_map/ppermute | solution.py:235
  66.2 2.0 %expand.4.refs_6_ = f32[384,256]{1,0:T(8,128)S(1)} custom-call(s32[2]{0:T(128)S(1)} %pad_add_fusion.place_ref, bf16[384,896]{1,0:T(8,128)(2,1)} %pack.1.refs_0_, bf16[384,896]{1,0:T(8,128)(2,1)} %collective-permute-done.8.refs_1_, bf16[1792,256]{1,0:T(8,128)(2,1)S(1)} %pad_maximum_fusion.refs_2_), custom_call_target="tpu_custom_call" | custom-call | flops 352321536 | bytes 688128 | tf_op jit(solution)/shard_map/expand/pallas_call | solution.py:137
  68.2 13.6 %collective-permute-done.6.refs_0_ = bf16[384,896]{1,0:T(8,128)(2,1)S(1)} collective-permute-done((bf16[384,896]{1,0:T(8,128)(2,1)}, bf16[384,896]{1,0:T(8,128)(2,1)S(1)}, u32[]{:S(2)}, u32[]{:S(2)}) %collective-permute-start.6) | collective-permute-done | bytes 688160 | tf_op jit(solution)/shard_map/ppermute | solution.py:235
  82.8 2.8 %collective-permute-start.9 = (bf16[384,896]{1,0:T(8,128)(2,1)S(1)}, bf16[384,896]{1,0:T(8,128)(2,1)S(1)}, u32[]{:S(2)}, u32[]{:S(2)}) collective-permute-start(bf16[384,896]{1,0:T(8,128)(2,1)S(1)} %broadcast_select_fusion), channel_id=1, source_target_pairs={{0,2},{1,7},{2,4},{3,1},{4,6},{5,3},{6,0},{7,5},{8,10},{9,15},{10,... | collective-permute-start | bytes 2064392 | tf_op jit(solution)/shard_map/ppermute | solution.py:244
  85.7 1.5 expand.5.refs_2_
  87.2 6.3 %collective-permute-done.9.refs_0_ = bf16[384,896]{1,0:T(8,128)(2,1)S(1)} collective-permute-done((bf16[384,896]{1,0:T(8,128)(2,1)S(1)}, bf16[384,896]{1,0:T(8,128)(2,1)S(1)}, u32[]{:S(2)}, u32[]{:S(2)}) %collective-permute-start.9) | collective-permute-done | bytes 688160 | tf_op jit(solution)/shard_map/ppermute | solution.py:244
  93.4 2.1 %collective-permute-start.12 = (bf16[384,896]{1,0:T(8,128)(2,1)S(1)}, bf16[384,896]{1,0:T(8,128)(2,1)S(1)}, u32[]{:S(2)}, u32[]{:S(2)}) collective-permute-start(bf16[384,896]{1,0:T(8,128)(2,1)S(1)} %collective-permute-done.9.refs_0_), channel_id=1, source_target_pairs={{0,1},{1,0},{2,3},{3,2},{4,5},{5,4},{6,7},{7,6},{8,9},{9,8},{10,11... | collective-permute-start | bytes 2064392 | tf_op jit(solution)/shard_map/ppermute | solution.py:235
  95.9 1.4 collective-permute-done.12.refs_0_
  97.8 2.6 %collective-permute-start.14 = (bf16[384,128]{1,0:T(8,128)(2,1)S(1)}, bf16[384,128]{1,0:T(8,128)(2,1)S(1)}, u32[]{:S(2)}, u32[]{:S(2)}) collective-permute-start(bf16[384,128]{1,0:T(8,128)(2,1)S(1)} %expand.7.refs_0_), channel_id=1, source_target_pairs={{0,4},{1,5},{2,6},{3,7},{4,0},{5,1},{6,2},{7,3},{8,12},{9,13},{10,... | collective-permute-start | bytes 294920 | tf_op jit(solution)/shard_map/ppermute | solution.py:235
  100.9 2.1 %collective-permute-done.13.refs_1_ = bf16[384,128]{1,0:T(8,128)(2,1)S(1)} collective-permute-done((bf16[384,128]{1,0:T(8,128)(2,1)S(1)}, bf16[384,128]{1,0:T(8,128)(2,1)S(1)}, u32[]{:S(2)}, u32[]{:S(2)}) %collective-permute-start.13) | collective-permute-done | bytes 98336 | tf_op jit(solution)/shard_map/ppermute | solution.py:235
  103.0 2.0 %collective-permute-done.14.refs_2_ = bf16[384,128]{1,0:T(8,128)(2,1)S(1)} collective-permute-done((bf16[384,128]{1,0:T(8,128)(2,1)S(1)}, bf16[384,128]{1,0:T(8,128)(2,1)S(1)}, u32[]{:S(2)}, u32[]{:S(2)}) %collective-permute-start.14) | collective-permute-done | bytes 98336 | tf_op jit(solution)/shard_map/ppermute | solution.py:235
  105.4 1.6 collective-permute-start.17
  108.4 3.4 %down.1 = bf16[5632,128]{1,0:T(8,128)(2,1)S(1)} custom-call(f32[384,1]{1,0:T(8,128)S(1)} %copy.9.weight_ref, s32[1,384]{1,0:T(1,128)S(1)} %copy-done.5, bf16[384,128]{1,0:T(8,128)(2,1)S(1)} %expand.7.refs_0_, bf16[384,128]{1,0:T(8,128)(2,1)S(1)} %collective-permute-done.13.refs_1_, bf16[384,128]{1,0:T(8,128)(2,1)S(1)} %collective-permute-done.14.refs_2_, ...), custom_call_target="tpu_custom_call" | custom-call | tf_op jit(solution)/shard_map/down/pallas_call | solution.py:175
  111.8 47.5 %all_to_all.10 = bf16[256,11,2,128]{3,2,1,0:T(2,128)(2,1)S(1)} all-to-all(bf16[256,11,2,128]{3,2,1,0:T(2,128)(2,1)S(1)} %bitcast.35), channel_id=1, replica_groups=mesh['node'=32,'x'=4,'core'=2] {'node','x','core'}, dimensions={0} | all-to-all | bytes 2883584 | tf_op jit(solution)/shard_map/all_to_all | solution.py:226
  159.3 2.0 %place.1 = bf16[128,7168]{1,0:T(8,128)(2,1)} custom-call(bf16[96,128]{1,0:T(8,128)(2,1)S(1)} %copy-done.3, bf16[5632,128]{1,0:T(8,128)(2,1)S(1)} %bitcast.34), custom_call_target="tpu_custom_call" | custom-call | tf_op jit(solution)/shard_map/place/pallas_call | solution.py:213
  (61 shorter events, 14.8 us)
Async XLA Ops:
  0.0 107.1 %copy-start = (f32[32,384]{1,0:T(8,128)S(1)}, f32[32,384]{1,0:T(8,128)}, u32[]{:S(2)}) copy-start(f32[32,384]{1,0:T(8,128)} %param.13) | copy-start | bytes 147460
  4.6 15.8 %copy-start.6 = (bf16[1,128,7168]{2,1,0:T(8,128)(2,1)S(1)}, bf16[1,128,7168]{2,1,0:T(8,128)(2,1)}, u32[]{:S(2)}) copy-start(bf16[1,128,7168]{2,1,0:T(8,128)(2,1)} %param.10) | copy-start | bytes 5505028
  4.6 54.6 %all-to-all-start = ((bf16[256,11,2,128]{3,2,1,0:T(2,128)(2,1)}), bf16[256,11,2,128]{3,2,1,0:T(2,128)(2,1)S(1)}, u32[]{:S(2)}, u32[]{:S(2)}) async-start(bf16[256,11,2,128]{3,2,1,0:T(2,128)(2,1)} %bitcast.42), calls=%async_computation | async-start | bytes 2883584 | tf_op jit(solution)/shard_map/all_to_all | solution.py:226
  22.3 12.2 %collective-permute-start = (bf16[2,128,896]{2,1,0:T(8,128)(2,1)}, bf16[2,128,896]{2,1,0:T(8,128)(2,1)}, u32[]{:S(2)}, u32[]{:S(2)}) collective-permute-start(bf16[2,128,896]{2,1,0:T(8,128)(2,1)} %pad_maximum_fusion.4), channel_id=1, source_target_pairs={{0,1},{1,0},{2,3},{3,2},{4,5},{5,4},{6,7},{7,6},{8,9},{9,8},{10,11... | collective-permute-start | bytes 1376264 | tf_op jit(solution)/shard_map/ppermute | solution.py:235
  24.4 37.4 %collective-permute-start.1 = (bf16[1,128,896]{2,1,0:T(8,128)(2,1)}, bf16[1,128,896]{2,1,0:T(8,128)(2,1)}, u32[]{:S(2)}, u32[]{:S(2)}) collective-permute-start(bf16[1,128,896]{2,1,0:T(8,128)(2,1)} %get-tuple-element.57), channel_id=1, source_target_pairs={{0,2},{1,3},{2,4},{3,5},{4,6},{5,7},{6,0},{7,1},{8,10},{9,11},{10,... | collective-permute-start | bytes 688136 | tf_op jit(solution)/shard_map/ppermute | solution.py:235
  24.5 37.4 %collective-permute-start.2 = (bf16[1,128,896]{2,1,0:T(8,128)(2,1)}, bf16[1,128,896]{2,1,0:T(8,128)(2,1)}, u32[]{:S(2)}, u32[]{:S(2)}) collective-permute-start(bf16[1,128,896]{2,1,0:T(8,128)(2,1)} %get-tuple-element.56), channel_id=1, source_target_pairs={{0,3},{1,2},{2,5},{3,4},{4,7},{5,6},{6,1},{7,0},{8,11},{9,10},{10,... | collective-permute-start | bytes 688136 | tf_op jit(solution)/shard_map/ppermute | solution.py:235
  25.6 36.3 %collective-permute-start.3 = (bf16[1,128,896]{2,1,0:T(8,128)(2,1)}, bf16[1,128,896]{2,1,0:T(8,128)(2,1)}, u32[]{:S(2)}, u32[]{:S(2)}) collective-permute-start(bf16[1,128,896]{2,1,0:T(8,128)(2,1)} %get-tuple-element.55), channel_id=1, source_target_pairs={{0,6},{1,7},{2,0},{3,1},{4,2},{5,3},{6,4},{7,5},{8,14},{9,15},{10,... | collective-permute-start | bytes 688136 | tf_op jit(solution)/shard_map/ppermute | solution.py:235
  27.1 34.7 %collective-permute-start.4 = (bf16[1,128,896]{2,1,0:T(8,128)(2,1)}, bf16[1,128,896]{2,1,0:T(8,128)(2,1)}, u32[]{:S(2)}, u32[]{:S(2)}) collective-permute-start(bf16[1,128,896]{2,1,0:T(8,128)(2,1)} %get-tuple-element.54), channel_id=1, source_target_pairs={{0,7},{1,6},{2,1},{3,0},{4,3},{5,2},{6,5},{7,4},{8,15},{9,14},{10,... | collective-permute-start | bytes 688136 | tf_op jit(solution)/shard_map/ppermute | solution.py:235
  36.3 25.6 %collective-permute-start.5 = (bf16[2,128,896]{2,1,0:T(8,128)(2,1)}, bf16[2,128,896]{2,1,0:T(8,128)(2,1)}, u32[]{:S(2)}, u32[]{:S(2)}) collective-permute-start(bf16[2,128,896]{2,1,0:T(8,128)(2,1)} %pad_maximum_fusion.5), channel_id=1, source_target_pairs={{0,4},{1,5},{2,6},{3,7},{4,0},{5,1},{6,2},{7,3},{8,12},{9,13},{10,... | collective-permute-start | bytes 1376264 | tf_op jit(solution)/shard_map/ppermute | solution.py:235
  61.9 4.3 %collective-permute-start.8 = (bf16[384,896]{1,0:T(8,128)(2,1)}, bf16[384,896]{1,0:T(8,128)(2,1)}, u32[]{:S(2)}, u32[]{:S(2)}) collective-permute-start(bf16[384,896]{1,0:T(8,128)(2,1)} %pack.1.refs_0_), channel_id=1, source_target_pairs={{0,1},{1,0},{2,3},{3,2},{4,5},{5,4},{6,7},{7,6},{8,9},{9,8},{10,11... | collective-permute-start | bytes 2064392 | tf_op jit(solution)/shard_map/ppermute | solution.py:235
  63.4 18.4 %collective-permute-start.6 = (bf16[384,896]{1,0:T(8,128)(2,1)}, bf16[384,896]{1,0:T(8,128)(2,1)S(1)}, u32[]{:S(2)}, u32[]{:S(2)}) collective-permute-start(bf16[384,896]{1,0:T(8,128)(2,1)} %pack.1.refs_0_), channel_id=1, source_target_pairs={{0,2},{1,3},{2,4},{3,5},{4,6},{5,7},{6,0},{7,1},{8,10},{9,11},{10,... | collective-permute-start | bytes 2064392 | tf_op jit(solution)/shard_map/ppermute | solution.py:235
  63.6 18.2 %collective-permute-start.7 = (bf16[384,896]{1,0:T(8,128)(2,1)}, bf16[384,896]{1,0:T(8,128)(2,1)S(1)}, u32[]{:S(2)}, u32[]{:S(2)}) collective-permute-start(bf16[384,896]{1,0:T(8,128)(2,1)} %pack.1.refs_0_), channel_id=1, source_target_pairs={{0,6},{1,7},{2,0},{3,1},{4,2},{5,3},{6,4},{7,5},{8,14},{9,15},{10,... | collective-permute-start | bytes 2064392 | tf_op jit(solution)/shard_map/ppermute | solution.py:235
  66.2 19.4 %copy-start.1 = (bf16[1792,256]{1,0:T(8,128)(2,1)S(1)}, bf16[1792,256]{1,0:T(8,128)(2,1)}, u32[]{:S(2)}) copy-start(bf16[1792,256]{1,0:T(8,128)(2,1)} %pad_maximum_fusion.3.refs_5_) | copy-start | bytes 2752516
  66.2 19.4 %copy-start.2 = (bf16[1792,256]{1,0:T(8,128)(2,1)S(1)}, bf16[1792,256]{1,0:T(8,128)(2,1)}, u32[]{:S(2)}) copy-start(bf16[1792,256]{1,0:T(8,128)(2,1)} %pad_maximum_fusion.1.refs_4_) | copy-start | bytes 2752516
  81.9 3.8 %collective-permute-start.10 = (bf16[384,896]{1,0:T(8,128)(2,1)S(1)}, bf16[384,896]{1,0:T(8,128)(2,1)S(1)}, u32[]{:S(2)}, u32[]{:S(2)}) collective-permute-start(bf16[384,896]{1,0:T(8,128)(2,1)S(1)} %collective-permute-done.6.refs_0_), channel_id=1, source_target_pairs={{0,1},{1,0},{2,3},{3,2},{4,5},{5,4},{6,7},{7,6},{8,9},{9,8},{10,11... | collective-permute-start | bytes 2064392 | tf_op jit(solution)/shard_map/ppermute | solution.py:235
  82.7 2.9 %collective-permute-start.11 = (bf16[384,896]{1,0:T(8,128)(2,1)S(1)}, bf16[384,896]{1,0:T(8,128)(2,1)S(1)}, u32[]{:S(2)}, u32[]{:S(2)}) collective-permute-start(bf16[384,896]{1,0:T(8,128)(2,1)S(1)} %collective-permute-done.7.refs_2_), channel_id=1, source_target_pairs={{0,1},{1,0},{2,3},{3,2},{4,5},{5,4},{6,7},{7,6},{8,9},{9,8},{10,11... | collective-permute-start | bytes 2064392 | tf_op jit(solution)/shard_map/ppermute | solution.py:235
  82.8 10.6 %collective-permute-start.9 = (bf16[384,896]{1,0:T(8,128)(2,1)S(1)}, bf16[384,896]{1,0:T(8,128)(2,1)S(1)}, u32[]{:S(2)}, u32[]{:S(2)}) collective-permute-start(bf16[384,896]{1,0:T(8,128)(2,1)S(1)} %broadcast_select_fusion), channel_id=1, source_target_pairs={{0,2},{1,7},{2,4},{3,1},{4,6},{5,3},{6,0},{7,5},{8,10},{9,15},{10,... | collective-permute-start | bytes 2064392 | tf_op jit(solution)/shard_map/ppermute | solution.py:244
  93.4 3.9 %collective-permute-start.12 = (bf16[384,896]{1,0:T(8,128)(2,1)S(1)}, bf16[384,896]{1,0:T(8,128)(2,1)S(1)}, u32[]{:S(2)}, u32[]{:S(2)}) collective-permute-start(bf16[384,896]{1,0:T(8,128)(2,1)S(1)} %collective-permute-done.9.refs_0_), channel_id=1, source_target_pairs={{0,1},{1,0},{2,3},{3,2},{4,5},{5,4},{6,7},{7,6},{8,9},{9,8},{10,11... | collective-permute-start | bytes 2064392 | tf_op jit(solution)/shard_map/ppermute | solution.py:235
  97.7 5.3 %collective-permute-start.13 = (bf16[384,128]{1,0:T(8,128)(2,1)S(1)}, bf16[384,128]{1,0:T(8,128)(2,1)S(1)}, u32[]{:S(2)}, u32[]{:S(2)}) collective-permute-start(bf16[384,128]{1,0:T(8,128)(2,1)S(1)} %expand.7.refs_0_), channel_id=1, source_target_pairs={{0,2},{1,3},{2,4},{3,5},{4,6},{5,7},{6,0},{7,1},{8,10},{9,11},{10,... | collective-permute-start | bytes 294920 | tf_op jit(solution)/shard_map/ppermute | solution.py:235
  97.8 7.3 %collective-permute-start.14 = (bf16[384,128]{1,0:T(8,128)(2,1)S(1)}, bf16[384,128]{1,0:T(8,128)(2,1)S(1)}, u32[]{:S(2)}, u32[]{:S(2)}) collective-permute-start(bf16[384,128]{1,0:T(8,128)(2,1)S(1)} %expand.7.refs_0_), channel_id=1, source_target_pairs={{0,4},{1,5},{2,6},{3,7},{4,0},{5,1},{6,2},{7,3},{8,12},{9,13},{10,... | collective-permute-start | bytes 294920 | tf_op jit(solution)/shard_map/ppermute | solution.py:235
  100.4 4.9 %collective-permute-start.15 = (bf16[384,128]{1,0:T(8,128)(2,1)S(1)}, bf16[384,128]{1,0:T(8,128)(2,1)S(1)}, u32[]{:S(2)}, u32[]{:S(2)}) collective-permute-start(bf16[384,128]{1,0:T(8,128)(2,1)S(1)} %expand.7.refs_0_), channel_id=1, source_target_pairs={{0,6},{1,7},{2,0},{3,1},{4,2},{5,3},{6,4},{7,5},{8,14},{9,15},{10,... | collective-permute-start | bytes 294920 | tf_op jit(solution)/shard_map/ppermute | solution.py:235
  105.4 3.0 %collective-permute-start.17 = (bf16[3,384,128]{2,1,0:T(8,128)(2,1)S(1)}, bf16[3,384,128]{2,1,0:T(8,128)(2,1)S(1)}, u32[]{:S(2)}, u32[]{:S(2)}) collective-permute-start(bf16[3,384,128]{2,1,0:T(8,128)(2,1)S(1)} %pad_maximum_fusion.6), channel_id=1, source_target_pairs={{0,1},{1,0},{2,3},{3,2},{4,5},{5,4},{6,7},{7,6},{8,9},{9,8},{10,11... | collective-permute-start | bytes 884744 | tf_op jit(solution)/shard_map/ppermute | solution.py:235
  107.0 1.3 collective-permute-start.16
  111.8 47.5 %copy-start.3 = (bf16[96,128]{1,0:T(8,128)(2,1)S(1)}, bf16[96,128]{1,0:T(8,128)(2,1)}, u32[]{:S(2)}) copy-start(bf16[96,128]{1,0:T(8,128)(2,1)} %get-tuple-element.28.sel_ref) | copy-start | bytes 73732
  (4 other events, 17.4 us)
